TPU v7x, 128 devices: a whole 4x4x4 slice. The times are simulated.
128 devices in a mesh: ent: 8 (over z, x_lo), qry: 16 (over y, x_hi, core).
Axes of the slice: x: 4 (x_hi: 2, x_lo: 2; x = x_hi * 2 + x_lo), y: 4, z: 4, core: 2. Of those that a mesh axis runs over, the one named last changes fastest.
Arguments:
- anchor_ids: int32 [16384, 20], P(('ent', 'qry')), may hold values from 0 to 19999
- relation_ids: int32 [16384, 5], P(('ent', 'qry')), may hold values from 0 to 821
- head_anchors: int32 [65536, 20], P(('ent', 'qry')), may hold values from 0 to 19999
- head_relations: int32 [65536, 5], P(('ent', 'qry')), may hold values from 0 to 821
- query_relation: int32 [65536], P(('ent', 'qry')), may hold values from 0 to 821
- targets: int32 [65536, 4], P(('ent', 'qry')), may hold values from 0 to 16383
- anchor_table: bfloat16 [20000, 200], replicated, may hold values from -6 to 6
- relation_table: bfloat16 [822, 200], replicated, may hold values from -6 to 6
- enc_weight: bfloat16 [5000, 200], replicated, may hold values from -0.078125 to 0.078125
- fc_weight: bfloat16 [200, 200], replicated, may hold values from -0.4375 to 0.4375
Outputs:
- entity_grad: float32 [200, 16384], P(None, ('ent', 'qry'))
- query_grad: float32 [65536, 200], P(('ent', 'qry'))
All inputs are finite; a program needn't handle non-finite values.
Results may differ from a plain program's by a relative error of at most 0.019.
Values may be sent and summed in bfloat16 or wider, within the bound.
No kernel may reach another device: no remote copies, remote signals or barrier semaphores. Data moves between devices by JAX's collectives and lax.ppermute only.
A program may use at most 128 MiB of HBM per device.

v0:
```python
import math

import jax
import jax.numpy as jnp
from jax import lax
from jax.experimental import pallas as pl
from jax.experimental.pallas import tpu as pltpu
from jax.sharding import PartitionSpec as P

AXES = ("ent", "qry")
BF16 = jnp.bfloat16
F32 = jnp.float32


def flat_of(x, y, z, core):
    return z * 32 + (x % 2) * 16 + y * 4 + (x // 2) * 2 + core


def coords_of(flat):
    x = ((flat // 2) % 2) * 2 + (flat // 16) % 2
    return x, (flat // 4) % 4, flat // 32, flat % 2


def moved(block, dx=0, dy=0, dz=0, dcore=0):
    route = []
    for to in range(128):
        x, y, z, core = coords_of(to)
        route.append((flat_of((x + dx) % 4, (y + dy) % 4, (z + dz) % 4, (core + dcore) % 2), to))
    return lax.ppermute(block, AXES, route)


def place():
    ent, qry = lax.axis_index("ent"), lax.axis_index("qry")
    return coords_of(ent * 16 + qry)


LANES = 128
CHUNK = 2048
UNROLL = 32


def gather_rows(ids, table, rows, count):
    def some(step, carry):
        first = step * UNROLL
        picked = [table[pl.ds(ids[first + k], 2), :] for k in range(UNROLL)]
        for k in range(UNROLL):
            rows[pl.ds(pl.multiple_of(first * 2, 2 * UNROLL) + 2 * k, 2), :] = picked[k]
        return carry

    lax.fori_loop(0, count // UNROLL, some, 0)


def encoded(anchors, rel_ids, weights, rel_table, rows, width):
    n_rel = rel_ids.shape[0]
    total = jnp.zeros((weights.shape[0], width), F32)
    for t in range(anchors):
        halves = [rows[pl.ds(t * 2 * width + h, width, stride=2), :] for h in range(2)]
        part = jnp.concatenate(halves, axis=1).astype(BF16)
        total = total + lax.dot_general(
            weights[:, t * 256 : (t + 1) * 256], part, (((1,), (1,)), ((), ())),
            preferred_element_type=F32,
        )
    for t in range(n_rel):
        part = relation_rows(rel_ids[t : t + 1, :], rel_table).astype(BF16)
        first = (anchors + t) * 256
        total = total + jnp.dot(weights[:, first : first + 256], part, preferred_element_type=F32)
    return total.astype(BF16)


def relation_rows(ids, rel_table):
    shape = (rel_table.shape[1], ids.shape[1])
    hot = lax.broadcasted_iota(jnp.int32, shape, 0) == jnp.broadcast_to(ids, shape)
    hot = jnp.where(hot, 1.0, 0.0).astype(BF16)
    return jnp.dot(rel_table[...], hot, preferred_element_type=F32)


def encode_kernel(
    own_ids, head_ids, tab_t, w_t, rel_table, own_rel, head_rel, asked, fc_t,
    own_out, query_out, table, rows, weights,
):
    step = pl.program_id(0)
    depth = tab_t.shape[0]
    tokens = weights.shape[1] // 256

    @pl.when(step == 0)
    def _():
        lane = lax.broadcasted_iota(jnp.int32, (depth, 256), 1)
        for t in range(tokens):
            start = t * depth
            base = start // LANES * LANES
            piece = w_t[:, base : base + 384].astype(F32)
            if start > base:
                piece = pltpu.roll(piece, 384 - (start - base), 1)
            weights[:, t * 256 : (t + 1) * 256] = jnp.where(
                lane < depth, piece[:, :256], 0.0
            ).astype(BF16)

    top = tab_t[:LANES, :].astype(F32).T
    rest = jnp.concatenate(
        [tab_t[LANES:, :].astype(F32), jnp.zeros((2 * LANES - depth, CHUNK), F32)], axis=0
    ).T
    table[pl.ds(step * 2 * CHUNK, CHUNK, stride=2), :] = top
    table[pl.ds(step * 2 * CHUNK + 1, CHUNK, stride=2), :] = rest

    @pl.when(step == pl.num_programs(0) - 1)
    def _():
        anchors = tokens - own_rel.shape[0]
        gather_rows(own_ids, table, rows, own_ids.shape[0])
        own_out[...] = encoded(anchors, own_rel, weights, rel_table, rows, own_rel.shape[1])
        gather_rows(head_ids, table, rows, head_ids.shape[0])
        head = encoded(anchors, head_rel, weights, rel_table, rows, head_rel.shape[1])
        mixed = head.astype(F32) * relation_rows(asked[...], rel_table)[:depth, :]
        query_out[...] = jnp.tanh(
            jnp.dot(fc_t[...], mixed.astype(BF16), preferred_element_type=F32)
        ).astype(BF16)


def encode_all(anchor_ids, relation_ids, head_anchors, head_relations, query_relation,
               anchor_table, relation_table, enc_weight, fc_weight):
    own, anchors = anchor_ids.shape
    heads = head_anchors.shape[0]
    depth = anchor_table.shape[1]
    steps = pl.cdiv(anchor_table.shape[0], CHUNK)
    tokens = anchors + relation_ids.shape[1]
    rels = pl.cdiv(relation_table.shape[0], LANES) * LANES
    rel_table = jnp.pad(
        relation_table.T, ((0, 256 - depth), (0, rels - relation_table.shape[0]))
    )
    w_lanes = pl.cdiv(tokens * depth + 256, LANES) * LANES
    whole = pl.BlockSpec(memory_space=pltpu.VMEM)
    smem = pl.BlockSpec(memory_space=pltpu.SMEM)
    return pl.pallas_call(
        encode_kernel,
        grid=(steps,),
        in_specs=[
            smem, smem,
            pl.BlockSpec((depth, CHUNK), lambda i: (0, i)),
            whole, whole, whole, whole, whole, whole,
        ],
        out_specs=[whole, whole],
        out_shape=[
            jax.ShapeDtypeStruct((depth, own), BF16),
            jax.ShapeDtypeStruct((depth, heads), BF16),
        ],
        scratch_shapes=[
            pltpu.VMEM((2 * steps * CHUNK, LANES), F32),
            pltpu.VMEM((2 * heads * anchors, LANES), F32),
            pltpu.VMEM((depth, tokens * 256), BF16),
        ],
        compiler_params=pltpu.CompilerParams(vmem_limit_bytes=56 * 1024 * 1024),
    )(
        (anchor_ids.T * 2).reshape(-1), (head_anchors.T * 2).reshape(-1),
        anchor_table.T, jnp.pad(enc_weight.T, ((0, 0), (0, w_lanes - tokens * depth))),
        rel_table, relation_ids.T, head_relations.T, query_relation[None, :], fc_weight.T,
    )


def score_terms(query, chosen, slab, ident, total_entities):
    scores = lax.dot_general(
        query, slab, (((0,), (0,)), ((), ())), preferred_element_type=F32
    ) * float(slab.shape[0]) ** (-0.5)
    struck = jnp.zeros(scores.shape, jnp.bool_)
    for k in range(chosen.shape[0]):
        struck = struck | (chosen[k][:, None] == ident[None, :])
    floor_label = 0.1 / total_entities
    labels = jnp.where(struck, 0.9 + floor_label, floor_label)
    residual = (jax.nn.sigmoid(scores) - labels).astype(BF16)
    ent_part = jnp.dot(query, residual, preferred_element_type=F32)
    query_part = lax.dot_general(
        slab, residual, (((1,), (1,)), ((), ())), preferred_element_type=F32
    )
    return (ent_part, query_part)


FAR = (1, 3, 2)


def body(
    anchor_ids,
    relation_ids,
    head_anchors,
    head_relations,
    query_relation,
    targets,
    anchor_table,
    relation_table,
    enc_weight,
    fc_weight,
):
    total = 128
    entities = anchor_ids.shape[0] * total
    queries = head_anchors.shape[0] * total
    x, y, z, core = place()
    wanted = targets.T
    wanted = jnp.concatenate([wanted, moved(wanted, dcore=1)], axis=1)
    wanted = [wanted] + [moved(wanted, dz=d) for d in FAR]
    own_cols, query = encode_all(
        anchor_ids,
        relation_ids,
        head_anchors,
        head_relations,
        query_relation,
        anchor_table,
        relation_table,
        enc_weight,
        fc_weight,
    )
    width = own_cols.shape[1]
    row = jnp.concatenate([own_cols] + [moved(own_cols, dx=d) for d in FAR], axis=1)
    slab = jnp.concatenate([row] + [moved(row, dy=d) for d in FAR], axis=1)
    within = jnp.arange(width, dtype=jnp.int32)
    ident = jnp.concatenate(
        [
            flat_of((x + dx) % 4, (y + dy) % 4, z, core) * width + within
            for dy in (0,) + FAR
            for dx in (0,) + FAR
        ]
    )
    far = [moved(query, dz=d) for d in FAR]
    pairs = [jnp.concatenate([q, moved(q, dcore=1)], axis=1) for q in [query] + far]
    count = query.shape[1]
    ent_total = jnp.zeros(slab.shape, F32)
    kept = []
    for k in (1, 2, 3, 0):
        ent_part, query_part = score_terms(pairs[k], wanted[k], slab, ident, entities)
        ent_total = ent_total + ent_part
        away = query_part[:, count:].astype(BF16)
        mine = query_part[:, :count] + moved(away, dcore=1).astype(F32)
        if k:
            mine = moved(mine.astype(BF16), dz=-FAR[k - 1]).astype(F32)
        kept.append(mine)
    query_total = kept[3] + kept[0] + kept[1] + kept[2]
    w4 = 4 * width
    ent_row = ent_total[:, :w4]
    for k, d in enumerate(FAR):
        block = ent_total[:, (k + 1) * w4 : (k + 2) * w4].astype(BF16)
        ent_row = ent_row + moved(block, dy=-d).astype(F32)
    ent_share = ent_row[:, :width]
    for k, d in enumerate(FAR):
        block = ent_row[:, (k + 1) * width : (k + 2) * width].astype(BF16)
        ent_share = ent_share + moved(block, dx=-d).astype(F32)
    return (ent_share / math.sqrt(queries), query_total.T / math.sqrt(entities))


def solution(mesh):
    spread = P(AXES, None)
    placed = (spread, spread, spread, spread, P(AXES), spread, P(), P(), P(), P())
    return jax.shard_map(
        body,
        mesh=mesh,
        in_specs=placed,
        out_specs=(P(None, AXES), spread),
        check_vma=False,
    )
```

profile of v0, /device:TPU:0, one launch (start us, length us, event | category | flops | bytes accessed | tf_op | source)
XLA Modules:
  0.0 142.0 jit_solution(8339661529211532007)
XLA Ops:
  5.0 1.8 %pad.9.rel_table = bf16[256,896]{1,0:T(8,128)(2,1)} pad(bf16[200,822]{1,0:T(8,128)(2,1)} %bitcast.59, bf16[]{:T(256)} %constant.256.clone.1), padding=0_56x0_74 | pad | bytes 787554 | tf_op jit(solution)/shard_map/jit(_pad)/pad | solution.py:126
  6.8 3.1 %pad.8.w_t = bf16[200,5376]{1,0:T(8,128)(2,1)} pad(bf16[200,5000]{1,0:T(8,128)(2,1)} %bitcast.57, bf16[]{:T(256)} %constant.256.clone.1), padding=0_0x0_376 | pad | bytes 4150402 | tf_op jit(solution)/shard_map/jit(_pad)/pad | solution.py:153
  9.9 29.7 %shard_map.113 = (bf16[200,128]{1,0:T(8,128)(2,1)}, bf16[200,512]{1,0:T(8,128)(2,1)}) custom-call(s32[2560]{0:T(1024)} %multiply_bitcast_fusion.1.own_ids, s32[10240]{0:T(1024)} %reshape.28.head_ids, bf16[200,20000]{1,0:T(8,128)(2,1)} %bitcast.56, bf16[200,5376]{1,0:T(8,128)(2,1)} %pad.8.w_t, bf16[256,896]{1,0:T(8,128)(2,1)} %pad.9.rel_table, ...), custom_call_target="tpu_custom_call" | custom-call | tf_op jit(solution)/shard_map/pallas_call | solution.py:132
  39.5 3.1 %collective-permute-start.4 = (bf16[200,128]{1,0:T(8,128)(2,1)}, bf16[200,128]{1,0:T(8,128)(2,1)S(1)}, u32[]{:S(2)}, u32[]{:S(2)}) collective-permute-start(bf16[200,128]{1,0:T(8,128)(2,1)} %get-tuple-element.5), channel_id=1, source_target_pairs={{2,0},{3,1},{0,2},{1,3},{6,4},{7,5},{4,6},{5,7},{10,8},{11,9},{8,1... | collective-permute-start | bytes 153608 | tf_op jit(solution)/shard_map/ppermute | solution.py:29
  43.2 2.6 %collective-permute-start.2 = (bf16[200,128]{1,0:T(8,128)(2,1)}, bf16[200,128]{1,0:T(8,128)(2,1)S(1)}, u32[]{:S(2)}, u32[]{:S(2)}) collective-permute-start(bf16[200,128]{1,0:T(8,128)(2,1)} %get-tuple-element.5), channel_id=1, source_target_pairs={{16,0},{17,1},{18,2},{19,3},{20,4},{21,5},{22,6},{23,7},{24,8},{25... | collective-permute-start | bytes 153608 | tf_op jit(solution)/shard_map/ppermute | solution.py:29
  48.5 4.0 %collective-permute-start.15 = (s32[4,1024]{1,0:T(4,128)S(1)}, s32[4,1024]{1,0:T(4,128)S(1)}, u32[]{:S(2)}, u32[]{:S(2)}) collective-permute-start(s32[4,1024]{1,0:T(4,128)S(1)} %pad_add_fusion), channel_id=1, source_target_pairs={{64,0},{65,1},{66,2},{67,3},{68,4},{69,5},{70,6},{71,7},{72,8},{73... | collective-permute-start | bytes 49160 | tf_op jit(solution)/shard_map/ppermute | solution.py:29
  55.8 3.8 %collective-permute-done.12 = s32[4,1024]{1,0:T(4,128)S(1)} collective-permute-done((s32[4,1024]{1,0:T(4,128)S(1)}, s32[4,1024]{1,0:T(4,128)S(1)}, u32[]{:S(2)}, u32[]{:S(2)}) %collective-permute-start.12) | collective-permute-done | bytes 16416 | tf_op jit(solution)/shard_map/ppermute | solution.py:29
  59.6 2.0 %collective-permute-start.9 = (s32[4,1024]{1,0:T(4,128)S(1)}, s32[4,1024]{1,0:T(4,128)S(1)}, u32[]{:S(2)}, u32[]{:S(2)}) collective-permute-start(s32[4,1024]{1,0:T(4,128)S(1)} %pad_add_fusion), channel_id=1, source_target_pairs={{32,0},{33,1},{34,2},{35,3},{36,4},{37,5},{38,6},{39,7},{40,8},{41... | collective-permute-start | bytes 49160 | tf_op jit(solution)/shard_map/ppermute | solution.py:29
  63.4 1.9 %collective-permute-start.13 = (bf16[200,512]{1,0:T(8,128)(2,1)}, bf16[200,512]{1,0:T(8,128)(2,1)S(1)}, u32[]{:S(2)}, u32[]{:S(2)}) collective-permute-start(bf16[200,512]{1,0:T(8,128)(2,1)} %get-tuple-element.4), channel_id=1, source_target_pairs={{64,0},{65,1},{66,2},{67,3},{68,4},{69,5},{70,6},{71,7},{72,8},{73... | collective-permute-start | bytes 614408 | tf_op jit(solution)/shard_map/ppermute | solution.py:29
  65.3 2.3 %collective-permute-start.10 = (bf16[200,512]{1,0:T(8,128)(2,1)}, bf16[200,512]{1,0:T(8,128)(2,1)S(1)}, u32[]{:S(2)}, u32[]{:S(2)}) collective-permute-start(bf16[200,512]{1,0:T(8,128)(2,1)} %get-tuple-element.4), channel_id=1, source_target_pairs={{96,0},{97,1},{98,2},{99,3},{100,4},{101,5},{102,6},{103,7},{104,8... | collective-permute-start | bytes 614408 | tf_op jit(solution)/shard_map/ppermute | solution.py:29
  68.8 3.3 %collective-permute-start.7 = (bf16[200,512]{1,0:T(8,128)(2,1)S(1)}, bf16[200,512]{1,0:T(8,128)(2,1)S(1)}, u32[]{:S(2)}, u32[]{:S(2)}) collective-permute-start(bf16[200,512]{1,0:T(8,128)(2,1)S(1)} %get-tuple-element.14), channel_id=1, source_target_pairs={{8,0},{9,1},{10,2},{11,3},{12,4},{13,5},{14,6},{15,7},{0,8},{1,9},... | collective-permute-start | bytes 614408 | tf_op jit(solution)/shard_map/ppermute | solution.py:29
  75.2 1.9 %collective-permute-start.5 = (bf16[200,512]{1,0:T(8,128)(2,1)S(1)}, bf16[200,512]{1,0:T(8,128)(2,1)S(1)}, u32[]{:S(2)}, u32[]{:S(2)}) collective-permute-start(bf16[200,512]{1,0:T(8,128)(2,1)S(1)} %get-tuple-element.14), channel_id=1, source_target_pairs={{4,0},{5,1},{6,2},{7,3},{8,4},{9,5},{10,6},{11,7},{12,8},{13,9},{1... | collective-permute-start | bytes 614408 | tf_op jit(solution)/shard_map/ppermute | solution.py:29
  77.9 3.3 %collective-permute-done.5 = bf16[200,512]{1,0:T(8,128)(2,1)S(1)} collective-permute-done((bf16[200,512]{1,0:T(8,128)(2,1)S(1)}, bf16[200,512]{1,0:T(8,128)(2,1)S(1)}, u32[]{:S(2)}, u32[]{:S(2)}) %collective-permute-start.5) | collective-permute-done | bytes 204832 | tf_op jit(solution)/shard_map/ppermute | solution.py:29
  81.3 4.5 %subtract_convert_fusion = bf16[1024,2048]{1,0:T(8,128)(2,1)S(1)} fusion(bf16[200,1024]{1,0:T(8,128)(2,1)S(1)} %constant_dynamic-update-slice_fusion.18, bf16[200,2048]{1,0:T(8,128)(2,1)S(1)} %constant_dynamic-update-slice_fusion.6, s32[2048]{0:T(1024)S(1)} %constant_dynamic-update-slice_fusion.26, s32[1024]{0:T(1024)S(1)} %bitcast.80, s32[1024]{0:T(1024)S(1)} %bitcast.79, ...), kind=kOutput, calls=%fused_computation | convolution fusion | flops 868220928 | bytes 5447680 | tf_op jit(solution)/shard_map/dot_general | solution.py:159
  89.0 4.4 %subtract_convert_fusion.1 = bf16[1024,2048]{1,0:T(8,128)(2,1)S(1)} fusion(bf16[200,1024]{1,0:T(8,128)(2,1)S(1)} %constant_dynamic-update-slice_fusion.16, bf16[200,2048]{1,0:T(8,128)(2,1)S(1)} %constant_dynamic-update-slice_fusion.6, s32[2048]{0:T(1024)S(1)} %constant_dynamic-update-slice_fusion.26, s32[1024]{0:T(1024)S(1)} %bitcast.74, ...), kind=kOutput, calls=%fused_computation.1 | convolution fusion | flops 868220928 | bytes 5447680 | tf_op jit(solution)/shard_map/dot_general | solution.py:159
  96.2 4.4 %subtract_convert_fusion.2 = bf16[1024,2048]{1,0:T(8,128)(2,1)S(1)} fusion(bf16[200,1024]{1,0:T(8,128)(2,1)S(1)} %constant_dynamic-update-slice_fusion.14, bf16[200,2048]{1,0:T(8,128)(2,1)S(1)} %constant_dynamic-update-slice_fusion.6, s32[2048]{0:T(1024)S(1)} %constant_dynamic-update-slice_fusion.26, s32[1024]{0:T(1024)S(1)} %bitcast.70, ...), kind=kOutput, calls=%fused_computation.2 | convolution fusion | flops 868220928 | bytes 5447680 | tf_op jit(solution)/shard_map/dot_general | solution.py:159
  104.1 4.4 %subtract_convert_fusion.3 = bf16[1024,2048]{1,0:T(8,128)(2,1)S(1)} fusion(bf16[200,1024]{1,0:T(8,128)(2,1)S(1)} %constant_dynamic-update-slice_fusion, bf16[200,2048]{1,0:T(8,128)(2,1)S(1)} %constant_dynamic-update-slice_fusion.6, s32[2048]{0:T(1024)S(1)} %constant_dynamic-update-slice_fusion.26, s32[1024]{0:T(1024)S(1)} %bitcast.66, ...), kind=kOutput, calls=%fused_computation.3 | convolution fusion | flops 868220928 | bytes 5447680 | tf_op jit(solution)/shard_map/dot_general | solution.py:159
  113.0 2.8 %collective-permute-start.19 = (bf16[200,512]{1,0:T(8,128)(2,1)S(1)}, bf16[200,512]{1,0:T(8,128)(2,1)S(1)}, u32[]{:S(2)}, u32[]{:S(2)}) collective-permute-start(bf16[200,512]{1,0:T(8,128)(2,1)S(1)} %get-tuple-element.9), channel_id=1, source_target_pairs={{8,0},{9,1},{10,2},{11,3},{12,4},{13,5},{14,6},{15,7},{0,8},{1,9},... | collective-permute-start | bytes 614408 | tf_op jit(solution)/shard_map/ppermute | solution.py:29
  117.0 2.6 %collective-permute-done.17 = bf16[200,512]{1,0:T(8,128)(2,1)S(1)} collective-permute-done((bf16[200,512]{1,0:T(8,128)(2,1)S(1)}, bf16[200,512]{1,0:T(8,128)(2,1)S(1)}, u32[]{:S(2)}, u32[]{:S(2)}) %collective-permute-start.17) | collective-permute-done | bytes 204832 | tf_op jit(solution)/shard_map/ppermute | solution.py:29
  119.6 5.5 %collective-permute-done.19 = bf16[200,512]{1,0:T(8,128)(2,1)S(1)} collective-permute-done((bf16[200,512]{1,0:T(8,128)(2,1)S(1)}, bf16[200,512]{1,0:T(8,128)(2,1)S(1)}, u32[]{:S(2)}, u32[]{:S(2)}) %collective-permute-start.19) | collective-permute-done | bytes 204832 | tf_op jit(solution)/shard_map/ppermute | solution.py:29
  129.6 2.5 %collective-permute-done.20 = bf16[200,128]{1,0:T(8,128)(2,1)S(1)} collective-permute-done((bf16[200,128]{1,0:T(8,128)(2,1)S(1)}, bf16[200,128]{1,0:T(8,128)(2,1)S(1)}, u32[]{:S(2)}, u32[]{:S(2)}) %collective-permute-start.20) | collective-permute-done | bytes 51232 | tf_op jit(solution)/shard_map/ppermute | solution.py:29
  132.1 2.1 %collective-permute-start.27 = (bf16[200,512]{1,0:T(8,128)(2,1)S(1)}, bf16[200,512]{1,0:T(8,128)(2,1)S(1)}, u32[]{:S(2)}, u32[]{:S(2)}) collective-permute-start(bf16[200,512]{1,0:T(8,128)(2,1)S(1)} %fusion.3), channel_id=1, source_target_pairs={{32,0},{33,1},{34,2},{35,3},{36,4},{37,5},{38,6},{39,7},{40,8},{41... | collective-permute-start | bytes 614408 | tf_op jit(solution)/shard_map/ppermute | solution.py:29
  135.4 3.0 %collective-permute-done.27 = bf16[200,512]{1,0:T(8,128)(2,1)S(1)} collective-permute-done((bf16[200,512]{1,0:T(8,128)(2,1)S(1)}, bf16[200,512]{1,0:T(8,128)(2,1)S(1)}, u32[]{:S(2)}, u32[]{:S(2)}) %collective-permute-start.27) | collective-permute-done | bytes 204832 | tf_op jit(solution)/shard_map/ppermute | solution.py:29
  138.5 2.6 %collective-permute-done.25 = bf16[200,512]{1,0:T(8,128)(2,1)S(1)} collective-permute-done((bf16[200,512]{1,0:T(8,128)(2,1)S(1)}, bf16[200,512]{1,0:T(8,128)(2,1)S(1)}, u32[]{:S(2)}, u32[]{:S(2)}) %collective-permute-start.25) | collective-permute-done | bytes 204832 | tf_op jit(solution)/shard_map/ppermute | solution.py:29
  (106 shorter events, 39.2 us)
Async XLA Ops:
  39.5 29.2 %collective-permute-start.4 = (bf16[200,128]{1,0:T(8,128)(2,1)}, bf16[200,128]{1,0:T(8,128)(2,1)S(1)}, u32[]{:S(2)}, u32[]{:S(2)}) collective-permute-start(bf16[200,128]{1,0:T(8,128)(2,1)} %get-tuple-element.5), channel_id=1, source_target_pairs={{2,0},{3,1},{0,2},{1,3},{6,4},{7,5},{4,6},{5,7},{10,8},{11,9},{8,1... | collective-permute-start | bytes 153608 | tf_op jit(solution)/shard_map/ppermute | solution.py:29
  42.6 25.0 %collective-permute-start.3 = (bf16[200,128]{1,0:T(8,128)(2,1)}, bf16[200,128]{1,0:T(8,128)(2,1)S(1)}, u32[]{:S(2)}, u32[]{:S(2)}) collective-permute-start(bf16[200,128]{1,0:T(8,128)(2,1)} %get-tuple-element.5), channel_id=1, source_target_pairs={{18,0},{19,1},{16,2},{17,3},{22,4},{23,5},{20,6},{21,7},{26,8},{27... | collective-permute-start | bytes 153608 | tf_op jit(solution)/shard_map/ppermute | solution.py:29
  43.2 22.0 %collective-permute-start.2 = (bf16[200,128]{1,0:T(8,128)(2,1)}, bf16[200,128]{1,0:T(8,128)(2,1)S(1)}, u32[]{:S(2)}, u32[]{:S(2)}) collective-permute-start(bf16[200,128]{1,0:T(8,128)(2,1)} %get-tuple-element.5), channel_id=1, source_target_pairs={{16,0},{17,1},{18,2},{19,3},{20,4},{21,5},{22,6},{23,7},{24,8},{25... | collective-permute-start | bytes 153608 | tf_op jit(solution)/shard_map/ppermute | solution.py:29
  45.9 31.4 %collective-permute-start.16 = (bf16[200,512]{1,0:T(8,128)(2,1)}, bf16[200,512]{1,0:T(8,128)(2,1)S(1)}, u32[]{:S(2)}, u32[]{:S(2)}) collective-permute-start(bf16[200,512]{1,0:T(8,128)(2,1)} %get-tuple-element.4), channel_id=1, source_target_pairs={{1,0},{0,1},{3,2},{2,3},{5,4},{4,5},{7,6},{6,7},{9,8},{8,9},{11,10... | collective-permute-start | bytes 614408 | tf_op jit(solution)/shard_map/ppermute | solution.py:29
  63.4 11.9 %collective-permute-start.13 = (bf16[200,512]{1,0:T(8,128)(2,1)}, bf16[200,512]{1,0:T(8,128)(2,1)S(1)}, u32[]{:S(2)}, u32[]{:S(2)}) collective-permute-start(bf16[200,512]{1,0:T(8,128)(2,1)} %get-tuple-element.4), channel_id=1, source_target_pairs={{64,0},{65,1},{66,2},{67,3},{68,4},{69,5},{70,6},{71,7},{72,8},{73... | collective-permute-start | bytes 614408 | tf_op jit(solution)/shard_map/ppermute | solution.py:29
  65.3 11.9 %collective-permute-start.10 = (bf16[200,512]{1,0:T(8,128)(2,1)}, bf16[200,512]{1,0:T(8,128)(2,1)S(1)}, u32[]{:S(2)}, u32[]{:S(2)}) collective-permute-start(bf16[200,512]{1,0:T(8,128)(2,1)} %get-tuple-element.4), channel_id=1, source_target_pairs={{96,0},{97,1},{98,2},{99,3},{100,4},{101,5},{102,6},{103,7},{104,8... | collective-permute-start | bytes 614408 | tf_op jit(solution)/shard_map/ppermute | solution.py:29
  67.6 6.0 %collective-permute-start = (bf16[200,512]{1,0:T(8,128)(2,1)}, bf16[200,512]{1,0:T(8,128)(2,1)S(1)}, u32[]{:S(2)}, u32[]{:S(2)}) collective-permute-start(bf16[200,512]{1,0:T(8,128)(2,1)} %get-tuple-element.4), channel_id=1, source_target_pairs={{32,0},{33,1},{34,2},{35,3},{36,4},{37,5},{38,6},{39,7},{40,8},{41... | collective-permute-start | bytes 614408 | tf_op jit(solution)/shard_map/ppermute | solution.py:29
  68.8 12.6 %collective-permute-start.7 = (bf16[200,512]{1,0:T(8,128)(2,1)S(1)}, bf16[200,512]{1,0:T(8,128)(2,1)S(1)}, u32[]{:S(2)}, u32[]{:S(2)}) collective-permute-start(bf16[200,512]{1,0:T(8,128)(2,1)S(1)} %get-tuple-element.14), channel_id=1, source_target_pairs={{8,0},{9,1},{10,2},{11,3},{12,4},{13,5},{14,6},{15,7},{0,8},{1,9},... | collective-permute-start | bytes 614408 | tf_op jit(solution)/shard_map/ppermute | solution.py:29
  73.6 7.6 %collective-permute-start.6 = (bf16[200,512]{1,0:T(8,128)(2,1)S(1)}, bf16[200,512]{1,0:T(8,128)(2,1)S(1)}, u32[]{:S(2)}, u32[]{:S(2)}) collective-permute-start(bf16[200,512]{1,0:T(8,128)(2,1)S(1)} %get-tuple-element.14), channel_id=1, source_target_pairs={{12,0},{13,1},{14,2},{15,3},{0,4},{1,5},{2,6},{3,7},{4,8},{5,9},{6... | collective-permute-start | bytes 614408 | tf_op jit(solution)/shard_map/ppermute | solution.py:29
  77.2 11.8 %collective-permute-start.14 = (bf16[200,512]{1,0:T(8,128)(2,1)S(1)}, bf16[200,512]{1,0:T(8,128)(2,1)S(1)}, u32[]{:S(2)}, u32[]{:S(2)}) collective-permute-start(bf16[200,512]{1,0:T(8,128)(2,1)S(1)} %collective-permute-done.13), channel_id=1, source_target_pairs={{1,0},{0,1},{3,2},{2,3},{5,4},{4,5},{7,6},{6,7},{9,8},{8,9},{11,10... | collective-permute-start | bytes 614408 | tf_op jit(solution)/shard_map/ppermute | solution.py:29
  77.3 18.9 %collective-permute-start.11 = (bf16[200,512]{1,0:T(8,128)(2,1)S(1)}, bf16[200,512]{1,0:T(8,128)(2,1)S(1)}, u32[]{:S(2)}, u32[]{:S(2)}) collective-permute-start(bf16[200,512]{1,0:T(8,128)(2,1)S(1)} %collective-permute-done.10), channel_id=1, source_target_pairs={{1,0},{0,1},{3,2},{2,3},{5,4},{4,5},{7,6},{6,7},{9,8},{8,9},{11,10... | collective-permute-start | bytes 614408 | tf_op jit(solution)/shard_map/ppermute | solution.py:29
  81.2 22.8 %collective-permute-start.1 = (bf16[200,512]{1,0:T(8,128)(2,1)S(1)}, bf16[200,512]{1,0:T(8,128)(2,1)S(1)}, u32[]{:S(2)}, u32[]{:S(2)}) collective-permute-start(bf16[200,512]{1,0:T(8,128)(2,1)S(1)} %collective-permute-done), channel_id=1, source_target_pairs={{1,0},{0,1},{3,2},{2,3},{5,4},{4,5},{7,6},{6,7},{9,8},{8,9},{11,10... | collective-permute-start | bytes 614408 | tf_op jit(solution)/shard_map/ppermute | solution.py:29
  87.4 48.1 %collective-permute-start.23 = (bf16[200,512]{1,0:T(8,128)(2,1)S(1)}, bf16[200,512]{1,0:T(8,128)(2,1)S(1)}, u32[]{:S(2)}, u32[]{:S(2)}) collective-permute-start(bf16[200,512]{1,0:T(8,128)(2,1)S(1)} %slice.237), channel_id=1, source_target_pairs={{1,0},{0,1},{3,2},{2,3},{5,4},{4,5},{7,6},{6,7},{9,8},{8,9},{11,10... | collective-permute-start | bytes 614408 | tf_op jit(solution)/shard_map/ppermute | solution.py:29
  95.0 20.7 %collective-permute-start.28 = (bf16[200,512]{1,0:T(8,128)(2,1)S(1)}, bf16[200,512]{1,0:T(8,128)(2,1)S(1)}, u32[]{:S(2)}, u32[]{:S(2)}) collective-permute-start(bf16[200,512]{1,0:T(8,128)(2,1)S(1)} %slice.234), channel_id=1, source_target_pairs={{1,0},{0,1},{3,2},{2,3},{5,4},{4,5},{7,6},{6,7},{9,8},{8,9},{11,10... | collective-permute-start | bytes 614408 | tf_op jit(solution)/shard_map/ppermute | solution.py:29
  102.2 24.0 %collective-permute-start.26 = (bf16[200,512]{1,0:T(8,128)(2,1)S(1)}, bf16[200,512]{1,0:T(8,128)(2,1)S(1)}, u32[]{:S(2)}, u32[]{:S(2)}) collective-permute-start(bf16[200,512]{1,0:T(8,128)(2,1)S(1)} %slice.235), channel_id=1, source_target_pairs={{1,0},{0,1},{3,2},{2,3},{5,4},{4,5},{7,6},{6,7},{9,8},{8,9},{11,10... | collective-permute-start | bytes 614408 | tf_op jit(solution)/shard_map/ppermute | solution.py:29
  111.3 8.3 %collective-permute-start.17 = (bf16[200,512]{1,0:T(8,128)(2,1)S(1)}, bf16[200,512]{1,0:T(8,128)(2,1)S(1)}, u32[]{:S(2)}, u32[]{:S(2)}) collective-permute-start(bf16[200,512]{1,0:T(8,128)(2,1)S(1)} %get-tuple-element.8), channel_id=1, source_target_pairs={{12,0},{13,1},{14,2},{15,3},{0,4},{1,5},{2,6},{3,7},{4,8},{5,9},{6... | collective-permute-start | bytes 614408 | tf_op jit(solution)/shard_map/ppermute | solution.py:29
  113.0 12.2 %collective-permute-start.19 = (bf16[200,512]{1,0:T(8,128)(2,1)S(1)}, bf16[200,512]{1,0:T(8,128)(2,1)S(1)}, u32[]{:S(2)}, u32[]{:S(2)}) collective-permute-start(bf16[200,512]{1,0:T(8,128)(2,1)S(1)} %get-tuple-element.9), channel_id=1, source_target_pairs={{8,0},{9,1},{10,2},{11,3},{12,4},{13,5},{14,6},{15,7},{0,8},{1,9},... | collective-permute-start | bytes 614408 | tf_op jit(solution)/shard_map/ppermute | solution.py:29
  115.8 10.2 %collective-permute-start.18 = (bf16[200,512]{1,0:T(8,128)(2,1)S(1)}, bf16[200,512]{1,0:T(8,128)(2,1)S(1)}, u32[]{:S(2)}, u32[]{:S(2)}) collective-permute-start(bf16[200,512]{1,0:T(8,128)(2,1)S(1)} %get-tuple-element.10), channel_id=1, source_target_pairs={{4,0},{5,1},{6,2},{7,3},{8,4},{9,5},{10,6},{11,7},{12,8},{13,9},{1... | collective-permute-start | bytes 614408 | tf_op jit(solution)/shard_map/ppermute | solution.py:29
  119.6 8.2 %collective-permute-start.24 = (bf16[200,512]{1,0:T(8,128)(2,1)S(1)}, bf16[200,512]{1,0:T(8,128)(2,1)S(1)}, u32[]{:S(2)}, u32[]{:S(2)}) collective-permute-start(bf16[200,512]{1,0:T(8,128)(2,1)S(1)} %slice.236), channel_id=1, source_target_pairs={{1,0},{0,1},{3,2},{2,3},{5,4},{4,5},{7,6},{6,7},{9,8},{8,9},{11,10... | collective-permute-start | bytes 614408 | tf_op jit(solution)/shard_map/ppermute | solution.py:29
  125.1 10.3 %collective-permute-start.29 = (bf16[200,512]{1,0:T(8,128)(2,1)S(1)}, bf16[200,512]{1,0:T(8,128)(2,1)S(1)}, u32[]{:S(2)}, u32[]{:S(2)}) collective-permute-start(bf16[200,512]{1,0:T(8,128)(2,1)S(1)} %fusion.2), channel_id=1, source_target_pairs={{64,0},{65,1},{66,2},{67,3},{68,4},{69,5},{70,6},{71,7},{72,8},{73... | collective-permute-start | bytes 614408 | tf_op jit(solution)/shard_map/ppermute | solution.py:29
  126.2 7.9 %collective-permute-start.22 = (bf16[200,128]{1,0:T(8,128)(2,1)S(1)}, bf16[200,128]{1,0:T(8,128)(2,1)S(1)}, u32[]{:S(2)}, u32[]{:S(2)}) collective-permute-start(bf16[200,128]{1,0:T(8,128)(2,1)S(1)} %get-tuple-element.12), channel_id=1, source_target_pairs={{2,0},{3,1},{0,2},{1,3},{6,4},{7,5},{4,6},{5,7},{10,8},{11,9},{8,1... | collective-permute-start | bytes 153608 | tf_op jit(solution)/shard_map/ppermute | solution.py:29
  127.8 6.9 %collective-permute-start.21 = (bf16[200,128]{1,0:T(8,128)(2,1)S(1)}, bf16[200,128]{1,0:T(8,128)(2,1)S(1)}, u32[]{:S(2)}, u32[]{:S(2)}) collective-permute-start(bf16[200,128]{1,0:T(8,128)(2,1)S(1)} %get-tuple-element.13), channel_id=1, source_target_pairs={{16,0},{17,1},{18,2},{19,3},{20,4},{21,5},{22,6},{23,7},{24,8},{25... | collective-permute-start | bytes 153608 | tf_op jit(solution)/shard_map/ppermute | solution.py:29
  132.1 6.4 %collective-permute-start.27 = (bf16[200,512]{1,0:T(8,128)(2,1)S(1)}, bf16[200,512]{1,0:T(8,128)(2,1)S(1)}, u32[]{:S(2)}, u32[]{:S(2)}) collective-permute-start(bf16[200,512]{1,0:T(8,128)(2,1)S(1)} %fusion.3), channel_id=1, source_target_pairs={{32,0},{33,1},{34,2},{35,3},{36,4},{37,5},{38,6},{39,7},{40,8},{41... | collective-permute-start | bytes 614408 | tf_op jit(solution)/shard_map/ppermute | solution.py:29
  134.1 7.0 %collective-permute-start.25 = (bf16[200,512]{1,0:T(8,128)(2,1)S(1)}, bf16[200,512]{1,0:T(8,128)(2,1)S(1)}, u32[]{:S(2)}, u32[]{:S(2)}) collective-permute-start(bf16[200,512]{1,0:T(8,128)(2,1)S(1)} %fusion.4), channel_id=1, source_target_pairs={{96,0},{97,1},{98,2},{99,3},{100,4},{101,5},{102,6},{103,7},{104,8... | collective-permute-start | bytes 614408 | tf_op jit(solution)/shard_map/ppermute | solution.py:29
  (7 other events, 65.4 us)
where the time goes:
time: 143 us; the launch traced here: 142 us
  starting transfers between devices  41 us (29%)
  Pallas kernels  29.7 us (21%)
  waiting for transfers between devices  28.5 us (20%)
  matrix products  28.1 us (20%)
  local copies, waits for them, and re-layouts  9.35 us (7%)
  other arithmetic  4.04 us (3%)
    ppermute x30, starting transfers between devices, moved(): return lax.ppermute(block, AXES, route)  41 us
    pallas_call x1, Pallas kernels, encode_all(): pl.pallas_call(encode_kernel, grid=(steps,), in_specs=[smem, smem, pl.Blo...  29.7 us
    ppermute x30, waiting for transfers between devices, moved(): return lax.ppermute(block, AXES, route)  28.5 us
    dot_general x4, matrix products, score_terms(): lax.dot_general(query, slab, (((0,), (0,)), ((), ())), preferred_element_...  17.7 us
    dot_general x4, matrix products, score_terms(): lax.dot_general(slab, residual, (((1,), (1,)), ((), ())), preferred_eleme...  6.05 us
    dot_general x4, matrix products, score_terms(): ent_part = jnp.dot(query, residual, preferred_element_type=F32)  4.4 us
    unnamed x12, local copies, waits for them, and re-layouts  3.54 us
    pad x1, local copies, waits for them, and re-layouts, encode_all(): jnp.pad(enc_weight.T, ((0, 0), (0, w_lanes - tokens * depth)))  3.08 us
  transfers between devices with their start and end apart: 30, of which 10 were waited for; matrix products, arithmetic and copies ran while one was open for 22% of the time, Pallas kernels for 0%

commit v1 on v0

v1 whole, which is shorter than its diff:
```python
import functools
import math

import jax
import jax.numpy as jnp
from jax import lax
from jax.experimental import pallas as pl
from jax.experimental.pallas import tpu as pltpu
from jax.sharding import PartitionSpec as P

AXES = ("ent", "qry")
BF16 = jnp.bfloat16
F32 = jnp.float32
LANES = 128
WIDE = 256
CHUNK = 4096
UNROLL = 64
SPAN = 512
VMEM_BYTES = 58 * 1024 * 1024
FAR = (1, 3, 2)


def flat_of(x, y, z, core):
    return z * 32 + (x % 2) * 16 + y * 4 + (x // 2) * 2 + core


def coords_of(flat):
    x = ((flat // 2) % 2) * 2 + (flat // 16) % 2
    return x, (flat // 4) % 4, flat // 32, flat % 2


def moved(block, dx=0, dy=0, dz=0, dcore=0):
    route = []
    for to in range(128):
        x, y, z, core = coords_of(to)
        route.append((flat_of((x + dx) % 4, (y + dy) % 4, (z + dz) % 4, (core + dcore) % 2), to))
    return lax.ppermute(block, AXES, route)


def place():
    return coords_of(lax.axis_index("ent") * 16 + lax.axis_index("qry"))


def gather_rows(ids, table, rows):
    def some(step, carry):
        first = step * UNROLL
        place = pl.multiple_of(step * (2 * UNROLL), 2 * UNROLL)
        picked = [table[pl.ds(ids[first + k], 2), :] for k in range(UNROLL)]
        for k in range(UNROLL):
            rows[pl.ds(place + 2 * k, 2), :] = picked[k]
        return carry

    lax.fori_loop(0, ids.shape[0] // UNROLL, some, 0)


def relation_rows(ids, rel_table):
    shape = (rel_table.shape[1], ids.shape[1])
    hot = lax.broadcasted_iota(jnp.int32, shape, 0) == jnp.broadcast_to(ids, shape)
    hot = jnp.where(hot, 1.0, 0.0).astype(BF16)
    return jnp.dot(rel_table[...], hot, preferred_element_type=F32)


def encoded(rows, rel_ids, weights, rel_table):
    n_rel, width = rel_ids.shape
    anchors = weights.shape[1] // WIDE - n_rel
    total = jnp.zeros((weights.shape[0], width), F32)
    for t in range(anchors):
        halves = [rows[pl.ds(t * 2 * width + h, width, stride=2), :] for h in range(2)]
        part = jnp.concatenate(halves, axis=1).astype(BF16)
        total = total + lax.dot_general(
            weights[:, t * WIDE : (t + 1) * WIDE],
            part,
            (((1,), (1,)), ((), ())),
            preferred_element_type=F32,
        )
    for t in range(n_rel):
        part = relation_rows(rel_ids[t : t + 1, :], rel_table).astype(BF16)
        first = (anchors + t) * WIDE
        total = total + jnp.dot(weights[:, first : first + WIDE], part, preferred_element_type=F32)
    return total


def prepare(tab_t, w_t, rel_t, table, weights, rel_table, relations):
    step = pl.program_id(0)
    depth = tab_t.shape[0]

    @pl.when(step == 0)
    def _():
        lane = lax.broadcasted_iota(jnp.int32, (depth, WIDE), 1)
        for t in range(weights.shape[1] // WIDE):
            start = t * depth
            base = start // LANES * LANES
            piece = w_t[:, base : base + 3 * LANES].astype(F32)
            if start > base:
                piece = pltpu.roll(piece, 3 * LANES - (start - base), 1)
            weights[:, t * WIDE : (t + 1) * WIDE] = jnp.where(
                lane < depth, piece[:, :WIDE], 0.0
            ).astype(BF16)
        known = lax.broadcasted_iota(jnp.int32, rel_t.shape, 1) < relations
        rel = jnp.where(known, rel_t[...].astype(F32), 0.0)
        rel_table[...] = jnp.concatenate(
            [rel, jnp.zeros((WIDE - depth, rel.shape[1]), F32)], axis=0
        ).astype(BF16)

    chunk = tab_t.shape[1]
    top = tab_t[:LANES, :].astype(F32).T
    rest = jnp.concatenate(
        [tab_t[LANES:, :].astype(F32), jnp.zeros((WIDE - depth, chunk), F32)], axis=0
    ).T
    table[pl.ds(step * 2 * chunk, chunk, stride=2), :] = top
    table[pl.ds(step * 2 * chunk + 1, chunk, stride=2), :] = rest


def encode_kernel(
    relations, scale, own_ids, head_ids, tab_t, w_t, rel_t, own_rel, head_rel, asked, wanted, fc,
    own_out, query_out, table, rows, weights, rel_table,
):
    prepare(tab_t, w_t, rel_t, table, weights, rel_table, relations)

    @pl.when(pl.program_id(0) == pl.num_programs(0) - 1)
    def _():
        gather_rows(own_ids, table, rows)
        own_out[...] = (encoded(rows, own_rel, weights, rel_table) * scale).astype(BF16)
        gather_rows(head_ids, table, rows)
        head = encoded(rows, head_rel, weights, rel_table).astype(BF16)
        mixed = head.astype(F32) * relation_rows(asked[...], rel_table)[: head.shape[0], :]
        query = jnp.tanh(
            lax.dot_general(
                fc[...], mixed.astype(BF16), (((0,), (0,)), ((), ())), preferred_element_type=F32
            )
        )
        digits = []
        for t in range(wanted.shape[0]):
            target = wanted[t : t + 1, :]
            digits += [target // LANES, target % LANES]
        query_out[...] = jnp.concatenate(
            [query, jnp.concatenate(digits, axis=0).astype(F32)], axis=0
        ).astype(BF16)


def encode_all(
    anchor_ids, relation_ids, head_anchors, head_relations, query_relation,
    targets, anchor_table, relation_table, enc_weight, fc_weight, scale,
):
    own, anchors = anchor_ids.shape
    heads = head_anchors.shape[0]
    count, depth = anchor_table.shape
    relations = relation_table.shape[0]
    steps = pl.cdiv(count, CHUNK)
    tokens = anchors + relation_ids.shape[1]
    rel_lanes = pl.cdiv(relations, LANES) * LANES
    w_lanes = pl.cdiv((tokens - 1) * depth // LANES * LANES + 3 * LANES, LANES) * LANES
    whole = pl.BlockSpec(memory_space=pltpu.VMEM)
    smem = pl.BlockSpec(memory_space=pltpu.SMEM)
    once = pl.Buffered(1)
    return pl.pallas_call(
        functools.partial(encode_kernel, relations, scale),
        grid=(steps,),
        in_specs=[
            smem,
            smem,
            pl.BlockSpec((depth, CHUNK), lambda i: (0, i)),
            pl.BlockSpec((depth, w_lanes), lambda i: (0, 0), pipeline_mode=once),
            pl.BlockSpec((depth, rel_lanes), lambda i: (0, 0), pipeline_mode=once),
            whole, whole, whole, whole, whole,
        ],
        out_specs=[whole, whole],
        out_shape=[
            jax.ShapeDtypeStruct((depth, own), BF16),
            jax.ShapeDtypeStruct((depth + 2 * targets.shape[1], heads), BF16),
        ],
        scratch_shapes=[
            pltpu.VMEM((2 * steps * CHUNK, LANES), F32),
            pltpu.VMEM((2 * heads * anchors, LANES), F32),
            pltpu.VMEM((depth, tokens * WIDE), BF16),
            pltpu.VMEM((WIDE, rel_lanes), BF16),
        ],
        compiler_params=pltpu.CompilerParams(vmem_limit_bytes=VMEM_BYTES),
    )(
        (anchor_ids.T * 2).reshape(-1), (head_anchors.T * 2).reshape(-1), anchor_table.T, enc_weight.T, relation_table.T,
        relation_ids.T, head_relations.T, query_relation[None, :], targets.T, fc_weight,
    )


def score_kernel(plain, struck_value, depth, count, started, last, *refs):
    spots, rows = refs[0], refs[1:5]
    blocks = refs[5 : 5 + count]
    refs = refs[5 + count :]
    if started:
        before, refs = refs[0], refs[1:]
    mine, away, refs = refs[: count // 2], refs[count // 2], refs[count // 2 + 1 :]
    if last:
        kept, sent, refs = refs[0], refs[1:4], refs[4:]
        totals, *refs = refs
    else:
        totals, *refs = refs
    slab, tall, queries, marks, asked, *held = refs
    width = blocks[0].shape[1]
    entities = slab.shape[1]
    tiles = SPAN // LANES

    row = entities // 4
    for k in range(4):
        at = slice(k * row, (k + 1) * row)
        slab[:, at] = rows[k][...]
        wide = jnp.concatenate(
            [rows[k][...].astype(F32), jnp.zeros((WIDE - depth, row), F32)], axis=0
        )
        tall[at, :] = wide.T.astype(BF16)
    within = lax.broadcasted_iota(jnp.int32, (LANES, width), 0)
    for b in range(count):
        query = blocks[b][...].astype(F32)
        queries[b] = jnp.concatenate(
            [query[:depth, :], jnp.zeros((WIDE - depth, width), F32)], axis=0
        ).astype(BF16)
        digits = query[depth:, :].astype(jnp.int32)
        marked = jnp.zeros((LANES, width), jnp.int32)
        for t in range(4):
            owner = digits[2 * t : 2 * t + 1, :]
            low = digits[2 * t + 1 : 2 * t + 2, :]
            bit = jnp.zeros(owner.shape, jnp.int32)
            for k in range(entities // LANES):
                bit = jnp.where(owner == spots[k], 1 << k, bit)
            marked = marked | jnp.where(within == low, bit, 0)
        marks[b] = marked

    per = entities // SPAN

    def residual_of(b, part):
        first = part * SPAN
        score = jnp.dot(tall[first : first + SPAN, :], queries[b], preferred_element_type=F32)
        marked = marks[b]
        for j in range(tiles):
            hit = (marked & (1 << (part * tiles + j))) != 0
            label = jnp.where(hit, struck_value, plain)
            held[part % 2][j * LANES : (j + 1) * LANES, :] = (
                jnp.tanh(score[j * LANES : (j + 1) * LANES, :]) + label
            ).astype(BF16)

    def use(b, part, fresh):
        first = part * SPAN
        residual = held[part % 2][...]
        ent = lax.dot_general(
            residual, queries[b], (((1,), (1,)), ((), ())), preferred_element_type=F32
        )
        at = slice(first, first + SPAN)
        if not fresh:
            totals[at, :] += ent
        elif started:
            totals[at, :] = before[at, :] + ent
        else:
            totals[at, :] = ent
        return jnp.dot(slab[:, at], residual, preferred_element_type=F32)

    residual_of(0, 0)
    for b in range(count):
        for part in range(per):
            following = b * per + part + 1
            if following < count * per:
                residual_of(following // per, following % per)
            ask = use(b, part, b == 0)
            if part == 0:
                asked[...] = ask
            elif part < per - 1:
                asked[...] += ask
            else:
                if b % 2:
                    away[:, b // 2 * width : (b // 2 + 1) * width] = (asked[...] + ask).astype(BF16)
                else:
                    mine[b // 2][...] = asked[...] + ask
    if last:
        kept[...] = totals[:row, :].T[:depth, :]
        for k in range(3):
            sent[k][...] = totals[(k + 1) * row : (k + 2) * row, :].T[:depth, :].astype(BF16)


def score(spots, rows, blocks, total_entities, before=None, last=False):
    depth, row = rows[0].shape
    entities = 4 * row
    count, width = len(blocks), blocks[0].shape[1]
    plain = 1.0 - 2.0 * (0.1 / total_entities)
    shape = jax.ShapeDtypeStruct
    outs = [shape((depth, width), F32)] * (count // 2)
    outs.append(shape((depth, width * (count // 2)), BF16))
    scratch = [
        pltpu.VMEM((depth, entities), BF16),
        pltpu.VMEM((entities, WIDE), BF16),
        pltpu.VMEM((count, WIDE, width), BF16),
        pltpu.VMEM((count, LANES, width), jnp.int32),
        pltpu.VMEM((depth, width), F32),
        pltpu.VMEM((SPAN, width), BF16),
        pltpu.VMEM((SPAN, width), BF16),
    ]
    if last:
        outs += [shape((depth, row), F32)] + [shape((depth, row), BF16)] * 3
        scratch.insert(0, pltpu.VMEM((entities, WIDE), F32))
    else:
        outs.append(shape((entities, WIDE), F32))
    whole = pl.BlockSpec(memory_space=pltpu.VMEM)
    extra = [] if before is None else [before]
    return pl.pallas_call(
        functools.partial(
            score_kernel, plain, plain - 1.8, depth, count, before is not None, last
        ),
        in_specs=[pl.BlockSpec(memory_space=pltpu.SMEM)] + [whole] * (4 + count + len(extra)),
        out_specs=[whole] * len(outs),
        out_shape=outs,
        scratch_shapes=scratch,
        compiler_params=pltpu.CompilerParams(vmem_limit_bytes=VMEM_BYTES),
    )(spots, *rows, *blocks, *extra)


def body(
    anchor_ids,
    relation_ids,
    head_anchors,
    head_relations,
    query_relation,
    targets,
    anchor_table,
    relation_table,
    enc_weight,
    fc_weight,
):
    width = anchor_ids.shape[0]
    entities = width * 128
    queries = head_anchors.shape[0] * 128
    scale = 0.5 * float(anchor_table.shape[1]) ** (-0.5)
    x, y, z, core = place()
    own_cols, query = encode_all(
        anchor_ids,
        relation_ids,
        head_anchors,
        head_relations,
        query_relation,
        targets,
        anchor_table,
        relation_table,
        enc_weight,
        fc_weight,
        scale,
    )
    spots = jnp.stack(
        [
            flat_of((x + dx) % 4, (y + dy) % 4, z, core)
            for dy in (0,) + FAR
            for dx in (0,) + FAR
        ]
    ).astype(jnp.int32)
    row = jnp.concatenate([own_cols] + [moved(own_cols, dx=d) for d in FAR], axis=1)
    far = [moved(query, dz=d) for d in FAR]
    rows = [row] + [moved(row, dy=d) for d in FAR]
    pairs = [[q, moved(q, dcore=1)] for q in [query] + far]
    mine0, away0, totals = score(spots, rows, pairs[0], entities)
    kept = [mine0 + moved(away0, dcore=1).astype(F32)]
    mine1, mine2, away12, totals = score(spots, rows, pairs[1] + pairs[2], entities, totals)
    back12 = moved(away12, dcore=1).astype(F32)
    mine3, away3, ent_row, *ent_sent = score(spots, rows, pairs[3], entities, totals, True)
    count = mine1.shape[1]
    ready = [
        mine1 + back12[:, :count],
        mine2 + back12[:, count:],
        mine3 + moved(away3, dcore=1).astype(F32),
    ]
    for d, block in zip(FAR, ent_sent):
        ent_row = ent_row + moved(block, dy=-d).astype(F32)
    kept += [moved(q.astype(BF16), dz=-d).astype(F32) for d, q in zip(FAR, ready)]
    ent_share = ent_row[:, :width]
    for k, d in enumerate(FAR):
        block = ent_row[:, (k + 1) * width : (k + 2) * width].astype(BF16)
        ent_share = ent_share + moved(block, dx=-d).astype(F32)
    query_total = kept[0] + kept[1] + kept[2] + kept[3]
    return (
        ent_share * (0.5 / math.sqrt(queries)),
        query_total.T * (0.5 / scale / math.sqrt(entities)),
    )


def solution(mesh):
    spread = P(AXES, None)
    placed = (spread, spread, spread, spread, P(AXES), spread, P(), P(), P(), P())
    return jax.shard_map(
        body,
        mesh=mesh,
        in_specs=placed,
        out_specs=(P(None, AXES), spread),
        check_vma=False,
    )
```

time: 143 us -> 122 us (0.85)
  matrix products: 28.1 us -> 0 us
  Pallas kernels: 29.7 us -> 50.1 us
  starting transfers between devices: 41 us -> 33 us
  local copies, waits for them, and re-layouts: 9.35 us -> 4.27 us
  other arithmetic: 4.04 us -> 6.1 us
    dot_general x12 -> x0, matrix products: 28.1 us -> none  [the longest x4 17.7 us: score_terms(): lax.dot_general(query, slab, (((0,), (0,)), ((), ())), preferred_element_...]
    pallas_call x1 -> x4, Pallas kernels: 29.7 us -> 50.1 us  [the longest x1 26.6 us: encode_all(): pl.pallas_call(functools.partial(encode_kernel, relations, scale), grid=(...]
    ppermute x30 -> x25, starting transfers between devices: 41 us -> 33 us  [moved(): return lax.ppermute(block, AXES, route)]
    pad x2 -> x0, local copies, waits for them, and re-layouts: 4.87 us -> none  [the longest x1 3.08 us: encode_all(): jnp.pad(enc_weight.T, ((0, 0), (0, w_lanes - tokens * depth)))]
    div x2 -> x0, other arithmetic: 1.56 us -> none  [body(): return (ent_share / math.sqrt(queries), query_total.T / math.sqrt(entities))]
    mul x0 -> x2, other arithmetic: none -> 1.56 us  [the longest x1 0.89 us: body(): query_total.T * (0.5 / scale / math.sqrt(entities))]
    ppermute x30 -> x25, waiting for transfers between devices: 28.5 us -> 27.4 us  [moved(): return lax.ppermute(block, AXES, route)]
    unnamed x12 -> x35, local copies, waits for them, and re-layouts: 3.54 us -> 2.97 us
  transfers between devices with their start and end apart: 30 -> 25, of which waited for: 10 -> 8; matrix products, arithmetic and copies ran while one was open for 22% -> 4% of each run, Pallas kernels for 0% -> 14%
where the time goes in v1:
time: 122 us
  Pallas kernels  50.1 us (41%)
  starting transfers between devices  33 us (27%)
  waiting for transfers between devices  27.4 us (22%)
  other arithmetic  6.1 us (5%)
  local copies, waits for them, and re-layouts  4.27 us (3%)
    ppermute x25, starting transfers between devices, moved(): return lax.ppermute(block, AXES, route)  33 us
    ppermute x25, waiting for transfers between devices, moved(): return lax.ppermute(block, AXES, route)  27.4 us
    pallas_call x1, Pallas kernels, encode_all(): pl.pallas_call(functools.partial(encode_kernel, relations, scale), grid=(...  26.6 us
    pallas_call x3, Pallas kernels, score(): pl.pallas_call(functools.partial(score_kernel, plain, plain - 1.8, depth,...  23.5 us
    unnamed x35, local copies, waits for them, and re-layouts  2.97 us
  transfers between devices with their start and end apart: 25, of which 8 were waited for; matrix products, arithmetic and copies ran while one was open for 4% of the time, Pallas kernels for 14%

profile of v1, /device:TPU:0, one launch (start us, length us, event | category | flops | bytes accessed | tf_op | source)
XLA Modules:
  0.0 121.9 jit_solution(11058943969314222041)
XLA Ops:
  2.1 1.3 %multiply_bitcast_fusion.2.own_ids = s32[2560]{0:T(1024)} fusion(s32[128,20]{0,1:T(8,128)} %param.10), kind=kLoop, calls=%fused_computation.12 | loop fusion | flops 2560 | bytes 20480 | tf_op jit(solution)/shard_map/reshape | solution.py:180
  3.4 26.6 %shard_map.113 = (bf16[200,128]{1,0:T(8,128)(2,1)}, bf16[208,512]{1,0:T(8,128)(2,1)}) custom-call(s32[2560]{0:T(1024)} %multiply_bitcast_fusion.2.own_ids, s32[10240]{0:T(1024)} %reshape.11.head_ids, bf16[200,20000]{1,0:T(8,128)(2,1)} %bitcast.31, bf16[200,5000]{1,0:T(8,128)(2,1)} %bitcast.32, bf16[200,822]{1,0:T(8,128)(2,1)} %bitcast.33, ...), custom_call_target="tpu_custom_call" | custom-call | tf_op jit(solution)/shard_map/pallas_call | solution.py:156
  30.0 2.8 %collective-permute-start = (bf16[200,128]{1,0:T(8,128)(2,1)}, bf16[200,128]{1,0:T(8,128)(2,1)S(1)}, u32[]{:S(2)}, u32[]{:S(2)}) collective-permute-start(bf16[200,128]{1,0:T(8,128)(2,1)} %get-tuple-element.17), channel_id=1, source_target_pairs={{16,0},{17,1},{18,2},{19,3},{20,4},{21,5},{22,6},{23,7},{24,8},{25... | collective-permute-start | bytes 153608 | tf_op jit(solution)/shard_map/ppermute | solution.py:37
  32.9 2.3 %collective-permute-start.2 = (bf16[200,128]{1,0:T(8,128)(2,1)}, bf16[200,128]{1,0:T(8,128)(2,1)S(1)}, u32[]{:S(2)}, u32[]{:S(2)}) collective-permute-start(bf16[200,128]{1,0:T(8,128)(2,1)} %get-tuple-element.17), channel_id=1, source_target_pairs={{2,0},{3,1},{0,2},{1,3},{6,4},{7,5},{4,6},{5,7},{10,8},{11,9},{8,1... | collective-permute-start | bytes 153608 | tf_op jit(solution)/shard_map/ppermute | solution.py:37
  35.1 1.9 %collective-permute-start.10 = (bf16[208,512]{1,0:T(8,128)(2,1)}, bf16[208,512]{1,0:T(8,128)(2,1)S(1)}, u32[]{:S(2)}, u32[]{:S(2)}) collective-permute-start(bf16[208,512]{1,0:T(8,128)(2,1)} %get-tuple-element.18.refs_5_), channel_id=1, source_target_pairs={{96,0},{97,1},{98,2},{99,3},{100,4},{101,5},{102,6},{103,7},{104,8... | collective-permute-start | bytes 638984 | tf_op jit(solution)/shard_map/ppermute | solution.py:37
  37.9 2.2 %collective-permute-start.8 = (bf16[208,512]{1,0:T(8,128)(2,1)}, bf16[208,512]{1,0:T(8,128)(2,1)S(1)}, u32[]{:S(2)}, u32[]{:S(2)}) collective-permute-start(bf16[208,512]{1,0:T(8,128)(2,1)} %get-tuple-element.18.refs_5_), channel_id=1, source_target_pairs={{32,0},{33,1},{34,2},{35,3},{36,4},{37,5},{38,6},{39,7},{40,8},{41... | collective-permute-start | bytes 638984 | tf_op jit(solution)/shard_map/ppermute | solution.py:37
  40.1 2.7 %collective-permute-start.6 = (bf16[208,512]{1,0:T(8,128)(2,1)}, bf16[208,512]{1,0:T(8,128)(2,1)S(1)}, u32[]{:S(2)}, u32[]{:S(2)}) collective-permute-start(bf16[208,512]{1,0:T(8,128)(2,1)} %get-tuple-element.18.refs_5_), channel_id=1, source_target_pairs={{64,0},{65,1},{66,2},{67,3},{68,4},{69,5},{70,6},{71,7},{72,8},{73... | collective-permute-start | bytes 638984 | tf_op jit(solution)/shard_map/ppermute | solution.py:37
  42.9 3.1 %collective-permute-start.3 = (bf16[200,512]{1,0:T(8,128)(2,1)S(1)}, bf16[200,512]{1,0:T(8,128)(2,1)S(1)}, u32[]{:S(2)}, u32[]{:S(2)}) collective-permute-start(bf16[200,512]{1,0:T(8,128)(2,1)S(1)} %constant_dynamic-update-slice_fusion.refs_1_), channel_id=1, source_target_pairs={{4,0},{5,1},{6,2},{7,3},{8,4},{9,5},{10,6},{11,7},{12,8},{13,9},{1... | collective-permute-start | bytes 614408 | tf_op jit(solution)/shard_map/ppermute | solution.py:37
  46.0 4.2 %collective-permute-done.8.refs_5_ = bf16[208,512]{1,0:T(8,128)(2,1)S(1)} collective-permute-done((bf16[208,512]{1,0:T(8,128)(2,1)}, bf16[208,512]{1,0:T(8,128)(2,1)S(1)}, u32[]{:S(2)}, u32[]{:S(2)}) %collective-permute-start.8) | collective-permute-done | bytes 213024 | tf_op jit(solution)/shard_map/ppermute | solution.py:37
  51.1 1.6 %collective-permute-start.4 = (bf16[200,512]{1,0:T(8,128)(2,1)S(1)}, bf16[200,512]{1,0:T(8,128)(2,1)S(1)}, u32[]{:S(2)}, u32[]{:S(2)}) collective-permute-start(bf16[200,512]{1,0:T(8,128)(2,1)S(1)} %constant_dynamic-update-slice_fusion.refs_1_), channel_id=1, source_target_pairs={{12,0},{13,1},{14,2},{15,3},{0,4},{1,5},{2,6},{3,7},{4,8},{5,9},{6... | collective-permute-start | bytes 614408 | tf_op jit(solution)/shard_map/ppermute | solution.py:37
  52.7 2.9 %collective-permute-start.5 = (bf16[200,512]{1,0:T(8,128)(2,1)S(1)}, bf16[200,512]{1,0:T(8,128)(2,1)S(1)}, u32[]{:S(2)}, u32[]{:S(2)}) collective-permute-start(bf16[200,512]{1,0:T(8,128)(2,1)S(1)} %constant_dynamic-update-slice_fusion.refs_1_), channel_id=1, source_target_pairs={{8,0},{9,1},{10,2},{11,3},{12,4},{13,5},{14,6},{15,7},{0,8},{1,9},... | collective-permute-start | bytes 614408 | tf_op jit(solution)/shard_map/ppermute | solution.py:37
  56.3 3.6 %collective-permute-done.4.refs_3_ = bf16[200,512]{1,0:T(8,128)(2,1)S(1)} collective-permute-done((bf16[200,512]{1,0:T(8,128)(2,1)S(1)}, bf16[200,512]{1,0:T(8,128)(2,1)S(1)}, u32[]{:S(2)}, u32[]{:S(2)}) %collective-permute-start.4) | collective-permute-done | bytes 204832 | tf_op jit(solution)/shard_map/ppermute | solution.py:37
  59.8 5.6 %collective-permute-done.5.refs_4_ = bf16[200,512]{1,0:T(8,128)(2,1)S(1)} collective-permute-done((bf16[200,512]{1,0:T(8,128)(2,1)S(1)}, bf16[200,512]{1,0:T(8,128)(2,1)S(1)}, u32[]{:S(2)}, u32[]{:S(2)}) %collective-permute-start.5) | collective-permute-done | bytes 204832 | tf_op jit(solution)/shard_map/ppermute | solution.py:37
  66.1 6.3 %shard_map.114 = (f32[200,512]{1,0:T(8,128)}, bf16[200,512]{1,0:T(8,128)(2,1)}, f32[2048,256]{1,0:T(8,128)}) custom-call(s32[16]{0:T(128)} %stack.67.refs_0_, bf16[200,512]{1,0:T(8,128)(2,1)} %copy-done, bf16[200,512]{1,0:T(8,128)(2,1)} %copy-done.1, bf16[200,512]{1,0:T(8,128)(2,1)} %copy-done.2, bf16[200,512]{1,0:T(8,128)(2,1)} %copy-done.3, ...), custom_call_target="tpu_custom_call" | custom-call | tf_op jit(solution)/shard_map/pallas_call | solution.py:301
  73.2 10.4 %shard_map.115 = (f32[200,512]{1,0:T(8,128)}, f32[200,512]{1,0:T(8,128)}, bf16[200,1024]{1,0:T(8,128)(2,1)}, f32[2048,256]{1,0:T(8,128)}) custom-call(s32[16]{0:T(128)} %stack.67.refs_0_, bf16[200,512]{1,0:T(8,128)(2,1)} %copy-done, bf16[200,512]{1,0:T(8,128)(2,1)} %copy-done.1, bf16[200,512]{1,0:T(8,128)(2,1)} %copy-done.2, bf16[200,512]{1,0:T(8,128)(2,1)} %copy-done.3, ...), custom_call_target="tpu_custom_call" | custom-call | tf_op jit(solution)/shard_map/pallas_call | solution.py:301
  84.2 6.9 %shard_map.116 = (f32[200,512]{1,0:T(8,128)}, bf16[200,512]{1,0:T(8,128)(2,1)}, f32[200,512]{1,0:T(8,128)}, bf16[200,512]{1,0:T(8,128)(2,1)}, bf16[200,512]{1,0:T(8,128)(2,1)}, /*index=5*/bf16[200,512]{1,0:T(8,128)(2,1)}) custom-call(s32[16]{0:T(128)} %stack.67.refs_0_, bf16[200,512]{1,0:T(8,128)(2,1)} %copy-done, bf16[200,512]{1,0:T(8,128)(2,1)} %copy-done.1, ...), custom_call_target="tpu_custom_call" | custom-call | tf_op jit(solution)/shard_map/pallas_call | solution.py:301
  91.8 3.2 %collective-permute-start.14 = (bf16[200,512]{1,0:T(8,128)(2,1)}, bf16[200,512]{1,0:T(8,128)(2,1)S(1)}, u32[]{:S(2)}, u32[]{:S(2)}) collective-permute-start(bf16[200,512]{1,0:T(8,128)(2,1)} %get-tuple-element.23), channel_id=1, source_target_pairs={{4,0},{5,1},{6,2},{7,3},{8,4},{9,5},{10,6},{11,7},{12,8},{13,9},{1... | collective-permute-start | bytes 614408 | tf_op jit(solution)/shard_map/ppermute | solution.py:37
  96.3 8.7 %collective-permute-done.13 = bf16[200,512]{1,0:T(8,128)(2,1)S(1)} collective-permute-done((bf16[200,512]{1,0:T(8,128)(2,1)}, bf16[200,512]{1,0:T(8,128)(2,1)S(1)}, u32[]{:S(2)}, u32[]{:S(2)}) %collective-permute-start.13) | collective-permute-done | bytes 204832 | tf_op jit(solution)/shard_map/ppermute | solution.py:37
  106.0 1.1 fusion.5
  107.1 1.9 %collective-permute-start.16 = (bf16[200,128]{1,0:T(8,128)(2,1)S(1)}, bf16[200,128]{1,0:T(8,128)(2,1)S(1)}, u32[]{:S(2)}, u32[]{:S(2)}) collective-permute-start(bf16[200,128]{1,0:T(8,128)(2,1)S(1)} %get-tuple-element.36), channel_id=1, source_target_pairs={{18,0},{19,1},{16,2},{17,3},{22,4},{23,5},{20,6},{21,7},{26,8},{27... | collective-permute-start | bytes 153608 | tf_op jit(solution)/shard_map/ppermute | solution.py:37
  109.0 1.4 %collective-permute-start.17 = (bf16[200,128]{1,0:T(8,128)(2,1)S(1)}, bf16[200,128]{1,0:T(8,128)(2,1)S(1)}, u32[]{:S(2)}, u32[]{:S(2)}) collective-permute-start(bf16[200,128]{1,0:T(8,128)(2,1)S(1)} %get-tuple-element.38), channel_id=1, source_target_pairs={{16,0},{17,1},{18,2},{19,3},{20,4},{21,5},{22,6},{23,7},{24,8},{25... | collective-permute-start | bytes 153608 | tf_op jit(solution)/shard_map/ppermute | solution.py:37
  112.5 2.7 %collective-permute-start.21 = (bf16[200,512]{1,0:T(8,128)(2,1)S(1)}, bf16[200,512]{1,0:T(8,128)(2,1)S(1)}, u32[]{:S(2)}, u32[]{:S(2)}) collective-permute-start(bf16[200,512]{1,0:T(8,128)(2,1)S(1)} %get-tuple-element.34), channel_id=1, source_target_pairs={{96,0},{97,1},{98,2},{99,3},{100,4},{101,5},{102,6},{103,7},{104,8... | collective-permute-start | bytes 614408 | tf_op jit(solution)/shard_map/ppermute | solution.py:37
  115.2 1.7 %collective-permute-start.22 = (bf16[200,512]{1,0:T(8,128)(2,1)S(1)}, bf16[200,512]{1,0:T(8,128)(2,1)S(1)}, u32[]{:S(2)}, u32[]{:S(2)}) collective-permute-start(bf16[200,512]{1,0:T(8,128)(2,1)S(1)} %get-tuple-element.35), channel_id=1, source_target_pairs={{32,0},{33,1},{34,2},{35,3},{36,4},{37,5},{38,6},{39,7},{40,8},{41... | collective-permute-start | bytes 614408 | tf_op jit(solution)/shard_map/ppermute | solution.py:37
  117.6 2.5 %collective-permute-done.21 = bf16[200,512]{1,0:T(8,128)(2,1)S(1)} collective-permute-done((bf16[200,512]{1,0:T(8,128)(2,1)S(1)}, bf16[200,512]{1,0:T(8,128)(2,1)S(1)}, u32[]{:S(2)}, u32[]{:S(2)}) %collective-permute-start.21) | collective-permute-done | bytes 204832 | tf_op jit(solution)/shard_map/ppermute | solution.py:37
  (77 shorter events, 13.4 us)
Async XLA Ops:
  30.0 7.9 %collective-permute-start = (bf16[200,128]{1,0:T(8,128)(2,1)}, bf16[200,128]{1,0:T(8,128)(2,1)S(1)}, u32[]{:S(2)}, u32[]{:S(2)}) collective-permute-start(bf16[200,128]{1,0:T(8,128)(2,1)} %get-tuple-element.17), channel_id=1, source_target_pairs={{16,0},{17,1},{18,2},{19,3},{20,4},{21,5},{22,6},{23,7},{24,8},{25... | collective-permute-start | bytes 153608 | tf_op jit(solution)/shard_map/ppermute | solution.py:37
  32.8 7.3 %collective-permute-start.1 = (bf16[200,128]{1,0:T(8,128)(2,1)}, bf16[200,128]{1,0:T(8,128)(2,1)S(1)}, u32[]{:S(2)}, u32[]{:S(2)}) collective-permute-start(bf16[200,128]{1,0:T(8,128)(2,1)} %get-tuple-element.17), channel_id=1, source_target_pairs={{18,0},{19,1},{16,2},{17,3},{22,4},{23,5},{20,6},{21,7},{26,8},{27... | collective-permute-start | bytes 153608 | tf_op jit(solution)/shard_map/ppermute | solution.py:37
  32.9 10.0 %collective-permute-start.2 = (bf16[200,128]{1,0:T(8,128)(2,1)}, bf16[200,128]{1,0:T(8,128)(2,1)S(1)}, u32[]{:S(2)}, u32[]{:S(2)}) collective-permute-start(bf16[200,128]{1,0:T(8,128)(2,1)} %get-tuple-element.17), channel_id=1, source_target_pairs={{2,0},{3,1},{0,2},{1,3},{6,4},{7,5},{4,6},{5,7},{10,8},{11,9},{8,1... | collective-permute-start | bytes 153608 | tf_op jit(solution)/shard_map/ppermute | solution.py:37
  35.1 15.9 %collective-permute-start.12 = (bf16[208,512]{1,0:T(8,128)(2,1)}, bf16[208,512]{1,0:T(8,128)(2,1)S(1)}, u32[]{:S(2)}, u32[]{:S(2)}) collective-permute-start(bf16[208,512]{1,0:T(8,128)(2,1)} %get-tuple-element.18.refs_5_), channel_id=1, source_target_pairs={{1,0},{0,1},{3,2},{2,3},{5,4},{4,5},{7,6},{6,7},{9,8},{8,9},{11,10... | collective-permute-start | bytes 638984 | tf_op jit(solution)/shard_map/ppermute | solution.py:37
  35.1 10.8 %collective-permute-start.10 = (bf16[208,512]{1,0:T(8,128)(2,1)}, bf16[208,512]{1,0:T(8,128)(2,1)S(1)}, u32[]{:S(2)}, u32[]{:S(2)}) collective-permute-start(bf16[208,512]{1,0:T(8,128)(2,1)} %get-tuple-element.18.refs_5_), channel_id=1, source_target_pairs={{96,0},{97,1},{98,2},{99,3},{100,4},{101,5},{102,6},{103,7},{104,8... | collective-permute-start | bytes 638984 | tf_op jit(solution)/shard_map/ppermute | solution.py:37
  37.9 12.3 %collective-permute-start.8 = (bf16[208,512]{1,0:T(8,128)(2,1)}, bf16[208,512]{1,0:T(8,128)(2,1)S(1)}, u32[]{:S(2)}, u32[]{:S(2)}) collective-permute-start(bf16[208,512]{1,0:T(8,128)(2,1)} %get-tuple-element.18.refs_5_), channel_id=1, source_target_pairs={{32,0},{33,1},{34,2},{35,3},{36,4},{37,5},{38,6},{39,7},{40,8},{41... | collective-permute-start | bytes 638984 | tf_op jit(solution)/shard_map/ppermute | solution.py:37
  40.1 10.9 %collective-permute-start.6 = (bf16[208,512]{1,0:T(8,128)(2,1)}, bf16[208,512]{1,0:T(8,128)(2,1)S(1)}, u32[]{:S(2)}, u32[]{:S(2)}) collective-permute-start(bf16[208,512]{1,0:T(8,128)(2,1)} %get-tuple-element.18.refs_5_), channel_id=1, source_target_pairs={{64,0},{65,1},{66,2},{67,3},{68,4},{69,5},{70,6},{71,7},{72,8},{73... | collective-permute-start | bytes 638984 | tf_op jit(solution)/shard_map/ppermute | solution.py:37
  42.9 9.9 %collective-permute-start.3 = (bf16[200,512]{1,0:T(8,128)(2,1)S(1)}, bf16[200,512]{1,0:T(8,128)(2,1)S(1)}, u32[]{:S(2)}, u32[]{:S(2)}) collective-permute-start(bf16[200,512]{1,0:T(8,128)(2,1)S(1)} %constant_dynamic-update-slice_fusion.refs_1_), channel_id=1, source_target_pairs={{4,0},{5,1},{6,2},{7,3},{8,4},{9,5},{10,6},{11,7},{12,8},{13,9},{1... | collective-permute-start | bytes 614408 | tf_op jit(solution)/shard_map/ppermute | solution.py:37
  46.0 26.4 %collective-permute-start.11 = (bf16[208,512]{1,0:T(8,128)(2,1)S(1)}, bf16[208,512]{1,0:T(8,128)(2,1)S(1)}, u32[]{:S(2)}, u32[]{:S(2)}) collective-permute-start(bf16[208,512]{1,0:T(8,128)(2,1)S(1)} %collective-permute-done.10.refs_7_), channel_id=1, source_target_pairs={{1,0},{0,1},{3,2},{2,3},{5,4},{4,5},{7,6},{6,7},{9,8},{8,9},{11,10... | collective-permute-start | bytes 638984 | tf_op jit(solution)/shard_map/ppermute | solution.py:37
  50.2 22.2 %collective-permute-start.9 = (bf16[208,512]{1,0:T(8,128)(2,1)S(1)}, bf16[208,512]{1,0:T(8,128)(2,1)S(1)}, u32[]{:S(2)}, u32[]{:S(2)}) collective-permute-start(bf16[208,512]{1,0:T(8,128)(2,1)S(1)} %collective-permute-done.8.refs_5_), channel_id=1, source_target_pairs={{1,0},{0,1},{3,2},{2,3},{5,4},{4,5},{7,6},{6,7},{9,8},{8,9},{11,10... | collective-permute-start | bytes 638984 | tf_op jit(solution)/shard_map/ppermute | solution.py:37
  51.1 32.5 %collective-permute-start.7 = (bf16[208,512]{1,0:T(8,128)(2,1)S(1)}, bf16[208,512]{1,0:T(8,128)(2,1)S(1)}, u32[]{:S(2)}, u32[]{:S(2)}) collective-permute-start(bf16[208,512]{1,0:T(8,128)(2,1)S(1)} %collective-permute-done.6.refs_5_), channel_id=1, source_target_pairs={{1,0},{0,1},{3,2},{2,3},{5,4},{4,5},{7,6},{6,7},{9,8},{8,9},{11,10... | collective-permute-start | bytes 638984 | tf_op jit(solution)/shard_map/ppermute | solution.py:37
  51.1 8.8 %collective-permute-start.4 = (bf16[200,512]{1,0:T(8,128)(2,1)S(1)}, bf16[200,512]{1,0:T(8,128)(2,1)S(1)}, u32[]{:S(2)}, u32[]{:S(2)}) collective-permute-start(bf16[200,512]{1,0:T(8,128)(2,1)S(1)} %constant_dynamic-update-slice_fusion.refs_1_), channel_id=1, source_target_pairs={{12,0},{13,1},{14,2},{15,3},{0,4},{1,5},{2,6},{3,7},{4,8},{5,9},{6... | collective-permute-start | bytes 614408 | tf_op jit(solution)/shard_map/ppermute | solution.py:37
  52.7 12.7 %collective-permute-start.5 = (bf16[200,512]{1,0:T(8,128)(2,1)S(1)}, bf16[200,512]{1,0:T(8,128)(2,1)S(1)}, u32[]{:S(2)}, u32[]{:S(2)}) collective-permute-start(bf16[200,512]{1,0:T(8,128)(2,1)S(1)} %constant_dynamic-update-slice_fusion.refs_1_), channel_id=1, source_target_pairs={{8,0},{9,1},{10,2},{11,3},{12,4},{13,5},{14,6},{15,7},{0,8},{1,9},... | collective-permute-start | bytes 614408 | tf_op jit(solution)/shard_map/ppermute | solution.py:37
  91.2 26.4 %collective-permute-start.19 = (bf16[200,512]{1,0:T(8,128)(2,1)S(1)}, bf16[200,512]{1,0:T(8,128)(2,1)S(1)}, u32[]{:S(2)}, u32[]{:S(2)}) collective-permute-start(bf16[200,512]{1,0:T(8,128)(2,1)S(1)} %copy-done.15), channel_id=1, source_target_pairs={{1,0},{0,1},{3,2},{2,3},{5,4},{4,5},{7,6},{6,7},{9,8},{8,9},{11,10... | collective-permute-start | bytes 614408 | tf_op jit(solution)/shard_map/ppermute | solution.py:37
  91.7 18.7 %collective-permute-start.20 = (bf16[200,1024]{1,0:T(8,128)(2,1)S(1)}, bf16[200,1024]{1,0:T(8,128)(2,1)S(1)}, u32[]{:S(2)}, u32[]{:S(2)}) collective-permute-start(bf16[200,1024]{1,0:T(8,128)(2,1)S(1)} %copy-done.14), channel_id=1, source_target_pairs={{1,0},{0,1},{3,2},{2,3},{5,4},{4,5},{7,6},{6,7},{9,8},{8,9},{11,10... | collective-permute-start | bytes 1228808 | tf_op jit(solution)/shard_map/ppermute | solution.py:37
  91.8 13.2 %collective-permute-start.13 = (bf16[200,512]{1,0:T(8,128)(2,1)}, bf16[200,512]{1,0:T(8,128)(2,1)S(1)}, u32[]{:S(2)}, u32[]{:S(2)}) collective-permute-start(bf16[200,512]{1,0:T(8,128)(2,1)} %get-tuple-element.22), channel_id=1, source_target_pairs={{12,0},{13,1},{14,2},{15,3},{0,4},{1,5},{2,6},{3,7},{4,8},{5,9},{6... | collective-permute-start | bytes 614408 | tf_op jit(solution)/shard_map/ppermute | solution.py:37
  91.8 14.1 %collective-permute-start.14 = (bf16[200,512]{1,0:T(8,128)(2,1)}, bf16[200,512]{1,0:T(8,128)(2,1)S(1)}, u32[]{:S(2)}, u32[]{:S(2)}) collective-permute-start(bf16[200,512]{1,0:T(8,128)(2,1)} %get-tuple-element.23), channel_id=1, source_target_pairs={{4,0},{5,1},{6,2},{7,3},{8,4},{9,5},{10,6},{11,7},{12,8},{13,9},{1... | collective-permute-start | bytes 614408 | tf_op jit(solution)/shard_map/ppermute | solution.py:37
  95.0 10.9 %collective-permute-start.15 = (bf16[200,512]{1,0:T(8,128)(2,1)}, bf16[200,512]{1,0:T(8,128)(2,1)S(1)}, u32[]{:S(2)}, u32[]{:S(2)}) collective-permute-start(bf16[200,512]{1,0:T(8,128)(2,1)} %get-tuple-element.24), channel_id=1, source_target_pairs={{8,0},{9,1},{10,2},{11,3},{12,4},{13,5},{14,6},{15,7},{0,8},{1,9},... | collective-permute-start | bytes 614408 | tf_op jit(solution)/shard_map/ppermute | solution.py:37
  105.0 12.5 %collective-permute-start.24 = (bf16[200,512]{1,0:T(8,128)(2,1)S(1)}, bf16[200,512]{1,0:T(8,128)(2,1)S(1)}, u32[]{:S(2)}, u32[]{:S(2)}) collective-permute-start(bf16[200,512]{1,0:T(8,128)(2,1)S(1)} %add_convert_fusion), channel_id=1, source_target_pairs={{64,0},{65,1},{66,2},{67,3},{68,4},{69,5},{70,6},{71,7},{72,8},{73... | collective-permute-start | bytes 614408 | tf_op jit(solution)/shard_map/ppermute | solution.py:37
  107.1 5.4 %collective-permute-start.16 = (bf16[200,128]{1,0:T(8,128)(2,1)S(1)}, bf16[200,128]{1,0:T(8,128)(2,1)S(1)}, u32[]{:S(2)}, u32[]{:S(2)}) collective-permute-start(bf16[200,128]{1,0:T(8,128)(2,1)S(1)} %get-tuple-element.36), channel_id=1, source_target_pairs={{18,0},{19,1},{16,2},{17,3},{22,4},{23,5},{20,6},{21,7},{26,8},{27... | collective-permute-start | bytes 153608 | tf_op jit(solution)/shard_map/ppermute | solution.py:37
  109.0 6.2 %collective-permute-start.17 = (bf16[200,128]{1,0:T(8,128)(2,1)S(1)}, bf16[200,128]{1,0:T(8,128)(2,1)S(1)}, u32[]{:S(2)}, u32[]{:S(2)}) collective-permute-start(bf16[200,128]{1,0:T(8,128)(2,1)S(1)} %get-tuple-element.38), channel_id=1, source_target_pairs={{16,0},{17,1},{18,2},{19,3},{20,4},{21,5},{22,6},{23,7},{24,8},{25... | collective-permute-start | bytes 153608 | tf_op jit(solution)/shard_map/ppermute | solution.py:37
  110.4 6.5 %collective-permute-start.18 = (bf16[200,128]{1,0:T(8,128)(2,1)S(1)}, bf16[200,128]{1,0:T(8,128)(2,1)S(1)}, u32[]{:S(2)}, u32[]{:S(2)}) collective-permute-start(bf16[200,128]{1,0:T(8,128)(2,1)S(1)} %get-tuple-element.37), channel_id=1, source_target_pairs={{2,0},{3,1},{0,2},{1,3},{6,4},{7,5},{4,6},{5,7},{10,8},{11,9},{8,1... | collective-permute-start | bytes 153608 | tf_op jit(solution)/shard_map/ppermute | solution.py:37
  112.5 7.5 %collective-permute-start.21 = (bf16[200,512]{1,0:T(8,128)(2,1)S(1)}, bf16[200,512]{1,0:T(8,128)(2,1)S(1)}, u32[]{:S(2)}, u32[]{:S(2)}) collective-permute-start(bf16[200,512]{1,0:T(8,128)(2,1)S(1)} %get-tuple-element.34), channel_id=1, source_target_pairs={{96,0},{97,1},{98,2},{99,3},{100,4},{101,5},{102,6},{103,7},{104,8... | collective-permute-start | bytes 614408 | tf_op jit(solution)/shard_map/ppermute | solution.py:37
  115.2 5.8 %collective-permute-start.22 = (bf16[200,512]{1,0:T(8,128)(2,1)S(1)}, bf16[200,512]{1,0:T(8,128)(2,1)S(1)}, u32[]{:S(2)}, u32[]{:S(2)}) collective-permute-start(bf16[200,512]{1,0:T(8,128)(2,1)S(1)} %get-tuple-element.35), channel_id=1, source_target_pairs={{32,0},{33,1},{34,2},{35,3},{36,4},{37,5},{38,6},{39,7},{40,8},{41... | collective-permute-start | bytes 614408 | tf_op jit(solution)/shard_map/ppermute | solution.py:37
  (17 other events, 213.2 us)

commit v2 on v1

v2 whole, which is shorter than its diff:
```python
import functools
import math

import jax
import jax.numpy as jnp
from jax import lax
from jax.experimental import pallas as pl
from jax.experimental.pallas import tpu as pltpu
from jax.sharding import PartitionSpec as P

AXES = ("ent", "qry")
BF16 = jnp.bfloat16
F32 = jnp.float32
LANES = 128
WIDE = 256
CHUNK = 4096
UNROLL = 64
SPAN = 512
VMEM_BYTES = 8 * 1024 * 1024
SCORE_BYTES = 40 * 1024 * 1024
CHUNKS = 2
FAR = (1, 3, 2)


def flat_of(x, y, z, core):
    return z * 32 + (x % 2) * 16 + y * 4 + (x // 2) * 2 + core


def coords_of(flat):
    x = ((flat // 2) % 2) * 2 + (flat // 16) % 2
    return x, (flat // 4) % 4, flat // 32, flat % 2


def moved(block, dx=0, dy=0, dz=0, dcore=0):
    route = []
    for to in range(128):
        x, y, z, core = coords_of(to)
        route.append((flat_of((x + dx) % 4, (y + dy) % 4, (z + dz) % 4, (core + dcore) % 2), to))
    return lax.ppermute(block, AXES, route)


def gather_rows(ids, table, rows, width, count, start, total):
    per = width // UNROLL

    def some(step, carry):
        first = step // per * count + start + step % per * UNROLL
        place = pl.multiple_of(step * (2 * UNROLL), 2 * UNROLL)
        picked = [table[pl.ds(ids[first + k], 2), :] for k in range(UNROLL)]
        for k in range(UNROLL):
            rows[pl.ds(place + 2 * k, 2), :] = picked[k]
        return carry

    lax.fori_loop(0, total // count * per, some, 0)


def relation_rows(ids, rel_table):
    shape = (rel_table.shape[1], ids.shape[1])
    hot = lax.broadcasted_iota(jnp.int32, shape, 0) == jnp.broadcast_to(ids, shape)
    hot = jnp.where(hot, 1.0, 0.0).astype(BF16)
    return jnp.dot(rel_table[...], hot, preferred_element_type=F32)


def encoded(rows, rel_ids, weights, rel_table):
    n_rel, width = rel_ids.shape
    anchors = weights.shape[1] // WIDE - n_rel
    total = jnp.zeros((weights.shape[0], width), F32)
    for t in range(anchors):
        halves = [rows[pl.ds(t * 2 * width + h, width, stride=2), :] for h in range(2)]
        part = jnp.concatenate(halves, axis=1).astype(BF16)
        total = total + lax.dot_general(
            weights[:, t * WIDE : (t + 1) * WIDE],
            part,
            (((1,), (1,)), ((), ())),
            preferred_element_type=F32,
        )
    for t in range(n_rel):
        part = relation_rows(rel_ids[t : t + 1, :], rel_table).astype(BF16)
        first = (anchors + t) * WIDE
        total = total + jnp.dot(weights[:, first : first + WIDE], part, preferred_element_type=F32)
    return total


def prepare(tab_t, w_t, rel_t, table, weights, rel_table, relations):
    step = pl.program_id(0)
    depth = tab_t.shape[0]

    @pl.when(step == 0)
    def _():
        lane = lax.broadcasted_iota(jnp.int32, (depth, WIDE), 1)
        for t in range(weights.shape[1] // WIDE):
            start = t * depth
            base = start // LANES * LANES
            piece = w_t[:, base : base + 3 * LANES].astype(F32)
            if start > base:
                piece = pltpu.roll(piece, 3 * LANES - (start - base), 1)
            weights[:, t * WIDE : (t + 1) * WIDE] = jnp.where(
                lane < depth, piece[:, :WIDE], 0.0
            ).astype(BF16)
        known = lax.broadcasted_iota(jnp.int32, rel_t.shape, 1) < relations
        rel = jnp.where(known, rel_t[...].astype(F32), 0.0)
        rel_table[...] = jnp.concatenate(
            [rel, jnp.zeros((WIDE - depth, rel.shape[1]), F32)], axis=0
        ).astype(BF16)

    chunk = tab_t.shape[1]
    top = tab_t[:LANES, :].astype(F32).T
    rest = jnp.concatenate(
        [tab_t[LANES:, :].astype(F32), jnp.zeros((WIDE - depth, chunk), F32)], axis=0
    ).T
    table[pl.ds(step * 2 * chunk, chunk, stride=2), :] = top
    table[pl.ds(step * 2 * chunk + 1, chunk, stride=2), :] = rest


def entity_kernel(
    relations, scale, own_ids, tab_t, w_t, rel_t, own_rel,
    own_out, table, weights, rel_table, rows,
):
    prepare(tab_t, w_t, rel_t, table, weights, rel_table, relations)

    @pl.when(pl.program_id(0) == pl.num_programs(0) - 1)
    def _():
        width = own_rel.shape[1]
        gather_rows(own_ids, table, rows, width, width, 0, own_ids.shape[0])
        own_out[...] = (encoded(rows, own_rel, weights, rel_table) * scale).astype(BF16)


def head_kernel(
    start, width, head_ids, head_rel, asked, wanted, fc, echo, table, weights, rel_table, *refs
):
    query_out, echo_out, rows = refs[-6], refs[-5], refs[-1]
    if start:
        query_out[:, :start] = refs[0][...]
    echo_out[...] = echo[...]
    part = slice(start, start + width)
    gather_rows(head_ids, table, rows, width, head_rel.shape[1], start, head_ids.shape[0])
    head = encoded(rows, head_rel[:, part], weights, rel_table).astype(BF16)
    mixed = head.astype(F32) * relation_rows(asked[:, part], rel_table)[: head.shape[0], :]
    query = jnp.tanh(
        lax.dot_general(
            fc[...], mixed.astype(BF16), (((0,), (0,)), ((), ())), preferred_element_type=F32
        )
    )
    digits = []
    for t in range(wanted.shape[0]):
        target = wanted[t : t + 1, part]
        digits += [target // LANES, target % LANES]
    query_out[:, query_out.shape[1] - width :] = jnp.concatenate(
        [query, jnp.concatenate(digits, axis=0).astype(F32)], axis=0
    ).astype(BF16)


def encode_entities(anchor_ids, relation_ids, anchor_table, relation_table, enc_weight, scale):
    own, anchors = anchor_ids.shape
    count, depth = anchor_table.shape
    relations = relation_table.shape[0]
    steps = pl.cdiv(count, CHUNK)
    tokens = anchors + relation_ids.shape[1]
    rel_lanes = pl.cdiv(relations, LANES) * LANES
    w_lanes = pl.cdiv((tokens - 1) * depth // LANES * LANES + 3 * LANES, LANES) * LANES
    whole = pl.BlockSpec(memory_space=pltpu.VMEM)
    once = pl.Buffered(1)
    return pl.pallas_call(
        functools.partial(entity_kernel, relations, scale),
        grid=(steps,),
        in_specs=[
            pl.BlockSpec(memory_space=pltpu.SMEM),
            pl.BlockSpec((depth, CHUNK), lambda i: (0, i)),
            pl.BlockSpec((depth, w_lanes), lambda i: (0, 0), pipeline_mode=once),
            pl.BlockSpec((depth, rel_lanes), lambda i: (0, 0), pipeline_mode=once),
            whole,
        ],
        out_specs=[whole] * 4,
        out_shape=[
            jax.ShapeDtypeStruct((depth, own), BF16),
            pltpu.VMEM((2 * steps * CHUNK, LANES), F32),
            pltpu.VMEM((depth, tokens * WIDE), BF16),
            pltpu.VMEM((WIDE, rel_lanes), BF16),
        ],
        scratch_shapes=[pltpu.VMEM((2 * own * anchors, LANES), F32)],
        compiler_params=pltpu.CompilerParams(vmem_limit_bytes=VMEM_BYTES),
    )(
        (anchor_ids.T * 2).reshape(-1), anchor_table.T, enc_weight.T, relation_table.T,
        relation_ids.T,
    )


def encode_heads(
    chunk, head_ids, head_relations, query_relation, targets, fc_weight, echo,
    table, weights, rel_table, earlier,
):
    heads = head_relations.shape[1] // CHUNKS
    depth = fc_weight.shape[0]
    anchors = weights.shape[1] // WIDE - head_relations.shape[0]
    whole = pl.BlockSpec(memory_space=pltpu.VMEM)
    return pl.pallas_call(
        functools.partial(head_kernel, chunk * heads, heads),
        in_specs=[pl.BlockSpec(memory_space=pltpu.SMEM)] + [whole] * (8 + len(earlier)),
        out_specs=[whole] * 5,
        out_shape=[
            jax.ShapeDtypeStruct((depth + 2 * targets.shape[0], heads * (chunk + 1)), BF16),
            jax.ShapeDtypeStruct(echo.shape, BF16),
            pltpu.VMEM(table.shape, F32),
            pltpu.VMEM(weights.shape, BF16),
            pltpu.VMEM(rel_table.shape, BF16),
        ],
        input_output_aliases={6: 2, 7: 3, 8: 4},
        scratch_shapes=[pltpu.VMEM((2 * heads * anchors, LANES), F32)],
        compiler_params=pltpu.CompilerParams(vmem_limit_bytes=VMEM_BYTES),
    )(
        head_ids, head_relations, query_relation, targets, fc_weight, echo,
        table, weights, rel_table, *earlier,
    )


def score_kernel(plain, struck_value, depth, parts, stage, me, slab, *refs):
    blocks, refs = refs[:4], refs[4:]
    if stage:
        before, refs = refs[0], refs[1:]
    if stage == 2:
        kept, sent, refs = refs[0], refs[1:4], refs[4:]
    else:
        asks, refs = refs[0], refs[1:]
    ent_outs, refs = refs[: len(parts)] if stage else refs[:1], refs[len(parts) if stage else 1 :]
    tall, queries, marks, totals, *held = refs[:6]
    if stage == 2:
        asks = refs[6]
    width = SPAN
    tiles = SPAN // LANES

    x, y, z, core = coords_of(me[0])
    if not stage:
        core = 1 - core
    spots = [
        flat_of((x + dx) % 4, (y + ((0,) + FAR)[part]) % 4, z, core)
        for part in parts
        for dx in (0,) + FAR
    ]
    for k, part in enumerate(parts):
        wide = jnp.concatenate(
            [
                slab[:, part * SPAN : (part + 1) * SPAN].astype(F32),
                jnp.zeros((WIDE - depth, SPAN), F32),
            ],
            axis=0,
        )
        tall[k * SPAN : (k + 1) * SPAN, :] = wide.T.astype(BF16)
    within = lax.broadcasted_iota(jnp.int32, (LANES, width), 0)
    for b in range(4):
        query = blocks[b][...].astype(F32)
        queries[b] = jnp.concatenate(
            [query[:depth, :], jnp.zeros((WIDE - depth, width), F32)], axis=0
        ).astype(BF16)
        digits = query[depth:, :].astype(jnp.int32)
        marked = jnp.zeros((LANES, width), jnp.int32)
        for t in range(digits.shape[0] // 2):
            owner = digits[2 * t : 2 * t + 1, :]
            low = digits[2 * t + 1 : 2 * t + 2, :]
            bit = jnp.zeros(owner.shape, jnp.int32)
            for k, spot in enumerate(spots):
                bit = jnp.where(owner == spot, 1 << k, bit)
            marked = marked | jnp.where(within == low, bit, 0)
        marks[b] = marked

    def residual_of(step):
        k, b = step // 4, step % 4
        score = jnp.dot(
            tall[k * SPAN : (k + 1) * SPAN, :], queries[b], preferred_element_type=F32
        )
        marked = marks[b]
        for j in range(tiles):
            hit = (marked & (1 << (k * tiles + j))) != 0
            label = jnp.where(hit, struck_value, plain)
            at = slice(j * LANES, (j + 1) * LANES)
            held[step % 2][at, :] = (jnp.tanh(score[at, :]) + label).astype(BF16)

    def use(step):
        k, b = step // 4, step % 4
        first = parts[k] * SPAN
        residual = held[step % 2][...]
        ent = lax.dot_general(
            residual, queries[b], (((1,), (1,)), ((), ())), preferred_element_type=F32
        )
        ask = jnp.dot(slab[:, first : first + SPAN], residual, preferred_element_type=F32)
        if b == 0:
            totals[...] = ent
        elif b < 3:
            totals[...] += ent
        else:
            ent = (totals[...] + ent).T[:depth, :]
            if stage:
                ent_outs[k][...] = ent
            else:
                ent_outs[0][:, k * SPAN : (k + 1) * SPAN] = ent.astype(BF16)
        if k:
            ask = asks[b] + ask
        elif stage:
            ask = before[b] + ask
        if stage == 2 and k == len(parts) - 1:
            if b:
                sent[b - 1][...] = ask.astype(BF16)
            else:
                kept[...] = ask
        else:
            asks[b] = ask

    steps = 4 * len(parts)
    residual_of(0)
    for step in range(steps):
        if step + 1 < steps:
            residual_of(step + 1)
        use(step)


def score(me, slab, blocks, parts, stage, total_entities, before=None):
    depth, entities = slab.shape
    plain = 1.0 - 2.0 * (0.1 / total_entities)
    shape = jax.ShapeDtypeStruct
    total = pltpu.VMEM((4, depth, SPAN), F32)
    outs = [total]
    if stage == 2:
        outs = [shape((depth, SPAN), F32)] + [shape((depth, SPAN), BF16)] * 3
    outs += [shape((depth, SPAN), F32)] * len(parts) if stage else [shape((depth, entities), BF16)]
    scratch = [
        pltpu.VMEM((len(parts) * SPAN, WIDE), BF16),
        pltpu.VMEM((4, WIDE, SPAN), BF16),
        pltpu.VMEM((4, LANES, SPAN), jnp.int32),
        pltpu.VMEM((SPAN, WIDE), F32),
        pltpu.VMEM((SPAN, SPAN), BF16),
        pltpu.VMEM((SPAN, SPAN), BF16),
    ]
    if stage == 2:
        scratch.append(total)
    whole = pl.BlockSpec(memory_space=pltpu.VMEM)
    extra = [before] if stage else []
    return pl.pallas_call(
        functools.partial(score_kernel, plain, plain - 1.8, depth, parts, stage),
        in_specs=[pl.BlockSpec(memory_space=pltpu.SMEM)] + [whole] * (1 + len(blocks) + len(extra)),
        out_specs=[whole] * len(outs),
        out_shape=outs,
        input_output_aliases={2 + len(blocks): 0} if stage == 1 else {},
        scratch_shapes=scratch,
        compiler_params=pltpu.CompilerParams(vmem_limit_bytes=SCORE_BYTES),
    )(me, slab, *blocks, *extra)


def body(
    anchor_ids,
    relation_ids,
    head_anchors,
    head_relations,
    query_relation,
    targets,
    anchor_table,
    relation_table,
    enc_weight,
    fc_weight,
):
    width = anchor_ids.shape[0]
    entities = width * 128
    queries = head_anchors.shape[0] * 128
    scale = 0.5 * float(anchor_table.shape[1]) ** (-0.5)
    me = (lax.axis_index("ent") * 16 + lax.axis_index("qry")).astype(jnp.int32)[None]
    own_cols, *shared = encode_entities(
        anchor_ids, relation_ids, anchor_table, relation_table, enc_weight, scale
    )
    head_ids = (head_anchors.T * 2).reshape(-1)
    query = []
    piece = own_cols
    for chunk in range(CHUNKS):
        axis = ("dx", "dy")[chunk]
        sent = [moved(piece, **{axis: d}) for d in FAR]
        part, piece, *shared = encode_heads(
            chunk,
            head_ids,
            head_relations.T,
            query_relation[None, :],
            targets.T,
            fc_weight,
            piece,
            *shared,
            query,
        )
        query = [part]
        piece = jnp.concatenate([piece] + sent, axis=1)
    slab = piece
    other = moved(slab, dcore=1)
    blocks = query + [moved(part, dz=d) for part in query for d in FAR]
    asks, away = score(me, other, blocks, (0, 1, 2, 3), 0, entities)
    back = moved(away, dcore=1).astype(F32)
    asks, *ents = score(me, slab, blocks, (1, 2, 3), 1, entities, asks)
    span = slab.shape[1] // 4
    ents = [
        moved((ent + back[:, (k + 1) * span : (k + 2) * span]).astype(BF16), dy=-d)
        for k, (d, ent) in enumerate(zip(FAR, ents))
    ]
    query_total, *far, ent_row = score(me, slab, blocks, (0,), 2, entities, asks)
    ent_row = ent_row + back[:, :span]
    for ent in ents:
        ent_row = ent_row + ent.astype(F32)
    for d, part in zip(FAR, far):
        query_total = query_total + moved(part, dz=-d).astype(F32)
    ent_share = ent_row[:, :width]
    for k, d in enumerate(FAR):
        block = ent_row[:, (k + 1) * width : (k + 2) * width].astype(BF16)
        ent_share = ent_share + moved(block, dx=-d).astype(F32)
    return (
        ent_share * (0.5 / math.sqrt(queries)),
        query_total.T * (0.5 / scale / math.sqrt(entities)),
    )


def solution(mesh):
    spread = P(AXES, None)
    placed = (spread, spread, spread, spread, P(AXES), spread, P(), P(), P(), P())
    return jax.shard_map(
        body,
        mesh=mesh,
        in_specs=placed,
        out_specs=(P(None, AXES), spread),
        check_vma=False,
    )
```

time: 122 us -> 129 us (1.057)
  local copies, waits for them, and re-layouts: 4.27 us -> 34.6 us
  waiting for transfers between devices: 27.4 us -> 19 us
  Pallas kernels: 50.1 us -> 41.8 us
  starting transfers between devices: 33 us -> 28.8 us
  other arithmetic: 6.1 us -> 2.89 us
    unnamed x35 -> x32, local copies, waits for them, and re-layouts: 2.97 us -> 34.5 us
    ppermute x25 -> x20, waiting for transfers between devices: 27.4 us -> 19 us  [moved(): return lax.ppermute(block, AXES, route)]
    pallas_call x3, Pallas kernels: 23.5 us -> 15.1 us  [score(): pl.pallas_call(functools.partial(score_kernel, plain, plain - 1.8, depth,...]
    ppermute x25 -> x20, starting transfers between devices: 33 us -> 28.8 us  [moved(): return lax.ppermute(block, AXES, route)]
    pallas_call x1 -> x3, Pallas kernels: 26.6 us -> 26.6 us  [the longest x2 16.4 us: encode_heads(): pl.pallas_call(functools.partial(head_kernel, chunk * heads, heads), in_s...]
  transfers between devices with their start and end apart: 25 -> 20, of which waited for: 8 -> 5; matrix products, arithmetic and copies ran while one was open for 4% -> 1% of each run, Pallas kernels for 14% -> 19%
where the time goes in v2:
time: 129 us; the launch traced here: 128 us
  Pallas kernels  41.8 us (32%)
  local copies, waits for them, and re-layouts  34.6 us (27%)
  starting transfers between devices  28.8 us (22%)
  waiting for transfers between devices  19 us (15%)
  other arithmetic  2.89 us (2%)
    unnamed x32, local copies, waits for them, and re-layouts  34.5 us
    ppermute x20, starting transfers between devices, moved(): return lax.ppermute(block, AXES, route)  28.8 us
    ppermute x20, waiting for transfers between devices, moved(): return lax.ppermute(block, AXES, route)  19 us
    pallas_call x2, Pallas kernels, encode_heads(): pl.pallas_call(functools.partial(head_kernel, chunk * heads, heads), in_s...  16.4 us
    pallas_call x3, Pallas kernels, score(): pl.pallas_call(functools.partial(score_kernel, plain, plain - 1.8, depth,...  15.1 us
    pallas_call x1, Pallas kernels, encode_entities(): pl.pallas_call(functools.partial(entity_kernel, relations, scale), grid=(...  10.2 us
  transfers between devices with their start and end apart: 20, of which 5 were waited for; matrix products, arithmetic and copies ran while one was open for 1% of the time, Pallas kernels for 19%

profile of v2, /device:TPU:0, one launch (start us, length us, event | category | flops | bytes accessed | tf_op | source)
XLA Modules:
  0.0 127.9 jit_solution(7559142705012227908)
XLA Ops:
  1.3 3.3 %copy-done.4 = bf16[20000,200]{0,1:T(8,128)(2,1)S(1)} copy-done((bf16[20000,200]{0,1:T(8,128)(2,1)S(1)}, bf16[20000,200]{0,1:T(8,128)(2,1)}, u32[]{:S(2)}) %copy-start.4) | copy-done | bytes 8000024
  7.9 10.2 %shard_map.113 = (bf16[200,128]{1,0:T(8,128)(2,1)S(1)}, f32[40960,128]{1,0:T(8,128)S(1)}, bf16[200,6400]{1,0:T(8,128)(2,1)S(1)}, bf16[256,896]{1,0:T(8,128)(2,1)S(1)}) custom-call(s32[2560]{0:T(1024)S(1)} %multiply_bitcast_fusion.2.own_ids, bf16[200,20000]{1,0:T(8,128)(2,1)S(1)} %bitcast.16, bf16[200,5000]{1,0:T(8,128)(2,1)S(1)} %bitcast.17, ...), custom_call_target="tpu_custom_call" | custom-call | tf_op jit(solution)/shard_map/pallas_call | solution.py:162
  18.1 7.0 %copy-done = f32[40960,128]{1,0:T(8,128)} copy-done((f32[40960,128]{1,0:T(8,128)}, f32[40960,128]{1,0:T(8,128)S(1)}, u32[]{:S(2)}) %copy-start) | copy-done | bytes 20971544
  25.1 2.8 %collective-permute-start = (bf16[200,128]{1,0:T(8,128)(2,1)S(1)}, bf16[200,128]{1,0:T(8,128)(2,1)S(1)}, u32[]{:S(2)}, u32[]{:S(2)}) collective-permute-start(bf16[200,128]{1,0:T(8,128)(2,1)S(1)} %get-tuple-element.24.echo), channel_id=1, source_target_pairs={{16,0},{17,1},{18,2},{19,3},{20,4},{21,5},{22,6},{23,7},{24,8},{25... | collective-permute-start | bytes 153608 | tf_op jit(solution)/shard_map/ppermute | solution.py:39
  28.0 2.3 %collective-permute-start.2 = (bf16[200,128]{1,0:T(8,128)(2,1)S(1)}, bf16[200,128]{1,0:T(8,128)(2,1)S(1)}, u32[]{:S(2)}, u32[]{:S(2)}) collective-permute-start(bf16[200,128]{1,0:T(8,128)(2,1)S(1)} %get-tuple-element.24.echo), channel_id=1, source_target_pairs={{2,0},{3,1},{0,2},{1,3},{6,4},{7,5},{4,6},{5,7},{10,8},{11,9},{8,1... | collective-permute-start | bytes 153608 | tf_op jit(solution)/shard_map/ppermute | solution.py:39
  30.3 7.0 %copy-done.1 = f32[40960,128]{1,0:T(8,128)S(1)} copy-done((f32[40960,128]{1,0:T(8,128)S(1)}, f32[40960,128]{1,0:T(8,128)}, u32[]{:S(2)}) %copy-start.1) | copy-done | bytes 20971544
  37.3 8.2 %shard_map.114 = (bf16[208,256]{1,0:T(8,128)(2,1)S(1)}, bf16[200,128]{1,0:T(8,128)(2,1)S(1)}, f32[40960,128]{1,0:T(8,128)S(1)}, bf16[200,6400]{1,0:T(8,128)(2,1)S(1)}, bf16[256,896]{1,0:T(8,128)(2,1)S(1)}) custom-call(s32[10240]{0:T(1024)S(1)} %reshape.10.head_ids, ...), custom_call_target="tpu_custom_call", output_to_operand_aliasing={{2}: (6, {}), {3}: (7, {}), {4}: (8, {})} | custom-call | tf_op jit(solution)/shard_map/pallas_call | solution.py:195
  45.5 7.0 %copy-done.2 = f32[40960,128]{1,0:T(8,128)} copy-done((f32[40960,128]{1,0:T(8,128)}, f32[40960,128]{1,0:T(8,128)S(1)}, u32[]{:S(2)}) %copy-start.2) | copy-done | bytes 20971544
  52.6 3.1 %collective-permute-start.3 = (bf16[200,512]{1,0:T(8,128)(2,1)S(1)}, bf16[200,512]{1,0:T(8,128)(2,1)S(1)}, u32[]{:S(2)}, u32[]{:S(2)}) collective-permute-start(bf16[200,512]{1,0:T(8,128)(2,1)S(1)} %constant_dynamic-update-slice_fusion.echo), channel_id=1, source_target_pairs={{4,0},{5,1},{6,2},{7,3},{8,4},{9,5},{10,6},{11,7},{12,8},{13,9},{1... | collective-permute-start | bytes 614408 | tf_op jit(solution)/shard_map/ppermute | solution.py:39
  55.6 2.2 %collective-permute-start.5 = (bf16[200,512]{1,0:T(8,128)(2,1)S(1)}, bf16[200,512]{1,0:T(8,128)(2,1)S(1)}, u32[]{:S(2)}, u32[]{:S(2)}) collective-permute-start(bf16[200,512]{1,0:T(8,128)(2,1)S(1)} %constant_dynamic-update-slice_fusion.echo), channel_id=1, source_target_pairs={{8,0},{9,1},{10,2},{11,3},{12,4},{13,5},{14,6},{15,7},{0,8},{1,9},... | collective-permute-start | bytes 614408 | tf_op jit(solution)/shard_map/ppermute | solution.py:39
  57.9 7.0 %copy-done.3 = f32[40960,128]{1,0:T(8,128)S(1)} copy-done((f32[40960,128]{1,0:T(8,128)S(1)}, f32[40960,128]{1,0:T(8,128)}, u32[]{:S(2)}) %copy-start.3) | copy-done | bytes 20971544
  64.8 8.2 %shard_map.115 = (bf16[208,512]{1,0:T(8,128)(2,1)S(1)}, bf16[200,512]{1,0:T(8,128)(2,1)S(1)}, f32[40960,128]{1,0:T(8,128)S(1)}, bf16[200,6400]{1,0:T(8,128)(2,1)S(1)}, bf16[256,896]{1,0:T(8,128)(2,1)S(1)}) custom-call(s32[10240]{0:T(1024)S(1)} %reshape.10.head_ids, ...), custom_call_target="tpu_custom_call", output_to_operand_aliasing={{2}: (6, {}), {3}: (7, {}), {4}: (8, {})} | custom-call | tf_op jit(solution)/shard_map/pallas_call | solution.py:195
  73.3 4.1 %collective-permute-start.6 = (bf16[208,512]{1,0:T(8,128)(2,1)S(1)}, bf16[208,512]{1,0:T(8,128)(2,1)S(1)}, u32[]{:S(2)}, u32[]{:S(2)}) collective-permute-start(bf16[208,512]{1,0:T(8,128)(2,1)S(1)} %get-tuple-element.34.refs_0_), channel_id=1, source_target_pairs={{32,0},{33,1},{34,2},{35,3},{36,4},{37,5},{38,6},{39,7},{40,8},{41... | collective-permute-start | bytes 638984 | tf_op jit(solution)/shard_map/ppermute | solution.py:39
  77.4 1.9 %collective-permute-start.8 = (bf16[208,512]{1,0:T(8,128)(2,1)S(1)}, bf16[208,512]{1,0:T(8,128)(2,1)S(1)}, u32[]{:S(2)}, u32[]{:S(2)}) collective-permute-start(bf16[208,512]{1,0:T(8,128)(2,1)S(1)} %get-tuple-element.34.refs_0_), channel_id=1, source_target_pairs={{64,0},{65,1},{66,2},{67,3},{68,4},{69,5},{70,6},{71,7},{72,8},{73... | collective-permute-start | bytes 638984 | tf_op jit(solution)/shard_map/ppermute | solution.py:39
  79.2 7.8 %collective-permute-done.6.refs_1_ = bf16[208,512]{1,0:T(8,128)(2,1)S(1)} collective-permute-done((bf16[208,512]{1,0:T(8,128)(2,1)S(1)}, bf16[208,512]{1,0:T(8,128)(2,1)S(1)}, u32[]{:S(2)}, u32[]{:S(2)}) %collective-permute-start.6) | collective-permute-done | bytes 213024 | tf_op jit(solution)/shard_map/ppermute | solution.py:39
  87.1 3.4 %collective-permute-done.7.refs_2_ = bf16[208,512]{1,0:T(8,128)(2,1)S(1)} collective-permute-done((bf16[208,512]{1,0:T(8,128)(2,1)S(1)}, bf16[208,512]{1,0:T(8,128)(2,1)S(1)}, u32[]{:S(2)}, u32[]{:S(2)}) %collective-permute-start.7) | collective-permute-done | bytes 213024 | tf_op jit(solution)/shard_map/ppermute | solution.py:39
  90.5 6.8 %shard_map.116 = (f32[4,200,512]{2,1,0:T(8,128)S(1)}, bf16[200,2048]{1,0:T(8,128)(2,1)S(1)}) custom-call(s32[1]{0:T(128)} %bitcast.me, bf16[200,2048]{1,0:T(8,128)(2,1)S(1)} %collective-permute-done.9.slab, bf16[208,512]{1,0:T(8,128)(2,1)S(1)} %get-tuple-element.34.refs_0_, bf16[208,512]{1,0:T(8,128)(2,1)S(1)} %collective-permute-done.6.refs_1_, ...), custom_call_target="tpu_custom_call" | custom-call | tf_op jit(solution)/shard_map/pallas_call | solution.py:335
  97.6 6.3 %shard_map.117 = (f32[4,200,512]{2,1,0:T(8,128)S(1)}, f32[200,512]{1,0:T(8,128)S(1)}, f32[200,512]{1,0:T(8,128)S(1)}, f32[200,512]{1,0:T(8,128)S(1)}) custom-call(s32[1]{0:T(128)} %bitcast.me, bf16[200,2048]{1,0:T(8,128)(2,1)S(1)} %constant_dynamic-update-slice_fusion.4.slab, ...), custom_call_target="tpu_custom_call", output_to_operand_aliasing={{0}: (6, {})} | custom-call | tf_op jit(solution)/shard_map/pallas_call | solution.py:335
  104.4 2.0 %collective-permute-start.11 = (bf16[200,512]{1,0:T(8,128)(2,1)S(1)}, bf16[200,512]{1,0:T(8,128)(2,1)S(1)}, u32[]{:S(2)}, u32[]{:S(2)}) collective-permute-start(bf16[200,512]{1,0:T(8,128)(2,1)S(1)} %get-tuple-element.48), channel_id=1, source_target_pairs={{12,0},{13,1},{14,2},{15,3},{0,4},{1,5},{2,6},{3,7},{4,8},{5,9},{6... | collective-permute-start | bytes 614408 | tf_op jit(solution)/shard_map/ppermute | solution.py:39
  108.5 2.0 %shard_map.118 = (f32[200,512]{1,0:T(8,128)S(1)}, bf16[200,512]{1,0:T(8,128)(2,1)S(1)}, bf16[200,512]{1,0:T(8,128)(2,1)S(1)}, bf16[200,512]{1,0:T(8,128)(2,1)S(1)}, f32[200,512]{1,0:T(8,128)S(1)}) custom-call(s32[1]{0:T(128)} %bitcast.me, bf16[200,2048]{1,0:T(8,128)(2,1)S(1)} %constant_dynamic-update-slice_fusion.4.slab, ...), custom_call_target="tpu_custom_call" | custom-call | tf_op jit(solution)/shard_map/pallas_call | solution.py:335
  110.6 3.2 %collective-permute-start.18 = (bf16[200,512]{1,0:T(8,128)(2,1)S(1)}, bf16[200,512]{1,0:T(8,128)(2,1)S(1)}, u32[]{:S(2)}, u32[]{:S(2)}) collective-permute-start(bf16[200,512]{1,0:T(8,128)(2,1)S(1)} %get-tuple-element.44), channel_id=1, source_target_pairs={{32,0},{33,1},{34,2},{35,3},{36,4},{37,5},{38,6},{39,7},{40,8},{41... | collective-permute-start | bytes 614408 | tf_op jit(solution)/shard_map/ppermute | solution.py:39
  113.9 3.7 %collective-permute-done.11 = bf16[200,512]{1,0:T(8,128)(2,1)S(1)} collective-permute-done((bf16[200,512]{1,0:T(8,128)(2,1)S(1)}, bf16[200,512]{1,0:T(8,128)(2,1)S(1)}, u32[]{:S(2)}, u32[]{:S(2)}) %collective-permute-start.11) | collective-permute-done | bytes 204832 | tf_op jit(solution)/shard_map/ppermute | solution.py:39
  118.3 1.9 %collective-permute-start.14 = (bf16[200,128]{1,0:T(8,128)(2,1)S(1)}, bf16[200,128]{1,0:T(8,128)(2,1)S(1)}, u32[]{:S(2)}, u32[]{:S(2)}) collective-permute-start(bf16[200,128]{1,0:T(8,128)(2,1)S(1)} %get-tuple-element.51), channel_id=1, source_target_pairs={{18,0},{19,1},{16,2},{17,3},{22,4},{23,5},{20,6},{21,7},{26,8},{27... | collective-permute-start | bytes 153608 | tf_op jit(solution)/shard_map/ppermute | solution.py:39
  122.3 3.4 %collective-permute-done.19 = bf16[200,512]{1,0:T(8,128)(2,1)S(1)} collective-permute-done((bf16[200,512]{1,0:T(8,128)(2,1)S(1)}, bf16[200,512]{1,0:T(8,128)(2,1)S(1)}, u32[]{:S(2)}, u32[]{:S(2)}) %collective-permute-start.19) | collective-permute-done | bytes 204832 | tf_op jit(solution)/shard_map/ppermute | solution.py:39
  (65 shorter events, 12.3 us)
Async XLA Ops:
  7.9 22.4 %copy-start.6 = (bf16[200,200]{1,0:T(8,128)(2,1)S(1)}, bf16[200,200]{1,0:T(8,128)(2,1)}, u32[]{:S(2)}) copy-start(bf16[200,200]{1,0:T(8,128)(2,1)} %fc.3) | copy-start | bytes 240004
  7.9 22.4 %copy-start.8 = (s32[512,5]{0,1:T(8,128)S(1)}, s32[512,5]{0,1:T(8,128)}, u32[]{:S(2)}) copy-start(s32[512,5]{0,1:T(8,128)} %param.13) | copy-start | bytes 30724
  7.9 22.4 %copy-start.9 = (s32[512,4]{0,1:T(4,128)S(1)}, s32[512,4]{0,1:T(4,128)}, u32[]{:S(2)}) copy-start(s32[512,4]{0,1:T(4,128)} %param.15) | copy-start | bytes 24580
  7.9 22.4 %copy-start.10 = (s32[512]{0:T(512)S(1)}, s32[512]{0:T(512)}, u32[]{:S(2)}) copy-start(s32[512]{0:T(512)} %param.14) | copy-start | bytes 6148
  25.1 27.4 %collective-permute-start = (bf16[200,128]{1,0:T(8,128)(2,1)S(1)}, bf16[200,128]{1,0:T(8,128)(2,1)S(1)}, u32[]{:S(2)}, u32[]{:S(2)}) collective-permute-start(bf16[200,128]{1,0:T(8,128)(2,1)S(1)} %get-tuple-element.24.echo), channel_id=1, source_target_pairs={{16,0},{17,1},{18,2},{19,3},{20,4},{21,5},{22,6},{23,7},{24,8},{25... | collective-permute-start | bytes 153608 | tf_op jit(solution)/shard_map/ppermute | solution.py:39
  28.0 24.5 %collective-permute-start.1 = (bf16[200,128]{1,0:T(8,128)(2,1)S(1)}, bf16[200,128]{1,0:T(8,128)(2,1)S(1)}, u32[]{:S(2)}, u32[]{:S(2)}) collective-permute-start(bf16[200,128]{1,0:T(8,128)(2,1)S(1)} %get-tuple-element.24.echo), channel_id=1, source_target_pairs={{18,0},{19,1},{16,2},{17,3},{22,4},{23,5},{20,6},{21,7},{26,8},{27... | collective-permute-start | bytes 153608 | tf_op jit(solution)/shard_map/ppermute | solution.py:39
  28.0 24.6 %collective-permute-start.2 = (bf16[200,128]{1,0:T(8,128)(2,1)S(1)}, bf16[200,128]{1,0:T(8,128)(2,1)S(1)}, u32[]{:S(2)}, u32[]{:S(2)}) collective-permute-start(bf16[200,128]{1,0:T(8,128)(2,1)S(1)} %get-tuple-element.24.echo), channel_id=1, source_target_pairs={{2,0},{3,1},{0,2},{1,3},{6,4},{7,5},{4,6},{5,7},{10,8},{11,9},{8,1... | collective-permute-start | bytes 153608 | tf_op jit(solution)/shard_map/ppermute | solution.py:39
  52.6 20.5 %collective-permute-start.3 = (bf16[200,512]{1,0:T(8,128)(2,1)S(1)}, bf16[200,512]{1,0:T(8,128)(2,1)S(1)}, u32[]{:S(2)}, u32[]{:S(2)}) collective-permute-start(bf16[200,512]{1,0:T(8,128)(2,1)S(1)} %constant_dynamic-update-slice_fusion.echo), channel_id=1, source_target_pairs={{4,0},{5,1},{6,2},{7,3},{8,4},{9,5},{10,6},{11,7},{12,8},{13,9},{1... | collective-permute-start | bytes 614408 | tf_op jit(solution)/shard_map/ppermute | solution.py:39
  55.6 17.5 %collective-permute-start.4 = (bf16[200,512]{1,0:T(8,128)(2,1)S(1)}, bf16[200,512]{1,0:T(8,128)(2,1)S(1)}, u32[]{:S(2)}, u32[]{:S(2)}) collective-permute-start(bf16[200,512]{1,0:T(8,128)(2,1)S(1)} %constant_dynamic-update-slice_fusion.echo), channel_id=1, source_target_pairs={{12,0},{13,1},{14,2},{15,3},{0,4},{1,5},{2,6},{3,7},{4,8},{5,9},{6... | collective-permute-start | bytes 614408 | tf_op jit(solution)/shard_map/ppermute | solution.py:39
  55.6 17.5 %collective-permute-start.5 = (bf16[200,512]{1,0:T(8,128)(2,1)S(1)}, bf16[200,512]{1,0:T(8,128)(2,1)S(1)}, u32[]{:S(2)}, u32[]{:S(2)}) collective-permute-start(bf16[200,512]{1,0:T(8,128)(2,1)S(1)} %constant_dynamic-update-slice_fusion.echo), channel_id=1, source_target_pairs={{8,0},{9,1},{10,2},{11,3},{12,4},{13,5},{14,6},{15,7},{0,8},{1,9},... | collective-permute-start | bytes 614408 | tf_op jit(solution)/shard_map/ppermute | solution.py:39
  73.2 17.3 %collective-permute-start.9 = (bf16[200,2048]{1,0:T(8,128)(2,1)S(1)}, bf16[200,2048]{1,0:T(8,128)(2,1)S(1)}, u32[]{:S(2)}, u32[]{:S(2)}) collective-permute-start(bf16[200,2048]{1,0:T(8,128)(2,1)S(1)} %constant_dynamic-update-slice_fusion.4.slab), channel_id=1, source_target_pairs={{1,0},{0,1},{3,2},{2,3},{5,4},{4,5},{7,6},{6,7},{9,8},{8,9},{11,10... | collective-permute-start | bytes 2457608 | tf_op jit(solution)/shard_map/ppermute | solution.py:39
  73.3 13.8 %collective-permute-start.6 = (bf16[208,512]{1,0:T(8,128)(2,1)S(1)}, bf16[208,512]{1,0:T(8,128)(2,1)S(1)}, u32[]{:S(2)}, u32[]{:S(2)}) collective-permute-start(bf16[208,512]{1,0:T(8,128)(2,1)S(1)} %get-tuple-element.34.refs_0_), channel_id=1, source_target_pairs={{32,0},{33,1},{34,2},{35,3},{36,4},{37,5},{38,6},{39,7},{40,8},{41... | collective-permute-start | bytes 638984 | tf_op jit(solution)/shard_map/ppermute | solution.py:39
  77.4 13.1 %collective-permute-start.7 = (bf16[208,512]{1,0:T(8,128)(2,1)S(1)}, bf16[208,512]{1,0:T(8,128)(2,1)S(1)}, u32[]{:S(2)}, u32[]{:S(2)}) collective-permute-start(bf16[208,512]{1,0:T(8,128)(2,1)S(1)} %get-tuple-element.34.refs_0_), channel_id=1, source_target_pairs={{96,0},{97,1},{98,2},{99,3},{100,4},{101,5},{102,6},{103,7},{104,8... | collective-permute-start | bytes 638984 | tf_op jit(solution)/shard_map/ppermute | solution.py:39
  77.4 13.1 %collective-permute-start.8 = (bf16[208,512]{1,0:T(8,128)(2,1)S(1)}, bf16[208,512]{1,0:T(8,128)(2,1)S(1)}, u32[]{:S(2)}, u32[]{:S(2)}) collective-permute-start(bf16[208,512]{1,0:T(8,128)(2,1)S(1)} %get-tuple-element.34.refs_0_), channel_id=1, source_target_pairs={{64,0},{65,1},{66,2},{67,3},{68,4},{69,5},{70,6},{71,7},{72,8},{73... | collective-permute-start | bytes 638984 | tf_op jit(solution)/shard_map/ppermute | solution.py:39
  97.3 6.6 %collective-permute-start.10 = (bf16[200,2048]{1,0:T(8,128)(2,1)S(1)}, bf16[200,2048]{1,0:T(8,128)(2,1)S(1)}, u32[]{:S(2)}, u32[]{:S(2)}) collective-permute-start(bf16[200,2048]{1,0:T(8,128)(2,1)S(1)} %get-tuple-element.38), channel_id=1, source_target_pairs={{1,0},{0,1},{3,2},{2,3},{5,4},{4,5},{7,6},{6,7},{9,8},{8,9},{11,10... | collective-permute-start | bytes 2457608 | tf_op jit(solution)/shard_map/ppermute | solution.py:39
  104.4 13.1 %collective-permute-start.11 = (bf16[200,512]{1,0:T(8,128)(2,1)S(1)}, bf16[200,512]{1,0:T(8,128)(2,1)S(1)}, u32[]{:S(2)}, u32[]{:S(2)}) collective-permute-start(bf16[200,512]{1,0:T(8,128)(2,1)S(1)} %get-tuple-element.48), channel_id=1, source_target_pairs={{12,0},{13,1},{14,2},{15,3},{0,4},{1,5},{2,6},{3,7},{4,8},{5,9},{6... | collective-permute-start | bytes 614408 | tf_op jit(solution)/shard_map/ppermute | solution.py:39
  106.4 11.8 %collective-permute-start.12 = (bf16[200,512]{1,0:T(8,128)(2,1)S(1)}, bf16[200,512]{1,0:T(8,128)(2,1)S(1)}, u32[]{:S(2)}, u32[]{:S(2)}) collective-permute-start(bf16[200,512]{1,0:T(8,128)(2,1)S(1)} %get-tuple-element.50), channel_id=1, source_target_pairs={{4,0},{5,1},{6,2},{7,3},{8,4},{9,5},{10,6},{11,7},{12,8},{13,9},{1... | collective-permute-start | bytes 614408 | tf_op jit(solution)/shard_map/ppermute | solution.py:39
  107.7 10.4 %collective-permute-start.13 = (bf16[200,512]{1,0:T(8,128)(2,1)S(1)}, bf16[200,512]{1,0:T(8,128)(2,1)S(1)}, u32[]{:S(2)}, u32[]{:S(2)}) collective-permute-start(bf16[200,512]{1,0:T(8,128)(2,1)S(1)} %get-tuple-element.49), channel_id=1, source_target_pairs={{8,0},{9,1},{10,2},{11,3},{12,4},{13,5},{14,6},{15,7},{0,8},{1,9},... | collective-permute-start | bytes 614408 | tf_op jit(solution)/shard_map/ppermute | solution.py:39
  110.6 11.1 %collective-permute-start.17 = (bf16[200,512]{1,0:T(8,128)(2,1)S(1)}, bf16[200,512]{1,0:T(8,128)(2,1)S(1)}, u32[]{:S(2)}, u32[]{:S(2)}) collective-permute-start(bf16[200,512]{1,0:T(8,128)(2,1)S(1)} %get-tuple-element.43), channel_id=1, source_target_pairs={{96,0},{97,1},{98,2},{99,3},{100,4},{101,5},{102,6},{103,7},{104,8... | collective-permute-start | bytes 614408 | tf_op jit(solution)/shard_map/ppermute | solution.py:39
  110.6 11.7 %collective-permute-start.18 = (bf16[200,512]{1,0:T(8,128)(2,1)S(1)}, bf16[200,512]{1,0:T(8,128)(2,1)S(1)}, u32[]{:S(2)}, u32[]{:S(2)}) collective-permute-start(bf16[200,512]{1,0:T(8,128)(2,1)S(1)} %get-tuple-element.44), channel_id=1, source_target_pairs={{32,0},{33,1},{34,2},{35,3},{36,4},{37,5},{38,6},{39,7},{40,8},{41... | collective-permute-start | bytes 614408 | tf_op jit(solution)/shard_map/ppermute | solution.py:39
  117.5 8.2 %collective-permute-start.19 = (bf16[200,512]{1,0:T(8,128)(2,1)S(1)}, bf16[200,512]{1,0:T(8,128)(2,1)S(1)}, u32[]{:S(2)}, u32[]{:S(2)}) collective-permute-start(bf16[200,512]{1,0:T(8,128)(2,1)S(1)} %get-tuple-element.45), channel_id=1, source_target_pairs={{64,0},{65,1},{66,2},{67,3},{68,4},{69,5},{70,6},{71,7},{72,8},{73... | collective-permute-start | bytes 614408 | tf_op jit(solution)/shard_map/ppermute | solution.py:39
  118.3 8.3 %collective-permute-start.14 = (bf16[200,128]{1,0:T(8,128)(2,1)S(1)}, bf16[200,128]{1,0:T(8,128)(2,1)S(1)}, u32[]{:S(2)}, u32[]{:S(2)}) collective-permute-start(bf16[200,128]{1,0:T(8,128)(2,1)S(1)} %get-tuple-element.51), channel_id=1, source_target_pairs={{18,0},{19,1},{16,2},{17,3},{22,4},{23,5},{20,6},{21,7},{26,8},{27... | collective-permute-start | bytes 153608 | tf_op jit(solution)/shard_map/ppermute | solution.py:39
  120.2 6.4 %collective-permute-start.15 = (bf16[200,128]{1,0:T(8,128)(2,1)S(1)}, bf16[200,128]{1,0:T(8,128)(2,1)S(1)}, u32[]{:S(2)}, u32[]{:S(2)}) collective-permute-start(bf16[200,128]{1,0:T(8,128)(2,1)S(1)} %get-tuple-element.53), channel_id=1, source_target_pairs={{16,0},{17,1},{18,2},{19,3},{20,4},{21,5},{22,6},{23,7},{24,8},{25... | collective-permute-start | bytes 153608 | tf_op jit(solution)/shard_map/ppermute | solution.py:39
  121.6 5.6 %collective-permute-start.16 = (bf16[200,128]{1,0:T(8,128)(2,1)S(1)}, bf16[200,128]{1,0:T(8,128)(2,1)S(1)}, u32[]{:S(2)}, u32[]{:S(2)}) collective-permute-start(bf16[200,128]{1,0:T(8,128)(2,1)S(1)} %get-tuple-element.52), channel_id=1, source_target_pairs={{2,0},{3,1},{0,2},{1,3},{6,4},{7,5},{4,6},{5,7},{10,8},{11,9},{8,1... | collective-permute-start | bytes 153608 | tf_op jit(solution)/shard_map/ppermute | solution.py:39
  (9 other events, 56.8 us)

commit v3 on v2

--- a/solution.py
+++ b/solution.py
@@ -16,8 +16,7 @@
 CHUNK = 4096
 UNROLL = 64
 SPAN = 512
-VMEM_BYTES = 8 * 1024 * 1024
-SCORE_BYTES = 40 * 1024 * 1024
+VMEM_BYTES = 12 * 1024 * 1024
 CHUNKS = 2
 FAR = (1, 3, 2)
 
@@ -39,7 +38,7 @@
     return lax.ppermute(block, AXES, route)
 
 
-def gather_rows(ids, table, rows, width, count, start, total):
+def gather_rows(ids, table, rows, width, count, start, anchors):
     per = width // UNROLL
 
     def some(step, carry):
@@ -50,7 +49,7 @@
             rows[pl.ds(place + 2 * k, 2), :] = picked[k]
         return carry
 
-    lax.fori_loop(0, total // count * per, some, 0)
+    lax.fori_loop(0, anchors * per, some, 0)
 
 
 def relation_rows(ids, rel_table):
@@ -120,7 +119,8 @@
     @pl.when(pl.program_id(0) == pl.num_programs(0) - 1)
     def _():
         width = own_rel.shape[1]
-        gather_rows(own_ids, table, rows, width, width, 0, own_ids.shape[0])
+        anchors = weights.shape[1] // WIDE - own_rel.shape[0]
+        gather_rows(own_ids, table, rows, width, width, 0, anchors)
         own_out[...] = (encoded(rows, own_rel, weights, rel_table) * scale).astype(BF16)
 
 
@@ -132,7 +132,10 @@
         query_out[:, :start] = refs[0][...]
     echo_out[...] = echo[...]
     part = slice(start, start + width)
-    gather_rows(head_ids, table, rows, width, head_rel.shape[1], start, head_ids.shape[0])
+    tokens, heads = head_rel.shape
+    anchors = weights.shape[1] // WIDE - tokens
+    before = head_ids.shape[0] - anchors * heads
+    gather_rows(head_ids, table, rows, width, heads, before + start, anchors)
     head = encoded(rows, head_rel[:, part], weights, rel_table).astype(BF16)
     mixed = head.astype(F32) * relation_rows(asked[:, part], rel_table)[: head.shape[0], :]
     query = jnp.tanh(
@@ -149,8 +152,8 @@
     ).astype(BF16)
 
 
-def encode_entities(anchor_ids, relation_ids, anchor_table, relation_table, enc_weight, scale):
-    own, anchors = anchor_ids.shape
+def encode_entities(ids, anchors, relation_ids, anchor_table, relation_table, enc_weight, scale):
+    own = relation_ids.shape[0]
     count, depth = anchor_table.shape
     relations = relation_table.shape[0]
     steps = pl.cdiv(count, CHUNK)
@@ -179,7 +182,8 @@
         scratch_shapes=[pltpu.VMEM((2 * own * anchors, LANES), F32)],
         compiler_params=pltpu.CompilerParams(vmem_limit_bytes=VMEM_BYTES),
     )(
-        (anchor_ids.T * 2).reshape(-1), anchor_table.T, enc_weight.T, relation_table.T,
+        ids,
+        pltpu.with_memory_space_constraint(anchor_table.T, pltpu.HBM), enc_weight.T, relation_table.T,
         relation_ids.T,
     )
 
@@ -339,7 +343,7 @@
         out_shape=outs,
         input_output_aliases={2 + len(blocks): 0} if stage == 1 else {},
         scratch_shapes=scratch,
-        compiler_params=pltpu.CompilerParams(vmem_limit_bytes=SCORE_BYTES),
+        compiler_params=pltpu.CompilerParams(vmem_limit_bytes=VMEM_BYTES),
     )(me, slab, *blocks, *extra)
 
 
@@ -360,10 +364,16 @@
     queries = head_anchors.shape[0] * 128
     scale = 0.5 * float(anchor_table.shape[1]) ** (-0.5)
     me = (lax.axis_index("ent") * 16 + lax.axis_index("qry")).astype(jnp.int32)[None]
+    ids = jnp.concatenate([anchor_ids.T.reshape(-1), head_anchors.T.reshape(-1)]) * 2
     own_cols, *shared = encode_entities(
-        anchor_ids, relation_ids, anchor_table, relation_table, enc_weight, scale
-    )
-    head_ids = (head_anchors.T * 2).reshape(-1)
+        ids,
+        anchor_ids.shape[1],
+        relation_ids,
+        anchor_table,
+        relation_table,
+        enc_weight,
+        scale,
+    )
     query = []
     piece = own_cols
     for chunk in range(CHUNKS):
@@ -371,7 +381,7 @@
         sent = [moved(piece, **{axis: d}) for d in FAR]
         part, piece, *shared = encode_heads(
             chunk,
-            head_ids,
+            ids,
             head_relations.T,
             query_relation[None, :],
             targets.T,

time: 129 us -> 102 us (0.79)
  local copies, waits for them, and re-layouts: 34.6 us -> 4.21 us
  Pallas kernels: 41.8 us -> 43.9 us
    unnamed x32 -> x20, local copies, waits for them, and re-layouts: 34.5 us -> 3.34 us
    pallas_call x1, Pallas kernels: 10.2 us -> 12 us  [encode_entities(): pl.pallas_call(functools.partial(entity_kernel, relations, scale), grid=(...]
  transfers between devices with their start and end apart: 20 -> 20, of which waited for: 5 -> 6; matrix products, arithmetic and copies ran while one was open for 1% -> 1% of each run, Pallas kernels for 19% -> 25%
where the time goes in v3:
time: 102 us; the launch traced here: 100 us
  Pallas kernels  43.9 us (43%)
  starting transfers between devices  28.2 us (28%)
  waiting for transfers between devices  20.2 us (20%)
  local copies, waits for them, and re-layouts  4.21 us (4%)
  other arithmetic  2.89 us (3%)
    ppermute x20, starting transfers between devices, moved(): return lax.ppermute(block, AXES, route)  28.2 us
    ppermute x20, waiting for transfers between devices, moved(): return lax.ppermute(block, AXES, route)  20.2 us
    pallas_call x2, Pallas kernels, encode_heads(): pl.pallas_call(functools.partial(head_kernel, chunk * heads, heads), in_s...  16.8 us
    pallas_call x3, Pallas kernels, score(): pl.pallas_call(functools.partial(score_kernel, plain, plain - 1.8, depth,...  15.1 us
    pallas_call x1, Pallas kernels, encode_entities(): pl.pallas_call(functools.partial(entity_kernel, relations, scale), grid=(...  12 us
    unnamed x20, local copies, waits for them, and re-layouts  3.34 us
  transfers between devices with their start and end apart: 20, of which 6 were waited for; matrix products, arithmetic and copies ran while one was open for 1% of the time, Pallas kernels for 25%

profile of v3, /device:TPU:0, one launch (start us, length us, event | category | flops | bytes accessed | tf_op | source)
XLA Modules:
  0.0 100.3 jit_solution(17050751316484075095)
XLA Ops:
  2.2 1.6 %copy-done = bf16[5000,200]{0,1:T(8,128)(2,1)S(1)} copy-done((bf16[5000,200]{0,1:T(8,128)(2,1)S(1)}, bf16[5000,200]{0,1:T(8,128)(2,1)}, u32[]{:S(2)}) %copy-start) | copy-done | bytes 2000024
  3.7 1.0 copy-done.2
  5.4 12.0 %shard_map.113 = (bf16[200,128]{1,0:T(8,128)(2,1)S(1)}, f32[40960,128]{1,0:T(8,128)S(1)}, bf16[200,6400]{1,0:T(8,128)(2,1)S(1)}, bf16[256,896]{1,0:T(8,128)(2,1)S(1)}) custom-call(s32[12800]{0:T(1024)S(1)} %add_multiply_fusion.own_ids.head_ids, bf16[200,20000]{1,0:T(8,128)(2,1)} %bitcast.23, bf16[200,5000]{1,0:T(8,128)(2,1)S(1)} %bitcast.14, ...), custom_call_target="tpu_custom_call" | custom-call | tf_op jit(solution)/shard_map/pallas_call | solution.py:165
  17.4 2.9 %collective-permute-start = (bf16[200,128]{1,0:T(8,128)(2,1)S(1)}, bf16[200,128]{1,0:T(8,128)(2,1)S(1)}, u32[]{:S(2)}, u32[]{:S(2)}) collective-permute-start(bf16[200,128]{1,0:T(8,128)(2,1)S(1)} %get-tuple-element.24.echo), channel_id=1, source_target_pairs={{16,0},{17,1},{18,2},{19,3},{20,4},{21,5},{22,6},{23,7},{24,8},{25... | collective-permute-start | bytes 153608 | tf_op jit(solution)/shard_map/ppermute | solution.py:38
  20.4 2.3 %collective-permute-start.2 = (bf16[200,128]{1,0:T(8,128)(2,1)S(1)}, bf16[200,128]{1,0:T(8,128)(2,1)S(1)}, u32[]{:S(2)}, u32[]{:S(2)}) collective-permute-start(bf16[200,128]{1,0:T(8,128)(2,1)S(1)} %get-tuple-element.24.echo), channel_id=1, source_target_pairs={{2,0},{3,1},{0,2},{1,3},{6,4},{7,5},{4,6},{5,7},{10,8},{11,9},{8,1... | collective-permute-start | bytes 153608 | tf_op jit(solution)/shard_map/ppermute | solution.py:38
  22.7 8.4 %shard_map.114 = (bf16[208,256]{1,0:T(8,128)(2,1)S(1)}, bf16[200,128]{1,0:T(8,128)(2,1)S(1)}, f32[40960,128]{1,0:T(8,128)S(1)}, bf16[200,6400]{1,0:T(8,128)(2,1)S(1)}, bf16[256,896]{1,0:T(8,128)(2,1)S(1)}) custom-call(s32[12800]{0:T(1024)S(1)} %add_multiply_fusion.own_ids.head_ids, ...), custom_call_target="tpu_custom_call", output_to_operand_aliasing={{2}: (6, {}), {3}: (7, {}), {4}: (8, {})} | custom-call | tf_op jit(solution)/shard_map/pallas_call | solution.py:199
  31.2 3.1 %collective-permute-start.3 = (bf16[200,512]{1,0:T(8,128)(2,1)S(1)}, bf16[200,512]{1,0:T(8,128)(2,1)S(1)}, u32[]{:S(2)}, u32[]{:S(2)}) collective-permute-start(bf16[200,512]{1,0:T(8,128)(2,1)S(1)} %constant_dynamic-update-slice_fusion.echo), channel_id=1, source_target_pairs={{4,0},{5,1},{6,2},{7,3},{8,4},{9,5},{10,6},{11,7},{12,8},{13,9},{1... | collective-permute-start | bytes 614408 | tf_op jit(solution)/shard_map/ppermute | solution.py:38
  34.2 2.2 %collective-permute-start.5 = (bf16[200,512]{1,0:T(8,128)(2,1)S(1)}, bf16[200,512]{1,0:T(8,128)(2,1)S(1)}, u32[]{:S(2)}, u32[]{:S(2)}) collective-permute-start(bf16[200,512]{1,0:T(8,128)(2,1)S(1)} %constant_dynamic-update-slice_fusion.echo), channel_id=1, source_target_pairs={{8,0},{9,1},{10,2},{11,3},{12,4},{13,5},{14,6},{15,7},{0,8},{1,9},... | collective-permute-start | bytes 614408 | tf_op jit(solution)/shard_map/ppermute | solution.py:38
  36.4 8.4 %shard_map.115 = (bf16[208,512]{1,0:T(8,128)(2,1)S(1)}, bf16[200,512]{1,0:T(8,128)(2,1)S(1)}, f32[40960,128]{1,0:T(8,128)S(1)}, bf16[200,6400]{1,0:T(8,128)(2,1)S(1)}, bf16[256,896]{1,0:T(8,128)(2,1)S(1)}) custom-call(s32[12800]{0:T(1024)S(1)} %add_multiply_fusion.own_ids.head_ids, ...), custom_call_target="tpu_custom_call", output_to_operand_aliasing={{2}: (6, {}), {3}: (7, {}), {4}: (8, {})} | custom-call | tf_op jit(solution)/shard_map/pallas_call | solution.py:199
  45.7 4.1 %collective-permute-start.6 = (bf16[208,512]{1,0:T(8,128)(2,1)S(1)}, bf16[208,512]{1,0:T(8,128)(2,1)S(1)}, u32[]{:S(2)}, u32[]{:S(2)}) collective-permute-start(bf16[208,512]{1,0:T(8,128)(2,1)S(1)} %get-tuple-element.34.refs_0_), channel_id=1, source_target_pairs={{32,0},{33,1},{34,2},{35,3},{36,4},{37,5},{38,6},{39,7},{40,8},{41... | collective-permute-start | bytes 638984 | tf_op jit(solution)/shard_map/ppermute | solution.py:38
  49.8 1.9 %collective-permute-start.8 = (bf16[208,512]{1,0:T(8,128)(2,1)S(1)}, bf16[208,512]{1,0:T(8,128)(2,1)S(1)}, u32[]{:S(2)}, u32[]{:S(2)}) collective-permute-start(bf16[208,512]{1,0:T(8,128)(2,1)S(1)} %get-tuple-element.34.refs_0_), channel_id=1, source_target_pairs={{64,0},{65,1},{66,2},{67,3},{68,4},{69,5},{70,6},{71,7},{72,8},{73... | collective-permute-start | bytes 638984 | tf_op jit(solution)/shard_map/ppermute | solution.py:38
  51.7 7.8 %collective-permute-done.6.refs_1_ = bf16[208,512]{1,0:T(8,128)(2,1)S(1)} collective-permute-done((bf16[208,512]{1,0:T(8,128)(2,1)S(1)}, bf16[208,512]{1,0:T(8,128)(2,1)S(1)}, u32[]{:S(2)}, u32[]{:S(2)}) %collective-permute-start.6) | collective-permute-done | bytes 213024 | tf_op jit(solution)/shard_map/ppermute | solution.py:38
  59.5 3.4 %collective-permute-done.7.refs_2_ = bf16[208,512]{1,0:T(8,128)(2,1)S(1)} collective-permute-done((bf16[208,512]{1,0:T(8,128)(2,1)S(1)}, bf16[208,512]{1,0:T(8,128)(2,1)S(1)}, u32[]{:S(2)}, u32[]{:S(2)}) %collective-permute-start.7) | collective-permute-done | bytes 213024 | tf_op jit(solution)/shard_map/ppermute | solution.py:38
  62.9 6.8 %shard_map.116 = (f32[4,200,512]{2,1,0:T(8,128)S(1)}, bf16[200,2048]{1,0:T(8,128)(2,1)S(1)}) custom-call(s32[1]{0:T(128)} %bitcast.me, bf16[200,2048]{1,0:T(8,128)(2,1)S(1)} %collective-permute-done.9.slab, bf16[208,512]{1,0:T(8,128)(2,1)S(1)} %get-tuple-element.34.refs_0_, bf16[208,512]{1,0:T(8,128)(2,1)S(1)} %collective-permute-done.6.refs_1_, ...), custom_call_target="tpu_custom_call" | custom-call | tf_op jit(solution)/shard_map/pallas_call | solution.py:339
  70.0 6.2 %shard_map.117 = (f32[4,200,512]{2,1,0:T(8,128)S(1)}, f32[200,512]{1,0:T(8,128)S(1)}, f32[200,512]{1,0:T(8,128)S(1)}, f32[200,512]{1,0:T(8,128)S(1)}) custom-call(s32[1]{0:T(128)} %bitcast.me, bf16[200,2048]{1,0:T(8,128)(2,1)S(1)} %constant_dynamic-update-slice_fusion.4.slab, ...), custom_call_target="tpu_custom_call", output_to_operand_aliasing={{0}: (6, {})} | custom-call | tf_op jit(solution)/shard_map/pallas_call | solution.py:339
  76.8 1.3 %collective-permute-start.11 = (bf16[200,512]{1,0:T(8,128)(2,1)S(1)}, bf16[200,512]{1,0:T(8,128)(2,1)S(1)}, u32[]{:S(2)}, u32[]{:S(2)}) collective-permute-start(bf16[200,512]{1,0:T(8,128)(2,1)S(1)} %get-tuple-element.48), channel_id=1, source_target_pairs={{12,0},{13,1},{14,2},{15,3},{0,4},{1,5},{2,6},{3,7},{4,8},{5,9},{6... | collective-permute-start | bytes 614408 | tf_op jit(solution)/shard_map/ppermute | solution.py:38
  78.1 2.0 %collective-permute-start.12 = (bf16[200,512]{1,0:T(8,128)(2,1)S(1)}, bf16[200,512]{1,0:T(8,128)(2,1)S(1)}, u32[]{:S(2)}, u32[]{:S(2)}) collective-permute-start(bf16[200,512]{1,0:T(8,128)(2,1)S(1)} %get-tuple-element.50), channel_id=1, source_target_pairs={{4,0},{5,1},{6,2},{7,3},{8,4},{9,5},{10,6},{11,7},{12,8},{13,9},{1... | collective-permute-start | bytes 614408 | tf_op jit(solution)/shard_map/ppermute | solution.py:38
  80.2 2.0 %shard_map.118 = (f32[200,512]{1,0:T(8,128)S(1)}, bf16[200,512]{1,0:T(8,128)(2,1)S(1)}, bf16[200,512]{1,0:T(8,128)(2,1)S(1)}, bf16[200,512]{1,0:T(8,128)(2,1)S(1)}, f32[200,512]{1,0:T(8,128)S(1)}) custom-call(s32[1]{0:T(128)} %bitcast.me, bf16[200,2048]{1,0:T(8,128)(2,1)S(1)} %constant_dynamic-update-slice_fusion.4.slab, ...), custom_call_target="tpu_custom_call" | custom-call | tf_op jit(solution)/shard_map/pallas_call | solution.py:339
  82.4 3.2 %collective-permute-start.18 = (bf16[200,512]{1,0:T(8,128)(2,1)S(1)}, bf16[200,512]{1,0:T(8,128)(2,1)S(1)}, u32[]{:S(2)}, u32[]{:S(2)}) collective-permute-start(bf16[200,512]{1,0:T(8,128)(2,1)S(1)} %get-tuple-element.44), channel_id=1, source_target_pairs={{32,0},{33,1},{34,2},{35,3},{36,4},{37,5},{38,6},{39,7},{40,8},{41... | collective-permute-start | bytes 614408 | tf_op jit(solution)/shard_map/ppermute | solution.py:38
  85.6 4.3 %collective-permute-done.11 = bf16[200,512]{1,0:T(8,128)(2,1)S(1)} collective-permute-done((bf16[200,512]{1,0:T(8,128)(2,1)S(1)}, bf16[200,512]{1,0:T(8,128)(2,1)S(1)}, u32[]{:S(2)}, u32[]{:S(2)}) %collective-permute-start.11) | collective-permute-done | bytes 204832 | tf_op jit(solution)/shard_map/ppermute | solution.py:38
  90.7 1.9 %collective-permute-start.14 = (bf16[200,128]{1,0:T(8,128)(2,1)S(1)}, bf16[200,128]{1,0:T(8,128)(2,1)S(1)}, u32[]{:S(2)}, u32[]{:S(2)}) collective-permute-start(bf16[200,128]{1,0:T(8,128)(2,1)S(1)} %get-tuple-element.51), channel_id=1, source_target_pairs={{18,0},{19,1},{16,2},{17,3},{22,4},{23,5},{20,6},{21,7},{26,8},{27... | collective-permute-start | bytes 153608 | tf_op jit(solution)/shard_map/ppermute | solution.py:38
  92.6 1.4 %collective-permute-start.15 = (bf16[200,128]{1,0:T(8,128)(2,1)S(1)}, bf16[200,128]{1,0:T(8,128)(2,1)S(1)}, u32[]{:S(2)}, u32[]{:S(2)}) collective-permute-start(bf16[200,128]{1,0:T(8,128)(2,1)S(1)} %get-tuple-element.53), channel_id=1, source_target_pairs={{16,0},{17,1},{18,2},{19,3},{20,4},{21,5},{22,6},{23,7},{24,8},{25... | collective-permute-start | bytes 153608 | tf_op jit(solution)/shard_map/ppermute | solution.py:38
  94.7 3.4 %collective-permute-done.19 = bf16[200,512]{1,0:T(8,128)(2,1)S(1)} collective-permute-done((bf16[200,512]{1,0:T(8,128)(2,1)S(1)}, bf16[200,512]{1,0:T(8,128)(2,1)S(1)}, u32[]{:S(2)}, u32[]{:S(2)}) %collective-permute-start.19) | collective-permute-done | bytes 204832 | tf_op jit(solution)/shard_map/ppermute | solution.py:38
  98.1 0.9 multiply_bitcast_fusion
  (52 shorter events, 6.9 us)
Async XLA Ops:
  5.4 17.3 %copy-start.1 = (bf16[200,200]{1,0:T(8,128)(2,1)S(1)}, bf16[200,200]{1,0:T(8,128)(2,1)}, u32[]{:S(2)}) copy-start(bf16[200,200]{1,0:T(8,128)(2,1)} %fc.3) | copy-start | bytes 240004
  5.4 17.3 %copy-start.3 = (s32[512,5]{0,1:T(8,128)S(1)}, s32[512,5]{0,1:T(8,128)}, u32[]{:S(2)}) copy-start(s32[512,5]{0,1:T(8,128)} %param.13) | copy-start | bytes 30724
  5.4 17.3 %copy-start.4 = (s32[512,4]{0,1:T(4,128)S(1)}, s32[512,4]{0,1:T(4,128)}, u32[]{:S(2)}) copy-start(s32[512,4]{0,1:T(4,128)} %param.15) | copy-start | bytes 24580
  5.4 17.3 %copy-start.5 = (s32[512]{0:T(512)S(1)}, s32[512]{0:T(512)}, u32[]{:S(2)}) copy-start(s32[512]{0:T(512)} %param.14) | copy-start | bytes 6148
  17.4 13.6 %collective-permute-start = (bf16[200,128]{1,0:T(8,128)(2,1)S(1)}, bf16[200,128]{1,0:T(8,128)(2,1)S(1)}, u32[]{:S(2)}, u32[]{:S(2)}) collective-permute-start(bf16[200,128]{1,0:T(8,128)(2,1)S(1)} %get-tuple-element.24.echo), channel_id=1, source_target_pairs={{16,0},{17,1},{18,2},{19,3},{20,4},{21,5},{22,6},{23,7},{24,8},{25... | collective-permute-start | bytes 153608 | tf_op jit(solution)/shard_map/ppermute | solution.py:38
  20.4 10.7 %collective-permute-start.1 = (bf16[200,128]{1,0:T(8,128)(2,1)S(1)}, bf16[200,128]{1,0:T(8,128)(2,1)S(1)}, u32[]{:S(2)}, u32[]{:S(2)}) collective-permute-start(bf16[200,128]{1,0:T(8,128)(2,1)S(1)} %get-tuple-element.24.echo), channel_id=1, source_target_pairs={{18,0},{19,1},{16,2},{17,3},{22,4},{23,5},{20,6},{21,7},{26,8},{27... | collective-permute-start | bytes 153608 | tf_op jit(solution)/shard_map/ppermute | solution.py:38
  20.4 10.8 %collective-permute-start.2 = (bf16[200,128]{1,0:T(8,128)(2,1)S(1)}, bf16[200,128]{1,0:T(8,128)(2,1)S(1)}, u32[]{:S(2)}, u32[]{:S(2)}) collective-permute-start(bf16[200,128]{1,0:T(8,128)(2,1)S(1)} %get-tuple-element.24.echo), channel_id=1, source_target_pairs={{2,0},{3,1},{0,2},{1,3},{6,4},{7,5},{4,6},{5,7},{10,8},{11,9},{8,1... | collective-permute-start | bytes 153608 | tf_op jit(solution)/shard_map/ppermute | solution.py:38
  31.2 13.7 %collective-permute-start.3 = (bf16[200,512]{1,0:T(8,128)(2,1)S(1)}, bf16[200,512]{1,0:T(8,128)(2,1)S(1)}, u32[]{:S(2)}, u32[]{:S(2)}) collective-permute-start(bf16[200,512]{1,0:T(8,128)(2,1)S(1)} %constant_dynamic-update-slice_fusion.echo), channel_id=1, source_target_pairs={{4,0},{5,1},{6,2},{7,3},{8,4},{9,5},{10,6},{11,7},{12,8},{13,9},{1... | collective-permute-start | bytes 614408 | tf_op jit(solution)/shard_map/ppermute | solution.py:38
  34.2 11.3 %collective-permute-start.4 = (bf16[200,512]{1,0:T(8,128)(2,1)S(1)}, bf16[200,512]{1,0:T(8,128)(2,1)S(1)}, u32[]{:S(2)}, u32[]{:S(2)}) collective-permute-start(bf16[200,512]{1,0:T(8,128)(2,1)S(1)} %constant_dynamic-update-slice_fusion.echo), channel_id=1, source_target_pairs={{12,0},{13,1},{14,2},{15,3},{0,4},{1,5},{2,6},{3,7},{4,8},{5,9},{6... | collective-permute-start | bytes 614408 | tf_op jit(solution)/shard_map/ppermute | solution.py:38
  34.2 11.3 %collective-permute-start.5 = (bf16[200,512]{1,0:T(8,128)(2,1)S(1)}, bf16[200,512]{1,0:T(8,128)(2,1)S(1)}, u32[]{:S(2)}, u32[]{:S(2)}) collective-permute-start(bf16[200,512]{1,0:T(8,128)(2,1)S(1)} %constant_dynamic-update-slice_fusion.echo), channel_id=1, source_target_pairs={{8,0},{9,1},{10,2},{11,3},{12,4},{13,5},{14,6},{15,7},{0,8},{1,9},... | collective-permute-start | bytes 614408 | tf_op jit(solution)/shard_map/ppermute | solution.py:38
  45.6 17.3 %collective-permute-start.9 = (bf16[200,2048]{1,0:T(8,128)(2,1)S(1)}, bf16[200,2048]{1,0:T(8,128)(2,1)S(1)}, u32[]{:S(2)}, u32[]{:S(2)}) collective-permute-start(bf16[200,2048]{1,0:T(8,128)(2,1)S(1)} %constant_dynamic-update-slice_fusion.4.slab), channel_id=1, source_target_pairs={{1,0},{0,1},{3,2},{2,3},{5,4},{4,5},{7,6},{6,7},{9,8},{8,9},{11,10... | collective-permute-start | bytes 2457608 | tf_op jit(solution)/shard_map/ppermute | solution.py:38
  45.7 13.8 %collective-permute-start.6 = (bf16[208,512]{1,0:T(8,128)(2,1)S(1)}, bf16[208,512]{1,0:T(8,128)(2,1)S(1)}, u32[]{:S(2)}, u32[]{:S(2)}) collective-permute-start(bf16[208,512]{1,0:T(8,128)(2,1)S(1)} %get-tuple-element.34.refs_0_), channel_id=1, source_target_pairs={{32,0},{33,1},{34,2},{35,3},{36,4},{37,5},{38,6},{39,7},{40,8},{41... | collective-permute-start | bytes 638984 | tf_op jit(solution)/shard_map/ppermute | solution.py:38
  49.8 13.1 %collective-permute-start.7 = (bf16[208,512]{1,0:T(8,128)(2,1)S(1)}, bf16[208,512]{1,0:T(8,128)(2,1)S(1)}, u32[]{:S(2)}, u32[]{:S(2)}) collective-permute-start(bf16[208,512]{1,0:T(8,128)(2,1)S(1)} %get-tuple-element.34.refs_0_), channel_id=1, source_target_pairs={{96,0},{97,1},{98,2},{99,3},{100,4},{101,5},{102,6},{103,7},{104,8... | collective-permute-start | bytes 638984 | tf_op jit(solution)/shard_map/ppermute | solution.py:38
  49.8 13.1 %collective-permute-start.8 = (bf16[208,512]{1,0:T(8,128)(2,1)S(1)}, bf16[208,512]{1,0:T(8,128)(2,1)S(1)}, u32[]{:S(2)}, u32[]{:S(2)}) collective-permute-start(bf16[208,512]{1,0:T(8,128)(2,1)S(1)} %get-tuple-element.34.refs_0_), channel_id=1, source_target_pairs={{64,0},{65,1},{66,2},{67,3},{68,4},{69,5},{70,6},{71,7},{72,8},{73... | collective-permute-start | bytes 638984 | tf_op jit(solution)/shard_map/ppermute | solution.py:38
  69.7 6.6 %collective-permute-start.10 = (bf16[200,2048]{1,0:T(8,128)(2,1)S(1)}, bf16[200,2048]{1,0:T(8,128)(2,1)S(1)}, u32[]{:S(2)}, u32[]{:S(2)}) collective-permute-start(bf16[200,2048]{1,0:T(8,128)(2,1)S(1)} %get-tuple-element.38), channel_id=1, source_target_pairs={{1,0},{0,1},{3,2},{2,3},{5,4},{4,5},{7,6},{6,7},{9,8},{8,9},{11,10... | collective-permute-start | bytes 2457608 | tf_op jit(solution)/shard_map/ppermute | solution.py:38
  76.8 13.1 %collective-permute-start.11 = (bf16[200,512]{1,0:T(8,128)(2,1)S(1)}, bf16[200,512]{1,0:T(8,128)(2,1)S(1)}, u32[]{:S(2)}, u32[]{:S(2)}) collective-permute-start(bf16[200,512]{1,0:T(8,128)(2,1)S(1)} %get-tuple-element.48), channel_id=1, source_target_pairs={{12,0},{13,1},{14,2},{15,3},{0,4},{1,5},{2,6},{3,7},{4,8},{5,9},{6... | collective-permute-start | bytes 614408 | tf_op jit(solution)/shard_map/ppermute | solution.py:38
  78.1 12.4 %collective-permute-start.12 = (bf16[200,512]{1,0:T(8,128)(2,1)S(1)}, bf16[200,512]{1,0:T(8,128)(2,1)S(1)}, u32[]{:S(2)}, u32[]{:S(2)}) collective-permute-start(bf16[200,512]{1,0:T(8,128)(2,1)S(1)} %get-tuple-element.50), channel_id=1, source_target_pairs={{4,0},{5,1},{6,2},{7,3},{8,4},{9,5},{10,6},{11,7},{12,8},{13,9},{1... | collective-permute-start | bytes 614408 | tf_op jit(solution)/shard_map/ppermute | solution.py:38
  80.1 10.4 %collective-permute-start.13 = (bf16[200,512]{1,0:T(8,128)(2,1)S(1)}, bf16[200,512]{1,0:T(8,128)(2,1)S(1)}, u32[]{:S(2)}, u32[]{:S(2)}) collective-permute-start(bf16[200,512]{1,0:T(8,128)(2,1)S(1)} %get-tuple-element.49), channel_id=1, source_target_pairs={{8,0},{9,1},{10,2},{11,3},{12,4},{13,5},{14,6},{15,7},{0,8},{1,9},... | collective-permute-start | bytes 614408 | tf_op jit(solution)/shard_map/ppermute | solution.py:38
  82.3 11.7 %collective-permute-start.17 = (bf16[200,512]{1,0:T(8,128)(2,1)S(1)}, bf16[200,512]{1,0:T(8,128)(2,1)S(1)}, u32[]{:S(2)}, u32[]{:S(2)}) collective-permute-start(bf16[200,512]{1,0:T(8,128)(2,1)S(1)} %get-tuple-element.43), channel_id=1, source_target_pairs={{96,0},{97,1},{98,2},{99,3},{100,4},{101,5},{102,6},{103,7},{104,8... | collective-permute-start | bytes 614408 | tf_op jit(solution)/shard_map/ppermute | solution.py:38
  82.4 12.3 %collective-permute-start.18 = (bf16[200,512]{1,0:T(8,128)(2,1)S(1)}, bf16[200,512]{1,0:T(8,128)(2,1)S(1)}, u32[]{:S(2)}, u32[]{:S(2)}) collective-permute-start(bf16[200,512]{1,0:T(8,128)(2,1)S(1)} %get-tuple-element.44), channel_id=1, source_target_pairs={{32,0},{33,1},{34,2},{35,3},{36,4},{37,5},{38,6},{39,7},{40,8},{41... | collective-permute-start | bytes 614408 | tf_op jit(solution)/shard_map/ppermute | solution.py:38
  89.9 8.2 %collective-permute-start.19 = (bf16[200,512]{1,0:T(8,128)(2,1)S(1)}, bf16[200,512]{1,0:T(8,128)(2,1)S(1)}, u32[]{:S(2)}, u32[]{:S(2)}) collective-permute-start(bf16[200,512]{1,0:T(8,128)(2,1)S(1)} %get-tuple-element.45), channel_id=1, source_target_pairs={{64,0},{65,1},{66,2},{67,3},{68,4},{69,5},{70,6},{71,7},{72,8},{73... | collective-permute-start | bytes 614408 | tf_op jit(solution)/shard_map/ppermute | solution.py:38
  90.7 8.3 %collective-permute-start.14 = (bf16[200,128]{1,0:T(8,128)(2,1)S(1)}, bf16[200,128]{1,0:T(8,128)(2,1)S(1)}, u32[]{:S(2)}, u32[]{:S(2)}) collective-permute-start(bf16[200,128]{1,0:T(8,128)(2,1)S(1)} %get-tuple-element.51), channel_id=1, source_target_pairs={{18,0},{19,1},{16,2},{17,3},{22,4},{23,5},{20,6},{21,7},{26,8},{27... | collective-permute-start | bytes 153608 | tf_op jit(solution)/shard_map/ppermute | solution.py:38
  92.6 6.4 %collective-permute-start.15 = (bf16[200,128]{1,0:T(8,128)(2,1)S(1)}, bf16[200,128]{1,0:T(8,128)(2,1)S(1)}, u32[]{:S(2)}, u32[]{:S(2)}) collective-permute-start(bf16[200,128]{1,0:T(8,128)(2,1)S(1)} %get-tuple-element.53), channel_id=1, source_target_pairs={{16,0},{17,1},{18,2},{19,3},{20,4},{21,5},{22,6},{23,7},{24,8},{25... | collective-permute-start | bytes 153608 | tf_op jit(solution)/shard_map/ppermute | solution.py:38
  94.0 5.6 %collective-permute-start.16 = (bf16[200,128]{1,0:T(8,128)(2,1)S(1)}, bf16[200,128]{1,0:T(8,128)(2,1)S(1)}, u32[]{:S(2)}, u32[]{:S(2)}) collective-permute-start(bf16[200,128]{1,0:T(8,128)(2,1)S(1)} %get-tuple-element.52), channel_id=1, source_target_pairs={{2,0},{3,1},{0,2},{1,3},{6,4},{7,5},{4,6},{5,7},{10,8},{11,9},{8,1... | collective-permute-start | bytes 153608 | tf_op jit(solution)/shard_map/ppermute | solution.py:38
  (3 other events, 3.2 us)

commit v4 on v3

--- a/solution.py
+++ b/solution.py
@@ -216,15 +216,23 @@
     )
 
 
+def leave(out, which, block, base):
+    half = SPAN // 2
+    places = ((0, half), (base + 4 * half, base + half), (base + 3 * half, base + 5 * half))
+    places += ((base, base + 2 * half),)
+    for k, at in enumerate(places[which]):
+        out[:, at : at + half] = block[:, k * half : (k + 1) * half].astype(out.dtype)
+
+
 def score_kernel(plain, struck_value, depth, parts, stage, me, slab, *refs):
-    blocks, refs = refs[:4], refs[4:]
+    blocks, refs = refs[:5], refs[5:]
     if stage:
         before, refs = refs[0], refs[1:]
     if stage == 2:
-        kept, sent, refs = refs[0], refs[1:4], refs[4:]
+        kept, sent, refs = refs[0], refs[1], refs[2:]
     else:
         asks, refs = refs[0], refs[1:]
-    ent_outs, refs = refs[: len(parts)] if stage else refs[:1], refs[len(parts) if stage else 1 :]
+    ents, refs = refs[0], refs[1:]
     tall, queries, marks, totals, *held = refs[:6]
     if stage == 2:
         asks = refs[6]
@@ -250,7 +258,8 @@
         tall[k * SPAN : (k + 1) * SPAN, :] = wide.T.astype(BF16)
     within = lax.broadcasted_iota(jnp.int32, (LANES, width), 0)
     for b in range(4):
-        query = blocks[b][...].astype(F32)
+        query = blocks[b][...] if b < 3 else jnp.concatenate([blocks[3][...], blocks[4][...]], axis=1)
+        query = query.astype(F32)
         queries[b] = jnp.concatenate(
             [query[:depth, :], jnp.zeros((WIDE - depth, width), F32)], axis=0
         ).astype(BF16)
@@ -291,17 +300,14 @@
             totals[...] += ent
         else:
             ent = (totals[...] + ent).T[:depth, :]
-            if stage:
-                ent_outs[k][...] = ent
-            else:
-                ent_outs[0][:, k * SPAN : (k + 1) * SPAN] = ent.astype(BF16)
+            leave(ents, parts[k], ent, 0 if stage else SPAN)
         if k:
             ask = asks[b] + ask
         elif stage:
             ask = before[b] + ask
         if stage == 2 and k == len(parts) - 1:
             if b:
-                sent[b - 1][...] = ask.astype(BF16)
+                leave(sent, b, ask, 0)
             else:
                 kept[...] = ask
         else:
@@ -322,8 +328,8 @@
     total = pltpu.VMEM((4, depth, SPAN), F32)
     outs = [total]
     if stage == 2:
-        outs = [shape((depth, SPAN), F32)] + [shape((depth, SPAN), BF16)] * 3
-    outs += [shape((depth, SPAN), F32)] * len(parts) if stage else [shape((depth, entities), BF16)]
+        outs = [shape((depth, SPAN), F32), shape((depth, 3 * SPAN), F32)]
+    outs.append(shape((depth, len(parts) * SPAN), F32 if stage else BF16))
     scratch = [
         pltpu.VMEM((len(parts) * SPAN, WIDE), BF16),
         pltpu.VMEM((4, WIDE, SPAN), BF16),
@@ -345,6 +351,23 @@
         scratch_shapes=scratch,
         compiler_params=pltpu.CompilerParams(vmem_limit_bytes=VMEM_BYTES),
     )(me, slab, *blocks, *extra)
+
+
+def first_hop(axis, sent):
+    half = sent.shape[1] // 6
+    up = moved(sent[:, : 2 * half].astype(BF16), **{axis: -1})
+    down = moved(sent[:, 2 * half : 4 * half].astype(BF16), **{axis: 1})
+    return up, down
+
+
+def second_hop(axis, sent, up, down):
+    half = sent.shape[1] // 6
+    up, down = up.astype(F32), down.astype(F32)
+    far_up = moved((sent[:, 4 * half : 5 * half] + up[:, :half]).astype(BF16), **{axis: -1})
+    far_down = moved((sent[:, 5 * half :] + down[:, :half]).astype(BF16), **{axis: 1})
+    return jnp.concatenate(
+        [down[:, half:] + far_up.astype(F32), up[:, half:] + far_down.astype(F32)], axis=1
+    )
 
 
 def body(
@@ -394,21 +417,20 @@
         piece = jnp.concatenate([piece] + sent, axis=1)
     slab = piece
     other = moved(slab, dcore=1)
-    blocks = query + [moved(part, dz=d) for part in query for d in FAR]
+    up, down = moved(query[0], dz=1), moved(query[0], dz=-1)
+    half = up.shape[1] // 2
+    blocks = [query[0], up, down, moved(up[:, :half], dz=1), moved(down[:, half:], dz=-1)]
     asks, away = score(me, other, blocks, (0, 1, 2, 3), 0, entities)
     back = moved(away, dcore=1).astype(F32)
-    asks, *ents = score(me, slab, blocks, (1, 2, 3), 1, entities, asks)
+    asks, ents = score(me, slab, blocks, (1, 2, 3), 1, entities, asks)
     span = slab.shape[1] // 4
-    ents = [
-        moved((ent + back[:, (k + 1) * span : (k + 2) * span]).astype(BF16), dy=-d)
-        for k, (d, ent) in enumerate(zip(FAR, ents))
-    ]
-    query_total, *far, ent_row = score(me, slab, blocks, (0,), 2, entities, asks)
-    ent_row = ent_row + back[:, :span]
-    for ent in ents:
-        ent_row = ent_row + ent.astype(F32)
-    for d, part in zip(FAR, far):
-        query_total = query_total + moved(part, dz=-d).astype(F32)
+    ents = ents + back[:, span:]
+    ent_hop = first_hop("dy", ents)
+    query_total, sent, ent_row = score(me, slab, blocks, (0,), 2, entities, asks)
+    sent, ent_row, *ent_hop = lax.optimization_barrier((sent, ent_row, *ent_hop))
+    query_hop = first_hop("dz", sent)
+    ent_row = ent_row + back[:, :span] + second_hop("dy", ents, *ent_hop)
+    query_total = query_total + second_hop("dz", sent, *query_hop)
     ent_share = ent_row[:, :width]
     for k, d in enumerate(FAR):
         block = ent_row[:, (k + 1) * width : (k + 2) * width].astype(BF16)

time: 102 us -> 112 us (1.098)
  waiting for transfers between devices: 20.2 us -> 25.2 us
  starting transfers between devices: 28.2 us -> 33.1 us
    ppermute x20 -> x23, waiting for transfers between devices: 20.2 us -> 25.2 us  [moved(): return lax.ppermute(block, AXES, route)]
    ppermute x20 -> x23, starting transfers between devices: 28.2 us -> 33.1 us  [moved(): return lax.ppermute(block, AXES, route)]
  transfers between devices with their start and end apart: 20 -> 23, of which waited for: 6 -> 10; matrix products, arithmetic and copies ran while one was open for 1% -> 1% of each run, Pallas kernels for 25% -> 23%
where the time goes in v4:
time: 112 us; the launch traced here: 111 us
  Pallas kernels  44 us (39%)
  starting transfers between devices  33.1 us (30%)
  waiting for transfers between devices  25.2 us (22%)
  local copies, waits for them, and re-layouts  4.28 us (4%)
  other arithmetic  3.15 us (3%)
    ppermute x23, starting transfers between devices, moved(): return lax.ppermute(block, AXES, route)  33.1 us
    ppermute x23, waiting for transfers between devices, moved(): return lax.ppermute(block, AXES, route)  25.2 us
    pallas_call x2, Pallas kernels, encode_heads(): pl.pallas_call(functools.partial(head_kernel, chunk * heads, heads), in_s...  16.8 us
    pallas_call x3, Pallas kernels, score(): pl.pallas_call(functools.partial(score_kernel, plain, plain - 1.8, depth,...  15.2 us
    pallas_call x1, Pallas kernels, encode_entities(): pl.pallas_call(functools.partial(entity_kernel, relations, scale), grid=(...  12 us
    unnamed x20, local copies, waits for them, and re-layouts  3.34 us
  transfers between devices with their start and end apart: 23, of which 10 were waited for; matrix products, arithmetic and copies ran while one was open for 1% of the time, Pallas kernels for 23%

profile of v4, /device:TPU:0, one launch (start us, length us, event | category | flops | bytes accessed | tf_op | source)
XLA Modules:
  0.0 110.7 jit_solution(16936602808040820773)
XLA Ops:
  5.4 12.0 %shard_map.113 = (bf16[200,128]{1,0:T(8,128)(2,1)S(1)}, f32[40960,128]{1,0:T(8,128)S(1)}, bf16[200,6400]{1,0:T(8,128)(2,1)S(1)}, bf16[256,896]{1,0:T(8,128)(2,1)S(1)}) custom-call(s32[12800]{0:T(1024)S(1)} %add_multiply_fusion.own_ids.head_ids, bf16[200,20000]{1,0:T(8,128)(2,1)} %bitcast.23, bf16[200,5000]{1,0:T(8,128)(2,1)S(1)} %bitcast.14, ...), custom_call_target="tpu_custom_call" | custom-call | tf_op jit(solution)/shard_map/pallas_call | solution.py:165
  17.4 2.9 %collective-permute-start = (bf16[200,128]{1,0:T(8,128)(2,1)S(1)}, bf16[200,128]{1,0:T(8,128)(2,1)S(1)}, u32[]{:S(2)}, u32[]{:S(2)}) collective-permute-start(bf16[200,128]{1,0:T(8,128)(2,1)S(1)} %get-tuple-element.24.echo), channel_id=1, source_target_pairs={{16,0},{17,1},{18,2},{19,3},{20,4},{21,5},{22,6},{23,7},{24,8},{25... | collective-permute-start | bytes 153608 | tf_op jit(solution)/shard_map/ppermute | solution.py:38
  20.4 2.3 %collective-permute-start.2 = (bf16[200,128]{1,0:T(8,128)(2,1)S(1)}, bf16[200,128]{1,0:T(8,128)(2,1)S(1)}, u32[]{:S(2)}, u32[]{:S(2)}) collective-permute-start(bf16[200,128]{1,0:T(8,128)(2,1)S(1)} %get-tuple-element.24.echo), channel_id=1, source_target_pairs={{2,0},{3,1},{0,2},{1,3},{6,4},{7,5},{4,6},{5,7},{10,8},{11,9},{8,1... | collective-permute-start | bytes 153608 | tf_op jit(solution)/shard_map/ppermute | solution.py:38
  22.7 8.4 %shard_map.114 = (bf16[208,256]{1,0:T(8,128)(2,1)S(1)}, bf16[200,128]{1,0:T(8,128)(2,1)S(1)}, f32[40960,128]{1,0:T(8,128)S(1)}, bf16[200,6400]{1,0:T(8,128)(2,1)S(1)}, bf16[256,896]{1,0:T(8,128)(2,1)S(1)}) custom-call(s32[12800]{0:T(1024)S(1)} %add_multiply_fusion.own_ids.head_ids, ...), custom_call_target="tpu_custom_call", output_to_operand_aliasing={{2}: (6, {}), {3}: (7, {}), {4}: (8, {})} | custom-call | tf_op jit(solution)/shard_map/pallas_call | solution.py:199
  31.2 3.1 %collective-permute-start.3 = (bf16[200,512]{1,0:T(8,128)(2,1)S(1)}, bf16[200,512]{1,0:T(8,128)(2,1)S(1)}, u32[]{:S(2)}, u32[]{:S(2)}) collective-permute-start(bf16[200,512]{1,0:T(8,128)(2,1)S(1)} %constant_dynamic-update-slice_fusion.echo), channel_id=1, source_target_pairs={{4,0},{5,1},{6,2},{7,3},{8,4},{9,5},{10,6},{11,7},{12,8},{13,9},{1... | collective-permute-start | bytes 614408 | tf_op jit(solution)/shard_map/ppermute | solution.py:38
  34.2 2.2 %collective-permute-start.5 = (bf16[200,512]{1,0:T(8,128)(2,1)S(1)}, bf16[200,512]{1,0:T(8,128)(2,1)S(1)}, u32[]{:S(2)}, u32[]{:S(2)}) collective-permute-start(bf16[200,512]{1,0:T(8,128)(2,1)S(1)} %constant_dynamic-update-slice_fusion.echo), channel_id=1, source_target_pairs={{8,0},{9,1},{10,2},{11,3},{12,4},{13,5},{14,6},{15,7},{0,8},{1,9},... | collective-permute-start | bytes 614408 | tf_op jit(solution)/shard_map/ppermute | solution.py:38
  36.4 8.4 %shard_map.115 = (bf16[208,512]{1,0:T(8,128)(2,1)S(1)}, bf16[200,512]{1,0:T(8,128)(2,1)S(1)}, f32[40960,128]{1,0:T(8,128)S(1)}, bf16[200,6400]{1,0:T(8,128)(2,1)S(1)}, bf16[256,896]{1,0:T(8,128)(2,1)S(1)}) custom-call(s32[12800]{0:T(1024)S(1)} %add_multiply_fusion.own_ids.head_ids, ...), custom_call_target="tpu_custom_call", output_to_operand_aliasing={{2}: (6, {}), {3}: (7, {}), {4}: (8, {})} | custom-call | tf_op jit(solution)/shard_map/pallas_call | solution.py:199
  45.7 4.1 %collective-permute-start.6 = (bf16[208,512]{1,0:T(8,128)(2,1)S(1)}, bf16[208,512]{1,0:T(8,128)(2,1)S(1)}, u32[]{:S(2)}, u32[]{:S(2)}) collective-permute-start(bf16[208,512]{1,0:T(8,128)(2,1)S(1)} %get-tuple-element.34.refs_0_), channel_id=1, source_target_pairs={{32,0},{33,1},{34,2},{35,3},{36,4},{37,5},{38,6},{39,7},{40,8},{41... | collective-permute-start | bytes 638984 | tf_op jit(solution)/shard_map/ppermute | solution.py:38
  49.8 5.1 %collective-permute-done.6.refs_1_ = bf16[208,512]{1,0:T(8,128)(2,1)S(1)} collective-permute-done((bf16[208,512]{1,0:T(8,128)(2,1)S(1)}, bf16[208,512]{1,0:T(8,128)(2,1)S(1)}, u32[]{:S(2)}, u32[]{:S(2)}) %collective-permute-start.6) | collective-permute-done | bytes 213024 | tf_op jit(solution)/shard_map/ppermute | solution.py:38
  54.9 3.8 %collective-permute-start.8 = (bf16[208,256]{1,0:T(8,128)(2,1)S(1)}, bf16[208,256]{1,0:T(8,128)(2,1)S(1)}, u32[]{:S(2)}, u32[]{:S(2)}) collective-permute-start(bf16[208,256]{1,0:T(8,128)(2,1)S(1)} %slice.103), channel_id=1, source_target_pairs={{32,0},{33,1},{34,2},{35,3},{36,4},{37,5},{38,6},{39,7},{40,8},{41... | collective-permute-start | bytes 319496 | tf_op jit(solution)/shard_map/ppermute | solution.py:38
  59.0 2.0 %collective-permute-done.8.refs_3_ = bf16[208,256]{1,0:T(8,128)(2,1)S(1)} collective-permute-done((bf16[208,256]{1,0:T(8,128)(2,1)S(1)}, bf16[208,256]{1,0:T(8,128)(2,1)S(1)}, u32[]{:S(2)}, u32[]{:S(2)}) %collective-permute-start.8) | collective-permute-done | bytes 106528 | tf_op jit(solution)/shard_map/ppermute | solution.py:38
  61.0 3.9 %collective-permute-done.9.refs_4_ = bf16[208,256]{1,0:T(8,128)(2,1)S(1)} collective-permute-done((bf16[208,256]{1,0:T(8,128)(2,1)S(1)}, bf16[208,256]{1,0:T(8,128)(2,1)S(1)}, u32[]{:S(2)}, u32[]{:S(2)}) %collective-permute-start.9) | collective-permute-done | bytes 106528 | tf_op jit(solution)/shard_map/ppermute | solution.py:38
  64.9 6.8 %shard_map.116 = (f32[4,200,512]{2,1,0:T(8,128)S(1)}, bf16[200,2048]{1,0:T(8,128)(2,1)S(1)}) custom-call(s32[1]{0:T(128)} %bitcast.me, bf16[200,2048]{1,0:T(8,128)(2,1)S(1)} %collective-permute-done.10.slab, bf16[208,512]{1,0:T(8,128)(2,1)S(1)} %get-tuple-element.34.refs_0_, bf16[208,512]{1,0:T(8,128)(2,1)S(1)} %collective-permute-done.6.refs_1_, ...), custom_call_target="tpu_custom_call" | custom-call | tf_op jit(solution)/shard_map/pallas_call | solution.py:345
  72.0 6.3 %shard_map.117 = (f32[4,200,512]{2,1,0:T(8,128)S(1)}, f32[200,1536]{1,0:T(8,128)S(1)}) custom-call(s32[1]{0:T(128)} %bitcast.me, bf16[200,2048]{1,0:T(8,128)(2,1)S(1)} %constant_dynamic-update-slice_fusion.4.slab, bf16[208,512]{1,0:T(8,128)(2,1)S(1)} %get-tuple-element.34.refs_0_, ...), custom_call_target="tpu_custom_call", output_to_operand_aliasing={{0}: (7, {})} | custom-call | tf_op jit(solution)/shard_map/pallas_call | solution.py:345
  80.0 2.0 %collective-permute-start.13 = (bf16[200,512]{1,0:T(8,128)(2,1)S(1)}, bf16[200,512]{1,0:T(8,128)(2,1)S(1)}, u32[]{:S(2)}, u32[]{:S(2)}) collective-permute-start(bf16[200,512]{1,0:T(8,128)(2,1)S(1)} %get-tuple-element.56), channel_id=1, source_target_pairs={{4,0},{5,1},{6,2},{7,3},{8,4},{9,5},{10,6},{11,7},{12,8},{13,9},{1... | collective-permute-start | bytes 614408 | tf_op jit(solution)/shard_map/ppermute | solution.py:38
  82.0 2.1 %shard_map.118 = (f32[200,512]{1,0:T(8,128)S(1)}, f32[200,1536]{1,0:T(8,128)S(1)}, f32[200,512]{1,0:T(8,128)S(1)}) custom-call(s32[1]{0:T(128)} %bitcast.me, bf16[200,2048]{1,0:T(8,128)(2,1)S(1)} %constant_dynamic-update-slice_fusion.4.slab, bf16[208,512]{1,0:T(8,128)(2,1)S(1)} %get-tuple-element.34.refs_0_, ...), custom_call_target="tpu_custom_call" | custom-call | tf_op jit(solution)/shard_map/pallas_call | solution.py:345
  84.1 3.4 %collective-permute-done.12 = bf16[200,512]{1,0:T(8,128)(2,1)S(1)} collective-permute-done((bf16[200,512]{1,0:T(8,128)(2,1)S(1)}, bf16[200,512]{1,0:T(8,128)(2,1)S(1)}, u32[]{:S(2)}, u32[]{:S(2)}) %collective-permute-start.12) | collective-permute-done | bytes 204832 | tf_op jit(solution)/shard_map/ppermute | solution.py:38
  88.0 2.0 %collective-permute-start.20 = (bf16[200,512]{1,0:T(8,128)(2,1)S(1)}, bf16[200,512]{1,0:T(8,128)(2,1)S(1)}, u32[]{:S(2)}, u32[]{:S(2)}) collective-permute-start(bf16[200,512]{1,0:T(8,128)(2,1)S(1)} %get-tuple-element.55), channel_id=1, source_target_pairs={{96,0},{97,1},{98,2},{99,3},{100,4},{101,5},{102,6},{103,7},{104,8... | collective-permute-start | bytes 614408 | tf_op jit(solution)/shard_map/ppermute | solution.py:38
  90.0 3.1 %collective-permute-start.15 = (bf16[200,256]{1,0:T(8,128)(2,1)S(1)}, bf16[200,256]{1,0:T(8,128)(2,1)S(1)}, u32[]{:S(2)}, u32[]{:S(2)}) collective-permute-start(bf16[200,256]{1,0:T(8,128)(2,1)S(1)} %get-tuple-element.53), channel_id=1, source_target_pairs={{4,0},{5,1},{6,2},{7,3},{8,4},{9,5},{10,6},{11,7},{12,8},{13,9},{1... | collective-permute-start | bytes 307208 | tf_op jit(solution)/shard_map/ppermute | solution.py:38
  93.7 1.7 %collective-permute-done.15 = bf16[200,256]{1,0:T(8,128)(2,1)S(1)} collective-permute-done((bf16[200,256]{1,0:T(8,128)(2,1)S(1)}, bf16[200,256]{1,0:T(8,128)(2,1)S(1)}, u32[]{:S(2)}, u32[]{:S(2)}) %collective-permute-start.15) | collective-permute-done | bytes 102432 | tf_op jit(solution)/shard_map/ppermute | solution.py:38
  95.6 1.9 %collective-permute-start.16 = (bf16[200,128]{1,0:T(8,128)(2,1)S(1)}, bf16[200,128]{1,0:T(8,128)(2,1)S(1)}, u32[]{:S(2)}, u32[]{:S(2)}) collective-permute-start(bf16[200,128]{1,0:T(8,128)(2,1)S(1)} %get-tuple-element.58), channel_id=1, source_target_pairs={{18,0},{19,1},{16,2},{17,3},{22,4},{23,5},{20,6},{21,7},{26,8},{27... | collective-permute-start | bytes 153608 | tf_op jit(solution)/shard_map/ppermute | solution.py:38
  99.9 1.6 %collective-permute-done.16 = bf16[200,128]{1,0:T(8,128)(2,1)S(1)} collective-permute-done((bf16[200,128]{1,0:T(8,128)(2,1)S(1)}, bf16[200,128]{1,0:T(8,128)(2,1)S(1)}, u32[]{:S(2)}, u32[]{:S(2)}) %collective-permute-start.16) | collective-permute-done | bytes 51232 | tf_op jit(solution)/shard_map/ppermute | solution.py:38
  101.6 2.9 %collective-permute-done.18 = bf16[200,128]{1,0:T(8,128)(2,1)S(1)} collective-permute-done((bf16[200,128]{1,0:T(8,128)(2,1)S(1)}, bf16[200,128]{1,0:T(8,128)(2,1)S(1)}, u32[]{:S(2)}, u32[]{:S(2)}) %collective-permute-start.18) | collective-permute-done | bytes 51232 | tf_op jit(solution)/shard_map/ppermute | solution.py:38
  106.5 3.3 %collective-permute-done.22 = bf16[200,256]{1,0:T(8,128)(2,1)S(1)} collective-permute-done((bf16[200,256]{1,0:T(8,128)(2,1)S(1)}, bf16[200,256]{1,0:T(8,128)(2,1)S(1)}, u32[]{:S(2)}, u32[]{:S(2)}) %collective-permute-start.22) | collective-permute-done | bytes 102432 | tf_op jit(solution)/shard_map/ppermute | solution.py:38
  (73 shorter events, 14.4 us)
Async XLA Ops:
  5.4 17.3 %copy-start.5 = (s32[512]{0:T(512)S(1)}, s32[512]{0:T(512)}, u32[]{:S(2)}) copy-start(s32[512]{0:T(512)} %param.14) | copy-start | bytes 6148
  17.4 13.6 %collective-permute-start = (bf16[200,128]{1,0:T(8,128)(2,1)S(1)}, bf16[200,128]{1,0:T(8,128)(2,1)S(1)}, u32[]{:S(2)}, u32[]{:S(2)}) collective-permute-start(bf16[200,128]{1,0:T(8,128)(2,1)S(1)} %get-tuple-element.24.echo), channel_id=1, source_target_pairs={{16,0},{17,1},{18,2},{19,3},{20,4},{21,5},{22,6},{23,7},{24,8},{25... | collective-permute-start | bytes 153608 | tf_op jit(solution)/shard_map/ppermute | solution.py:38
  20.4 10.7 %collective-permute-start.1 = (bf16[200,128]{1,0:T(8,128)(2,1)S(1)}, bf16[200,128]{1,0:T(8,128)(2,1)S(1)}, u32[]{:S(2)}, u32[]{:S(2)}) collective-permute-start(bf16[200,128]{1,0:T(8,128)(2,1)S(1)} %get-tuple-element.24.echo), channel_id=1, source_target_pairs={{18,0},{19,1},{16,2},{17,3},{22,4},{23,5},{20,6},{21,7},{26,8},{27... | collective-permute-start | bytes 153608 | tf_op jit(solution)/shard_map/ppermute | solution.py:38
  20.4 10.8 %collective-permute-start.2 = (bf16[200,128]{1,0:T(8,128)(2,1)S(1)}, bf16[200,128]{1,0:T(8,128)(2,1)S(1)}, u32[]{:S(2)}, u32[]{:S(2)}) collective-permute-start(bf16[200,128]{1,0:T(8,128)(2,1)S(1)} %get-tuple-element.24.echo), channel_id=1, source_target_pairs={{2,0},{3,1},{0,2},{1,3},{6,4},{7,5},{4,6},{5,7},{10,8},{11,9},{8,1... | collective-permute-start | bytes 153608 | tf_op jit(solution)/shard_map/ppermute | solution.py:38
  31.2 13.7 %collective-permute-start.3 = (bf16[200,512]{1,0:T(8,128)(2,1)S(1)}, bf16[200,512]{1,0:T(8,128)(2,1)S(1)}, u32[]{:S(2)}, u32[]{:S(2)}) collective-permute-start(bf16[200,512]{1,0:T(8,128)(2,1)S(1)} %constant_dynamic-update-slice_fusion.echo), channel_id=1, source_target_pairs={{4,0},{5,1},{6,2},{7,3},{8,4},{9,5},{10,6},{11,7},{12,8},{13,9},{1... | collective-permute-start | bytes 614408 | tf_op jit(solution)/shard_map/ppermute | solution.py:38
  34.2 11.3 %collective-permute-start.4 = (bf16[200,512]{1,0:T(8,128)(2,1)S(1)}, bf16[200,512]{1,0:T(8,128)(2,1)S(1)}, u32[]{:S(2)}, u32[]{:S(2)}) collective-permute-start(bf16[200,512]{1,0:T(8,128)(2,1)S(1)} %constant_dynamic-update-slice_fusion.echo), channel_id=1, source_target_pairs={{12,0},{13,1},{14,2},{15,3},{0,4},{1,5},{2,6},{3,7},{4,8},{5,9},{6... | collective-permute-start | bytes 614408 | tf_op jit(solution)/shard_map/ppermute | solution.py:38
  34.2 11.3 %collective-permute-start.5 = (bf16[200,512]{1,0:T(8,128)(2,1)S(1)}, bf16[200,512]{1,0:T(8,128)(2,1)S(1)}, u32[]{:S(2)}, u32[]{:S(2)}) collective-permute-start(bf16[200,512]{1,0:T(8,128)(2,1)S(1)} %constant_dynamic-update-slice_fusion.echo), channel_id=1, source_target_pairs={{8,0},{9,1},{10,2},{11,3},{12,4},{13,5},{14,6},{15,7},{0,8},{1,9},... | collective-permute-start | bytes 614408 | tf_op jit(solution)/shard_map/ppermute | solution.py:38
  45.6 19.3 %collective-permute-start.10 = (bf16[200,2048]{1,0:T(8,128)(2,1)S(1)}, bf16[200,2048]{1,0:T(8,128)(2,1)S(1)}, u32[]{:S(2)}, u32[]{:S(2)}) collective-permute-start(bf16[200,2048]{1,0:T(8,128)(2,1)S(1)} %constant_dynamic-update-slice_fusion.4.slab), channel_id=1, source_target_pairs={{1,0},{0,1},{3,2},{2,3},{5,4},{4,5},{7,6},{6,7},{9,8},{8,9},{11,10... | collective-permute-start | bytes 2457608 | tf_op jit(solution)/shard_map/ppermute | solution.py:38
  45.7 9.2 %collective-permute-start.6 = (bf16[208,512]{1,0:T(8,128)(2,1)S(1)}, bf16[208,512]{1,0:T(8,128)(2,1)S(1)}, u32[]{:S(2)}, u32[]{:S(2)}) collective-permute-start(bf16[208,512]{1,0:T(8,128)(2,1)S(1)} %get-tuple-element.34.refs_0_), channel_id=1, source_target_pairs={{32,0},{33,1},{34,2},{35,3},{36,4},{37,5},{38,6},{39,7},{40,8},{41... | collective-permute-start | bytes 638984 | tf_op jit(solution)/shard_map/ppermute | solution.py:38
  49.8 8.9 %collective-permute-start.7 = (bf16[208,512]{1,0:T(8,128)(2,1)S(1)}, bf16[208,512]{1,0:T(8,128)(2,1)S(1)}, u32[]{:S(2)}, u32[]{:S(2)}) collective-permute-start(bf16[208,512]{1,0:T(8,128)(2,1)S(1)} %get-tuple-element.34.refs_0_), channel_id=1, source_target_pairs={{96,0},{97,1},{98,2},{99,3},{100,4},{101,5},{102,6},{103,7},{104,8... | collective-permute-start | bytes 638984 | tf_op jit(solution)/shard_map/ppermute | solution.py:38
  54.9 6.1 %collective-permute-start.8 = (bf16[208,256]{1,0:T(8,128)(2,1)S(1)}, bf16[208,256]{1,0:T(8,128)(2,1)S(1)}, u32[]{:S(2)}, u32[]{:S(2)}) collective-permute-start(bf16[208,256]{1,0:T(8,128)(2,1)S(1)} %slice.103), channel_id=1, source_target_pairs={{32,0},{33,1},{34,2},{35,3},{36,4},{37,5},{38,6},{39,7},{40,8},{41... | collective-permute-start | bytes 319496 | tf_op jit(solution)/shard_map/ppermute | solution.py:38
  58.7 6.2 %collective-permute-start.9 = (bf16[208,256]{1,0:T(8,128)(2,1)S(1)}, bf16[208,256]{1,0:T(8,128)(2,1)S(1)}, u32[]{:S(2)}, u32[]{:S(2)}) collective-permute-start(bf16[208,256]{1,0:T(8,128)(2,1)S(1)} %slice.104), channel_id=1, source_target_pairs={{96,0},{97,1},{98,2},{99,3},{100,4},{101,5},{102,6},{103,7},{104,8... | collective-permute-start | bytes 319496 | tf_op jit(solution)/shard_map/ppermute | solution.py:38
  71.7 6.6 %collective-permute-start.11 = (bf16[200,2048]{1,0:T(8,128)(2,1)S(1)}, bf16[200,2048]{1,0:T(8,128)(2,1)S(1)}, u32[]{:S(2)}, u32[]{:S(2)}) collective-permute-start(bf16[200,2048]{1,0:T(8,128)(2,1)S(1)} %get-tuple-element.40), channel_id=1, source_target_pairs={{1,0},{0,1},{3,2},{2,3},{5,4},{4,5},{7,6},{6,7},{9,8},{8,9},{11,10... | collective-permute-start | bytes 2457608 | tf_op jit(solution)/shard_map/ppermute | solution.py:38
  78.7 8.8 %collective-permute-start.12 = (bf16[200,512]{1,0:T(8,128)(2,1)S(1)}, bf16[200,512]{1,0:T(8,128)(2,1)S(1)}, u32[]{:S(2)}, u32[]{:S(2)}) collective-permute-start(bf16[200,512]{1,0:T(8,128)(2,1)S(1)} %get-tuple-element.57), channel_id=1, source_target_pairs={{12,0},{13,1},{14,2},{15,3},{0,4},{1,5},{2,6},{3,7},{4,8},{5,9},{6... | collective-permute-start | bytes 614408 | tf_op jit(solution)/shard_map/ppermute | solution.py:38
  80.0 7.4 %collective-permute-start.13 = (bf16[200,512]{1,0:T(8,128)(2,1)S(1)}, bf16[200,512]{1,0:T(8,128)(2,1)S(1)}, u32[]{:S(2)}, u32[]{:S(2)}) collective-permute-start(bf16[200,512]{1,0:T(8,128)(2,1)S(1)} %get-tuple-element.56), channel_id=1, source_target_pairs={{4,0},{5,1},{6,2},{7,3},{8,4},{9,5},{10,6},{11,7},{12,8},{13,9},{1... | collective-permute-start | bytes 614408 | tf_op jit(solution)/shard_map/ppermute | solution.py:38
  87.7 5.9 %collective-permute-start.14 = (bf16[200,256]{1,0:T(8,128)(2,1)S(1)}, bf16[200,256]{1,0:T(8,128)(2,1)S(1)}, u32[]{:S(2)}, u32[]{:S(2)}) collective-permute-start(bf16[200,256]{1,0:T(8,128)(2,1)S(1)} %get-tuple-element.52), channel_id=1, source_target_pairs={{12,0},{13,1},{14,2},{15,3},{0,4},{1,5},{2,6},{3,7},{4,8},{5,9},{6... | collective-permute-start | bytes 307208 | tf_op jit(solution)/shard_map/ppermute | solution.py:38
  87.9 11.7 %collective-permute-start.19 = (bf16[200,512]{1,0:T(8,128)(2,1)S(1)}, bf16[200,512]{1,0:T(8,128)(2,1)S(1)}, u32[]{:S(2)}, u32[]{:S(2)}) collective-permute-start(bf16[200,512]{1,0:T(8,128)(2,1)S(1)} %get-tuple-element.54), channel_id=1, source_target_pairs={{32,0},{33,1},{34,2},{35,3},{36,4},{37,5},{38,6},{39,7},{40,8},{41... | collective-permute-start | bytes 614408 | tf_op jit(solution)/shard_map/ppermute | solution.py:38
  88.0 11.6 %collective-permute-start.20 = (bf16[200,512]{1,0:T(8,128)(2,1)S(1)}, bf16[200,512]{1,0:T(8,128)(2,1)S(1)}, u32[]{:S(2)}, u32[]{:S(2)}) collective-permute-start(bf16[200,512]{1,0:T(8,128)(2,1)S(1)} %get-tuple-element.55), channel_id=1, source_target_pairs={{96,0},{97,1},{98,2},{99,3},{100,4},{101,5},{102,6},{103,7},{104,8... | collective-permute-start | bytes 614408 | tf_op jit(solution)/shard_map/ppermute | solution.py:38
  90.0 5.4 %collective-permute-start.15 = (bf16[200,256]{1,0:T(8,128)(2,1)S(1)}, bf16[200,256]{1,0:T(8,128)(2,1)S(1)}, u32[]{:S(2)}, u32[]{:S(2)}) collective-permute-start(bf16[200,256]{1,0:T(8,128)(2,1)S(1)} %get-tuple-element.53), channel_id=1, source_target_pairs={{4,0},{5,1},{6,2},{7,3},{8,4},{9,5},{10,6},{11,7},{12,8},{13,9},{1... | collective-permute-start | bytes 307208 | tf_op jit(solution)/shard_map/ppermute | solution.py:38
  95.6 5.9 %collective-permute-start.16 = (bf16[200,128]{1,0:T(8,128)(2,1)S(1)}, bf16[200,128]{1,0:T(8,128)(2,1)S(1)}, u32[]{:S(2)}, u32[]{:S(2)}) collective-permute-start(bf16[200,128]{1,0:T(8,128)(2,1)S(1)} %get-tuple-element.58), channel_id=1, source_target_pairs={{18,0},{19,1},{16,2},{17,3},{22,4},{23,5},{20,6},{21,7},{26,8},{27... | collective-permute-start | bytes 153608 | tf_op jit(solution)/shard_map/ppermute | solution.py:38
  97.4 4.1 %collective-permute-start.17 = (bf16[200,128]{1,0:T(8,128)(2,1)S(1)}, bf16[200,128]{1,0:T(8,128)(2,1)S(1)}, u32[]{:S(2)}, u32[]{:S(2)}) collective-permute-start(bf16[200,128]{1,0:T(8,128)(2,1)S(1)} %get-tuple-element.60), channel_id=1, source_target_pairs={{16,0},{17,1},{18,2},{19,3},{20,4},{21,5},{22,6},{23,7},{24,8},{25... | collective-permute-start | bytes 153608 | tf_op jit(solution)/shard_map/ppermute | solution.py:38
  98.9 5.6 %collective-permute-start.18 = (bf16[200,128]{1,0:T(8,128)(2,1)S(1)}, bf16[200,128]{1,0:T(8,128)(2,1)S(1)}, u32[]{:S(2)}, u32[]{:S(2)}) collective-permute-start(bf16[200,128]{1,0:T(8,128)(2,1)S(1)} %get-tuple-element.59), channel_id=1, source_target_pairs={{2,0},{3,1},{0,2},{1,3},{6,4},{7,5},{4,6},{5,7},{10,8},{11,9},{8,1... | collective-permute-start | bytes 153608 | tf_op jit(solution)/shard_map/ppermute | solution.py:38
  99.8 6.7 %collective-permute-start.21 = (bf16[200,256]{1,0:T(8,128)(2,1)S(1)}, bf16[200,256]{1,0:T(8,128)(2,1)S(1)}, u32[]{:S(2)}, u32[]{:S(2)}) collective-permute-start(bf16[200,256]{1,0:T(8,128)(2,1)S(1)} %get-tuple-element.50), channel_id=1, source_target_pairs={{96,0},{97,1},{98,2},{99,3},{100,4},{101,5},{102,6},{103,7},{104,8... | collective-permute-start | bytes 307208 | tf_op jit(solution)/shard_map/ppermute | solution.py:38
  105.2 4.7 %collective-permute-start.22 = (bf16[200,256]{1,0:T(8,128)(2,1)S(1)}, bf16[200,256]{1,0:T(8,128)(2,1)S(1)}, u32[]{:S(2)}, u32[]{:S(2)}) collective-permute-start(bf16[200,256]{1,0:T(8,128)(2,1)S(1)} %get-tuple-element.51), channel_id=1, source_target_pairs={{32,0},{33,1},{34,2},{35,3},{36,4},{37,5},{38,6},{39,7},{40,8},{41... | collective-permute-start | bytes 307208 | tf_op jit(solution)/shard_map/ppermute | solution.py:38
  (6 other events, 55.0 us)

commit v5 on v3

--- a/solution.py
+++ b/solution.py
@@ -127,9 +127,12 @@
 def head_kernel(
     start, width, head_ids, head_rel, asked, wanted, fc, echo, table, weights, rel_table, *refs
 ):
-    query_out, echo_out, rows = refs[-6], refs[-5], refs[-1]
+    rows = refs[-1]
     if start:
-        query_out[:, :start] = refs[0][...]
+        earlier, query_out, echo_out, whole_out = refs[:4]
+        whole_out[:, :start] = earlier[...]
+    else:
+        query_out, echo_out = refs[:2]
     echo_out[...] = echo[...]
     part = slice(start, start + width)
     tokens, heads = head_rel.shape
@@ -147,9 +150,12 @@
     for t in range(wanted.shape[0]):
         target = wanted[t : t + 1, part]
         digits += [target // LANES, target % LANES]
-    query_out[:, query_out.shape[1] - width :] = jnp.concatenate(
+    query = jnp.concatenate(
         [query, jnp.concatenate(digits, axis=0).astype(F32)], axis=0
     ).astype(BF16)
+    query_out[...] = query
+    if start:
+        whole_out[:, start:] = query
 
 
 def encode_entities(ids, anchors, relation_ids, anchor_table, relation_table, enc_weight, scale):
@@ -183,14 +189,16 @@
         compiler_params=pltpu.CompilerParams(vmem_limit_bytes=VMEM_BYTES),
     )(
         ids,
-        pltpu.with_memory_space_constraint(anchor_table.T, pltpu.HBM), enc_weight.T, relation_table.T,
+        pltpu.with_memory_space_constraint(anchor_table.T, pltpu.HBM),
+        pltpu.with_memory_space_constraint(enc_weight.T, pltpu.HBM),
+        pltpu.with_memory_space_constraint(relation_table.T, pltpu.HBM),
         relation_ids.T,
     )
 
 
 def encode_heads(
     chunk, head_ids, head_relations, query_relation, targets, fc_weight, echo,
-    table, weights, rel_table, earlier,
+    table, weights, rel_table, *earlier,
 ):
     heads = head_relations.shape[1] // CHUNKS
     depth = fc_weight.shape[0]
@@ -198,16 +206,17 @@
     whole = pl.BlockSpec(memory_space=pltpu.VMEM)
     return pl.pallas_call(
         functools.partial(head_kernel, chunk * heads, heads),
-        in_specs=[pl.BlockSpec(memory_space=pltpu.SMEM)] + [whole] * (8 + len(earlier)),
-        out_specs=[whole] * 5,
+        in_specs=[pl.BlockSpec(memory_space=pltpu.SMEM)] + [whole] * (8 + chunk),
+        out_specs=[whole] * (5 + chunk),
         out_shape=[
-            jax.ShapeDtypeStruct((depth + 2 * targets.shape[0], heads * (chunk + 1)), BF16),
+            jax.ShapeDtypeStruct((depth + 2 * targets.shape[0], heads), BF16),
             jax.ShapeDtypeStruct(echo.shape, BF16),
+            *[jax.ShapeDtypeStruct((depth + 2 * targets.shape[0], 2 * heads), BF16)] * chunk,
             pltpu.VMEM(table.shape, F32),
             pltpu.VMEM(weights.shape, BF16),
             pltpu.VMEM(rel_table.shape, BF16),
         ],
-        input_output_aliases={6: 2, 7: 3, 8: 4},
+        input_output_aliases={6 + k: 2 + chunk + k for k in range(3)},
         scratch_shapes=[pltpu.VMEM((2 * heads * anchors, LANES), F32)],
         compiler_params=pltpu.CompilerParams(vmem_limit_bytes=VMEM_BYTES),
     )(
@@ -217,7 +226,7 @@
 
 
 def score_kernel(plain, struck_value, depth, parts, stage, me, slab, *refs):
-    blocks, refs = refs[:4], refs[4:]
+    blocks, refs = (refs[:1], refs[1:3], refs[3:4], refs[4:6]), refs[6:]
     if stage:
         before, refs = refs[0], refs[1:]
     if stage == 2:
@@ -250,7 +259,7 @@
         tall[k * SPAN : (k + 1) * SPAN, :] = wide.T.astype(BF16)
     within = lax.broadcasted_iota(jnp.int32, (LANES, width), 0)
     for b in range(4):
-        query = blocks[b][...].astype(F32)
+        query = jnp.concatenate([piece[...] for piece in blocks[b]], axis=1).astype(F32)
         queries[b] = jnp.concatenate(
             [query[:depth, :], jnp.zeros((WIDE - depth, width), F32)], axis=0
         ).astype(BF16)
@@ -374,27 +383,18 @@
         enc_weight,
         scale,
     )
-    query = []
-    piece = own_cols
-    for chunk in range(CHUNKS):
-        axis = ("dx", "dy")[chunk]
-        sent = [moved(piece, **{axis: d}) for d in FAR]
-        part, piece, *shared = encode_heads(
-            chunk,
-            ids,
-            head_relations.T,
-            query_relation[None, :],
-            targets.T,
-            fc_weight,
-            piece,
-            *shared,
-            query,
-        )
-        query = [part]
-        piece = jnp.concatenate([piece] + sent, axis=1)
-    slab = piece
+    heads = (head_relations.T, query_relation[None, :], targets.T, fc_weight)
+    sent = [moved(own_cols, dx=d) for d in FAR]
+    early, own_cols, *shared = encode_heads(0, ids, *heads, own_cols, *shared)
+    row = jnp.concatenate([own_cols] + sent, axis=1)
+    first = [moved(early, dz=d) for d in (1, 2)]
+    sent = [moved(row, dy=d) for d in FAR]
+    late, row, query, *shared = encode_heads(1, ids, *heads, row, *shared, early)
+    late, query, row, *first = lax.optimization_barrier((late, query, row, *first))
+    slab = jnp.concatenate([row] + sent, axis=1)
     other = moved(slab, dcore=1)
-    blocks = query + [moved(part, dz=d) for part in query for d in FAR]
+    second = [moved(late, dz=d) for d in (1, 2)]
+    blocks = [query, first[0], second[0], moved(query, dz=3), first[1], second[1]]
     asks, away = score(me, other, blocks, (0, 1, 2, 3), 0, entities)
     back = moved(away, dcore=1).astype(F32)
     asks, *ents = score(me, slab, blocks, (1, 2, 3), 1, entities, asks)
@@ -403,11 +403,11 @@
         moved((ent + back[:, (k + 1) * span : (k + 2) * span]).astype(BF16), dy=-d)
         for k, (d, ent) in enumerate(zip(FAR, ents))
     ]
-    query_total, *far, ent_row = score(me, slab, blocks, (0,), 2, entities, asks)
+    query_total, *sums, ent_row = score(me, slab, blocks, (0,), 2, entities, asks)
     ent_row = ent_row + back[:, :span]
     for ent in ents:
         ent_row = ent_row + ent.astype(F32)
-    for d, part in zip(FAR, far):
+    for d, part in zip(FAR, sums):
         query_total = query_total + moved(part, dz=-d).astype(F32)
     ent_share = ent_row[:, :width]
     for k, d in enumerate(FAR):

time: 102 us -> 98.1 us (0.962); the launches traced: 100 us -> 97.8 us
  waiting for transfers between devices: 20.2 us -> 13.6 us
  starting transfers between devices: 28.2 us -> 34.1 us
  local copies, waits for them, and re-layouts: 4.21 us -> 1.65 us
    ppermute x20 -> x22, waiting for transfers between devices: 20.2 us -> 13.6 us  [moved(): return lax.ppermute(block, AXES, route)]
    ppermute x20 -> x22, starting transfers between devices: 28.2 us -> 34.1 us  [moved(): return lax.ppermute(block, AXES, route)]
    unnamed x20 -> x16, local copies, waits for them, and re-layouts: 3.34 us -> 0.79 us
  transfers between devices with their start and end apart: 20 -> 22, of which waited for: 6 -> 5; matrix products, arithmetic and copies ran while one was open for 1% -> 1% of each run, Pallas kernels for 25% -> 26%
where the time goes in v5:
time: 98.1 us; the launch traced here: 97.8 us
  Pallas kernels  44.7 us (46%)
  starting transfers between devices  34.1 us (35%)
  waiting for transfers between devices  13.6 us (14%)
  other arithmetic  2.89 us (3%)
  local copies, waits for them, and re-layouts  1.65 us (2%)
    ppermute x22, starting transfers between devices, moved(): return lax.ppermute(block, AXES, route)  34.1 us
    pallas_call x2, Pallas kernels, encode_heads(): pl.pallas_call(functools.partial(head_kernel, chunk * heads, heads), in_s...  16.9 us
    pallas_call x3, Pallas kernels, score(): pl.pallas_call(functools.partial(score_kernel, plain, plain - 1.8, depth,...  15.2 us
    ppermute x22, waiting for transfers between devices, moved(): return lax.ppermute(block, AXES, route)  13.6 us
    pallas_call x1, Pallas kernels, encode_entities(): pl.pallas_call(functools.partial(entity_kernel, relations, scale), grid=(...  12.7 us
  transfers between devices with their start and end apart: 22, of which 5 were waited for; matrix products, arithmetic and copies ran while one was open for 1% of the time, Pallas kernels for 26%

profile of v5, /device:TPU:0, one launch (start us, length us, event | category | flops | bytes accessed | tf_op | source)
XLA Modules:
  0.0 97.8 jit_solution(12222590641032068440)
XLA Ops:
  2.8 12.7 %shard_map.113 = (bf16[200,128]{1,0:T(8,128)(2,1)S(1)}, f32[40960,128]{1,0:T(8,128)S(1)}, bf16[200,6400]{1,0:T(8,128)(2,1)S(1)}, bf16[256,896]{1,0:T(8,128)(2,1)S(1)}) custom-call(s32[12800]{0:T(1024)S(1)} %add_multiply_fusion.own_ids.head_ids, bf16[200,20000]{1,0:T(8,128)(2,1)} %bitcast.21, bf16[200,5000]{1,0:T(8,128)(2,1)} %bitcast.22, ...), custom_call_target="tpu_custom_call" | custom-call | tf_op jit(solution)/shard_map/pallas_call | solution.py:171
  15.5 2.9 %collective-permute-start = (bf16[200,128]{1,0:T(8,128)(2,1)S(1)}, bf16[200,128]{1,0:T(8,128)(2,1)S(1)}, u32[]{:S(2)}, u32[]{:S(2)}) collective-permute-start(bf16[200,128]{1,0:T(8,128)(2,1)S(1)} %get-tuple-element.30.echo), channel_id=1, source_target_pairs={{16,0},{17,1},{18,2},{19,3},{20,4},{21,5},{22,6},{23,7},{24,8},{25... | collective-permute-start | bytes 153608 | tf_op jit(solution)/shard_map/ppermute | solution.py:38
  18.4 2.3 %collective-permute-start.2 = (bf16[200,128]{1,0:T(8,128)(2,1)S(1)}, bf16[200,128]{1,0:T(8,128)(2,1)S(1)}, u32[]{:S(2)}, u32[]{:S(2)}) collective-permute-start(bf16[200,128]{1,0:T(8,128)(2,1)S(1)} %get-tuple-element.30.echo), channel_id=1, source_target_pairs={{2,0},{3,1},{0,2},{1,3},{6,4},{7,5},{4,6},{5,7},{10,8},{11,9},{8,1... | collective-permute-start | bytes 153608 | tf_op jit(solution)/shard_map/ppermute | solution.py:38
  20.7 8.4 %shard_map.114 = (bf16[208,256]{1,0:T(8,128)(2,1)S(1)}, bf16[200,128]{1,0:T(8,128)(2,1)S(1)}, f32[40960,128]{1,0:T(8,128)S(1)}, bf16[200,6400]{1,0:T(8,128)(2,1)S(1)}, bf16[256,896]{1,0:T(8,128)(2,1)S(1)}) custom-call(s32[12800]{0:T(1024)S(1)} %add_multiply_fusion.own_ids.head_ids, ...), custom_call_target="tpu_custom_call", output_to_operand_aliasing={{2}: (6, {}), {3}: (7, {}), {4}: (8, {})} | custom-call | tf_op jit(solution)/shard_map/pallas_call | solution.py:207
  29.2 4.1 %collective-permute-start.3 = (bf16[208,256]{1,0:T(8,128)(2,1)S(1)}, bf16[208,256]{1,0:T(8,128)(2,1)S(1)}, u32[]{:S(2)}, u32[]{:S(2)}) collective-permute-start(bf16[208,256]{1,0:T(8,128)(2,1)S(1)} %get-tuple-element.38.refs_0_), channel_id=1, source_target_pairs={{32,0},{33,1},{34,2},{35,3},{36,4},{37,5},{38,6},{39,7},{40,8},{41... | collective-permute-start | bytes 319496 | tf_op jit(solution)/shard_map/ppermute | solution.py:38
  33.4 3.1 %collective-permute-start.5 = (bf16[200,512]{1,0:T(8,128)(2,1)S(1)}, bf16[200,512]{1,0:T(8,128)(2,1)S(1)}, u32[]{:S(2)}, u32[]{:S(2)}) collective-permute-start(bf16[200,512]{1,0:T(8,128)(2,1)S(1)} %constant_dynamic-update-slice_fusion.echo), channel_id=1, source_target_pairs={{4,0},{5,1},{6,2},{7,3},{8,4},{9,5},{10,6},{11,7},{12,8},{13,9},{1... | collective-permute-start | bytes 614408 | tf_op jit(solution)/shard_map/ppermute | solution.py:38
  36.5 2.2 %collective-permute-start.7 = (bf16[200,512]{1,0:T(8,128)(2,1)S(1)}, bf16[200,512]{1,0:T(8,128)(2,1)S(1)}, u32[]{:S(2)}, u32[]{:S(2)}) collective-permute-start(bf16[200,512]{1,0:T(8,128)(2,1)S(1)} %constant_dynamic-update-slice_fusion.echo), channel_id=1, source_target_pairs={{8,0},{9,1},{10,2},{11,3},{12,4},{13,5},{14,6},{15,7},{0,8},{1,9},... | collective-permute-start | bytes 614408 | tf_op jit(solution)/shard_map/ppermute | solution.py:38
  38.7 8.4 %shard_map.115 = (bf16[208,256]{1,0:T(8,128)(2,1)S(1)}, bf16[200,512]{1,0:T(8,128)(2,1)S(1)}, bf16[208,512]{1,0:T(8,128)(2,1)S(1)}, f32[40960,128]{1,0:T(8,128)S...) custom-call(s32[12800]{0:T(1024)S(1)} %add_multiply_fusion.own_ids.h, ...), custom_call_target="tpu_custom_call", output_to_operand_aliasing={{3}: (6, {}), {4}: (7, {}), {5}: (8, {})} | custom-call | tf_op jit(solution)/shard_map/pallas_call | solution.py:207
  47.7 1.1 %collective-permute-start.9 = (bf16[208,512]{1,0:T(8,128)(2,1)S(1)}, bf16[208,512]{1,0:T(8,128)(2,1)S(1)}, u32[]{:S(2)}, u32[]{:S(2)}) collective-permute-start(bf16[208,512]{1,0:T(8,128)(2,1)S(1)} %get-tuple-element.43.refs_0_), channel_id=1, source_target_pairs={{96,0},{97,1},{98,2},{99,3},{100,4},{101,5},{102,6},{103,7},{104,8... | collective-permute-start | bytes 638984 | tf_op jit(solution)/shard_map/ppermute | solution.py:38
  48.7 2.4 %collective-permute-start.10 = (bf16[208,256]{1,0:T(8,128)(2,1)S(1)}, bf16[208,256]{1,0:T(8,128)(2,1)S(1)}, u32[]{:S(2)}, u32[]{:S(2)}) collective-permute-start(bf16[208,256]{1,0:T(8,128)(2,1)S(1)} %get-tuple-element.45), channel_id=1, source_target_pairs={{64,0},{65,1},{66,2},{67,3},{68,4},{69,5},{70,6},{71,7},{72,8},{73... | collective-permute-start | bytes 319496 | tf_op jit(solution)/shard_map/ppermute | solution.py:38
  51.1 2.5 %collective-permute-start.8 = (bf16[208,256]{1,0:T(8,128)(2,1)S(1)}, bf16[208,256]{1,0:T(8,128)(2,1)S(1)}, u32[]{:S(2)}, u32[]{:S(2)}) collective-permute-start(bf16[208,256]{1,0:T(8,128)(2,1)S(1)} %get-tuple-element.45), channel_id=1, source_target_pairs={{32,0},{33,1},{34,2},{35,3},{36,4},{37,5},{38,6},{39,7},{40,8},{41... | collective-permute-start | bytes 319496 | tf_op jit(solution)/shard_map/ppermute | solution.py:38
  53.6 5.5 %collective-permute-done.10.refs_5_ = bf16[208,256]{1,0:T(8,128)(2,1)S(1)} collective-permute-done((bf16[208,256]{1,0:T(8,128)(2,1)S(1)}, bf16[208,256]{1,0:T(8,128)(2,1)S(1)}, u32[]{:S(2)}, u32[]{:S(2)}) %collective-permute-start.10) | collective-permute-done | bytes 106528 | tf_op jit(solution)/shard_map/ppermute | solution.py:38
  59.1 6.9 %shard_map.116 = (f32[4,200,512]{2,1,0:T(8,128)S(1)}, bf16[200,2048]{1,0:T(8,128)(2,1)S(1)}) custom-call(s32[1]{0:T(128)} %bitcast.me, bf16[200,2048]{1,0:T(8,128)(2,1)S(1)} %collective-permute-done.11.slab, bf16[208,512]{1,0:T(8,128)(2,1)S(1)} %get-tuple-element.43.refs_0_, bf16[208,256]{1,0:T(8,128)(2,1)S(1)} %collective-permute-done.3.refs_1_, ...), custom_call_target="tpu_custom_call" | custom-call | tf_op jit(solution)/shard_map/pallas_call | solution.py:348
  66.3 6.3 %shard_map.117 = (f32[4,200,512]{2,1,0:T(8,128)S(1)}, f32[200,512]{1,0:T(8,128)S(1)}, f32[200,512]{1,0:T(8,128)S(1)}, f32[200,512]{1,0:T(8,128)S(1)}) custom-call(s32[1]{0:T(128)} %bitcast.me, bf16[200,2048]{1,0:T(8,128)(2,1)S(1)} %constant_dynamic-update-slice_fusion.4.slab, ...), custom_call_target="tpu_custom_call", output_to_operand_aliasing={{0}: (8, {})} | custom-call | tf_op jit(solution)/shard_map/pallas_call | solution.py:348
  73.1 2.0 %collective-permute-start.13 = (bf16[200,512]{1,0:T(8,128)(2,1)S(1)}, bf16[200,512]{1,0:T(8,128)(2,1)S(1)}, u32[]{:S(2)}, u32[]{:S(2)}) collective-permute-start(bf16[200,512]{1,0:T(8,128)(2,1)S(1)} %get-tuple-element.60), channel_id=1, source_target_pairs={{12,0},{13,1},{14,2},{15,3},{0,4},{1,5},{2,6},{3,7},{4,8},{5,9},{6... | collective-permute-start | bytes 614408 | tf_op jit(solution)/shard_map/ppermute | solution.py:38
  75.1 1.3 %collective-permute-start.14 = (bf16[200,512]{1,0:T(8,128)(2,1)S(1)}, bf16[200,512]{1,0:T(8,128)(2,1)S(1)}, u32[]{:S(2)}, u32[]{:S(2)}) collective-permute-start(bf16[200,512]{1,0:T(8,128)(2,1)S(1)} %get-tuple-element.62), channel_id=1, source_target_pairs={{4,0},{5,1},{6,2},{7,3},{8,4},{9,5},{10,6},{11,7},{12,8},{13,9},{1... | collective-permute-start | bytes 614408 | tf_op jit(solution)/shard_map/ppermute | solution.py:38
  77.2 2.0 %shard_map.118 = (f32[200,512]{1,0:T(8,128)S(1)}, bf16[200,512]{1,0:T(8,128)(2,1)S(1)}, bf16[200,512]{1,0:T(8,128)(2,1)S(1)}, bf16[200,512]{1,0:T(8,128)(2,1)S(1)}, f32[200,512]{1,0:T(8,128)S(1)}) custom-call(s32[1]{0:T(128)} %bitcast.me, bf16[200,2048]{1,0:T(8,128)(2,1)S(1)} %constant_dynamic-update-slice_fusion.4.slab, ...), custom_call_target="tpu_custom_call" | custom-call | tf_op jit(solution)/shard_map/pallas_call | solution.py:348
  79.3 3.2 %collective-permute-start.20 = (bf16[200,512]{1,0:T(8,128)(2,1)S(1)}, bf16[200,512]{1,0:T(8,128)(2,1)S(1)}, u32[]{:S(2)}, u32[]{:S(2)}) collective-permute-start(bf16[200,512]{1,0:T(8,128)(2,1)S(1)} %get-tuple-element.56), channel_id=1, source_target_pairs={{32,0},{33,1},{34,2},{35,3},{36,4},{37,5},{38,6},{39,7},{40,8},{41... | collective-permute-start | bytes 614408 | tf_op jit(solution)/shard_map/ppermute | solution.py:38
  82.6 3.7 %collective-permute-done.13 = bf16[200,512]{1,0:T(8,128)(2,1)S(1)} collective-permute-done((bf16[200,512]{1,0:T(8,128)(2,1)S(1)}, bf16[200,512]{1,0:T(8,128)(2,1)S(1)}, u32[]{:S(2)}, u32[]{:S(2)}) %collective-permute-start.13) | collective-permute-done | bytes 204832 | tf_op jit(solution)/shard_map/ppermute | solution.py:38
  86.3 1.7 %collective-permute-start.21 = (bf16[200,512]{1,0:T(8,128)(2,1)S(1)}, bf16[200,512]{1,0:T(8,128)(2,1)S(1)}, u32[]{:S(2)}, u32[]{:S(2)}) collective-permute-start(bf16[200,512]{1,0:T(8,128)(2,1)S(1)} %get-tuple-element.57), channel_id=1, source_target_pairs={{64,0},{65,1},{66,2},{67,3},{68,4},{69,5},{70,6},{71,7},{72,8},{73... | collective-permute-start | bytes 614408 | tf_op jit(solution)/shard_map/ppermute | solution.py:38
  88.2 1.9 %collective-permute-start.16 = (bf16[200,128]{1,0:T(8,128)(2,1)S(1)}, bf16[200,128]{1,0:T(8,128)(2,1)S(1)}, u32[]{:S(2)}, u32[]{:S(2)}) collective-permute-start(bf16[200,128]{1,0:T(8,128)(2,1)S(1)} %get-tuple-element.63), channel_id=1, source_target_pairs={{18,0},{19,1},{16,2},{17,3},{22,4},{23,5},{20,6},{21,7},{26,8},{27... | collective-permute-start | bytes 153608 | tf_op jit(solution)/shard_map/ppermute | solution.py:38
  90.1 1.4 %collective-permute-start.17 = (bf16[200,128]{1,0:T(8,128)(2,1)S(1)}, bf16[200,128]{1,0:T(8,128)(2,1)S(1)}, u32[]{:S(2)}, u32[]{:S(2)}) collective-permute-start(bf16[200,128]{1,0:T(8,128)(2,1)S(1)} %get-tuple-element.65), channel_id=1, source_target_pairs={{16,0},{17,1},{18,2},{19,3},{20,4},{21,5},{22,6},{23,7},{24,8},{25... | collective-permute-start | bytes 153608 | tf_op jit(solution)/shard_map/ppermute | solution.py:38
  92.2 2.2 %collective-permute-done.21 = bf16[200,512]{1,0:T(8,128)(2,1)S(1)} collective-permute-done((bf16[200,512]{1,0:T(8,128)(2,1)S(1)}, bf16[200,512]{1,0:T(8,128)(2,1)S(1)}, u32[]{:S(2)}, u32[]{:S(2)}) %collective-permute-start.21) | collective-permute-done | bytes 204832 | tf_op jit(solution)/shard_map/ppermute | solution.py:38
  95.3 1.8 %collective-permute-done.18 = bf16[200,128]{1,0:T(8,128)(2,1)S(1)} collective-permute-done((bf16[200,128]{1,0:T(8,128)(2,1)S(1)}, bf16[200,128]{1,0:T(8,128)(2,1)S(1)}, u32[]{:S(2)}, u32[]{:S(2)}) %collective-permute-start.18) | collective-permute-done | bytes 51232 | tf_op jit(solution)/shard_map/ppermute | solution.py:38
  (52 shorter events, 6.9 us)
Async XLA Ops:
  2.8 17.9 %copy-start.2 = (s32[512,4]{0,1:T(4,128)S(1)}, s32[512,4]{0,1:T(4,128)}, u32[]{:S(2)}) copy-start(s32[512,4]{0,1:T(4,128)} %param.15) | copy-start | bytes 24580
  2.8 17.9 %copy-start.3 = (s32[512]{0:T(512)S(1)}, s32[512]{0:T(512)}, u32[]{:S(2)}) copy-start(s32[512]{0:T(512)} %param.14) | copy-start | bytes 6148
  15.5 17.8 %collective-permute-start = (bf16[200,128]{1,0:T(8,128)(2,1)S(1)}, bf16[200,128]{1,0:T(8,128)(2,1)S(1)}, u32[]{:S(2)}, u32[]{:S(2)}) collective-permute-start(bf16[200,128]{1,0:T(8,128)(2,1)S(1)} %get-tuple-element.30.echo), channel_id=1, source_target_pairs={{16,0},{17,1},{18,2},{19,3},{20,4},{21,5},{22,6},{23,7},{24,8},{25... | collective-permute-start | bytes 153608 | tf_op jit(solution)/shard_map/ppermute | solution.py:38
  18.4 14.9 %collective-permute-start.1 = (bf16[200,128]{1,0:T(8,128)(2,1)S(1)}, bf16[200,128]{1,0:T(8,128)(2,1)S(1)}, u32[]{:S(2)}, u32[]{:S(2)}) collective-permute-start(bf16[200,128]{1,0:T(8,128)(2,1)S(1)} %get-tuple-element.30.echo), channel_id=1, source_target_pairs={{18,0},{19,1},{16,2},{17,3},{22,4},{23,5},{20,6},{21,7},{26,8},{27... | collective-permute-start | bytes 153608 | tf_op jit(solution)/shard_map/ppermute | solution.py:38
  18.4 14.9 %collective-permute-start.2 = (bf16[200,128]{1,0:T(8,128)(2,1)S(1)}, bf16[200,128]{1,0:T(8,128)(2,1)S(1)}, u32[]{:S(2)}, u32[]{:S(2)}) collective-permute-start(bf16[200,128]{1,0:T(8,128)(2,1)S(1)} %get-tuple-element.30.echo), channel_id=1, source_target_pairs={{2,0},{3,1},{0,2},{1,3},{6,4},{7,5},{4,6},{5,7},{10,8},{11,9},{8,1... | collective-permute-start | bytes 153608 | tf_op jit(solution)/shard_map/ppermute | solution.py:38
  29.2 18.0 %collective-permute-start.3 = (bf16[208,256]{1,0:T(8,128)(2,1)S(1)}, bf16[208,256]{1,0:T(8,128)(2,1)S(1)}, u32[]{:S(2)}, u32[]{:S(2)}) collective-permute-start(bf16[208,256]{1,0:T(8,128)(2,1)S(1)} %get-tuple-element.38.refs_0_), channel_id=1, source_target_pairs={{32,0},{33,1},{34,2},{35,3},{36,4},{37,5},{38,6},{39,7},{40,8},{41... | collective-permute-start | bytes 319496 | tf_op jit(solution)/shard_map/ppermute | solution.py:38
  33.3 13.9 %collective-permute-start.4 = (bf16[208,256]{1,0:T(8,128)(2,1)S(1)}, bf16[208,256]{1,0:T(8,128)(2,1)S(1)}, u32[]{:S(2)}, u32[]{:S(2)}) collective-permute-start(bf16[208,256]{1,0:T(8,128)(2,1)S(1)} %get-tuple-element.38.refs_0_), channel_id=1, source_target_pairs={{64,0},{65,1},{66,2},{67,3},{68,4},{69,5},{70,6},{71,7},{72,8},{73... | collective-permute-start | bytes 319496 | tf_op jit(solution)/shard_map/ppermute | solution.py:38
  33.4 13.8 %collective-permute-start.5 = (bf16[200,512]{1,0:T(8,128)(2,1)S(1)}, bf16[200,512]{1,0:T(8,128)(2,1)S(1)}, u32[]{:S(2)}, u32[]{:S(2)}) collective-permute-start(bf16[200,512]{1,0:T(8,128)(2,1)S(1)} %constant_dynamic-update-slice_fusion.echo), channel_id=1, source_target_pairs={{4,0},{5,1},{6,2},{7,3},{8,4},{9,5},{10,6},{11,7},{12,8},{13,9},{1... | collective-permute-start | bytes 614408 | tf_op jit(solution)/shard_map/ppermute | solution.py:38
  36.5 11.0 %collective-permute-start.6 = (bf16[200,512]{1,0:T(8,128)(2,1)S(1)}, bf16[200,512]{1,0:T(8,128)(2,1)S(1)}, u32[]{:S(2)}, u32[]{:S(2)}) collective-permute-start(bf16[200,512]{1,0:T(8,128)(2,1)S(1)} %constant_dynamic-update-slice_fusion.echo), channel_id=1, source_target_pairs={{12,0},{13,1},{14,2},{15,3},{0,4},{1,5},{2,6},{3,7},{4,8},{5,9},{6... | collective-permute-start | bytes 614408 | tf_op jit(solution)/shard_map/ppermute | solution.py:38
  36.5 11.0 %collective-permute-start.7 = (bf16[200,512]{1,0:T(8,128)(2,1)S(1)}, bf16[200,512]{1,0:T(8,128)(2,1)S(1)}, u32[]{:S(2)}, u32[]{:S(2)}) collective-permute-start(bf16[200,512]{1,0:T(8,128)(2,1)S(1)} %constant_dynamic-update-slice_fusion.echo), channel_id=1, source_target_pairs={{8,0},{9,1},{10,2},{11,3},{12,4},{13,5},{14,6},{15,7},{0,8},{1,9},... | collective-permute-start | bytes 614408 | tf_op jit(solution)/shard_map/ppermute | solution.py:38
  47.6 11.6 %collective-permute-start.11 = (bf16[200,2048]{1,0:T(8,128)(2,1)S(1)}, bf16[200,2048]{1,0:T(8,128)(2,1)S(1)}, u32[]{:S(2)}, u32[]{:S(2)}) collective-permute-start(bf16[200,2048]{1,0:T(8,128)(2,1)S(1)} %constant_dynamic-update-slice_fusion.4.slab), channel_id=1, source_target_pairs={{1,0},{0,1},{3,2},{2,3},{5,4},{4,5},{7,6},{6,7},{9,8},{8,9},{11,10... | collective-permute-start | bytes 2457608 | tf_op jit(solution)/shard_map/ppermute | solution.py:38
  47.7 11.5 %collective-permute-start.9 = (bf16[208,512]{1,0:T(8,128)(2,1)S(1)}, bf16[208,512]{1,0:T(8,128)(2,1)S(1)}, u32[]{:S(2)}, u32[]{:S(2)}) collective-permute-start(bf16[208,512]{1,0:T(8,128)(2,1)S(1)} %get-tuple-element.43.refs_0_), channel_id=1, source_target_pairs={{96,0},{97,1},{98,2},{99,3},{100,4},{101,5},{102,6},{103,7},{104,8... | collective-permute-start | bytes 638984 | tf_op jit(solution)/shard_map/ppermute | solution.py:38
  48.7 10.4 %collective-permute-start.10 = (bf16[208,256]{1,0:T(8,128)(2,1)S(1)}, bf16[208,256]{1,0:T(8,128)(2,1)S(1)}, u32[]{:S(2)}, u32[]{:S(2)}) collective-permute-start(bf16[208,256]{1,0:T(8,128)(2,1)S(1)} %get-tuple-element.45), channel_id=1, source_target_pairs={{64,0},{65,1},{66,2},{67,3},{68,4},{69,5},{70,6},{71,7},{72,8},{73... | collective-permute-start | bytes 319496 | tf_op jit(solution)/shard_map/ppermute | solution.py:38
  51.1 8.0 %collective-permute-start.8 = (bf16[208,256]{1,0:T(8,128)(2,1)S(1)}, bf16[208,256]{1,0:T(8,128)(2,1)S(1)}, u32[]{:S(2)}, u32[]{:S(2)}) collective-permute-start(bf16[208,256]{1,0:T(8,128)(2,1)S(1)} %get-tuple-element.45), channel_id=1, source_target_pairs={{32,0},{33,1},{34,2},{35,3},{36,4},{37,5},{38,6},{39,7},{40,8},{41... | collective-permute-start | bytes 319496 | tf_op jit(solution)/shard_map/ppermute | solution.py:38
  66.0 6.6 %collective-permute-start.12 = (bf16[200,2048]{1,0:T(8,128)(2,1)S(1)}, bf16[200,2048]{1,0:T(8,128)(2,1)S(1)}, u32[]{:S(2)}, u32[]{:S(2)}) collective-permute-start(bf16[200,2048]{1,0:T(8,128)(2,1)S(1)} %get-tuple-element.50), channel_id=1, source_target_pairs={{1,0},{0,1},{3,2},{2,3},{5,4},{4,5},{7,6},{6,7},{9,8},{8,9},{11,10... | collective-permute-start | bytes 2457608 | tf_op jit(solution)/shard_map/ppermute | solution.py:38
  73.1 13.1 %collective-permute-start.13 = (bf16[200,512]{1,0:T(8,128)(2,1)S(1)}, bf16[200,512]{1,0:T(8,128)(2,1)S(1)}, u32[]{:S(2)}, u32[]{:S(2)}) collective-permute-start(bf16[200,512]{1,0:T(8,128)(2,1)S(1)} %get-tuple-element.60), channel_id=1, source_target_pairs={{12,0},{13,1},{14,2},{15,3},{0,4},{1,5},{2,6},{3,7},{4,8},{5,9},{6... | collective-permute-start | bytes 614408 | tf_op jit(solution)/shard_map/ppermute | solution.py:38
  75.1 12.9 %collective-permute-start.14 = (bf16[200,512]{1,0:T(8,128)(2,1)S(1)}, bf16[200,512]{1,0:T(8,128)(2,1)S(1)}, u32[]{:S(2)}, u32[]{:S(2)}) collective-permute-start(bf16[200,512]{1,0:T(8,128)(2,1)S(1)} %get-tuple-element.62), channel_id=1, source_target_pairs={{4,0},{5,1},{6,2},{7,3},{8,4},{9,5},{10,6},{11,7},{12,8},{13,9},{1... | collective-permute-start | bytes 614408 | tf_op jit(solution)/shard_map/ppermute | solution.py:38
  76.4 11.6 %collective-permute-start.15 = (bf16[200,512]{1,0:T(8,128)(2,1)S(1)}, bf16[200,512]{1,0:T(8,128)(2,1)S(1)}, u32[]{:S(2)}, u32[]{:S(2)}) collective-permute-start(bf16[200,512]{1,0:T(8,128)(2,1)S(1)} %get-tuple-element.61), channel_id=1, source_target_pairs={{8,0},{9,1},{10,2},{11,3},{12,4},{13,5},{14,6},{15,7},{0,8},{1,9},... | collective-permute-start | bytes 614408 | tf_op jit(solution)/shard_map/ppermute | solution.py:38
  79.2 12.3 %collective-permute-start.19 = (bf16[200,512]{1,0:T(8,128)(2,1)S(1)}, bf16[200,512]{1,0:T(8,128)(2,1)S(1)}, u32[]{:S(2)}, u32[]{:S(2)}) collective-permute-start(bf16[200,512]{1,0:T(8,128)(2,1)S(1)} %get-tuple-element.55), channel_id=1, source_target_pairs={{96,0},{97,1},{98,2},{99,3},{100,4},{101,5},{102,6},{103,7},{104,8... | collective-permute-start | bytes 614408 | tf_op jit(solution)/shard_map/ppermute | solution.py:38
  79.3 12.9 %collective-permute-start.20 = (bf16[200,512]{1,0:T(8,128)(2,1)S(1)}, bf16[200,512]{1,0:T(8,128)(2,1)S(1)}, u32[]{:S(2)}, u32[]{:S(2)}) collective-permute-start(bf16[200,512]{1,0:T(8,128)(2,1)S(1)} %get-tuple-element.56), channel_id=1, source_target_pairs={{32,0},{33,1},{34,2},{35,3},{36,4},{37,5},{38,6},{39,7},{40,8},{41... | collective-permute-start | bytes 614408 | tf_op jit(solution)/shard_map/ppermute | solution.py:38
  86.3 8.2 %collective-permute-start.21 = (bf16[200,512]{1,0:T(8,128)(2,1)S(1)}, bf16[200,512]{1,0:T(8,128)(2,1)S(1)}, u32[]{:S(2)}, u32[]{:S(2)}) collective-permute-start(bf16[200,512]{1,0:T(8,128)(2,1)S(1)} %get-tuple-element.57), channel_id=1, source_target_pairs={{64,0},{65,1},{66,2},{67,3},{68,4},{69,5},{70,6},{71,7},{72,8},{73... | collective-permute-start | bytes 614408 | tf_op jit(solution)/shard_map/ppermute | solution.py:38
  88.2 7.1 %collective-permute-start.16 = (bf16[200,128]{1,0:T(8,128)(2,1)S(1)}, bf16[200,128]{1,0:T(8,128)(2,1)S(1)}, u32[]{:S(2)}, u32[]{:S(2)}) collective-permute-start(bf16[200,128]{1,0:T(8,128)(2,1)S(1)} %get-tuple-element.63), channel_id=1, source_target_pairs={{18,0},{19,1},{16,2},{17,3},{22,4},{23,5},{20,6},{21,7},{26,8},{27... | collective-permute-start | bytes 153608 | tf_op jit(solution)/shard_map/ppermute | solution.py:38
  90.1 5.2 %collective-permute-start.17 = (bf16[200,128]{1,0:T(8,128)(2,1)S(1)}, bf16[200,128]{1,0:T(8,128)(2,1)S(1)}, u32[]{:S(2)}, u32[]{:S(2)}) collective-permute-start(bf16[200,128]{1,0:T(8,128)(2,1)S(1)} %get-tuple-element.65), channel_id=1, source_target_pairs={{16,0},{17,1},{18,2},{19,3},{20,4},{21,5},{22,6},{23,7},{24,8},{25... | collective-permute-start | bytes 153608 | tf_op jit(solution)/shard_map/ppermute | solution.py:38
  91.5 5.6 %collective-permute-start.18 = (bf16[200,128]{1,0:T(8,128)(2,1)S(1)}, bf16[200,128]{1,0:T(8,128)(2,1)S(1)}, u32[]{:S(2)}, u32[]{:S(2)}) collective-permute-start(bf16[200,128]{1,0:T(8,128)(2,1)S(1)} %get-tuple-element.64), channel_id=1, source_target_pairs={{2,0},{3,1},{0,2},{1,3},{6,4},{7,5},{4,6},{5,7},{10,8},{11,9},{8,1... | collective-permute-start | bytes 153608 | tf_op jit(solution)/shard_map/ppermute | solution.py:38
  (3 other events, 36.5 us)

commit v6 on v5

--- a/solution.py
+++ b/solution.py
@@ -79,22 +79,29 @@
     return total
 
 
-def prepare(tab_t, w_t, rel_t, table, weights, rel_table, relations):
+def prepare(tab_t, w_t, rel_t, table, weights, rel_table, relations, steps):
     step = pl.program_id(0)
     depth = tab_t.shape[0]
 
+    tokens = weights.shape[1] // WIDE
+    share = pl.cdiv(tokens, steps)
+    for turn in range(steps):
+
+        @pl.when(step == turn)
+        def _(turn=turn):
+            lane = lax.broadcasted_iota(jnp.int32, (depth, WIDE), 1)
+            for t in range(turn * share, min((turn + 1) * share, tokens)):
+                start = t * depth
+                base = start // LANES * LANES
+                piece = w_t[:, base : base + 3 * LANES].astype(F32)
+                if start > base:
+                    piece = pltpu.roll(piece, 3 * LANES - (start - base), 1)
+                weights[:, t * WIDE : (t + 1) * WIDE] = jnp.where(
+                    lane < depth, piece[:, :WIDE], 0.0
+                ).astype(BF16)
+
     @pl.when(step == 0)
     def _():
-        lane = lax.broadcasted_iota(jnp.int32, (depth, WIDE), 1)
-        for t in range(weights.shape[1] // WIDE):
-            start = t * depth
-            base = start // LANES * LANES
-            piece = w_t[:, base : base + 3 * LANES].astype(F32)
-            if start > base:
-                piece = pltpu.roll(piece, 3 * LANES - (start - base), 1)
-            weights[:, t * WIDE : (t + 1) * WIDE] = jnp.where(
-                lane < depth, piece[:, :WIDE], 0.0
-            ).astype(BF16)
         known = lax.broadcasted_iota(jnp.int32, rel_t.shape, 1) < relations
         rel = jnp.where(known, rel_t[...].astype(F32), 0.0)
         rel_table[...] = jnp.concatenate(
@@ -111,10 +118,10 @@
 
 
 def entity_kernel(
-    relations, scale, own_ids, tab_t, w_t, rel_t, own_rel,
+    relations, steps, scale, own_ids, tab_t, w_t, rel_t, own_rel,
     own_out, table, weights, rel_table, rows,
 ):
-    prepare(tab_t, w_t, rel_t, table, weights, rel_table, relations)
+    prepare(tab_t, w_t, rel_t, table, weights, rel_table, relations, steps)
 
     @pl.when(pl.program_id(0) == pl.num_programs(0) - 1)
     def _():
@@ -169,7 +176,7 @@
     whole = pl.BlockSpec(memory_space=pltpu.VMEM)
     once = pl.Buffered(1)
     return pl.pallas_call(
-        functools.partial(entity_kernel, relations, scale),
+        functools.partial(entity_kernel, relations, steps, scale),
         grid=(steps,),
         in_specs=[
             pl.BlockSpec(memory_space=pltpu.SMEM),
@@ -225,23 +232,31 @@
     )
 
 
-def score_kernel(plain, struck_value, depth, parts, stage, me, slab, *refs):
-    blocks, refs = (refs[:1], refs[1:3], refs[3:4], refs[4:6]), refs[6:]
-    if stage:
+def score_kernel(plain, struck_value, depth, parts, pieces, stage, me, slab, *refs):
+    blocks = []
+    for count in pieces:
+        blocks.append(refs[:count])
+        refs = refs[count:]
+    before = None
+    if stage > 1:
         before, refs = refs[0], refs[1:]
-    if stage == 2:
+    if stage == 3:
         kept, sent, refs = refs[0], refs[1:4], refs[4:]
+        kept[...] = before[0]
     else:
         asks, refs = refs[0], refs[1:]
-    ent_outs, refs = refs[: len(parts)] if stage else refs[:1], refs[len(parts) if stage else 1 :]
-    tall, queries, marks, totals, *held = refs[:6]
+    ents, tall, queries, marks, totals, *held = refs[:7]
+    if stage == 3:
+        asks = refs[7]
     if stage == 2:
-        asks = refs[6]
+        asks[0] = before[0]
+    number = len(blocks)
+    base = 1 if stage > 1 else 0
     width = SPAN
     tiles = SPAN // LANES
 
     x, y, z, core = coords_of(me[0])
-    if not stage:
+    if stage == 1:
         core = 1 - core
     spots = [
         flat_of((x + dx) % 4, (y + ((0,) + FAR)[part]) % 4, z, core)
@@ -258,7 +273,7 @@
         )
         tall[k * SPAN : (k + 1) * SPAN, :] = wide.T.astype(BF16)
     within = lax.broadcasted_iota(jnp.int32, (LANES, width), 0)
-    for b in range(4):
+    for b in range(number):
         query = jnp.concatenate([piece[...] for piece in blocks[b]], axis=1).astype(F32)
         queries[b] = jnp.concatenate(
             [query[:depth, :], jnp.zeros((WIDE - depth, width), F32)], axis=0
@@ -275,7 +290,7 @@
         marks[b] = marked
 
     def residual_of(step):
-        k, b = step // 4, step % 4
+        k, b = step // number, step % number
         score = jnp.dot(
             tall[k * SPAN : (k + 1) * SPAN, :], queries[b], preferred_element_type=F32
         )
@@ -287,36 +302,29 @@
             held[step % 2][at, :] = (jnp.tanh(score[at, :]) + label).astype(BF16)
 
     def use(step):
-        k, b = step // 4, step % 4
+        k, b = step // number, step % number
         first = parts[k] * SPAN
         residual = held[step % 2][...]
         ent = lax.dot_general(
             residual, queries[b], (((1,), (1,)), ((), ())), preferred_element_type=F32
         )
         ask = jnp.dot(slab[:, first : first + SPAN], residual, preferred_element_type=F32)
-        if b == 0:
+        if b:
+            ent = totals[...] + ent
+        if b < number - 1:
             totals[...] = ent
-        elif b < 3:
-            totals[...] += ent
         else:
-            ent = (totals[...] + ent).T[:depth, :]
-            if stage:
-                ent_outs[k][...] = ent
-            else:
-                ent_outs[0][:, k * SPAN : (k + 1) * SPAN] = ent.astype(BF16)
+            ents[:, k * SPAN : (k + 1) * SPAN] = ent.T[:depth, :].astype(ents.dtype)
         if k:
-            ask = asks[b] + ask
-        elif stage:
-            ask = before[b] + ask
-        if stage == 2 and k == len(parts) - 1:
-            if b:
-                sent[b - 1][...] = ask.astype(BF16)
-            else:
-                kept[...] = ask
+            ask = asks[base + b] + ask
+        elif stage > 1:
+            ask = before[base + b] + ask
+        if stage == 3 and k == len(parts) - 1:
+            sent[b][...] = ask.astype(BF16)
         else:
-            asks[b] = ask
-
-    steps = 4 * len(parts)
+            asks[base + b] = ask
+
+    steps = number * len(parts)
     residual_of(0)
     for step in range(steps):
         if step + 1 < steps:
@@ -325,35 +333,38 @@
 
 
 def score(me, slab, blocks, parts, stage, total_entities, before=None):
-    depth, entities = slab.shape
+    depth = slab.shape[0]
     plain = 1.0 - 2.0 * (0.1 / total_entities)
     shape = jax.ShapeDtypeStruct
-    total = pltpu.VMEM((4, depth, SPAN), F32)
+    number = len(blocks)
+    total = pltpu.VMEM((1 if stage == 0 else 4, depth, SPAN), F32)
     outs = [total]
-    if stage == 2:
+    if stage == 3:
         outs = [shape((depth, SPAN), F32)] + [shape((depth, SPAN), BF16)] * 3
-    outs += [shape((depth, SPAN), F32)] * len(parts) if stage else [shape((depth, entities), BF16)]
+    outs.append(shape((depth, len(parts) * SPAN), BF16 if stage == 1 else F32))
     scratch = [
         pltpu.VMEM((len(parts) * SPAN, WIDE), BF16),
-        pltpu.VMEM((4, WIDE, SPAN), BF16),
-        pltpu.VMEM((4, LANES, SPAN), jnp.int32),
+        pltpu.VMEM((number, WIDE, SPAN), BF16),
+        pltpu.VMEM((number, LANES, SPAN), jnp.int32),
         pltpu.VMEM((SPAN, WIDE), F32),
         pltpu.VMEM((SPAN, SPAN), BF16),
         pltpu.VMEM((SPAN, SPAN), BF16),
     ]
-    if stage == 2:
+    if stage == 3:
         scratch.append(total)
     whole = pl.BlockSpec(memory_space=pltpu.VMEM)
-    extra = [before] if stage else []
+    given = [piece for block in blocks for piece in block] + ([before] if stage > 1 else [])
     return pl.pallas_call(
-        functools.partial(score_kernel, plain, plain - 1.8, depth, parts, stage),
-        in_specs=[pl.BlockSpec(memory_space=pltpu.SMEM)] + [whole] * (1 + len(blocks) + len(extra)),
+        functools.partial(
+            score_kernel, plain, plain - 1.8, depth, parts, [len(b) for b in blocks], stage
+        ),
+        in_specs=[pl.BlockSpec(memory_space=pltpu.SMEM)] + [whole] * (1 + len(given)),
         out_specs=[whole] * len(outs),
         out_shape=outs,
-        input_output_aliases={2 + len(blocks): 0} if stage == 1 else {},
+        input_output_aliases={1 + len(given): 0} if stage == 2 else {},
         scratch_shapes=scratch,
         compiler_params=pltpu.CompilerParams(vmem_limit_bytes=VMEM_BYTES),
-    )(me, slab, *blocks, *extra)
+    )(me, slab, *given)
 
 
 def body(
@@ -394,17 +405,26 @@
     slab = jnp.concatenate([row] + sent, axis=1)
     other = moved(slab, dcore=1)
     second = [moved(late, dz=d) for d in (1, 2)]
-    blocks = [query, first[0], second[0], moved(query, dz=3), first[1], second[1]]
-    asks, away = score(me, other, blocks, (0, 1, 2, 3), 0, entities)
-    back = moved(away, dcore=1).astype(F32)
-    asks, *ents = score(me, slab, blocks, (1, 2, 3), 1, entities, asks)
+    own_asks, own_ents = score(me, slab, [[query]], (0, 1, 2, 3), 0, entities)
+    own_asks, own_ents, last, *second = lax.optimization_barrier(
+        (own_asks, own_ents, moved(query, dz=3), *second)
+    )
+    blocks = [[query], [first[0], second[0]], [last], [first[1], second[1]]]
+    asks, away = score(me, other, blocks, (0, 1, 2, 3), 1, entities)
+    back = moved(away, dcore=1)
+    asks, ents = score(me, slab, blocks[1:], (1, 2, 3), 2, entities, asks)
     span = slab.shape[1] // 4
-    ents = [
-        moved((ent + back[:, (k + 1) * span : (k + 2) * span]).astype(BF16), dy=-d)
-        for k, (d, ent) in enumerate(zip(FAR, ents))
-    ]
-    query_total, *sums, ent_row = score(me, slab, blocks, (0,), 2, entities, asks)
-    ent_row = ent_row + back[:, :span]
+
+    def slab_sum(part, k):
+        at = slice(k * span, (k + 1) * span)
+        return part + own_ents[:, at] + back[:, at].astype(F32)
+
+    ents = [ents[:, k * span : (k + 1) * span] for k in range(3)]
+    ents = [slab_sum(part, k + 1).astype(BF16) for k, part in enumerate(ents)]
+    ents = [moved(part, dy=-d) for d, part in zip(FAR, ents)]
+    query_total, *sums, ent_row = score(me, slab, blocks[1:], (0,), 3, entities, asks)
+    query_total = query_total + own_asks[0]
+    ent_row = slab_sum(ent_row, 0)
     for ent in ents:
         ent_row = ent_row + ent.astype(F32)
     for d, part in zip(FAR, sums):

time: 98.1 us -> 96.4 us (0.983)
  waiting for transfers between devices: 13.6 us -> 12.1 us
    ppermute x22, waiting for transfers between devices: 13.6 us -> 12.1 us  [moved(): return lax.ppermute(block, AXES, route)]
    pallas_call x3 -> x4, Pallas kernels: 15.2 us -> 15.3 us  [score(): pl.pallas_call(functools.partial(score_kernel, plain, plain - 1.8, depth,...]
where the time goes in v6:
time: 96.4 us; the launch traced here: 96 us
  Pallas kernels  44.5 us (46%)
  starting transfers between devices  34.1 us (35%)
  waiting for transfers between devices  12.1 us (13%)
  other arithmetic  2.85 us (3%)
  local copies, waits for them, and re-layouts  1.65 us (2%)
    ppermute x22, starting transfers between devices, moved(): return lax.ppermute(block, AXES, route)  34.1 us
    pallas_call x2, Pallas kernels, encode_heads(): pl.pallas_call(functools.partial(head_kernel, chunk * heads, heads), in_s...  16.8 us
    pallas_call x4, Pallas kernels, score(): pl.pallas_call(functools.partial(score_kernel, plain, plain - 1.8, depth,...  15.3 us
    pallas_call x1, Pallas kernels, encode_entities(): pl.pallas_call(functools.partial(entity_kernel, relations, steps, scale),...  12.4 us
    ppermute x22, waiting for transfers between devices, moved(): return lax.ppermute(block, AXES, route)  12.1 us
  transfers between devices with their start and end apart: 22, of which 5 were waited for; matrix products, arithmetic and copies ran while one was open for 1% of the time, Pallas kernels for 26%

profile of v6, /device:TPU:0, one launch (start us, length us, event | category | flops | bytes accessed | tf_op | source)
XLA Modules:
  0.0 96.0 jit_solution(6197759228303151764)
XLA Ops:
  2.8 12.4 %shard_map.113 = (bf16[200,128]{1,0:T(8,128)(2,1)S(1)}, f32[40960,128]{1,0:T(8,128)S(1)}, bf16[200,6400]{1,0:T(8,128)(2,1)S(1)}, bf16[256,896]{1,0:T(8,128)(2,1)S(1)}) custom-call(s32[12800]{0:T(1024)S(1)} %add_multiply_fusion.own_ids.head_ids, bf16[200,20000]{1,0:T(8,128)(2,1)} %bitcast.33, bf16[200,5000]{1,0:T(8,128)(2,1)} %bitcast.34, ...), custom_call_target="tpu_custom_call" | custom-call | tf_op jit(solution)/shard_map/pallas_call | solution.py:178
  15.3 2.9 %collective-permute-start = (bf16[200,128]{1,0:T(8,128)(2,1)S(1)}, bf16[200,128]{1,0:T(8,128)(2,1)S(1)}, u32[]{:S(2)}, u32[]{:S(2)}) collective-permute-start(bf16[200,128]{1,0:T(8,128)(2,1)S(1)} %get-tuple-element.35.echo), channel_id=1, source_target_pairs={{16,0},{17,1},{18,2},{19,3},{20,4},{21,5},{22,6},{23,7},{24,8},{25... | collective-permute-start | bytes 153608 | tf_op jit(solution)/shard_map/ppermute | solution.py:38
  18.2 2.3 %collective-permute-start.2 = (bf16[200,128]{1,0:T(8,128)(2,1)S(1)}, bf16[200,128]{1,0:T(8,128)(2,1)S(1)}, u32[]{:S(2)}, u32[]{:S(2)}) collective-permute-start(bf16[200,128]{1,0:T(8,128)(2,1)S(1)} %get-tuple-element.35.echo), channel_id=1, source_target_pairs={{2,0},{3,1},{0,2},{1,3},{6,4},{7,5},{4,6},{5,7},{10,8},{11,9},{8,1... | collective-permute-start | bytes 153608 | tf_op jit(solution)/shard_map/ppermute | solution.py:38
  20.5 8.4 %shard_map.114 = (bf16[208,256]{1,0:T(8,128)(2,1)S(1)}, bf16[200,128]{1,0:T(8,128)(2,1)S(1)}, f32[40960,128]{1,0:T(8,128)S(1)}, bf16[200,6400]{1,0:T(8,128)(2,1)S(1)}, bf16[256,896]{1,0:T(8,128)(2,1)S(1)}) custom-call(s32[12800]{0:T(1024)S(1)} %add_multiply_fusion.own_ids.head_ids, ...), custom_call_target="tpu_custom_call", output_to_operand_aliasing={{2}: (6, {}), {3}: (7, {}), {4}: (8, {})} | custom-call | tf_op jit(solution)/shard_map/pallas_call | solution.py:214
  28.9 4.1 %collective-permute-start.3 = (bf16[208,256]{1,0:T(8,128)(2,1)S(1)}, bf16[208,256]{1,0:T(8,128)(2,1)S(1)}, u32[]{:S(2)}, u32[]{:S(2)}) collective-permute-start(bf16[208,256]{1,0:T(8,128)(2,1)S(1)} %get-tuple-element.43.refs_0_), channel_id=1, source_target_pairs={{32,0},{33,1},{34,2},{35,3},{36,4},{37,5},{38,6},{39,7},{40,8},{41... | collective-permute-start | bytes 319496 | tf_op jit(solution)/shard_map/ppermute | solution.py:38
  33.1 3.1 %collective-permute-start.5 = (bf16[200,512]{1,0:T(8,128)(2,1)S(1)}, bf16[200,512]{1,0:T(8,128)(2,1)S(1)}, u32[]{:S(2)}, u32[]{:S(2)}) collective-permute-start(bf16[200,512]{1,0:T(8,128)(2,1)S(1)} %constant_dynamic-update-slice_fusion.echo), channel_id=1, source_target_pairs={{4,0},{5,1},{6,2},{7,3},{8,4},{9,5},{10,6},{11,7},{12,8},{13,9},{1... | collective-permute-start | bytes 614408 | tf_op jit(solution)/shard_map/ppermute | solution.py:38
  36.2 2.2 %collective-permute-start.7 = (bf16[200,512]{1,0:T(8,128)(2,1)S(1)}, bf16[200,512]{1,0:T(8,128)(2,1)S(1)}, u32[]{:S(2)}, u32[]{:S(2)}) collective-permute-start(bf16[200,512]{1,0:T(8,128)(2,1)S(1)} %constant_dynamic-update-slice_fusion.echo), channel_id=1, source_target_pairs={{8,0},{9,1},{10,2},{11,3},{12,4},{13,5},{14,6},{15,7},{0,8},{1,9},... | collective-permute-start | bytes 614408 | tf_op jit(solution)/shard_map/ppermute | solution.py:38
  38.4 8.4 %shard_map.115 = (bf16[208,256]{1,0:T(8,128)(2,1)S(1)}, bf16[200,512]{1,0:T(8,128)(2,1)S(1)}, bf16[208,512]{1,0:T(8,128)(2,1)S(1)}, f32[40960,128]{1,0:T(8,128)S...) custom-call(s32[12800]{0:T(1024)S(1)} %add_multiply_fusion.own_ids.h, ...), custom_call_target="tpu_custom_call", output_to_operand_aliasing={{3}: (6, {}), {4}: (7, {}), {5}: (8, {})} | custom-call | tf_op jit(solution)/shard_map/pallas_call | solution.py:214
  48.4 2.4 %collective-permute-start.10 = (bf16[208,256]{1,0:T(8,128)(2,1)S(1)}, bf16[208,256]{1,0:T(8,128)(2,1)S(1)}, u32[]{:S(2)}, u32[]{:S(2)}) collective-permute-start(bf16[208,256]{1,0:T(8,128)(2,1)S(1)} %get-tuple-element.52), channel_id=1, source_target_pairs={{64,0},{65,1},{66,2},{67,3},{68,4},{69,5},{70,6},{71,7},{72,8},{73... | collective-permute-start | bytes 319496 | tf_op jit(solution)/shard_map/ppermute | solution.py:38
  50.8 2.5 %collective-permute-start.9 = (bf16[208,256]{1,0:T(8,128)(2,1)S(1)}, bf16[208,256]{1,0:T(8,128)(2,1)S(1)}, u32[]{:S(2)}, u32[]{:S(2)}) collective-permute-start(bf16[208,256]{1,0:T(8,128)(2,1)S(1)} %get-tuple-element.52), channel_id=1, source_target_pairs={{32,0},{33,1},{34,2},{35,3},{36,4},{37,5},{38,6},{39,7},{40,8},{41... | collective-permute-start | bytes 319496 | tf_op jit(solution)/shard_map/ppermute | solution.py:38
  53.3 1.9 %shard_map.116 = (f32[1,200,512]{2,1,0:T(8,128)S(1)}, f32[200,2048]{1,0:T(8,128)S(1)}) custom-call(s32[1]{0:T(128)} %bitcast.me, bf16[200,2048]{1,0:T(8,128)(2,1)S(1)} %constant_dynamic-update-slice_fusion.4.slab, bf16[208,512]{1,0:T(8,128)(2,1)S(1)} %get-tuple-element.49.refs_0_), custom_call_target="tpu_custom_call" | custom-call | tf_op jit(solution)/shard_map/pallas_call | solution.py:357
  55.3 3.5 %collective-permute-done.10.refs_5_.refs_4_ = bf16[208,256]{1,0:T(8,128)(2,1)S(1)} collective-permute-done((bf16[208,256]{1,0:T(8,128)(2,1)S(1)}, bf16[208,256]{1,0:T(8,128)(2,1)S(1)}, u32[]{:S(2)}, u32[]{:S(2)}) %collective-permute-start.10) | collective-permute-done | bytes 106528 | tf_op jit(solution)/shard_map/ppermute | solution.py:38
  58.8 6.9 %shard_map.117 = (f32[4,200,512]{2,1,0:T(8,128)S(1)}, bf16[200,2048]{1,0:T(8,128)(2,1)S(1)}) custom-call(s32[1]{0:T(128)} %bitcast.me, bf16[200,2048]{1,0:T(8,128)(2,1)S(1)} %collective-permute-done.11.slab, bf16[208,512]{1,0:T(8,128)(2,1)S(1)} %get-tuple-element.49.refs_0_, bf16[208,256]{1,0:T(8,128)(2,1)S(1)} %collective-permute-done.3.refs_1_.refs_0_, ...), custom_call_target="tpu_custom_call" | custom-call | tf_op jit(solution)/shard_map/pallas_call | solution.py:357
  66.0 4.9 %shard_map.118 = (f32[4,200,512]{2,1,0:T(8,128)S(1)}, f32[200,1536]{1,0:T(8,128)S(1)}) custom-call(s32[1]{0:T(128)} %bitcast.me, bf16[200,2048]{1,0:T(8,128)(2,1)S(1)} %constant_dynamic-update-slice_fusion.4.slab, bf16[208,256]{1,0:T(8,128)(2,1)S(1)} %collective-permute-done.3.refs_1_.refs_0_, ...), custom_call_target="tpu_custom_call", output_to_operand_aliasing={{0}: (7, {})} | custom-call | tf_op jit(solution)/shard_map/pallas_call | solution.py:357
  71.3 1.9 %collective-permute-start.13 = (bf16[200,512]{1,0:T(8,128)(2,1)S(1)}, bf16[200,512]{1,0:T(8,128)(2,1)S(1)}, u32[]{:S(2)}, u32[]{:S(2)}) collective-permute-start(bf16[200,512]{1,0:T(8,128)(2,1)S(1)} %get-tuple-element.70), channel_id=1, source_target_pairs={{12,0},{13,1},{14,2},{15,3},{0,4},{1,5},{2,6},{3,7},{4,8},{5,9},{6... | collective-permute-start | bytes 614408 | tf_op jit(solution)/shard_map/ppermute | solution.py:38
  73.2 1.4 %collective-permute-start.14 = (bf16[200,512]{1,0:T(8,128)(2,1)S(1)}, bf16[200,512]{1,0:T(8,128)(2,1)S(1)}, u32[]{:S(2)}, u32[]{:S(2)}) collective-permute-start(bf16[200,512]{1,0:T(8,128)(2,1)S(1)} %get-tuple-element.72), channel_id=1, source_target_pairs={{4,0},{5,1},{6,2},{7,3},{8,4},{9,5},{10,6},{11,7},{12,8},{13,9},{1... | collective-permute-start | bytes 614408 | tf_op jit(solution)/shard_map/ppermute | solution.py:38
  75.4 1.6 %shard_map.119 = (f32[200,512]{1,0:T(8,128)S(1)}, bf16[200,512]{1,0:T(8,128)(2,1)S(1)}, bf16[200,512]{1,0:T(8,128)(2,1)S(1)}, bf16[200,512]{1,0:T(8,128)(2,1)S(1)}, f32[200,512]{1,0:T(8,128)S(1)}) custom-call(s32[1]{0:T(128)} %bitcast.me, bf16[200,2048]{1,0:T(8,128)(2,1)S(1)} %constant_dynamic-update-slice_fusion.4.slab, ...), custom_call_target="tpu_custom_call" | custom-call | tf_op jit(solution)/shard_map/pallas_call | solution.py:357
  77.1 3.2 %collective-permute-start.20 = (bf16[200,512]{1,0:T(8,128)(2,1)S(1)}, bf16[200,512]{1,0:T(8,128)(2,1)S(1)}, u32[]{:S(2)}, u32[]{:S(2)}) collective-permute-start(bf16[200,512]{1,0:T(8,128)(2,1)S(1)} %get-tuple-element.66), channel_id=1, source_target_pairs={{32,0},{33,1},{34,2},{35,3},{36,4},{37,5},{38,6},{39,7},{40,8},{41... | collective-permute-start | bytes 614408 | tf_op jit(solution)/shard_map/ppermute | solution.py:38
  80.3 4.2 %collective-permute-done.13 = bf16[200,512]{1,0:T(8,128)(2,1)S(1)} collective-permute-done((bf16[200,512]{1,0:T(8,128)(2,1)S(1)}, bf16[200,512]{1,0:T(8,128)(2,1)S(1)}, u32[]{:S(2)}, u32[]{:S(2)}) %collective-permute-start.13) | collective-permute-done | bytes 204832 | tf_op jit(solution)/shard_map/ppermute | solution.py:38
  84.5 1.7 %collective-permute-start.21 = (bf16[200,512]{1,0:T(8,128)(2,1)S(1)}, bf16[200,512]{1,0:T(8,128)(2,1)S(1)}, u32[]{:S(2)}, u32[]{:S(2)}) collective-permute-start(bf16[200,512]{1,0:T(8,128)(2,1)S(1)} %get-tuple-element.67), channel_id=1, source_target_pairs={{64,0},{65,1},{66,2},{67,3},{68,4},{69,5},{70,6},{71,7},{72,8},{73... | collective-permute-start | bytes 614408 | tf_op jit(solution)/shard_map/ppermute | solution.py:38
  86.4 1.9 %collective-permute-start.16 = (bf16[200,128]{1,0:T(8,128)(2,1)S(1)}, bf16[200,128]{1,0:T(8,128)(2,1)S(1)}, u32[]{:S(2)}, u32[]{:S(2)}) collective-permute-start(bf16[200,128]{1,0:T(8,128)(2,1)S(1)} %get-tuple-element.73), channel_id=1, source_target_pairs={{18,0},{19,1},{16,2},{17,3},{22,4},{23,5},{20,6},{21,7},{26,8},{27... | collective-permute-start | bytes 153608 | tf_op jit(solution)/shard_map/ppermute | solution.py:38
  88.3 1.4 %collective-permute-start.17 = (bf16[200,128]{1,0:T(8,128)(2,1)S(1)}, bf16[200,128]{1,0:T(8,128)(2,1)S(1)}, u32[]{:S(2)}, u32[]{:S(2)}) collective-permute-start(bf16[200,128]{1,0:T(8,128)(2,1)S(1)} %get-tuple-element.75), channel_id=1, source_target_pairs={{16,0},{17,1},{18,2},{19,3},{20,4},{21,5},{22,6},{23,7},{24,8},{25... | collective-permute-start | bytes 153608 | tf_op jit(solution)/shard_map/ppermute | solution.py:38
  90.5 2.2 %collective-permute-done.21 = bf16[200,512]{1,0:T(8,128)(2,1)S(1)} collective-permute-done((bf16[200,512]{1,0:T(8,128)(2,1)S(1)}, bf16[200,512]{1,0:T(8,128)(2,1)S(1)}, u32[]{:S(2)}, u32[]{:S(2)}) %collective-permute-start.21) | collective-permute-done | bytes 204832 | tf_op jit(solution)/shard_map/ppermute | solution.py:38
  93.5 1.8 %collective-permute-done.18 = bf16[200,128]{1,0:T(8,128)(2,1)S(1)} collective-permute-done((bf16[200,128]{1,0:T(8,128)(2,1)S(1)}, bf16[200,128]{1,0:T(8,128)(2,1)S(1)}, u32[]{:S(2)}, u32[]{:S(2)}) %collective-permute-start.18) | collective-permute-done | bytes 51232 | tf_op jit(solution)/shard_map/ppermute | solution.py:38
  (52 shorter events, 7.9 us)
Async XLA Ops:
  2.8 17.7 %copy-start.2 = (s32[512,4]{0,1:T(4,128)S(1)}, s32[512,4]{0,1:T(4,128)}, u32[]{:S(2)}) copy-start(s32[512,4]{0,1:T(4,128)} %param.15) | copy-start | bytes 24580
  2.8 17.7 %copy-start.3 = (s32[512]{0:T(512)S(1)}, s32[512]{0:T(512)}, u32[]{:S(2)}) copy-start(s32[512]{0:T(512)} %param.14) | copy-start | bytes 6148
  15.3 17.7 %collective-permute-start = (bf16[200,128]{1,0:T(8,128)(2,1)S(1)}, bf16[200,128]{1,0:T(8,128)(2,1)S(1)}, u32[]{:S(2)}, u32[]{:S(2)}) collective-permute-start(bf16[200,128]{1,0:T(8,128)(2,1)S(1)} %get-tuple-element.35.echo), channel_id=1, source_target_pairs={{16,0},{17,1},{18,2},{19,3},{20,4},{21,5},{22,6},{23,7},{24,8},{25... | collective-permute-start | bytes 153608 | tf_op jit(solution)/shard_map/ppermute | solution.py:38
  18.2 14.8 %collective-permute-start.1 = (bf16[200,128]{1,0:T(8,128)(2,1)S(1)}, bf16[200,128]{1,0:T(8,128)(2,1)S(1)}, u32[]{:S(2)}, u32[]{:S(2)}) collective-permute-start(bf16[200,128]{1,0:T(8,128)(2,1)S(1)} %get-tuple-element.35.echo), channel_id=1, source_target_pairs={{18,0},{19,1},{16,2},{17,3},{22,4},{23,5},{20,6},{21,7},{26,8},{27... | collective-permute-start | bytes 153608 | tf_op jit(solution)/shard_map/ppermute | solution.py:38
  18.2 14.9 %collective-permute-start.2 = (bf16[200,128]{1,0:T(8,128)(2,1)S(1)}, bf16[200,128]{1,0:T(8,128)(2,1)S(1)}, u32[]{:S(2)}, u32[]{:S(2)}) collective-permute-start(bf16[200,128]{1,0:T(8,128)(2,1)S(1)} %get-tuple-element.35.echo), channel_id=1, source_target_pairs={{2,0},{3,1},{0,2},{1,3},{6,4},{7,5},{4,6},{5,7},{10,8},{11,9},{8,1... | collective-permute-start | bytes 153608 | tf_op jit(solution)/shard_map/ppermute | solution.py:38
  28.9 17.9 %collective-permute-start.3 = (bf16[208,256]{1,0:T(8,128)(2,1)S(1)}, bf16[208,256]{1,0:T(8,128)(2,1)S(1)}, u32[]{:S(2)}, u32[]{:S(2)}) collective-permute-start(bf16[208,256]{1,0:T(8,128)(2,1)S(1)} %get-tuple-element.43.refs_0_), channel_id=1, source_target_pairs={{32,0},{33,1},{34,2},{35,3},{36,4},{37,5},{38,6},{39,7},{40,8},{41... | collective-permute-start | bytes 319496 | tf_op jit(solution)/shard_map/ppermute | solution.py:38
  33.0 13.8 %collective-permute-start.4 = (bf16[208,256]{1,0:T(8,128)(2,1)S(1)}, bf16[208,256]{1,0:T(8,128)(2,1)S(1)}, u32[]{:S(2)}, u32[]{:S(2)}) collective-permute-start(bf16[208,256]{1,0:T(8,128)(2,1)S(1)} %get-tuple-element.43.refs_0_), channel_id=1, source_target_pairs={{64,0},{65,1},{66,2},{67,3},{68,4},{69,5},{70,6},{71,7},{72,8},{73... | collective-permute-start | bytes 319496 | tf_op jit(solution)/shard_map/ppermute | solution.py:38
  33.1 13.7 %collective-permute-start.5 = (bf16[200,512]{1,0:T(8,128)(2,1)S(1)}, bf16[200,512]{1,0:T(8,128)(2,1)S(1)}, u32[]{:S(2)}, u32[]{:S(2)}) collective-permute-start(bf16[200,512]{1,0:T(8,128)(2,1)S(1)} %constant_dynamic-update-slice_fusion.echo), channel_id=1, source_target_pairs={{4,0},{5,1},{6,2},{7,3},{8,4},{9,5},{10,6},{11,7},{12,8},{13,9},{1... | collective-permute-start | bytes 614408 | tf_op jit(solution)/shard_map/ppermute | solution.py:38
  36.2 11.0 %collective-permute-start.6 = (bf16[200,512]{1,0:T(8,128)(2,1)S(1)}, bf16[200,512]{1,0:T(8,128)(2,1)S(1)}, u32[]{:S(2)}, u32[]{:S(2)}) collective-permute-start(bf16[200,512]{1,0:T(8,128)(2,1)S(1)} %constant_dynamic-update-slice_fusion.echo), channel_id=1, source_target_pairs={{12,0},{13,1},{14,2},{15,3},{0,4},{1,5},{2,6},{3,7},{4,8},{5,9},{6... | collective-permute-start | bytes 614408 | tf_op jit(solution)/shard_map/ppermute | solution.py:38
  36.2 11.0 %collective-permute-start.7 = (bf16[200,512]{1,0:T(8,128)(2,1)S(1)}, bf16[200,512]{1,0:T(8,128)(2,1)S(1)}, u32[]{:S(2)}, u32[]{:S(2)}) collective-permute-start(bf16[200,512]{1,0:T(8,128)(2,1)S(1)} %constant_dynamic-update-slice_fusion.echo), channel_id=1, source_target_pairs={{8,0},{9,1},{10,2},{11,3},{12,4},{13,5},{14,6},{15,7},{0,8},{1,9},... | collective-permute-start | bytes 614408 | tf_op jit(solution)/shard_map/ppermute | solution.py:38
  47.3 11.5 %collective-permute-start.11 = (bf16[200,2048]{1,0:T(8,128)(2,1)S(1)}, bf16[200,2048]{1,0:T(8,128)(2,1)S(1)}, u32[]{:S(2)}, u32[]{:S(2)}) collective-permute-start(bf16[200,2048]{1,0:T(8,128)(2,1)S(1)} %constant_dynamic-update-slice_fusion.4.slab), channel_id=1, source_target_pairs={{1,0},{0,1},{3,2},{2,3},{5,4},{4,5},{7,6},{6,7},{9,8},{8,9},{11,10... | collective-permute-start | bytes 2457608 | tf_op jit(solution)/shard_map/ppermute | solution.py:38
  47.4 11.4 %collective-permute-start.8 = (bf16[208,512]{1,0:T(8,128)(2,1)S(1)}, bf16[208,512]{1,0:T(8,128)(2,1)S(1)}, u32[]{:S(2)}, u32[]{:S(2)}) collective-permute-start(bf16[208,512]{1,0:T(8,128)(2,1)S(1)} %get-tuple-element.49.refs_0_), channel_id=1, source_target_pairs={{96,0},{97,1},{98,2},{99,3},{100,4},{101,5},{102,6},{103,7},{104,8... | collective-permute-start | bytes 638984 | tf_op jit(solution)/shard_map/ppermute | solution.py:38
  48.4 10.4 %collective-permute-start.10 = (bf16[208,256]{1,0:T(8,128)(2,1)S(1)}, bf16[208,256]{1,0:T(8,128)(2,1)S(1)}, u32[]{:S(2)}, u32[]{:S(2)}) collective-permute-start(bf16[208,256]{1,0:T(8,128)(2,1)S(1)} %get-tuple-element.52), channel_id=1, source_target_pairs={{64,0},{65,1},{66,2},{67,3},{68,4},{69,5},{70,6},{71,7},{72,8},{73... | collective-permute-start | bytes 319496 | tf_op jit(solution)/shard_map/ppermute | solution.py:38
  50.8 8.0 %collective-permute-start.9 = (bf16[208,256]{1,0:T(8,128)(2,1)S(1)}, bf16[208,256]{1,0:T(8,128)(2,1)S(1)}, u32[]{:S(2)}, u32[]{:S(2)}) collective-permute-start(bf16[208,256]{1,0:T(8,128)(2,1)S(1)} %get-tuple-element.52), channel_id=1, source_target_pairs={{32,0},{33,1},{34,2},{35,3},{36,4},{37,5},{38,6},{39,7},{40,8},{41... | collective-permute-start | bytes 319496 | tf_op jit(solution)/shard_map/ppermute | solution.py:38
  65.7 5.2 %collective-permute-start.12 = (bf16[200,2048]{1,0:T(8,128)(2,1)S(1)}, bf16[200,2048]{1,0:T(8,128)(2,1)S(1)}, u32[]{:S(2)}, u32[]{:S(2)}) collective-permute-start(bf16[200,2048]{1,0:T(8,128)(2,1)S(1)} %get-tuple-element.61), channel_id=1, source_target_pairs={{1,0},{0,1},{3,2},{2,3},{5,4},{4,5},{7,6},{6,7},{9,8},{8,9},{11,10... | collective-permute-start | bytes 2457608 | tf_op jit(solution)/shard_map/ppermute | solution.py:38
  71.3 13.1 %collective-permute-start.13 = (bf16[200,512]{1,0:T(8,128)(2,1)S(1)}, bf16[200,512]{1,0:T(8,128)(2,1)S(1)}, u32[]{:S(2)}, u32[]{:S(2)}) collective-permute-start(bf16[200,512]{1,0:T(8,128)(2,1)S(1)} %get-tuple-element.70), channel_id=1, source_target_pairs={{12,0},{13,1},{14,2},{15,3},{0,4},{1,5},{2,6},{3,7},{4,8},{5,9},{6... | collective-permute-start | bytes 614408 | tf_op jit(solution)/shard_map/ppermute | solution.py:38
  73.2 13.0 %collective-permute-start.14 = (bf16[200,512]{1,0:T(8,128)(2,1)S(1)}, bf16[200,512]{1,0:T(8,128)(2,1)S(1)}, u32[]{:S(2)}, u32[]{:S(2)}) collective-permute-start(bf16[200,512]{1,0:T(8,128)(2,1)S(1)} %get-tuple-element.72), channel_id=1, source_target_pairs={{4,0},{5,1},{6,2},{7,3},{8,4},{9,5},{10,6},{11,7},{12,8},{13,9},{1... | collective-permute-start | bytes 614408 | tf_op jit(solution)/shard_map/ppermute | solution.py:38
  74.6 11.6 %collective-permute-start.15 = (bf16[200,512]{1,0:T(8,128)(2,1)S(1)}, bf16[200,512]{1,0:T(8,128)(2,1)S(1)}, u32[]{:S(2)}, u32[]{:S(2)}) collective-permute-start(bf16[200,512]{1,0:T(8,128)(2,1)S(1)} %get-tuple-element.71), channel_id=1, source_target_pairs={{8,0},{9,1},{10,2},{11,3},{12,4},{13,5},{14,6},{15,7},{0,8},{1,9},... | collective-permute-start | bytes 614408 | tf_op jit(solution)/shard_map/ppermute | solution.py:38
  77.0 12.8 %collective-permute-start.19 = (bf16[200,512]{1,0:T(8,128)(2,1)S(1)}, bf16[200,512]{1,0:T(8,128)(2,1)S(1)}, u32[]{:S(2)}, u32[]{:S(2)}) collective-permute-start(bf16[200,512]{1,0:T(8,128)(2,1)S(1)} %get-tuple-element.65), channel_id=1, source_target_pairs={{96,0},{97,1},{98,2},{99,3},{100,4},{101,5},{102,6},{103,7},{104,8... | collective-permute-start | bytes 614408 | tf_op jit(solution)/shard_map/ppermute | solution.py:38
  77.1 13.4 %collective-permute-start.20 = (bf16[200,512]{1,0:T(8,128)(2,1)S(1)}, bf16[200,512]{1,0:T(8,128)(2,1)S(1)}, u32[]{:S(2)}, u32[]{:S(2)}) collective-permute-start(bf16[200,512]{1,0:T(8,128)(2,1)S(1)} %get-tuple-element.66), channel_id=1, source_target_pairs={{32,0},{33,1},{34,2},{35,3},{36,4},{37,5},{38,6},{39,7},{40,8},{41... | collective-permute-start | bytes 614408 | tf_op jit(solution)/shard_map/ppermute | solution.py:38
  84.5 8.2 %collective-permute-start.21 = (bf16[200,512]{1,0:T(8,128)(2,1)S(1)}, bf16[200,512]{1,0:T(8,128)(2,1)S(1)}, u32[]{:S(2)}, u32[]{:S(2)}) collective-permute-start(bf16[200,512]{1,0:T(8,128)(2,1)S(1)} %get-tuple-element.67), channel_id=1, source_target_pairs={{64,0},{65,1},{66,2},{67,3},{68,4},{69,5},{70,6},{71,7},{72,8},{73... | collective-permute-start | bytes 614408 | tf_op jit(solution)/shard_map/ppermute | solution.py:38
  86.4 7.1 %collective-permute-start.16 = (bf16[200,128]{1,0:T(8,128)(2,1)S(1)}, bf16[200,128]{1,0:T(8,128)(2,1)S(1)}, u32[]{:S(2)}, u32[]{:S(2)}) collective-permute-start(bf16[200,128]{1,0:T(8,128)(2,1)S(1)} %get-tuple-element.73), channel_id=1, source_target_pairs={{18,0},{19,1},{16,2},{17,3},{22,4},{23,5},{20,6},{21,7},{26,8},{27... | collective-permute-start | bytes 153608 | tf_op jit(solution)/shard_map/ppermute | solution.py:38
  88.3 5.2 %collective-permute-start.17 = (bf16[200,128]{1,0:T(8,128)(2,1)S(1)}, bf16[200,128]{1,0:T(8,128)(2,1)S(1)}, u32[]{:S(2)}, u32[]{:S(2)}) collective-permute-start(bf16[200,128]{1,0:T(8,128)(2,1)S(1)} %get-tuple-element.75), channel_id=1, source_target_pairs={{16,0},{17,1},{18,2},{19,3},{20,4},{21,5},{22,6},{23,7},{24,8},{25... | collective-permute-start | bytes 153608 | tf_op jit(solution)/shard_map/ppermute | solution.py:38
  89.8 5.6 %collective-permute-start.18 = (bf16[200,128]{1,0:T(8,128)(2,1)S(1)}, bf16[200,128]{1,0:T(8,128)(2,1)S(1)}, u32[]{:S(2)}, u32[]{:S(2)}) collective-permute-start(bf16[200,128]{1,0:T(8,128)(2,1)S(1)} %get-tuple-element.74), channel_id=1, source_target_pairs={{2,0},{3,1},{0,2},{1,3},{6,4},{7,5},{4,6},{5,7},{10,8},{11,9},{8,1... | collective-permute-start | bytes 153608 | tf_op jit(solution)/shard_map/ppermute | solution.py:38
  (3 other events, 36.0 us)

commit v7 on v6

--- a/solution.py
+++ b/solution.py
@@ -238,20 +238,18 @@
         blocks.append(refs[:count])
         refs = refs[count:]
     before = None
-    if stage > 1:
+    if stage:
         before, refs = refs[0], refs[1:]
     if stage == 3:
         kept, sent, refs = refs[0], refs[1:4], refs[4:]
         kept[...] = before[0]
     else:
         asks, refs = refs[0], refs[1:]
-    ents, tall, queries, marks, totals, *held = refs[:7]
-    if stage == 3:
-        asks = refs[7]
+    ents, tall, queries, marks, totals, *held = refs
     if stage == 2:
-        asks[0] = before[0]
+        asks[:2] = before[:2]
     number = len(blocks)
-    base = 1 if stage > 1 else 0
+    base = 2 if stage > 1 else 0
     width = SPAN
     tiles = SPAN // LANES
 
@@ -317,10 +315,15 @@
             ents[:, k * SPAN : (k + 1) * SPAN] = ent.T[:depth, :].astype(ents.dtype)
         if k:
             ask = asks[base + b] + ask
-        elif stage > 1:
+        elif stage > 1 or stage == 1 and b < 2:
             ask = before[base + b] + ask
-        if stage == 3 and k == len(parts) - 1:
-            sent[b][...] = ask.astype(BF16)
+        if stage == 3 and b:
+            sent[1][...] = ask.astype(BF16)
+        elif stage == 3:
+            half = width // 2
+            for out, at in ((sent[0], slice(0, half)), (sent[2], slice(half, width))):
+                out[:, :half] = before[1, :, at].astype(BF16)
+                out[:, half:] = ask[:, at].astype(BF16)
         else:
             asks[base + b] = ask
 
@@ -337,8 +340,7 @@
     plain = 1.0 - 2.0 * (0.1 / total_entities)
     shape = jax.ShapeDtypeStruct
     number = len(blocks)
-    total = pltpu.VMEM((1 if stage == 0 else 4, depth, SPAN), F32)
-    outs = [total]
+    outs = [pltpu.VMEM((4 if stage else 2, depth, SPAN), F32)]
     if stage == 3:
         outs = [shape((depth, SPAN), F32)] + [shape((depth, SPAN), BF16)] * 3
     outs.append(shape((depth, len(parts) * SPAN), BF16 if stage == 1 else F32))
@@ -350,10 +352,8 @@
         pltpu.VMEM((SPAN, SPAN), BF16),
         pltpu.VMEM((SPAN, SPAN), BF16),
     ]
-    if stage == 3:
-        scratch.append(total)
     whole = pl.BlockSpec(memory_space=pltpu.VMEM)
-    given = [piece for block in blocks for piece in block] + ([before] if stage > 1 else [])
+    given = [piece for block in blocks for piece in block] + ([before] if stage else [])
     return pl.pallas_call(
         functools.partial(
             score_kernel, plain, plain - 1.8, depth, parts, [len(b) for b in blocks], stage
@@ -405,14 +405,14 @@
     slab = jnp.concatenate([row] + sent, axis=1)
     other = moved(slab, dcore=1)
     second = [moved(late, dz=d) for d in (1, 2)]
-    own_asks, own_ents = score(me, slab, [[query]], (0, 1, 2, 3), 0, entities)
-    own_asks, own_ents, last, *second = lax.optimization_barrier(
-        (own_asks, own_ents, moved(query, dz=3), *second)
-    )
-    blocks = [[query], [first[0], second[0]], [last], [first[1], second[1]]]
-    asks, away = score(me, other, blocks, (0, 1, 2, 3), 1, entities)
+    asks, own_ents = score(me, slab, [[query], first], (0, 1, 2, 3), 0, entities)
+    asks, own_ents, last, *second = lax.optimization_barrier(
+        (asks, own_ents, moved(query, dz=3), *second)
+    )
+    blocks = [[query], first, second, [last]]
+    asks, away = score(me, other, blocks, (0, 1, 2, 3), 1, entities, asks)
     back = moved(away, dcore=1)
-    asks, ents = score(me, slab, blocks[1:], (1, 2, 3), 2, entities, asks)
+    asks, ents = score(me, slab, blocks[2:], (1, 2, 3), 2, entities, asks)
     span = slab.shape[1] // 4
 
     def slab_sum(part, k):
@@ -422,8 +422,7 @@
     ents = [ents[:, k * span : (k + 1) * span] for k in range(3)]
     ents = [slab_sum(part, k + 1).astype(BF16) for k, part in enumerate(ents)]
     ents = [moved(part, dy=-d) for d, part in zip(FAR, ents)]
-    query_total, *sums, ent_row = score(me, slab, blocks[1:], (0,), 3, entities, asks)
-    query_total = query_total + own_asks[0]
+    query_total, *sums, ent_row = score(me, slab, blocks[2:], (0,), 3, entities, asks)
     ent_row = slab_sum(ent_row, 0)
     for ent in ents:
         ent_row = ent_row + ent.astype(F32)

time: 96.4 us -> 94.3 us (0.978)
  waiting for transfers between devices: 12.1 us -> 10.7 us
    ppermute x22, waiting for transfers between devices: 12.1 us -> 10.7 us  [moved(): return lax.ppermute(block, AXES, route)]
where the time goes in v7:
time: 94.3 us; the launch traced here: 94 us
  Pallas kernels  44 us (47%)
  starting transfers between devices  34.1 us (36%)
  waiting for transfers between devices  10.7 us (11%)
  other arithmetic  2.79 us (3%)
  local copies, waits for them, and re-layouts  1.65 us (2%)
    ppermute x22, starting transfers between devices, moved(): return lax.ppermute(block, AXES, route)  34.1 us
    pallas_call x2, Pallas kernels, encode_heads(): pl.pallas_call(functools.partial(head_kernel, chunk * heads, heads), in_s...  16.8 us
    pallas_call x4, Pallas kernels, score(): pl.pallas_call(functools.partial(score_kernel, plain, plain - 1.8, depth,...  14.8 us
    pallas_call x1, Pallas kernels, encode_entities(): pl.pallas_call(functools.partial(entity_kernel, relations, steps, scale),...  12.4 us
    ppermute x22, waiting for transfers between devices, moved(): return lax.ppermute(block, AXES, route)  10.7 us
  transfers between devices with their start and end apart: 22, of which 5 were waited for; matrix products, arithmetic and copies ran while one was open for 1% of the time, Pallas kernels for 26%

profile of v7, /device:TPU:0, one launch (start us, length us, event | category | flops | bytes accessed | tf_op | source)
XLA Modules:
  0.0 94.0 jit_solution(7106910470583455951)
XLA Ops:
  2.8 12.4 %shard_map.113 = (bf16[200,128]{1,0:T(8,128)(2,1)S(1)}, f32[40960,128]{1,0:T(8,128)S(1)}, bf16[200,6400]{1,0:T(8,128)(2,1)S(1)}, bf16[256,896]{1,0:T(8,128)(2,1)S(1)}) custom-call(s32[12800]{0:T(1024)S(1)} %add_multiply_fusion.own_ids.head_ids, bf16[200,20000]{1,0:T(8,128)(2,1)} %bitcast.21, bf16[200,5000]{1,0:T(8,128)(2,1)} %bitcast.22, ...), custom_call_target="tpu_custom_call" | custom-call | tf_op jit(solution)/shard_map/pallas_call | solution.py:178
  15.3 2.9 %collective-permute-start = (bf16[200,128]{1,0:T(8,128)(2,1)S(1)}, bf16[200,128]{1,0:T(8,128)(2,1)S(1)}, u32[]{:S(2)}, u32[]{:S(2)}) collective-permute-start(bf16[200,128]{1,0:T(8,128)(2,1)S(1)} %get-tuple-element.35.echo), channel_id=1, source_target_pairs={{16,0},{17,1},{18,2},{19,3},{20,4},{21,5},{22,6},{23,7},{24,8},{25... | collective-permute-start | bytes 153608 | tf_op jit(solution)/shard_map/ppermute | solution.py:38
  18.2 2.3 %collective-permute-start.2 = (bf16[200,128]{1,0:T(8,128)(2,1)S(1)}, bf16[200,128]{1,0:T(8,128)(2,1)S(1)}, u32[]{:S(2)}, u32[]{:S(2)}) collective-permute-start(bf16[200,128]{1,0:T(8,128)(2,1)S(1)} %get-tuple-element.35.echo), channel_id=1, source_target_pairs={{2,0},{3,1},{0,2},{1,3},{6,4},{7,5},{4,6},{5,7},{10,8},{11,9},{8,1... | collective-permute-start | bytes 153608 | tf_op jit(solution)/shard_map/ppermute | solution.py:38
  20.5 8.4 %shard_map.114 = (bf16[208,256]{1,0:T(8,128)(2,1)S(1)}, bf16[200,128]{1,0:T(8,128)(2,1)S(1)}, f32[40960,128]{1,0:T(8,128)S(1)}, bf16[200,6400]{1,0:T(8,128)(2,1)S(1)}, bf16[256,896]{1,0:T(8,128)(2,1)S(1)}) custom-call(s32[12800]{0:T(1024)S(1)} %add_multiply_fusion.own_ids.head_ids, ...), custom_call_target="tpu_custom_call", output_to_operand_aliasing={{2}: (6, {}), {3}: (7, {}), {4}: (8, {})} | custom-call | tf_op jit(solution)/shard_map/pallas_call | solution.py:214
  28.9 4.1 %collective-permute-start.3 = (bf16[208,256]{1,0:T(8,128)(2,1)S(1)}, bf16[208,256]{1,0:T(8,128)(2,1)S(1)}, u32[]{:S(2)}, u32[]{:S(2)}) collective-permute-start(bf16[208,256]{1,0:T(8,128)(2,1)S(1)} %get-tuple-element.43.refs_0_), channel_id=1, source_target_pairs={{32,0},{33,1},{34,2},{35,3},{36,4},{37,5},{38,6},{39,7},{40,8},{41... | collective-permute-start | bytes 319496 | tf_op jit(solution)/shard_map/ppermute | solution.py:38
  33.1 3.1 %collective-permute-start.5 = (bf16[200,512]{1,0:T(8,128)(2,1)S(1)}, bf16[200,512]{1,0:T(8,128)(2,1)S(1)}, u32[]{:S(2)}, u32[]{:S(2)}) collective-permute-start(bf16[200,512]{1,0:T(8,128)(2,1)S(1)} %constant_dynamic-update-slice_fusion.echo), channel_id=1, source_target_pairs={{4,0},{5,1},{6,2},{7,3},{8,4},{9,5},{10,6},{11,7},{12,8},{13,9},{1... | collective-permute-start | bytes 614408 | tf_op jit(solution)/shard_map/ppermute | solution.py:38
  36.2 2.2 %collective-permute-start.7 = (bf16[200,512]{1,0:T(8,128)(2,1)S(1)}, bf16[200,512]{1,0:T(8,128)(2,1)S(1)}, u32[]{:S(2)}, u32[]{:S(2)}) collective-permute-start(bf16[200,512]{1,0:T(8,128)(2,1)S(1)} %constant_dynamic-update-slice_fusion.echo), channel_id=1, source_target_pairs={{8,0},{9,1},{10,2},{11,3},{12,4},{13,5},{14,6},{15,7},{0,8},{1,9},... | collective-permute-start | bytes 614408 | tf_op jit(solution)/shard_map/ppermute | solution.py:38
  38.4 8.4 %shard_map.115 = (bf16[208,256]{1,0:T(8,128)(2,1)S(1)}, bf16[200,512]{1,0:T(8,128)(2,1)S(1)}, bf16[208,512]{1,0:T(8,128)(2,1)S(1)}, f32[40960,128]{1,0:T(8,128)S...) custom-call(s32[12800]{0:T(1024)S(1)} %add_multiply_fusion.own_ids.h, ...), custom_call_target="tpu_custom_call", output_to_operand_aliasing={{3}: (6, {}), {4}: (7, {}), {5}: (8, {})} | custom-call | tf_op jit(solution)/shard_map/pallas_call | solution.py:214
  48.4 2.4 %collective-permute-start.10 = (bf16[208,256]{1,0:T(8,128)(2,1)S(1)}, bf16[208,256]{1,0:T(8,128)(2,1)S(1)}, u32[]{:S(2)}, u32[]{:S(2)}) collective-permute-start(bf16[208,256]{1,0:T(8,128)(2,1)S(1)} %get-tuple-element.53), channel_id=1, source_target_pairs={{64,0},{65,1},{66,2},{67,3},{68,4},{69,5},{70,6},{71,7},{72,8},{73... | collective-permute-start | bytes 319496 | tf_op jit(solution)/shard_map/ppermute | solution.py:38
  50.8 2.5 %collective-permute-start.9 = (bf16[208,256]{1,0:T(8,128)(2,1)S(1)}, bf16[208,256]{1,0:T(8,128)(2,1)S(1)}, u32[]{:S(2)}, u32[]{:S(2)}) collective-permute-start(bf16[208,256]{1,0:T(8,128)(2,1)S(1)} %get-tuple-element.53), channel_id=1, source_target_pairs={{32,0},{33,1},{34,2},{35,3},{36,4},{37,5},{38,6},{39,7},{40,8},{41... | collective-permute-start | bytes 319496 | tf_op jit(solution)/shard_map/ppermute | solution.py:38
  53.3 3.8 %shard_map.116 = (f32[2,200,512]{2,1,0:T(8,128)S(1)}, f32[200,2048]{1,0:T(8,128)S(1)}) custom-call(s32[1]{0:T(128)} %bitcast.me, bf16[200,2048]{1,0:T(8,128)(2,1)S(1)} %constant_dynamic-update-slice_fusion.4.slab, bf16[208,512]{1,0:T(8,128)(2,1)S(1)} %get-tuple-element.48.refs_0_, bf16[208,256]{1,0:T(8,128)(2,1)S(1)} %collective-permute-done.3.refs_1_, ...), custom_call_target="tpu_custom_call" | custom-call | tf_op jit(solution)/shard_map/pallas_call | solution.py:357
  57.1 1.7 %collective-permute-done.10.refs_4_.refs_1_ = bf16[208,256]{1,0:T(8,128)(2,1)S(1)} collective-permute-done((bf16[208,256]{1,0:T(8,128)(2,1)S(1)}, bf16[208,256]{1,0:T(8,128)(2,1)S(1)}, u32[]{:S(2)}, u32[]{:S(2)}) %collective-permute-start.10) | collective-permute-done | bytes 106528 | tf_op jit(solution)/shard_map/ppermute | solution.py:38
  58.8 6.9 %shard_map.117 = (f32[4,200,512]{2,1,0:T(8,128)S(1)}, bf16[200,2048]{1,0:T(8,128)(2,1)S(1)}) custom-call(s32[1]{0:T(128)} %bitcast.me, bf16[200,2048]{1,0:T(8,128)(2,1)S(1)} %collective-permute-done.11.slab, bf16[208,512]{1,0:T(8,128)(2,1)S(1)} %get-tuple-element.48.refs_0_, bf16[208,256]{1,0:T(8,128)(2,1)S(1)} %collective-permute-done.3.refs_1_, ...), custom_call_target="tpu_custom_call" | custom-call | tf_op jit(solution)/shard_map/pallas_call | solution.py:357
  66.1 2.8 %shard_map.118 = (f32[4,200,512]{2,1,0:T(8,128)S(1)}, f32[200,1536]{1,0:T(8,128)S(1)}) custom-call(s32[1]{0:T(128)} %bitcast.me, bf16[200,2048]{1,0:T(8,128)(2,1)S(1)} %constant_dynamic-update-slice_fusion.4.slab, bf16[208,256]{1,0:T(8,128)(2,1)S(1)} %collective-permute-done.9.refs_3_.refs_0_, ...), custom_call_target="tpu_custom_call", output_to_operand_aliasing={{0}: (5, {})} | custom-call | tf_op jit(solution)/shard_map/pallas_call | solution.py:357
  69.3 1.9 %collective-permute-start.13 = (bf16[200,512]{1,0:T(8,128)(2,1)S(1)}, bf16[200,512]{1,0:T(8,128)(2,1)S(1)}, u32[]{:S(2)}, u32[]{:S(2)}) collective-permute-start(bf16[200,512]{1,0:T(8,128)(2,1)S(1)} %get-tuple-element.70), channel_id=1, source_target_pairs={{12,0},{13,1},{14,2},{15,3},{0,4},{1,5},{2,6},{3,7},{4,8},{5,9},{6... | collective-permute-start | bytes 614408 | tf_op jit(solution)/shard_map/ppermute | solution.py:38
  71.2 1.4 %collective-permute-start.14 = (bf16[200,512]{1,0:T(8,128)(2,1)S(1)}, bf16[200,512]{1,0:T(8,128)(2,1)S(1)}, u32[]{:S(2)}, u32[]{:S(2)}) collective-permute-start(bf16[200,512]{1,0:T(8,128)(2,1)S(1)} %get-tuple-element.72), channel_id=1, source_target_pairs={{4,0},{5,1},{6,2},{7,3},{8,4},{9,5},{10,6},{11,7},{12,8},{13,9},{1... | collective-permute-start | bytes 614408 | tf_op jit(solution)/shard_map/ppermute | solution.py:38
  73.3 1.2 %shard_map.119 = (f32[200,512]{1,0:T(8,128)S(1)}, bf16[200,512]{1,0:T(8,128)(2,1)S(1)}, bf16[200,512]{1,0:T(8,128)(2,1)S(1)}, bf16[200,512]{1,0:T(8,128)(2,1)S(1)}, f32[200,512]{1,0:T(8,128)S(1)}) custom-call(s32[1]{0:T(128)} %bitcast.me, bf16[200,2048]{1,0:T(8,128)(2,1)S(1)} %constant_dynamic-update-slice_fusion.4.slab, ...), custom_call_target="tpu_custom_call" | custom-call | tf_op jit(solution)/shard_map/pallas_call | solution.py:357
  74.6 3.2 %collective-permute-start.20 = (bf16[200,512]{1,0:T(8,128)(2,1)S(1)}, bf16[200,512]{1,0:T(8,128)(2,1)S(1)}, u32[]{:S(2)}, u32[]{:S(2)}) collective-permute-start(bf16[200,512]{1,0:T(8,128)(2,1)S(1)} %get-tuple-element.66), channel_id=1, source_target_pairs={{32,0},{33,1},{34,2},{35,3},{36,4},{37,5},{38,6},{39,7},{40,8},{41... | collective-permute-start | bytes 614408 | tf_op jit(solution)/shard_map/ppermute | solution.py:38
  77.8 4.6 %collective-permute-done.13 = bf16[200,512]{1,0:T(8,128)(2,1)S(1)} collective-permute-done((bf16[200,512]{1,0:T(8,128)(2,1)S(1)}, bf16[200,512]{1,0:T(8,128)(2,1)S(1)}, u32[]{:S(2)}, u32[]{:S(2)}) %collective-permute-start.13) | collective-permute-done | bytes 204832 | tf_op jit(solution)/shard_map/ppermute | solution.py:38
  82.4 1.7 %collective-permute-start.21 = (bf16[200,512]{1,0:T(8,128)(2,1)S(1)}, bf16[200,512]{1,0:T(8,128)(2,1)S(1)}, u32[]{:S(2)}, u32[]{:S(2)}) collective-permute-start(bf16[200,512]{1,0:T(8,128)(2,1)S(1)} %get-tuple-element.67), channel_id=1, source_target_pairs={{64,0},{65,1},{66,2},{67,3},{68,4},{69,5},{70,6},{71,7},{72,8},{73... | collective-permute-start | bytes 614408 | tf_op jit(solution)/shard_map/ppermute | solution.py:38
  84.4 1.9 %collective-permute-start.16 = (bf16[200,128]{1,0:T(8,128)(2,1)S(1)}, bf16[200,128]{1,0:T(8,128)(2,1)S(1)}, u32[]{:S(2)}, u32[]{:S(2)}) collective-permute-start(bf16[200,128]{1,0:T(8,128)(2,1)S(1)} %get-tuple-element.73), channel_id=1, source_target_pairs={{18,0},{19,1},{16,2},{17,3},{22,4},{23,5},{20,6},{21,7},{26,8},{27... | collective-permute-start | bytes 153608 | tf_op jit(solution)/shard_map/ppermute | solution.py:38
  86.3 1.4 %collective-permute-start.17 = (bf16[200,128]{1,0:T(8,128)(2,1)S(1)}, bf16[200,128]{1,0:T(8,128)(2,1)S(1)}, u32[]{:S(2)}, u32[]{:S(2)}) collective-permute-start(bf16[200,128]{1,0:T(8,128)(2,1)S(1)} %get-tuple-element.75), channel_id=1, source_target_pairs={{16,0},{17,1},{18,2},{19,3},{20,4},{21,5},{22,6},{23,7},{24,8},{25... | collective-permute-start | bytes 153608 | tf_op jit(solution)/shard_map/ppermute | solution.py:38
  88.4 2.2 %collective-permute-done.21 = bf16[200,512]{1,0:T(8,128)(2,1)S(1)} collective-permute-done((bf16[200,512]{1,0:T(8,128)(2,1)S(1)}, bf16[200,512]{1,0:T(8,128)(2,1)S(1)}, u32[]{:S(2)}, u32[]{:S(2)}) %collective-permute-start.21) | collective-permute-done | bytes 204832 | tf_op jit(solution)/shard_map/ppermute | solution.py:38
  91.5 1.8 %collective-permute-done.18 = bf16[200,128]{1,0:T(8,128)(2,1)S(1)} collective-permute-done((bf16[200,128]{1,0:T(8,128)(2,1)S(1)}, bf16[200,128]{1,0:T(8,128)(2,1)S(1)}, u32[]{:S(2)}, u32[]{:S(2)}) %collective-permute-start.18) | collective-permute-done | bytes 51232 | tf_op jit(solution)/shard_map/ppermute | solution.py:38
  (52 shorter events, 7.8 us)
Async XLA Ops:
  2.8 17.7 %copy-start.2 = (s32[512,4]{0,1:T(4,128)S(1)}, s32[512,4]{0,1:T(4,128)}, u32[]{:S(2)}) copy-start(s32[512,4]{0,1:T(4,128)} %param.15) | copy-start | bytes 24580
  2.8 17.7 %copy-start.3 = (s32[512]{0:T(512)S(1)}, s32[512]{0:T(512)}, u32[]{:S(2)}) copy-start(s32[512]{0:T(512)} %param.14) | copy-start | bytes 6148
  15.3 17.7 %collective-permute-start = (bf16[200,128]{1,0:T(8,128)(2,1)S(1)}, bf16[200,128]{1,0:T(8,128)(2,1)S(1)}, u32[]{:S(2)}, u32[]{:S(2)}) collective-permute-start(bf16[200,128]{1,0:T(8,128)(2,1)S(1)} %get-tuple-element.35.echo), channel_id=1, source_target_pairs={{16,0},{17,1},{18,2},{19,3},{20,4},{21,5},{22,6},{23,7},{24,8},{25... | collective-permute-start | bytes 153608 | tf_op jit(solution)/shard_map/ppermute | solution.py:38
  18.2 14.8 %collective-permute-start.1 = (bf16[200,128]{1,0:T(8,128)(2,1)S(1)}, bf16[200,128]{1,0:T(8,128)(2,1)S(1)}, u32[]{:S(2)}, u32[]{:S(2)}) collective-permute-start(bf16[200,128]{1,0:T(8,128)(2,1)S(1)} %get-tuple-element.35.echo), channel_id=1, source_target_pairs={{18,0},{19,1},{16,2},{17,3},{22,4},{23,5},{20,6},{21,7},{26,8},{27... | collective-permute-start | bytes 153608 | tf_op jit(solution)/shard_map/ppermute | solution.py:38
  18.2 14.9 %collective-permute-start.2 = (bf16[200,128]{1,0:T(8,128)(2,1)S(1)}, bf16[200,128]{1,0:T(8,128)(2,1)S(1)}, u32[]{:S(2)}, u32[]{:S(2)}) collective-permute-start(bf16[200,128]{1,0:T(8,128)(2,1)S(1)} %get-tuple-element.35.echo), channel_id=1, source_target_pairs={{2,0},{3,1},{0,2},{1,3},{6,4},{7,5},{4,6},{5,7},{10,8},{11,9},{8,1... | collective-permute-start | bytes 153608 | tf_op jit(solution)/shard_map/ppermute | solution.py:38
  28.9 17.9 %collective-permute-start.3 = (bf16[208,256]{1,0:T(8,128)(2,1)S(1)}, bf16[208,256]{1,0:T(8,128)(2,1)S(1)}, u32[]{:S(2)}, u32[]{:S(2)}) collective-permute-start(bf16[208,256]{1,0:T(8,128)(2,1)S(1)} %get-tuple-element.43.refs_0_), channel_id=1, source_target_pairs={{32,0},{33,1},{34,2},{35,3},{36,4},{37,5},{38,6},{39,7},{40,8},{41... | collective-permute-start | bytes 319496 | tf_op jit(solution)/shard_map/ppermute | solution.py:38
  33.0 13.8 %collective-permute-start.4 = (bf16[208,256]{1,0:T(8,128)(2,1)S(1)}, bf16[208,256]{1,0:T(8,128)(2,1)S(1)}, u32[]{:S(2)}, u32[]{:S(2)}) collective-permute-start(bf16[208,256]{1,0:T(8,128)(2,1)S(1)} %get-tuple-element.43.refs_0_), channel_id=1, source_target_pairs={{64,0},{65,1},{66,2},{67,3},{68,4},{69,5},{70,6},{71,7},{72,8},{73... | collective-permute-start | bytes 319496 | tf_op jit(solution)/shard_map/ppermute | solution.py:38
  33.1 13.7 %collective-permute-start.5 = (bf16[200,512]{1,0:T(8,128)(2,1)S(1)}, bf16[200,512]{1,0:T(8,128)(2,1)S(1)}, u32[]{:S(2)}, u32[]{:S(2)}) collective-permute-start(bf16[200,512]{1,0:T(8,128)(2,1)S(1)} %constant_dynamic-update-slice_fusion.echo), channel_id=1, source_target_pairs={{4,0},{5,1},{6,2},{7,3},{8,4},{9,5},{10,6},{11,7},{12,8},{13,9},{1... | collective-permute-start | bytes 614408 | tf_op jit(solution)/shard_map/ppermute | solution.py:38
  36.2 11.0 %collective-permute-start.6 = (bf16[200,512]{1,0:T(8,128)(2,1)S(1)}, bf16[200,512]{1,0:T(8,128)(2,1)S(1)}, u32[]{:S(2)}, u32[]{:S(2)}) collective-permute-start(bf16[200,512]{1,0:T(8,128)(2,1)S(1)} %constant_dynamic-update-slice_fusion.echo), channel_id=1, source_target_pairs={{12,0},{13,1},{14,2},{15,3},{0,4},{1,5},{2,6},{3,7},{4,8},{5,9},{6... | collective-permute-start | bytes 614408 | tf_op jit(solution)/shard_map/ppermute | solution.py:38
  36.2 11.0 %collective-permute-start.7 = (bf16[200,512]{1,0:T(8,128)(2,1)S(1)}, bf16[200,512]{1,0:T(8,128)(2,1)S(1)}, u32[]{:S(2)}, u32[]{:S(2)}) collective-permute-start(bf16[200,512]{1,0:T(8,128)(2,1)S(1)} %constant_dynamic-update-slice_fusion.echo), channel_id=1, source_target_pairs={{8,0},{9,1},{10,2},{11,3},{12,4},{13,5},{14,6},{15,7},{0,8},{1,9},... | collective-permute-start | bytes 614408 | tf_op jit(solution)/shard_map/ppermute | solution.py:38
  47.3 11.5 %collective-permute-start.11 = (bf16[200,2048]{1,0:T(8,128)(2,1)S(1)}, bf16[200,2048]{1,0:T(8,128)(2,1)S(1)}, u32[]{:S(2)}, u32[]{:S(2)}) collective-permute-start(bf16[200,2048]{1,0:T(8,128)(2,1)S(1)} %constant_dynamic-update-slice_fusion.4.slab), channel_id=1, source_target_pairs={{1,0},{0,1},{3,2},{2,3},{5,4},{4,5},{7,6},{6,7},{9,8},{8,9},{11,10... | collective-permute-start | bytes 2457608 | tf_op jit(solution)/shard_map/ppermute | solution.py:38
  47.4 11.4 %collective-permute-start.8 = (bf16[208,512]{1,0:T(8,128)(2,1)S(1)}, bf16[208,512]{1,0:T(8,128)(2,1)S(1)}, u32[]{:S(2)}, u32[]{:S(2)}) collective-permute-start(bf16[208,512]{1,0:T(8,128)(2,1)S(1)} %get-tuple-element.48.refs_0_), channel_id=1, source_target_pairs={{96,0},{97,1},{98,2},{99,3},{100,4},{101,5},{102,6},{103,7},{104,8... | collective-permute-start | bytes 638984 | tf_op jit(solution)/shard_map/ppermute | solution.py:38
  48.4 10.4 %collective-permute-start.10 = (bf16[208,256]{1,0:T(8,128)(2,1)S(1)}, bf16[208,256]{1,0:T(8,128)(2,1)S(1)}, u32[]{:S(2)}, u32[]{:S(2)}) collective-permute-start(bf16[208,256]{1,0:T(8,128)(2,1)S(1)} %get-tuple-element.53), channel_id=1, source_target_pairs={{64,0},{65,1},{66,2},{67,3},{68,4},{69,5},{70,6},{71,7},{72,8},{73... | collective-permute-start | bytes 319496 | tf_op jit(solution)/shard_map/ppermute | solution.py:38
  50.8 8.0 %collective-permute-start.9 = (bf16[208,256]{1,0:T(8,128)(2,1)S(1)}, bf16[208,256]{1,0:T(8,128)(2,1)S(1)}, u32[]{:S(2)}, u32[]{:S(2)}) collective-permute-start(bf16[208,256]{1,0:T(8,128)(2,1)S(1)} %get-tuple-element.53), channel_id=1, source_target_pairs={{32,0},{33,1},{34,2},{35,3},{36,4},{37,5},{38,6},{39,7},{40,8},{41... | collective-permute-start | bytes 319496 | tf_op jit(solution)/shard_map/ppermute | solution.py:38
  65.8 3.2 %collective-permute-start.12 = (bf16[200,2048]{1,0:T(8,128)(2,1)S(1)}, bf16[200,2048]{1,0:T(8,128)(2,1)S(1)}, u32[]{:S(2)}, u32[]{:S(2)}) collective-permute-start(bf16[200,2048]{1,0:T(8,128)(2,1)S(1)} %get-tuple-element.62), channel_id=1, source_target_pairs={{1,0},{0,1},{3,2},{2,3},{5,4},{4,5},{7,6},{6,7},{9,8},{8,9},{11,10... | collective-permute-start | bytes 2457608 | tf_op jit(solution)/shard_map/ppermute | solution.py:38
  69.3 13.1 %collective-permute-start.13 = (bf16[200,512]{1,0:T(8,128)(2,1)S(1)}, bf16[200,512]{1,0:T(8,128)(2,1)S(1)}, u32[]{:S(2)}, u32[]{:S(2)}) collective-permute-start(bf16[200,512]{1,0:T(8,128)(2,1)S(1)} %get-tuple-element.70), channel_id=1, source_target_pairs={{12,0},{13,1},{14,2},{15,3},{0,4},{1,5},{2,6},{3,7},{4,8},{5,9},{6... | collective-permute-start | bytes 614408 | tf_op jit(solution)/shard_map/ppermute | solution.py:38
  71.2 13.0 %collective-permute-start.14 = (bf16[200,512]{1,0:T(8,128)(2,1)S(1)}, bf16[200,512]{1,0:T(8,128)(2,1)S(1)}, u32[]{:S(2)}, u32[]{:S(2)}) collective-permute-start(bf16[200,512]{1,0:T(8,128)(2,1)S(1)} %get-tuple-element.72), channel_id=1, source_target_pairs={{4,0},{5,1},{6,2},{7,3},{8,4},{9,5},{10,6},{11,7},{12,8},{13,9},{1... | collective-permute-start | bytes 614408 | tf_op jit(solution)/shard_map/ppermute | solution.py:38
  72.6 11.6 %collective-permute-start.15 = (bf16[200,512]{1,0:T(8,128)(2,1)S(1)}, bf16[200,512]{1,0:T(8,128)(2,1)S(1)}, u32[]{:S(2)}, u32[]{:S(2)}) collective-permute-start(bf16[200,512]{1,0:T(8,128)(2,1)S(1)} %get-tuple-element.71), channel_id=1, source_target_pairs={{8,0},{9,1},{10,2},{11,3},{12,4},{13,5},{14,6},{15,7},{0,8},{1,9},... | collective-permute-start | bytes 614408 | tf_op jit(solution)/shard_map/ppermute | solution.py:38
  74.5 13.2 %collective-permute-start.19 = (bf16[200,512]{1,0:T(8,128)(2,1)S(1)}, bf16[200,512]{1,0:T(8,128)(2,1)S(1)}, u32[]{:S(2)}, u32[]{:S(2)}) collective-permute-start(bf16[200,512]{1,0:T(8,128)(2,1)S(1)} %get-tuple-element.65), channel_id=1, source_target_pairs={{96,0},{97,1},{98,2},{99,3},{100,4},{101,5},{102,6},{103,7},{104,8... | collective-permute-start | bytes 614408 | tf_op jit(solution)/shard_map/ppermute | solution.py:38
  74.6 13.9 %collective-permute-start.20 = (bf16[200,512]{1,0:T(8,128)(2,1)S(1)}, bf16[200,512]{1,0:T(8,128)(2,1)S(1)}, u32[]{:S(2)}, u32[]{:S(2)}) collective-permute-start(bf16[200,512]{1,0:T(8,128)(2,1)S(1)} %get-tuple-element.66), channel_id=1, source_target_pairs={{32,0},{33,1},{34,2},{35,3},{36,4},{37,5},{38,6},{39,7},{40,8},{41... | collective-permute-start | bytes 614408 | tf_op jit(solution)/shard_map/ppermute | solution.py:38
  82.4 8.2 %collective-permute-start.21 = (bf16[200,512]{1,0:T(8,128)(2,1)S(1)}, bf16[200,512]{1,0:T(8,128)(2,1)S(1)}, u32[]{:S(2)}, u32[]{:S(2)}) collective-permute-start(bf16[200,512]{1,0:T(8,128)(2,1)S(1)} %get-tuple-element.67), channel_id=1, source_target_pairs={{64,0},{65,1},{66,2},{67,3},{68,4},{69,5},{70,6},{71,7},{72,8},{73... | collective-permute-start | bytes 614408 | tf_op jit(solution)/shard_map/ppermute | solution.py:38
  84.4 7.1 %collective-permute-start.16 = (bf16[200,128]{1,0:T(8,128)(2,1)S(1)}, bf16[200,128]{1,0:T(8,128)(2,1)S(1)}, u32[]{:S(2)}, u32[]{:S(2)}) collective-permute-start(bf16[200,128]{1,0:T(8,128)(2,1)S(1)} %get-tuple-element.73), channel_id=1, source_target_pairs={{18,0},{19,1},{16,2},{17,3},{22,4},{23,5},{20,6},{21,7},{26,8},{27... | collective-permute-start | bytes 153608 | tf_op jit(solution)/shard_map/ppermute | solution.py:38
  86.3 5.2 %collective-permute-start.17 = (bf16[200,128]{1,0:T(8,128)(2,1)S(1)}, bf16[200,128]{1,0:T(8,128)(2,1)S(1)}, u32[]{:S(2)}, u32[]{:S(2)}) collective-permute-start(bf16[200,128]{1,0:T(8,128)(2,1)S(1)} %get-tuple-element.75), channel_id=1, source_target_pairs={{16,0},{17,1},{18,2},{19,3},{20,4},{21,5},{22,6},{23,7},{24,8},{25... | collective-permute-start | bytes 153608 | tf_op jit(solution)/shard_map/ppermute | solution.py:38
  87.7 5.6 %collective-permute-start.18 = (bf16[200,128]{1,0:T(8,128)(2,1)S(1)}, bf16[200,128]{1,0:T(8,128)(2,1)S(1)}, u32[]{:S(2)}, u32[]{:S(2)}) collective-permute-start(bf16[200,128]{1,0:T(8,128)(2,1)S(1)} %get-tuple-element.74), channel_id=1, source_target_pairs={{2,0},{3,1},{0,2},{1,3},{6,4},{7,5},{4,6},{5,7},{10,8},{11,9},{8,1... | collective-permute-start | bytes 153608 | tf_op jit(solution)/shard_map/ppermute | solution.py:38
  (3 other events, 36.0 us)

commit v8 on v7

--- a/solution.py
+++ b/solution.py
@@ -14,7 +14,7 @@
 LANES = 128
 WIDE = 256
 CHUNK = 4096
-UNROLL = 64
+UNROLL = 256
 SPAN = 512
 VMEM_BYTES = 12 * 1024 * 1024
 CHUNKS = 2
@@ -39,13 +39,14 @@
 
 
 def gather_rows(ids, table, rows, width, count, start, anchors):
-    per = width // UNROLL
+    unroll = min(UNROLL, width)
+    per = width // unroll
 
     def some(step, carry):
-        first = step // per * count + start + step % per * UNROLL
-        place = pl.multiple_of(step * (2 * UNROLL), 2 * UNROLL)
-        picked = [table[pl.ds(ids[first + k], 2), :] for k in range(UNROLL)]
-        for k in range(UNROLL):
+        first = step // per * count + start + step % per * unroll
+        place = pl.multiple_of(step * (2 * unroll), 2 * unroll)
+        picked = [table[pl.ds(ids[first + k], 2), :] for k in range(unroll)]
+        for k in range(unroll):
             rows[pl.ds(place + 2 * k, 2), :] = picked[k]
         return carry
 

time: 94.3 us -> 93.2 us (0.988)
  Pallas kernels: 44 us -> 42 us
  waiting for transfers between devices: 10.7 us -> 12.2 us
    pallas_call x2, Pallas kernels: 16.8 us -> 15.2 us  [encode_heads(): pl.pallas_call(functools.partial(head_kernel, chunk * heads, heads), in_s...]
    ppermute x22, waiting for transfers between devices: 10.7 us -> 12.2 us  [moved(): return lax.ppermute(block, AXES, route)]
  transfers between devices with their start and end apart: 22 -> 22, of which waited for: 5 -> 5; matrix products, arithmetic and copies ran while one was open for 1% -> 1% of each run, Pallas kernels for 26% -> 25%
where the time goes in v8:
time: 93.2 us; the launch traced here: 92.9 us
  Pallas kernels  42 us (45%)
  starting transfers between devices  33.3 us (36%)
  waiting for transfers between devices  12.2 us (13%)
  other arithmetic  2.79 us (3%)
  local copies, waits for them, and re-layouts  1.65 us (2%)
    ppermute x22, starting transfers between devices, moved(): return lax.ppermute(block, AXES, route)  33.3 us
    pallas_call x2, Pallas kernels, encode_heads(): pl.pallas_call(functools.partial(head_kernel, chunk * heads, heads), in_s...  15.2 us
    pallas_call x4, Pallas kernels, score(): pl.pallas_call(functools.partial(score_kernel, plain, plain - 1.8, depth,...  14.8 us
    ppermute x22, waiting for transfers between devices, moved(): return lax.ppermute(block, AXES, route)  12.2 us
    pallas_call x1, Pallas kernels, encode_entities(): pl.pallas_call(functools.partial(entity_kernel, relations, steps, scale),...  12.1 us
  transfers between devices with their start and end apart: 22, of which 5 were waited for; matrix products, arithmetic and copies ran while one was open for 1% of the time, Pallas kernels for 25%

profile of v8, /device:TPU:0, one launch (start us, length us, event | category | flops | bytes accessed | tf_op | source)
XLA Modules:
  0.0 92.9 jit_solution(2905942385666678704)
XLA Ops:
  2.8 12.1 %shard_map.113 = (bf16[200,128]{1,0:T(8,128)(2,1)S(1)}, f32[40960,128]{1,0:T(8,128)S(1)}, bf16[200,6400]{1,0:T(8,128)(2,1)S(1)}, bf16[256,896]{1,0:T(8,128)(2,1)S(1)}) custom-call(s32[12800]{0:T(1024)S(1)} %add_multiply_fusion.own_ids.head_ids, bf16[200,20000]{1,0:T(8,128)(2,1)} %bitcast.21, bf16[200,5000]{1,0:T(8,128)(2,1)} %bitcast.22, ...), custom_call_target="tpu_custom_call" | custom-call | tf_op jit(solution)/shard_map/pallas_call | solution.py:179
  15.0 2.9 %collective-permute-start = (bf16[200,128]{1,0:T(8,128)(2,1)S(1)}, bf16[200,128]{1,0:T(8,128)(2,1)S(1)}, u32[]{:S(2)}, u32[]{:S(2)}) collective-permute-start(bf16[200,128]{1,0:T(8,128)(2,1)S(1)} %get-tuple-element.35.echo), channel_id=1, source_target_pairs={{16,0},{17,1},{18,2},{19,3},{20,4},{21,5},{22,6},{23,7},{24,8},{25... | collective-permute-start | bytes 153608 | tf_op jit(solution)/shard_map/ppermute | solution.py:38
  17.9 2.3 %collective-permute-start.2 = (bf16[200,128]{1,0:T(8,128)(2,1)S(1)}, bf16[200,128]{1,0:T(8,128)(2,1)S(1)}, u32[]{:S(2)}, u32[]{:S(2)}) collective-permute-start(bf16[200,128]{1,0:T(8,128)(2,1)S(1)} %get-tuple-element.35.echo), channel_id=1, source_target_pairs={{2,0},{3,1},{0,2},{1,3},{6,4},{7,5},{4,6},{5,7},{10,8},{11,9},{8,1... | collective-permute-start | bytes 153608 | tf_op jit(solution)/shard_map/ppermute | solution.py:38
  20.2 7.6 %shard_map.114 = (bf16[208,256]{1,0:T(8,128)(2,1)S(1)}, bf16[200,128]{1,0:T(8,128)(2,1)S(1)}, f32[40960,128]{1,0:T(8,128)S(1)}, bf16[200,6400]{1,0:T(8,128)(2,1)S(1)}, bf16[256,896]{1,0:T(8,128)(2,1)S(1)}) custom-call(s32[12800]{0:T(1024)S(1)} %add_multiply_fusion.own_ids.head_ids, ...), custom_call_target="tpu_custom_call", output_to_operand_aliasing={{2}: (6, {}), {3}: (7, {}), {4}: (8, {})} | custom-call | tf_op jit(solution)/shard_map/pallas_call | solution.py:215
  27.8 4.1 %collective-permute-start.3 = (bf16[208,256]{1,0:T(8,128)(2,1)S(1)}, bf16[208,256]{1,0:T(8,128)(2,1)S(1)}, u32[]{:S(2)}, u32[]{:S(2)}) collective-permute-start(bf16[208,256]{1,0:T(8,128)(2,1)S(1)} %get-tuple-element.43.refs_0_), channel_id=1, source_target_pairs={{32,0},{33,1},{34,2},{35,3},{36,4},{37,5},{38,6},{39,7},{40,8},{41... | collective-permute-start | bytes 319496 | tf_op jit(solution)/shard_map/ppermute | solution.py:38
  32.0 3.1 %collective-permute-start.5 = (bf16[200,512]{1,0:T(8,128)(2,1)S(1)}, bf16[200,512]{1,0:T(8,128)(2,1)S(1)}, u32[]{:S(2)}, u32[]{:S(2)}) collective-permute-start(bf16[200,512]{1,0:T(8,128)(2,1)S(1)} %constant_dynamic-update-slice_fusion.echo), channel_id=1, source_target_pairs={{4,0},{5,1},{6,2},{7,3},{8,4},{9,5},{10,6},{11,7},{12,8},{13,9},{1... | collective-permute-start | bytes 614408 | tf_op jit(solution)/shard_map/ppermute | solution.py:38
  35.1 2.2 %collective-permute-start.7 = (bf16[200,512]{1,0:T(8,128)(2,1)S(1)}, bf16[200,512]{1,0:T(8,128)(2,1)S(1)}, u32[]{:S(2)}, u32[]{:S(2)}) collective-permute-start(bf16[200,512]{1,0:T(8,128)(2,1)S(1)} %constant_dynamic-update-slice_fusion.echo), channel_id=1, source_target_pairs={{8,0},{9,1},{10,2},{11,3},{12,4},{13,5},{14,6},{15,7},{0,8},{1,9},... | collective-permute-start | bytes 614408 | tf_op jit(solution)/shard_map/ppermute | solution.py:38
  37.3 7.6 %shard_map.115 = (bf16[208,256]{1,0:T(8,128)(2,1)S(1)}, bf16[200,512]{1,0:T(8,128)(2,1)S(1)}, bf16[208,512]{1,0:T(8,128)(2,1)S(1)}, f32[40960,128]{1,0:T(8,128)S...) custom-call(s32[12800]{0:T(1024)S(1)} %add_multiply_fusion.own_ids.h, ...), custom_call_target="tpu_custom_call", output_to_operand_aliasing={{3}: (6, {}), {4}: (7, {}), {5}: (8, {})} | custom-call | tf_op jit(solution)/shard_map/pallas_call | solution.py:215
  45.0 1.1 %collective-permute-done.6 = bf16[200,512]{1,0:T(8,128)(2,1)S(1)} collective-permute-done((bf16[200,512]{1,0:T(8,128)(2,1)S(1)}, bf16[200,512]{1,0:T(8,128)(2,1)S(1)}, u32[]{:S(2)}, u32[]{:S(2)}) %collective-permute-start.6) | collective-permute-done | bytes 204832 | tf_op jit(solution)/shard_map/ppermute | solution.py:38
  47.3 2.4 %collective-permute-start.10 = (bf16[208,256]{1,0:T(8,128)(2,1)S(1)}, bf16[208,256]{1,0:T(8,128)(2,1)S(1)}, u32[]{:S(2)}, u32[]{:S(2)}) collective-permute-start(bf16[208,256]{1,0:T(8,128)(2,1)S(1)} %get-tuple-element.53), channel_id=1, source_target_pairs={{64,0},{65,1},{66,2},{67,3},{68,4},{69,5},{70,6},{71,7},{72,8},{73... | collective-permute-start | bytes 319496 | tf_op jit(solution)/shard_map/ppermute | solution.py:38
  49.6 2.5 %collective-permute-start.9 = (bf16[208,256]{1,0:T(8,128)(2,1)S(1)}, bf16[208,256]{1,0:T(8,128)(2,1)S(1)}, u32[]{:S(2)}, u32[]{:S(2)}) collective-permute-start(bf16[208,256]{1,0:T(8,128)(2,1)S(1)} %get-tuple-element.53), channel_id=1, source_target_pairs={{32,0},{33,1},{34,2},{35,3},{36,4},{37,5},{38,6},{39,7},{40,8},{41... | collective-permute-start | bytes 319496 | tf_op jit(solution)/shard_map/ppermute | solution.py:38
  52.2 3.8 %shard_map.116 = (f32[2,200,512]{2,1,0:T(8,128)S(1)}, f32[200,2048]{1,0:T(8,128)S(1)}) custom-call(s32[1]{0:T(128)} %bitcast.me, bf16[200,2048]{1,0:T(8,128)(2,1)S(1)} %constant_dynamic-update-slice_fusion.4.slab, bf16[208,512]{1,0:T(8,128)(2,1)S(1)} %get-tuple-element.48.refs_0_, bf16[208,256]{1,0:T(8,128)(2,1)S(1)} %collective-permute-done.3.refs_1_, ...), custom_call_target="tpu_custom_call" | custom-call | tf_op jit(solution)/shard_map/pallas_call | solution.py:358
  56.0 1.7 %collective-permute-done.10.refs_4_.refs_1_ = bf16[208,256]{1,0:T(8,128)(2,1)S(1)} collective-permute-done((bf16[208,256]{1,0:T(8,128)(2,1)S(1)}, bf16[208,256]{1,0:T(8,128)(2,1)S(1)}, u32[]{:S(2)}, u32[]{:S(2)}) %collective-permute-start.10) | collective-permute-done | bytes 106528 | tf_op jit(solution)/shard_map/ppermute | solution.py:38
  57.7 6.9 %shard_map.117 = (f32[4,200,512]{2,1,0:T(8,128)S(1)}, bf16[200,2048]{1,0:T(8,128)(2,1)S(1)}) custom-call(s32[1]{0:T(128)} %bitcast.me, bf16[200,2048]{1,0:T(8,128)(2,1)S(1)} %collective-permute-done.11.slab, bf16[208,512]{1,0:T(8,128)(2,1)S(1)} %get-tuple-element.48.refs_0_, bf16[208,256]{1,0:T(8,128)(2,1)S(1)} %collective-permute-done.3.refs_1_, ...), custom_call_target="tpu_custom_call" | custom-call | tf_op jit(solution)/shard_map/pallas_call | solution.py:358
  65.0 2.8 %shard_map.118 = (f32[4,200,512]{2,1,0:T(8,128)S(1)}, f32[200,1536]{1,0:T(8,128)S(1)}) custom-call(s32[1]{0:T(128)} %bitcast.me, bf16[200,2048]{1,0:T(8,128)(2,1)S(1)} %constant_dynamic-update-slice_fusion.4.slab, bf16[208,256]{1,0:T(8,128)(2,1)S(1)} %collective-permute-done.9.refs_3_.refs_0_, ...), custom_call_target="tpu_custom_call", output_to_operand_aliasing={{0}: (5, {})} | custom-call | tf_op jit(solution)/shard_map/pallas_call | solution.py:358
  69.3 2.2 %collective-permute-start.14 = (bf16[200,512]{1,0:T(8,128)(2,1)S(1)}, bf16[200,512]{1,0:T(8,128)(2,1)S(1)}, u32[]{:S(2)}, u32[]{:S(2)}) collective-permute-start(bf16[200,512]{1,0:T(8,128)(2,1)S(1)} %get-tuple-element.72), channel_id=1, source_target_pairs={{4,0},{5,1},{6,2},{7,3},{8,4},{9,5},{10,6},{11,7},{12,8},{13,9},{1... | collective-permute-start | bytes 614408 | tf_op jit(solution)/shard_map/ppermute | solution.py:38
  71.5 1.2 %shard_map.119 = (f32[200,512]{1,0:T(8,128)S(1)}, bf16[200,512]{1,0:T(8,128)(2,1)S(1)}, bf16[200,512]{1,0:T(8,128)(2,1)S(1)}, bf16[200,512]{1,0:T(8,128)(2,1)S(1)}, f32[200,512]{1,0:T(8,128)S(1)}) custom-call(s32[1]{0:T(128)} %bitcast.me, bf16[200,2048]{1,0:T(8,128)(2,1)S(1)} %constant_dynamic-update-slice_fusion.4.slab, ...), custom_call_target="tpu_custom_call" | custom-call | tf_op jit(solution)/shard_map/pallas_call | solution.py:358
  72.7 3.2 %collective-permute-start.20 = (bf16[200,512]{1,0:T(8,128)(2,1)S(1)}, bf16[200,512]{1,0:T(8,128)(2,1)S(1)}, u32[]{:S(2)}, u32[]{:S(2)}) collective-permute-start(bf16[200,512]{1,0:T(8,128)(2,1)S(1)} %get-tuple-element.66), channel_id=1, source_target_pairs={{32,0},{33,1},{34,2},{35,3},{36,4},{37,5},{38,6},{39,7},{40,8},{41... | collective-permute-start | bytes 614408 | tf_op jit(solution)/shard_map/ppermute | solution.py:38
  76.0 5.4 %collective-permute-done.13 = bf16[200,512]{1,0:T(8,128)(2,1)S(1)} collective-permute-done((bf16[200,512]{1,0:T(8,128)(2,1)S(1)}, bf16[200,512]{1,0:T(8,128)(2,1)S(1)}, u32[]{:S(2)}, u32[]{:S(2)}) %collective-permute-start.13) | collective-permute-done | bytes 204832 | tf_op jit(solution)/shard_map/ppermute | solution.py:38
  81.3 1.7 %collective-permute-start.21 = (bf16[200,512]{1,0:T(8,128)(2,1)S(1)}, bf16[200,512]{1,0:T(8,128)(2,1)S(1)}, u32[]{:S(2)}, u32[]{:S(2)}) collective-permute-start(bf16[200,512]{1,0:T(8,128)(2,1)S(1)} %get-tuple-element.67), channel_id=1, source_target_pairs={{64,0},{65,1},{66,2},{67,3},{68,4},{69,5},{70,6},{71,7},{72,8},{73... | collective-permute-start | bytes 614408 | tf_op jit(solution)/shard_map/ppermute | solution.py:38
  83.3 1.9 %collective-permute-start.16 = (bf16[200,128]{1,0:T(8,128)(2,1)S(1)}, bf16[200,128]{1,0:T(8,128)(2,1)S(1)}, u32[]{:S(2)}, u32[]{:S(2)}) collective-permute-start(bf16[200,128]{1,0:T(8,128)(2,1)S(1)} %get-tuple-element.73), channel_id=1, source_target_pairs={{18,0},{19,1},{16,2},{17,3},{22,4},{23,5},{20,6},{21,7},{26,8},{27... | collective-permute-start | bytes 153608 | tf_op jit(solution)/shard_map/ppermute | solution.py:38
  85.1 1.4 %collective-permute-start.17 = (bf16[200,128]{1,0:T(8,128)(2,1)S(1)}, bf16[200,128]{1,0:T(8,128)(2,1)S(1)}, u32[]{:S(2)}, u32[]{:S(2)}) collective-permute-start(bf16[200,128]{1,0:T(8,128)(2,1)S(1)} %get-tuple-element.75), channel_id=1, source_target_pairs={{16,0},{17,1},{18,2},{19,3},{20,4},{21,5},{22,6},{23,7},{24,8},{25... | collective-permute-start | bytes 153608 | tf_op jit(solution)/shard_map/ppermute | solution.py:38
  87.3 2.2 %collective-permute-done.21 = bf16[200,512]{1,0:T(8,128)(2,1)S(1)} collective-permute-done((bf16[200,512]{1,0:T(8,128)(2,1)S(1)}, bf16[200,512]{1,0:T(8,128)(2,1)S(1)}, u32[]{:S(2)}, u32[]{:S(2)}) %collective-permute-start.21) | collective-permute-done | bytes 204832 | tf_op jit(solution)/shard_map/ppermute | solution.py:38
  90.4 1.8 %collective-permute-done.18 = bf16[200,128]{1,0:T(8,128)(2,1)S(1)} collective-permute-done((bf16[200,128]{1,0:T(8,128)(2,1)S(1)}, bf16[200,128]{1,0:T(8,128)(2,1)S(1)}, u32[]{:S(2)}, u32[]{:S(2)}) %collective-permute-start.18) | collective-permute-done | bytes 51232 | tf_op jit(solution)/shard_map/ppermute | solution.py:38
  (52 shorter events, 7.8 us)
Async XLA Ops:
  2.8 17.3 %copy-start.2 = (s32[512,4]{0,1:T(4,128)S(1)}, s32[512,4]{0,1:T(4,128)}, u32[]{:S(2)}) copy-start(s32[512,4]{0,1:T(4,128)} %param.15) | copy-start | bytes 24580
  2.8 17.3 %copy-start.3 = (s32[512]{0:T(512)S(1)}, s32[512]{0:T(512)}, u32[]{:S(2)}) copy-start(s32[512]{0:T(512)} %param.14) | copy-start | bytes 6148
  15.0 16.9 %collective-permute-start = (bf16[200,128]{1,0:T(8,128)(2,1)S(1)}, bf16[200,128]{1,0:T(8,128)(2,1)S(1)}, u32[]{:S(2)}, u32[]{:S(2)}) collective-permute-start(bf16[200,128]{1,0:T(8,128)(2,1)S(1)} %get-tuple-element.35.echo), channel_id=1, source_target_pairs={{16,0},{17,1},{18,2},{19,3},{20,4},{21,5},{22,6},{23,7},{24,8},{25... | collective-permute-start | bytes 153608 | tf_op jit(solution)/shard_map/ppermute | solution.py:38
  17.9 14.0 %collective-permute-start.1 = (bf16[200,128]{1,0:T(8,128)(2,1)S(1)}, bf16[200,128]{1,0:T(8,128)(2,1)S(1)}, u32[]{:S(2)}, u32[]{:S(2)}) collective-permute-start(bf16[200,128]{1,0:T(8,128)(2,1)S(1)} %get-tuple-element.35.echo), channel_id=1, source_target_pairs={{18,0},{19,1},{16,2},{17,3},{22,4},{23,5},{20,6},{21,7},{26,8},{27... | collective-permute-start | bytes 153608 | tf_op jit(solution)/shard_map/ppermute | solution.py:38
  17.9 14.1 %collective-permute-start.2 = (bf16[200,128]{1,0:T(8,128)(2,1)S(1)}, bf16[200,128]{1,0:T(8,128)(2,1)S(1)}, u32[]{:S(2)}, u32[]{:S(2)}) collective-permute-start(bf16[200,128]{1,0:T(8,128)(2,1)S(1)} %get-tuple-element.35.echo), channel_id=1, source_target_pairs={{2,0},{3,1},{0,2},{1,3},{6,4},{7,5},{4,6},{5,7},{10,8},{11,9},{8,1... | collective-permute-start | bytes 153608 | tf_op jit(solution)/shard_map/ppermute | solution.py:38
  27.8 17.1 %collective-permute-start.3 = (bf16[208,256]{1,0:T(8,128)(2,1)S(1)}, bf16[208,256]{1,0:T(8,128)(2,1)S(1)}, u32[]{:S(2)}, u32[]{:S(2)}) collective-permute-start(bf16[208,256]{1,0:T(8,128)(2,1)S(1)} %get-tuple-element.43.refs_0_), channel_id=1, source_target_pairs={{32,0},{33,1},{34,2},{35,3},{36,4},{37,5},{38,6},{39,7},{40,8},{41... | collective-permute-start | bytes 319496 | tf_op jit(solution)/shard_map/ppermute | solution.py:38
  31.9 13.0 %collective-permute-start.4 = (bf16[208,256]{1,0:T(8,128)(2,1)S(1)}, bf16[208,256]{1,0:T(8,128)(2,1)S(1)}, u32[]{:S(2)}, u32[]{:S(2)}) collective-permute-start(bf16[208,256]{1,0:T(8,128)(2,1)S(1)} %get-tuple-element.43.refs_0_), channel_id=1, source_target_pairs={{64,0},{65,1},{66,2},{67,3},{68,4},{69,5},{70,6},{71,7},{72,8},{73... | collective-permute-start | bytes 319496 | tf_op jit(solution)/shard_map/ppermute | solution.py:38
  32.0 12.9 %collective-permute-start.5 = (bf16[200,512]{1,0:T(8,128)(2,1)S(1)}, bf16[200,512]{1,0:T(8,128)(2,1)S(1)}, u32[]{:S(2)}, u32[]{:S(2)}) collective-permute-start(bf16[200,512]{1,0:T(8,128)(2,1)S(1)} %constant_dynamic-update-slice_fusion.echo), channel_id=1, source_target_pairs={{4,0},{5,1},{6,2},{7,3},{8,4},{9,5},{10,6},{11,7},{12,8},{13,9},{1... | collective-permute-start | bytes 614408 | tf_op jit(solution)/shard_map/ppermute | solution.py:38
  35.1 11.0 %collective-permute-start.6 = (bf16[200,512]{1,0:T(8,128)(2,1)S(1)}, bf16[200,512]{1,0:T(8,128)(2,1)S(1)}, u32[]{:S(2)}, u32[]{:S(2)}) collective-permute-start(bf16[200,512]{1,0:T(8,128)(2,1)S(1)} %constant_dynamic-update-slice_fusion.echo), channel_id=1, source_target_pairs={{12,0},{13,1},{14,2},{15,3},{0,4},{1,5},{2,6},{3,7},{4,8},{5,9},{6... | collective-permute-start | bytes 614408 | tf_op jit(solution)/shard_map/ppermute | solution.py:38
  35.1 11.0 %collective-permute-start.7 = (bf16[200,512]{1,0:T(8,128)(2,1)S(1)}, bf16[200,512]{1,0:T(8,128)(2,1)S(1)}, u32[]{:S(2)}, u32[]{:S(2)}) collective-permute-start(bf16[200,512]{1,0:T(8,128)(2,1)S(1)} %constant_dynamic-update-slice_fusion.echo), channel_id=1, source_target_pairs={{8,0},{9,1},{10,2},{11,3},{12,4},{13,5},{14,6},{15,7},{0,8},{1,9},... | collective-permute-start | bytes 614408 | tf_op jit(solution)/shard_map/ppermute | solution.py:38
  46.1 11.5 %collective-permute-start.11 = (bf16[200,2048]{1,0:T(8,128)(2,1)S(1)}, bf16[200,2048]{1,0:T(8,128)(2,1)S(1)}, u32[]{:S(2)}, u32[]{:S(2)}) collective-permute-start(bf16[200,2048]{1,0:T(8,128)(2,1)S(1)} %constant_dynamic-update-slice_fusion.4.slab), channel_id=1, source_target_pairs={{1,0},{0,1},{3,2},{2,3},{5,4},{4,5},{7,6},{6,7},{9,8},{8,9},{11,10... | collective-permute-start | bytes 2457608 | tf_op jit(solution)/shard_map/ppermute | solution.py:38
  46.2 11.4 %collective-permute-start.8 = (bf16[208,512]{1,0:T(8,128)(2,1)S(1)}, bf16[208,512]{1,0:T(8,128)(2,1)S(1)}, u32[]{:S(2)}, u32[]{:S(2)}) collective-permute-start(bf16[208,512]{1,0:T(8,128)(2,1)S(1)} %get-tuple-element.48.refs_0_), channel_id=1, source_target_pairs={{96,0},{97,1},{98,2},{99,3},{100,4},{101,5},{102,6},{103,7},{104,8... | collective-permute-start | bytes 638984 | tf_op jit(solution)/shard_map/ppermute | solution.py:38
  47.3 10.4 %collective-permute-start.10 = (bf16[208,256]{1,0:T(8,128)(2,1)S(1)}, bf16[208,256]{1,0:T(8,128)(2,1)S(1)}, u32[]{:S(2)}, u32[]{:S(2)}) collective-permute-start(bf16[208,256]{1,0:T(8,128)(2,1)S(1)} %get-tuple-element.53), channel_id=1, source_target_pairs={{64,0},{65,1},{66,2},{67,3},{68,4},{69,5},{70,6},{71,7},{72,8},{73... | collective-permute-start | bytes 319496 | tf_op jit(solution)/shard_map/ppermute | solution.py:38
  49.6 8.0 %collective-permute-start.9 = (bf16[208,256]{1,0:T(8,128)(2,1)S(1)}, bf16[208,256]{1,0:T(8,128)(2,1)S(1)}, u32[]{:S(2)}, u32[]{:S(2)}) collective-permute-start(bf16[208,256]{1,0:T(8,128)(2,1)S(1)} %get-tuple-element.53), channel_id=1, source_target_pairs={{32,0},{33,1},{34,2},{35,3},{36,4},{37,5},{38,6},{39,7},{40,8},{41... | collective-permute-start | bytes 319496 | tf_op jit(solution)/shard_map/ppermute | solution.py:38
  64.6 3.2 %collective-permute-start.12 = (bf16[200,2048]{1,0:T(8,128)(2,1)S(1)}, bf16[200,2048]{1,0:T(8,128)(2,1)S(1)}, u32[]{:S(2)}, u32[]{:S(2)}) collective-permute-start(bf16[200,2048]{1,0:T(8,128)(2,1)S(1)} %get-tuple-element.62), channel_id=1, source_target_pairs={{1,0},{0,1},{3,2},{2,3},{5,4},{4,5},{7,6},{6,7},{9,8},{8,9},{11,10... | collective-permute-start | bytes 2457608 | tf_op jit(solution)/shard_map/ppermute | solution.py:38
  68.2 13.1 %collective-permute-start.13 = (bf16[200,512]{1,0:T(8,128)(2,1)S(1)}, bf16[200,512]{1,0:T(8,128)(2,1)S(1)}, u32[]{:S(2)}, u32[]{:S(2)}) collective-permute-start(bf16[200,512]{1,0:T(8,128)(2,1)S(1)} %get-tuple-element.70), channel_id=1, source_target_pairs={{12,0},{13,1},{14,2},{15,3},{0,4},{1,5},{2,6},{3,7},{4,8},{5,9},{6... | collective-permute-start | bytes 614408 | tf_op jit(solution)/shard_map/ppermute | solution.py:38
  69.3 13.8 %collective-permute-start.14 = (bf16[200,512]{1,0:T(8,128)(2,1)S(1)}, bf16[200,512]{1,0:T(8,128)(2,1)S(1)}, u32[]{:S(2)}, u32[]{:S(2)}) collective-permute-start(bf16[200,512]{1,0:T(8,128)(2,1)S(1)} %get-tuple-element.72), channel_id=1, source_target_pairs={{4,0},{5,1},{6,2},{7,3},{8,4},{9,5},{10,6},{11,7},{12,8},{13,9},{1... | collective-permute-start | bytes 614408 | tf_op jit(solution)/shard_map/ppermute | solution.py:38
  71.5 11.6 %collective-permute-start.15 = (bf16[200,512]{1,0:T(8,128)(2,1)S(1)}, bf16[200,512]{1,0:T(8,128)(2,1)S(1)}, u32[]{:S(2)}, u32[]{:S(2)}) collective-permute-start(bf16[200,512]{1,0:T(8,128)(2,1)S(1)} %get-tuple-element.71), channel_id=1, source_target_pairs={{8,0},{9,1},{10,2},{11,3},{12,4},{13,5},{14,6},{15,7},{0,8},{1,9},... | collective-permute-start | bytes 614408 | tf_op jit(solution)/shard_map/ppermute | solution.py:38
  72.6 13.9 %collective-permute-start.19 = (bf16[200,512]{1,0:T(8,128)(2,1)S(1)}, bf16[200,512]{1,0:T(8,128)(2,1)S(1)}, u32[]{:S(2)}, u32[]{:S(2)}) collective-permute-start(bf16[200,512]{1,0:T(8,128)(2,1)S(1)} %get-tuple-element.65), channel_id=1, source_target_pairs={{96,0},{97,1},{98,2},{99,3},{100,4},{101,5},{102,6},{103,7},{104,8... | collective-permute-start | bytes 614408 | tf_op jit(solution)/shard_map/ppermute | solution.py:38
  72.7 14.6 %collective-permute-start.20 = (bf16[200,512]{1,0:T(8,128)(2,1)S(1)}, bf16[200,512]{1,0:T(8,128)(2,1)S(1)}, u32[]{:S(2)}, u32[]{:S(2)}) collective-permute-start(bf16[200,512]{1,0:T(8,128)(2,1)S(1)} %get-tuple-element.66), channel_id=1, source_target_pairs={{32,0},{33,1},{34,2},{35,3},{36,4},{37,5},{38,6},{39,7},{40,8},{41... | collective-permute-start | bytes 614408 | tf_op jit(solution)/shard_map/ppermute | solution.py:38
  81.3 8.2 %collective-permute-start.21 = (bf16[200,512]{1,0:T(8,128)(2,1)S(1)}, bf16[200,512]{1,0:T(8,128)(2,1)S(1)}, u32[]{:S(2)}, u32[]{:S(2)}) collective-permute-start(bf16[200,512]{1,0:T(8,128)(2,1)S(1)} %get-tuple-element.67), channel_id=1, source_target_pairs={{64,0},{65,1},{66,2},{67,3},{68,4},{69,5},{70,6},{71,7},{72,8},{73... | collective-permute-start | bytes 614408 | tf_op jit(solution)/shard_map/ppermute | solution.py:38
  83.3 7.1 %collective-permute-start.16 = (bf16[200,128]{1,0:T(8,128)(2,1)S(1)}, bf16[200,128]{1,0:T(8,128)(2,1)S(1)}, u32[]{:S(2)}, u32[]{:S(2)}) collective-permute-start(bf16[200,128]{1,0:T(8,128)(2,1)S(1)} %get-tuple-element.73), channel_id=1, source_target_pairs={{18,0},{19,1},{16,2},{17,3},{22,4},{23,5},{20,6},{21,7},{26,8},{27... | collective-permute-start | bytes 153608 | tf_op jit(solution)/shard_map/ppermute | solution.py:38
  85.1 5.2 %collective-permute-start.17 = (bf16[200,128]{1,0:T(8,128)(2,1)S(1)}, bf16[200,128]{1,0:T(8,128)(2,1)S(1)}, u32[]{:S(2)}, u32[]{:S(2)}) collective-permute-start(bf16[200,128]{1,0:T(8,128)(2,1)S(1)} %get-tuple-element.75), channel_id=1, source_target_pairs={{16,0},{17,1},{18,2},{19,3},{20,4},{21,5},{22,6},{23,7},{24,8},{25... | collective-permute-start | bytes 153608 | tf_op jit(solution)/shard_map/ppermute | solution.py:38
  86.6 5.6 %collective-permute-start.18 = (bf16[200,128]{1,0:T(8,128)(2,1)S(1)}, bf16[200,128]{1,0:T(8,128)(2,1)S(1)}, u32[]{:S(2)}, u32[]{:S(2)}) collective-permute-start(bf16[200,128]{1,0:T(8,128)(2,1)S(1)} %get-tuple-element.74), channel_id=1, source_target_pairs={{2,0},{3,1},{0,2},{1,3},{6,4},{7,5},{4,6},{5,7},{10,8},{11,9},{8,1... | collective-permute-start | bytes 153608 | tf_op jit(solution)/shard_map/ppermute | solution.py:38
  (3 other events, 35.4 us)

commit v9 on v8

--- a/solution.py
+++ b/solution.py
@@ -13,7 +13,7 @@
 F32 = jnp.float32
 LANES = 128
 WIDE = 256
-CHUNK = 4096
+CHUNK = 5120
 UNROLL = 256
 SPAN = 512
 VMEM_BYTES = 12 * 1024 * 1024
@@ -422,12 +422,12 @@
 
     ents = [ents[:, k * span : (k + 1) * span] for k in range(3)]
     ents = [slab_sum(part, k + 1).astype(BF16) for k, part in enumerate(ents)]
-    ents = [moved(part, dy=-d) for d, part in zip(FAR, ents)]
+    ents = [moved(part, dy=-d) for d, part in zip((3, 1, 2), (ents[1], ents[0], ents[2]))]
     query_total, *sums, ent_row = score(me, slab, blocks[2:], (0,), 3, entities, asks)
     ent_row = slab_sum(ent_row, 0)
     for ent in ents:
         ent_row = ent_row + ent.astype(F32)
-    for d, part in zip(FAR, sums):
+    for d, part in zip((1, 2, 3), (sums[0], sums[2], sums[1])):
         query_total = query_total + moved(part, dz=-d).astype(F32)
     ent_share = ent_row[:, :width]
     for k, d in enumerate(FAR):

time: 93.2 us -> 91.4 us (0.981)
  starting transfers between devices: 33.3 us -> 31.8 us
    ppermute x22, starting transfers between devices: 33.3 us -> 31.8 us  [moved(): return lax.ppermute(block, AXES, route)]
  transfers between devices with their start and end apart: 22 -> 22, of which waited for: 5 -> 7; matrix products, arithmetic and copies ran while one was open for 1% -> 1% of each run, Pallas kernels for 25% -> 25%
where the time goes in v9:
time: 91.4 us; the launch traced here: 90.9 us
  Pallas kernels  41.5 us (45%)
  starting transfers between devices  31.8 us (35%)
  waiting for transfers between devices  12.3 us (13%)
  other arithmetic  2.8 us (3%)
  local copies, waits for them, and re-layouts  1.65 us (2%)
    ppermute x22, starting transfers between devices, moved(): return lax.ppermute(block, AXES, route)  31.8 us
    pallas_call x2, Pallas kernels, encode_heads(): pl.pallas_call(functools.partial(head_kernel, chunk * heads, heads), in_s...  15.2 us
    pallas_call x4, Pallas kernels, score(): pl.pallas_call(functools.partial(score_kernel, plain, plain - 1.8, depth,...  14.8 us
    ppermute x22, waiting for transfers between devices, moved(): return lax.ppermute(block, AXES, route)  12.3 us
    pallas_call x1, Pallas kernels, encode_entities(): pl.pallas_call(functools.partial(entity_kernel, relations, steps, scale),...  11.6 us
  transfers between devices with their start and end apart: 22, of which 7 were waited for; matrix products, arithmetic and copies ran while one was open for 1% of the time, Pallas kernels for 25%

profile of v9, /device:TPU:0, one launch (start us, length us, event | category | flops | bytes accessed | tf_op | source)
XLA Modules:
  0.0 90.9 jit_solution(14558808861241335748)
XLA Ops:
  2.8 11.6 %shard_map.113 = (bf16[200,128]{1,0:T(8,128)(2,1)S(1)}, f32[40960,128]{1,0:T(8,128)S(1)}, bf16[200,6400]{1,0:T(8,128)(2,1)S(1)}, bf16[256,896]{1,0:T(8,128)(2,1)S(1)}) custom-call(s32[12800]{0:T(1024)S(1)} %add_multiply_fusion.own_ids.head_ids, bf16[200,20000]{1,0:T(8,128)(2,1)} %bitcast.21, bf16[200,5000]{1,0:T(8,128)(2,1)} %bitcast.22, ...), custom_call_target="tpu_custom_call" | custom-call | tf_op jit(solution)/shard_map/pallas_call | solution.py:179
  14.4 2.9 %collective-permute-start = (bf16[200,128]{1,0:T(8,128)(2,1)S(1)}, bf16[200,128]{1,0:T(8,128)(2,1)S(1)}, u32[]{:S(2)}, u32[]{:S(2)}) collective-permute-start(bf16[200,128]{1,0:T(8,128)(2,1)S(1)} %get-tuple-element.35.echo), channel_id=1, source_target_pairs={{16,0},{17,1},{18,2},{19,3},{20,4},{21,5},{22,6},{23,7},{24,8},{25... | collective-permute-start | bytes 153608 | tf_op jit(solution)/shard_map/ppermute | solution.py:38
  17.3 2.3 %collective-permute-start.2 = (bf16[200,128]{1,0:T(8,128)(2,1)S(1)}, bf16[200,128]{1,0:T(8,128)(2,1)S(1)}, u32[]{:S(2)}, u32[]{:S(2)}) collective-permute-start(bf16[200,128]{1,0:T(8,128)(2,1)S(1)} %get-tuple-element.35.echo), channel_id=1, source_target_pairs={{2,0},{3,1},{0,2},{1,3},{6,4},{7,5},{4,6},{5,7},{10,8},{11,9},{8,1... | collective-permute-start | bytes 153608 | tf_op jit(solution)/shard_map/ppermute | solution.py:38
  19.6 7.6 %shard_map.114 = (bf16[208,256]{1,0:T(8,128)(2,1)S(1)}, bf16[200,128]{1,0:T(8,128)(2,1)S(1)}, f32[40960,128]{1,0:T(8,128)S(1)}, bf16[200,6400]{1,0:T(8,128)(2,1)S(1)}, bf16[256,896]{1,0:T(8,128)(2,1)S(1)}) custom-call(s32[12800]{0:T(1024)S(1)} %add_multiply_fusion.own_ids.head_ids, ...), custom_call_target="tpu_custom_call", output_to_operand_aliasing={{2}: (6, {}), {3}: (7, {}), {4}: (8, {})} | custom-call | tf_op jit(solution)/shard_map/pallas_call | solution.py:215
  27.2 4.1 %collective-permute-start.3 = (bf16[208,256]{1,0:T(8,128)(2,1)S(1)}, bf16[208,256]{1,0:T(8,128)(2,1)S(1)}, u32[]{:S(2)}, u32[]{:S(2)}) collective-permute-start(bf16[208,256]{1,0:T(8,128)(2,1)S(1)} %get-tuple-element.43.refs_0_), channel_id=1, source_target_pairs={{32,0},{33,1},{34,2},{35,3},{36,4},{37,5},{38,6},{39,7},{40,8},{41... | collective-permute-start | bytes 319496 | tf_op jit(solution)/shard_map/ppermute | solution.py:38
  31.4 3.1 %collective-permute-start.5 = (bf16[200,512]{1,0:T(8,128)(2,1)S(1)}, bf16[200,512]{1,0:T(8,128)(2,1)S(1)}, u32[]{:S(2)}, u32[]{:S(2)}) collective-permute-start(bf16[200,512]{1,0:T(8,128)(2,1)S(1)} %constant_dynamic-update-slice_fusion.echo), channel_id=1, source_target_pairs={{4,0},{5,1},{6,2},{7,3},{8,4},{9,5},{10,6},{11,7},{12,8},{13,9},{1... | collective-permute-start | bytes 614408 | tf_op jit(solution)/shard_map/ppermute | solution.py:38
  34.5 2.2 %collective-permute-start.7 = (bf16[200,512]{1,0:T(8,128)(2,1)S(1)}, bf16[200,512]{1,0:T(8,128)(2,1)S(1)}, u32[]{:S(2)}, u32[]{:S(2)}) collective-permute-start(bf16[200,512]{1,0:T(8,128)(2,1)S(1)} %constant_dynamic-update-slice_fusion.echo), channel_id=1, source_target_pairs={{8,0},{9,1},{10,2},{11,3},{12,4},{13,5},{14,6},{15,7},{0,8},{1,9},... | collective-permute-start | bytes 614408 | tf_op jit(solution)/shard_map/ppermute | solution.py:38
  36.7 7.6 %shard_map.115 = (bf16[208,256]{1,0:T(8,128)(2,1)S(1)}, bf16[200,512]{1,0:T(8,128)(2,1)S(1)}, bf16[208,512]{1,0:T(8,128)(2,1)S(1)}, f32[40960,128]{1,0:T(8,128)S...) custom-call(s32[12800]{0:T(1024)S(1)} %add_multiply_fusion.own_ids.h, ...), custom_call_target="tpu_custom_call", output_to_operand_aliasing={{3}: (6, {}), {4}: (7, {}), {5}: (8, {})} | custom-call | tf_op jit(solution)/shard_map/pallas_call | solution.py:215
  44.4 1.1 %collective-permute-done.6 = bf16[200,512]{1,0:T(8,128)(2,1)S(1)} collective-permute-done((bf16[200,512]{1,0:T(8,128)(2,1)S(1)}, bf16[200,512]{1,0:T(8,128)(2,1)S(1)}, u32[]{:S(2)}, u32[]{:S(2)}) %collective-permute-start.6) | collective-permute-done | bytes 204832 | tf_op jit(solution)/shard_map/ppermute | solution.py:38
  46.7 2.4 %collective-permute-start.10 = (bf16[208,256]{1,0:T(8,128)(2,1)S(1)}, bf16[208,256]{1,0:T(8,128)(2,1)S(1)}, u32[]{:S(2)}, u32[]{:S(2)}) collective-permute-start(bf16[208,256]{1,0:T(8,128)(2,1)S(1)} %get-tuple-element.53), channel_id=1, source_target_pairs={{64,0},{65,1},{66,2},{67,3},{68,4},{69,5},{70,6},{71,7},{72,8},{73... | collective-permute-start | bytes 319496 | tf_op jit(solution)/shard_map/ppermute | solution.py:38
  49.1 2.5 %collective-permute-start.9 = (bf16[208,256]{1,0:T(8,128)(2,1)S(1)}, bf16[208,256]{1,0:T(8,128)(2,1)S(1)}, u32[]{:S(2)}, u32[]{:S(2)}) collective-permute-start(bf16[208,256]{1,0:T(8,128)(2,1)S(1)} %get-tuple-element.53), channel_id=1, source_target_pairs={{32,0},{33,1},{34,2},{35,3},{36,4},{37,5},{38,6},{39,7},{40,8},{41... | collective-permute-start | bytes 319496 | tf_op jit(solution)/shard_map/ppermute | solution.py:38
  51.6 3.8 %shard_map.116 = (f32[2,200,512]{2,1,0:T(8,128)S(1)}, f32[200,2048]{1,0:T(8,128)S(1)}) custom-call(s32[1]{0:T(128)} %bitcast.me, bf16[200,2048]{1,0:T(8,128)(2,1)S(1)} %constant_dynamic-update-slice_fusion.4.slab, bf16[208,512]{1,0:T(8,128)(2,1)S(1)} %get-tuple-element.48.refs_0_, bf16[208,256]{1,0:T(8,128)(2,1)S(1)} %collective-permute-done.3.refs_1_, ...), custom_call_target="tpu_custom_call" | custom-call | tf_op jit(solution)/shard_map/pallas_call | solution.py:358
  55.5 1.6 %collective-permute-done.10.refs_4_.refs_1_ = bf16[208,256]{1,0:T(8,128)(2,1)S(1)} collective-permute-done((bf16[208,256]{1,0:T(8,128)(2,1)S(1)}, bf16[208,256]{1,0:T(8,128)(2,1)S(1)}, u32[]{:S(2)}, u32[]{:S(2)}) %collective-permute-start.10) | collective-permute-done | bytes 106528 | tf_op jit(solution)/shard_map/ppermute | solution.py:38
  57.1 6.9 %shard_map.117 = (f32[4,200,512]{2,1,0:T(8,128)S(1)}, bf16[200,2048]{1,0:T(8,128)(2,1)S(1)}) custom-call(s32[1]{0:T(128)} %bitcast.me, bf16[200,2048]{1,0:T(8,128)(2,1)S(1)} %collective-permute-done.11.slab, bf16[208,512]{1,0:T(8,128)(2,1)S(1)} %get-tuple-element.48.refs_0_, bf16[208,256]{1,0:T(8,128)(2,1)S(1)} %collective-permute-done.3.refs_1_, ...), custom_call_target="tpu_custom_call" | custom-call | tf_op jit(solution)/shard_map/pallas_call | solution.py:358
  64.4 2.8 %shard_map.118 = (f32[4,200,512]{2,1,0:T(8,128)S(1)}, f32[200,1536]{1,0:T(8,128)S(1)}) custom-call(s32[1]{0:T(128)} %bitcast.me, bf16[200,2048]{1,0:T(8,128)(2,1)S(1)} %constant_dynamic-update-slice_fusion.4.slab, bf16[208,256]{1,0:T(8,128)(2,1)S(1)} %collective-permute-done.9.refs_3_.refs_0_, ...), custom_call_target="tpu_custom_call", output_to_operand_aliasing={{0}: (5, {})} | custom-call | tf_op jit(solution)/shard_map/pallas_call | solution.py:358
  68.3 1.4 %collective-permute-start.14 = (bf16[200,512]{1,0:T(8,128)(2,1)S(1)}, bf16[200,512]{1,0:T(8,128)(2,1)S(1)}, u32[]{:S(2)}, u32[]{:S(2)}) collective-permute-start(bf16[200,512]{1,0:T(8,128)(2,1)S(1)} %get-tuple-element.72), channel_id=1, source_target_pairs={{12,0},{13,1},{14,2},{15,3},{0,4},{1,5},{2,6},{3,7},{4,8},{5,9},{6... | collective-permute-start | bytes 614408 | tf_op jit(solution)/shard_map/ppermute | solution.py:38
  70.8 1.2 %shard_map.119 = (f32[200,512]{1,0:T(8,128)S(1)}, bf16[200,512]{1,0:T(8,128)(2,1)S(1)}, bf16[200,512]{1,0:T(8,128)(2,1)S(1)}, bf16[200,512]{1,0:T(8,128)(2,1)S(1)}, f32[200,512]{1,0:T(8,128)S(1)}) custom-call(s32[1]{0:T(128)} %bitcast.me, bf16[200,2048]{1,0:T(8,128)(2,1)S(1)} %constant_dynamic-update-slice_fusion.4.slab, ...), custom_call_target="tpu_custom_call" | custom-call | tf_op jit(solution)/shard_map/pallas_call | solution.py:358
  72.0 2.3 %collective-permute-start.20 = (bf16[200,512]{1,0:T(8,128)(2,1)S(1)}, bf16[200,512]{1,0:T(8,128)(2,1)S(1)}, u32[]{:S(2)}, u32[]{:S(2)}) collective-permute-start(bf16[200,512]{1,0:T(8,128)(2,1)S(1)} %get-tuple-element.66), channel_id=1, source_target_pairs={{64,0},{65,1},{66,2},{67,3},{68,4},{69,5},{70,6},{71,7},{72,8},{73... | collective-permute-start | bytes 614408 | tf_op jit(solution)/shard_map/ppermute | solution.py:38
  74.3 1.2 %collective-permute-done.13 = bf16[200,512]{1,0:T(8,128)(2,1)S(1)} collective-permute-done((bf16[200,512]{1,0:T(8,128)(2,1)S(1)}, bf16[200,512]{1,0:T(8,128)(2,1)S(1)}, u32[]{:S(2)}, u32[]{:S(2)}) %collective-permute-start.13) | collective-permute-done | bytes 204832 | tf_op jit(solution)/shard_map/ppermute | solution.py:38
  76.5 4.6 %collective-permute-done.14 = bf16[200,512]{1,0:T(8,128)(2,1)S(1)} collective-permute-done((bf16[200,512]{1,0:T(8,128)(2,1)S(1)}, bf16[200,512]{1,0:T(8,128)(2,1)S(1)}, u32[]{:S(2)}, u32[]{:S(2)}) %collective-permute-start.14) | collective-permute-done | bytes 204832 | tf_op jit(solution)/shard_map/ppermute | solution.py:38
  81.3 1.8 %collective-permute-start.16 = (bf16[200,128]{1,0:T(8,128)(2,1)S(1)}, bf16[200,128]{1,0:T(8,128)(2,1)S(1)}, u32[]{:S(2)}, u32[]{:S(2)}) collective-permute-start(bf16[200,128]{1,0:T(8,128)(2,1)S(1)} %get-tuple-element.73), channel_id=1, source_target_pairs={{18,0},{19,1},{16,2},{17,3},{22,4},{23,5},{20,6},{21,7},{26,8},{27... | collective-permute-start | bytes 153608 | tf_op jit(solution)/shard_map/ppermute | solution.py:38
  83.2 1.5 %collective-permute-start.17 = (bf16[200,128]{1,0:T(8,128)(2,1)S(1)}, bf16[200,128]{1,0:T(8,128)(2,1)S(1)}, u32[]{:S(2)}, u32[]{:S(2)}) collective-permute-start(bf16[200,128]{1,0:T(8,128)(2,1)S(1)} %get-tuple-element.75), channel_id=1, source_target_pairs={{16,0},{17,1},{18,2},{19,3},{20,4},{21,5},{22,6},{23,7},{24,8},{25... | collective-permute-start | bytes 153608 | tf_op jit(solution)/shard_map/ppermute | solution.py:38
  84.7 1.1 %collective-permute-start.18 = (bf16[200,128]{1,0:T(8,128)(2,1)S(1)}, bf16[200,128]{1,0:T(8,128)(2,1)S(1)}, u32[]{:S(2)}, u32[]{:S(2)}) collective-permute-start(bf16[200,128]{1,0:T(8,128)(2,1)S(1)} %get-tuple-element.74), channel_id=1, source_target_pairs={{2,0},{3,1},{0,2},{1,3},{6,4},{7,5},{4,6},{5,7},{10,8},{11,9},{8,1... | collective-permute-start | bytes 153608 | tf_op jit(solution)/shard_map/ppermute | solution.py:38
  87.3 3.0 %collective-permute-done.18 = bf16[200,128]{1,0:T(8,128)(2,1)S(1)} collective-permute-done((bf16[200,128]{1,0:T(8,128)(2,1)S(1)}, bf16[200,128]{1,0:T(8,128)(2,1)S(1)}, u32[]{:S(2)}, u32[]{:S(2)}) %collective-permute-start.18) | collective-permute-done | bytes 51232 | tf_op jit(solution)/shard_map/ppermute | solution.py:38
  (52 shorter events, 9.4 us)
Async XLA Ops:
  2.8 16.8 %copy-start.2 = (s32[512,4]{0,1:T(4,128)S(1)}, s32[512,4]{0,1:T(4,128)}, u32[]{:S(2)}) copy-start(s32[512,4]{0,1:T(4,128)} %param.15) | copy-start | bytes 24580
  2.8 16.8 %copy-start.3 = (s32[512]{0:T(512)S(1)}, s32[512]{0:T(512)}, u32[]{:S(2)}) copy-start(s32[512]{0:T(512)} %param.14) | copy-start | bytes 6148
  14.4 16.9 %collective-permute-start = (bf16[200,128]{1,0:T(8,128)(2,1)S(1)}, bf16[200,128]{1,0:T(8,128)(2,1)S(1)}, u32[]{:S(2)}, u32[]{:S(2)}) collective-permute-start(bf16[200,128]{1,0:T(8,128)(2,1)S(1)} %get-tuple-element.35.echo), channel_id=1, source_target_pairs={{16,0},{17,1},{18,2},{19,3},{20,4},{21,5},{22,6},{23,7},{24,8},{25... | collective-permute-start | bytes 153608 | tf_op jit(solution)/shard_map/ppermute | solution.py:38
  17.3 14.0 %collective-permute-start.1 = (bf16[200,128]{1,0:T(8,128)(2,1)S(1)}, bf16[200,128]{1,0:T(8,128)(2,1)S(1)}, u32[]{:S(2)}, u32[]{:S(2)}) collective-permute-start(bf16[200,128]{1,0:T(8,128)(2,1)S(1)} %get-tuple-element.35.echo), channel_id=1, source_target_pairs={{18,0},{19,1},{16,2},{17,3},{22,4},{23,5},{20,6},{21,7},{26,8},{27... | collective-permute-start | bytes 153608 | tf_op jit(solution)/shard_map/ppermute | solution.py:38
  17.3 14.1 %collective-permute-start.2 = (bf16[200,128]{1,0:T(8,128)(2,1)S(1)}, bf16[200,128]{1,0:T(8,128)(2,1)S(1)}, u32[]{:S(2)}, u32[]{:S(2)}) collective-permute-start(bf16[200,128]{1,0:T(8,128)(2,1)S(1)} %get-tuple-element.35.echo), channel_id=1, source_target_pairs={{2,0},{3,1},{0,2},{1,3},{6,4},{7,5},{4,6},{5,7},{10,8},{11,9},{8,1... | collective-permute-start | bytes 153608 | tf_op jit(solution)/shard_map/ppermute | solution.py:38
  27.2 17.1 %collective-permute-start.3 = (bf16[208,256]{1,0:T(8,128)(2,1)S(1)}, bf16[208,256]{1,0:T(8,128)(2,1)S(1)}, u32[]{:S(2)}, u32[]{:S(2)}) collective-permute-start(bf16[208,256]{1,0:T(8,128)(2,1)S(1)} %get-tuple-element.43.refs_0_), channel_id=1, source_target_pairs={{32,0},{33,1},{34,2},{35,3},{36,4},{37,5},{38,6},{39,7},{40,8},{41... | collective-permute-start | bytes 319496 | tf_op jit(solution)/shard_map/ppermute | solution.py:38
  31.3 13.0 %collective-permute-start.4 = (bf16[208,256]{1,0:T(8,128)(2,1)S(1)}, bf16[208,256]{1,0:T(8,128)(2,1)S(1)}, u32[]{:S(2)}, u32[]{:S(2)}) collective-permute-start(bf16[208,256]{1,0:T(8,128)(2,1)S(1)} %get-tuple-element.43.refs_0_), channel_id=1, source_target_pairs={{64,0},{65,1},{66,2},{67,3},{68,4},{69,5},{70,6},{71,7},{72,8},{73... | collective-permute-start | bytes 319496 | tf_op jit(solution)/shard_map/ppermute | solution.py:38
  31.4 12.9 %collective-permute-start.5 = (bf16[200,512]{1,0:T(8,128)(2,1)S(1)}, bf16[200,512]{1,0:T(8,128)(2,1)S(1)}, u32[]{:S(2)}, u32[]{:S(2)}) collective-permute-start(bf16[200,512]{1,0:T(8,128)(2,1)S(1)} %constant_dynamic-update-slice_fusion.echo), channel_id=1, source_target_pairs={{4,0},{5,1},{6,2},{7,3},{8,4},{9,5},{10,6},{11,7},{12,8},{13,9},{1... | collective-permute-start | bytes 614408 | tf_op jit(solution)/shard_map/ppermute | solution.py:38
  34.5 11.0 %collective-permute-start.6 = (bf16[200,512]{1,0:T(8,128)(2,1)S(1)}, bf16[200,512]{1,0:T(8,128)(2,1)S(1)}, u32[]{:S(2)}, u32[]{:S(2)}) collective-permute-start(bf16[200,512]{1,0:T(8,128)(2,1)S(1)} %constant_dynamic-update-slice_fusion.echo), channel_id=1, source_target_pairs={{12,0},{13,1},{14,2},{15,3},{0,4},{1,5},{2,6},{3,7},{4,8},{5,9},{6... | collective-permute-start | bytes 614408 | tf_op jit(solution)/shard_map/ppermute | solution.py:38
  34.5 11.0 %collective-permute-start.7 = (bf16[200,512]{1,0:T(8,128)(2,1)S(1)}, bf16[200,512]{1,0:T(8,128)(2,1)S(1)}, u32[]{:S(2)}, u32[]{:S(2)}) collective-permute-start(bf16[200,512]{1,0:T(8,128)(2,1)S(1)} %constant_dynamic-update-slice_fusion.echo), channel_id=1, source_target_pairs={{8,0},{9,1},{10,2},{11,3},{12,4},{13,5},{14,6},{15,7},{0,8},{1,9},... | collective-permute-start | bytes 614408 | tf_op jit(solution)/shard_map/ppermute | solution.py:38
  45.6 11.5 %collective-permute-start.11 = (bf16[200,2048]{1,0:T(8,128)(2,1)S(1)}, bf16[200,2048]{1,0:T(8,128)(2,1)S(1)}, u32[]{:S(2)}, u32[]{:S(2)}) collective-permute-start(bf16[200,2048]{1,0:T(8,128)(2,1)S(1)} %constant_dynamic-update-slice_fusion.4.slab), channel_id=1, source_target_pairs={{1,0},{0,1},{3,2},{2,3},{5,4},{4,5},{7,6},{6,7},{9,8},{8,9},{11,10... | collective-permute-start | bytes 2457608 | tf_op jit(solution)/shard_map/ppermute | solution.py:38
  45.7 11.4 %collective-permute-start.8 = (bf16[208,512]{1,0:T(8,128)(2,1)S(1)}, bf16[208,512]{1,0:T(8,128)(2,1)S(1)}, u32[]{:S(2)}, u32[]{:S(2)}) collective-permute-start(bf16[208,512]{1,0:T(8,128)(2,1)S(1)} %get-tuple-element.48.refs_0_), channel_id=1, source_target_pairs={{96,0},{97,1},{98,2},{99,3},{100,4},{101,5},{102,6},{103,7},{104,8... | collective-permute-start | bytes 638984 | tf_op jit(solution)/shard_map/ppermute | solution.py:38
  46.7 10.4 %collective-permute-start.10 = (bf16[208,256]{1,0:T(8,128)(2,1)S(1)}, bf16[208,256]{1,0:T(8,128)(2,1)S(1)}, u32[]{:S(2)}, u32[]{:S(2)}) collective-permute-start(bf16[208,256]{1,0:T(8,128)(2,1)S(1)} %get-tuple-element.53), channel_id=1, source_target_pairs={{64,0},{65,1},{66,2},{67,3},{68,4},{69,5},{70,6},{71,7},{72,8},{73... | collective-permute-start | bytes 319496 | tf_op jit(solution)/shard_map/ppermute | solution.py:38
  49.1 8.0 %collective-permute-start.9 = (bf16[208,256]{1,0:T(8,128)(2,1)S(1)}, bf16[208,256]{1,0:T(8,128)(2,1)S(1)}, u32[]{:S(2)}, u32[]{:S(2)}) collective-permute-start(bf16[208,256]{1,0:T(8,128)(2,1)S(1)} %get-tuple-element.53), channel_id=1, source_target_pairs={{32,0},{33,1},{34,2},{35,3},{36,4},{37,5},{38,6},{39,7},{40,8},{41... | collective-permute-start | bytes 319496 | tf_op jit(solution)/shard_map/ppermute | solution.py:38
  64.1 3.1 %collective-permute-start.12 = (bf16[200,2048]{1,0:T(8,128)(2,1)S(1)}, bf16[200,2048]{1,0:T(8,128)(2,1)S(1)}, u32[]{:S(2)}, u32[]{:S(2)}) collective-permute-start(bf16[200,2048]{1,0:T(8,128)(2,1)S(1)} %get-tuple-element.62), channel_id=1, source_target_pairs={{1,0},{0,1},{3,2},{2,3},{5,4},{4,5},{7,6},{6,7},{9,8},{8,9},{11,10... | collective-permute-start | bytes 2457608 | tf_op jit(solution)/shard_map/ppermute | solution.py:38
  67.6 7.9 %collective-permute-start.13 = (bf16[200,512]{1,0:T(8,128)(2,1)S(1)}, bf16[200,512]{1,0:T(8,128)(2,1)S(1)}, u32[]{:S(2)}, u32[]{:S(2)}) collective-permute-start(bf16[200,512]{1,0:T(8,128)(2,1)S(1)} %get-tuple-element.70), channel_id=1, source_target_pairs={{4,0},{5,1},{6,2},{7,3},{8,4},{9,5},{10,6},{11,7},{12,8},{13,9},{1... | collective-permute-start | bytes 614408 | tf_op jit(solution)/shard_map/ppermute | solution.py:38
  68.3 12.8 %collective-permute-start.14 = (bf16[200,512]{1,0:T(8,128)(2,1)S(1)}, bf16[200,512]{1,0:T(8,128)(2,1)S(1)}, u32[]{:S(2)}, u32[]{:S(2)}) collective-permute-start(bf16[200,512]{1,0:T(8,128)(2,1)S(1)} %get-tuple-element.72), channel_id=1, source_target_pairs={{12,0},{13,1},{14,2},{15,3},{0,4},{1,5},{2,6},{3,7},{4,8},{5,9},{6... | collective-permute-start | bytes 614408 | tf_op jit(solution)/shard_map/ppermute | solution.py:38
  69.7 11.4 %collective-permute-start.15 = (bf16[200,512]{1,0:T(8,128)(2,1)S(1)}, bf16[200,512]{1,0:T(8,128)(2,1)S(1)}, u32[]{:S(2)}, u32[]{:S(2)}) collective-permute-start(bf16[200,512]{1,0:T(8,128)(2,1)S(1)} %get-tuple-element.71), channel_id=1, source_target_pairs={{8,0},{9,1},{10,2},{11,3},{12,4},{13,5},{14,6},{15,7},{0,8},{1,9},... | collective-permute-start | bytes 614408 | tf_op jit(solution)/shard_map/ppermute | solution.py:38
  71.9 12.7 %collective-permute-start.19 = (bf16[200,512]{1,0:T(8,128)(2,1)S(1)}, bf16[200,512]{1,0:T(8,128)(2,1)S(1)}, u32[]{:S(2)}, u32[]{:S(2)}) collective-permute-start(bf16[200,512]{1,0:T(8,128)(2,1)S(1)} %get-tuple-element.65), channel_id=1, source_target_pairs={{96,0},{97,1},{98,2},{99,3},{100,4},{101,5},{102,6},{103,7},{104,8... | collective-permute-start | bytes 614408 | tf_op jit(solution)/shard_map/ppermute | solution.py:38
  72.0 13.7 %collective-permute-start.20 = (bf16[200,512]{1,0:T(8,128)(2,1)S(1)}, bf16[200,512]{1,0:T(8,128)(2,1)S(1)}, u32[]{:S(2)}, u32[]{:S(2)}) collective-permute-start(bf16[200,512]{1,0:T(8,128)(2,1)S(1)} %get-tuple-element.66), channel_id=1, source_target_pairs={{64,0},{65,1},{66,2},{67,3},{68,4},{69,5},{70,6},{71,7},{72,8},{73... | collective-permute-start | bytes 614408 | tf_op jit(solution)/shard_map/ppermute | solution.py:38
  75.5 10.2 %collective-permute-start.21 = (bf16[200,512]{1,0:T(8,128)(2,1)S(1)}, bf16[200,512]{1,0:T(8,128)(2,1)S(1)}, u32[]{:S(2)}, u32[]{:S(2)}) collective-permute-start(bf16[200,512]{1,0:T(8,128)(2,1)S(1)} %get-tuple-element.67), channel_id=1, source_target_pairs={{32,0},{33,1},{34,2},{35,3},{36,4},{37,5},{38,6},{39,7},{40,8},{41... | collective-permute-start | bytes 614408 | tf_op jit(solution)/shard_map/ppermute | solution.py:38
  81.3 5.4 %collective-permute-start.16 = (bf16[200,128]{1,0:T(8,128)(2,1)S(1)}, bf16[200,128]{1,0:T(8,128)(2,1)S(1)}, u32[]{:S(2)}, u32[]{:S(2)}) collective-permute-start(bf16[200,128]{1,0:T(8,128)(2,1)S(1)} %get-tuple-element.73), channel_id=1, source_target_pairs={{18,0},{19,1},{16,2},{17,3},{22,4},{23,5},{20,6},{21,7},{26,8},{27... | collective-permute-start | bytes 153608 | tf_op jit(solution)/shard_map/ppermute | solution.py:38
  83.2 4.1 %collective-permute-start.17 = (bf16[200,128]{1,0:T(8,128)(2,1)S(1)}, bf16[200,128]{1,0:T(8,128)(2,1)S(1)}, u32[]{:S(2)}, u32[]{:S(2)}) collective-permute-start(bf16[200,128]{1,0:T(8,128)(2,1)S(1)} %get-tuple-element.75), channel_id=1, source_target_pairs={{16,0},{17,1},{18,2},{19,3},{20,4},{21,5},{22,6},{23,7},{24,8},{25... | collective-permute-start | bytes 153608 | tf_op jit(solution)/shard_map/ppermute | solution.py:38
  84.7 5.6 %collective-permute-start.18 = (bf16[200,128]{1,0:T(8,128)(2,1)S(1)}, bf16[200,128]{1,0:T(8,128)(2,1)S(1)}, u32[]{:S(2)}, u32[]{:S(2)}) collective-permute-start(bf16[200,128]{1,0:T(8,128)(2,1)S(1)} %get-tuple-element.74), channel_id=1, source_target_pairs={{2,0},{3,1},{0,2},{1,3},{6,4},{7,5},{4,6},{5,7},{10,8},{11,9},{8,1... | collective-permute-start | bytes 153608 | tf_op jit(solution)/shard_map/ppermute | solution.py:38
  (3 other events, 34.2 us)

commit v10 on v9

--- a/solution.py
+++ b/solution.py
@@ -430,7 +430,7 @@
     for d, part in zip((1, 2, 3), (sums[0], sums[2], sums[1])):
         query_total = query_total + moved(part, dz=-d).astype(F32)
     ent_share = ent_row[:, :width]
-    for k, d in enumerate(FAR):
+    for k, d in ((2, 2), (0, 1), (1, 3)):
         block = ent_row[:, (k + 1) * width : (k + 2) * width].astype(BF16)
         ent_share = ent_share + moved(block, dx=-d).astype(F32)
     return (

time: 91.4 us -> 89.9 us (0.984)
  starting transfers between devices: 31.8 us -> 30.8 us
    ppermute x22, starting transfers between devices: 31.8 us -> 30.8 us  [moved(): return lax.ppermute(block, AXES, route)]
  transfers between devices with their start and end apart: 22 -> 22, of which waited for: 7 -> 8; matrix products, arithmetic and copies ran while one was open for 1% -> 1% of each run, Pallas kernels for 25% -> 26%
where the time goes in v10:
time: 89.9 us; the launch traced here: 89.3 us
  Pallas kernels  41.5 us (46%)
  starting transfers between devices  30.8 us (34%)
  waiting for transfers between devices  11.7 us (13%)
  other arithmetic  2.8 us (3%)
  local copies, waits for them, and re-layouts  1.65 us (2%)
    ppermute x22, starting transfers between devices, moved(): return lax.ppermute(block, AXES, route)  30.8 us
    pallas_call x2, Pallas kernels, encode_heads(): pl.pallas_call(functools.partial(head_kernel, chunk * heads, heads), in_s...  15.2 us
    pallas_call x4, Pallas kernels, score(): pl.pallas_call(functools.partial(score_kernel, plain, plain - 1.8, depth,...  14.8 us
    ppermute x22, waiting for transfers between devices, moved(): return lax.ppermute(block, AXES, route)  11.7 us
    pallas_call x1, Pallas kernels, encode_entities(): pl.pallas_call(functools.partial(entity_kernel, relations, steps, scale),...  11.6 us
  transfers between devices with their start and end apart: 22, of which 8 were waited for; matrix products, arithmetic and copies ran while one was open for 1% of the time, Pallas kernels for 26%

profile of v10, /device:TPU:0, one launch (start us, length us, event | category | flops | bytes accessed | tf_op | source)
XLA Modules:
  0.0 89.3 jit_solution(7446582716323899614)
XLA Ops:
  2.8 11.6 %shard_map.113 = (bf16[200,128]{1,0:T(8,128)(2,1)S(1)}, f32[40960,128]{1,0:T(8,128)S(1)}, bf16[200,6400]{1,0:T(8,128)(2,1)S(1)}, bf16[256,896]{1,0:T(8,128)(2,1)S(1)}) custom-call(s32[12800]{0:T(1024)S(1)} %add_multiply_fusion.own_ids.head_ids, bf16[200,20000]{1,0:T(8,128)(2,1)} %bitcast.21, bf16[200,5000]{1,0:T(8,128)(2,1)} %bitcast.22, ...), custom_call_target="tpu_custom_call" | custom-call | tf_op jit(solution)/shard_map/pallas_call | solution.py:179
  14.4 2.9 %collective-permute-start = (bf16[200,128]{1,0:T(8,128)(2,1)S(1)}, bf16[200,128]{1,0:T(8,128)(2,1)S(1)}, u32[]{:S(2)}, u32[]{:S(2)}) collective-permute-start(bf16[200,128]{1,0:T(8,128)(2,1)S(1)} %get-tuple-element.35.echo), channel_id=1, source_target_pairs={{16,0},{17,1},{18,2},{19,3},{20,4},{21,5},{22,6},{23,7},{24,8},{25... | collective-permute-start | bytes 153608 | tf_op jit(solution)/shard_map/ppermute | solution.py:38
  17.3 2.3 %collective-permute-start.2 = (bf16[200,128]{1,0:T(8,128)(2,1)S(1)}, bf16[200,128]{1,0:T(8,128)(2,1)S(1)}, u32[]{:S(2)}, u32[]{:S(2)}) collective-permute-start(bf16[200,128]{1,0:T(8,128)(2,1)S(1)} %get-tuple-element.35.echo), channel_id=1, source_target_pairs={{2,0},{3,1},{0,2},{1,3},{6,4},{7,5},{4,6},{5,7},{10,8},{11,9},{8,1... | collective-permute-start | bytes 153608 | tf_op jit(solution)/shard_map/ppermute | solution.py:38
  19.6 7.6 %shard_map.114 = (bf16[208,256]{1,0:T(8,128)(2,1)S(1)}, bf16[200,128]{1,0:T(8,128)(2,1)S(1)}, f32[40960,128]{1,0:T(8,128)S(1)}, bf16[200,6400]{1,0:T(8,128)(2,1)S(1)}, bf16[256,896]{1,0:T(8,128)(2,1)S(1)}) custom-call(s32[12800]{0:T(1024)S(1)} %add_multiply_fusion.own_ids.head_ids, ...), custom_call_target="tpu_custom_call", output_to_operand_aliasing={{2}: (6, {}), {3}: (7, {}), {4}: (8, {})} | custom-call | tf_op jit(solution)/shard_map/pallas_call | solution.py:215
  27.2 4.1 %collective-permute-start.3 = (bf16[208,256]{1,0:T(8,128)(2,1)S(1)}, bf16[208,256]{1,0:T(8,128)(2,1)S(1)}, u32[]{:S(2)}, u32[]{:S(2)}) collective-permute-start(bf16[208,256]{1,0:T(8,128)(2,1)S(1)} %get-tuple-element.43.refs_0_), channel_id=1, source_target_pairs={{32,0},{33,1},{34,2},{35,3},{36,4},{37,5},{38,6},{39,7},{40,8},{41... | collective-permute-start | bytes 319496 | tf_op jit(solution)/shard_map/ppermute | solution.py:38
  31.4 3.1 %collective-permute-start.5 = (bf16[200,512]{1,0:T(8,128)(2,1)S(1)}, bf16[200,512]{1,0:T(8,128)(2,1)S(1)}, u32[]{:S(2)}, u32[]{:S(2)}) collective-permute-start(bf16[200,512]{1,0:T(8,128)(2,1)S(1)} %constant_dynamic-update-slice_fusion.echo), channel_id=1, source_target_pairs={{4,0},{5,1},{6,2},{7,3},{8,4},{9,5},{10,6},{11,7},{12,8},{13,9},{1... | collective-permute-start | bytes 614408 | tf_op jit(solution)/shard_map/ppermute | solution.py:38
  34.5 2.2 %collective-permute-start.7 = (bf16[200,512]{1,0:T(8,128)(2,1)S(1)}, bf16[200,512]{1,0:T(8,128)(2,1)S(1)}, u32[]{:S(2)}, u32[]{:S(2)}) collective-permute-start(bf16[200,512]{1,0:T(8,128)(2,1)S(1)} %constant_dynamic-update-slice_fusion.echo), channel_id=1, source_target_pairs={{8,0},{9,1},{10,2},{11,3},{12,4},{13,5},{14,6},{15,7},{0,8},{1,9},... | collective-permute-start | bytes 614408 | tf_op jit(solution)/shard_map/ppermute | solution.py:38
  36.7 7.6 %shard_map.115 = (bf16[208,256]{1,0:T(8,128)(2,1)S(1)}, bf16[200,512]{1,0:T(8,128)(2,1)S(1)}, bf16[208,512]{1,0:T(8,128)(2,1)S(1)}, f32[40960,128]{1,0:T(8,128)S...) custom-call(s32[12800]{0:T(1024)S(1)} %add_multiply_fusion.own_ids.h, ...), custom_call_target="tpu_custom_call", output_to_operand_aliasing={{3}: (6, {}), {4}: (7, {}), {5}: (8, {})} | custom-call | tf_op jit(solution)/shard_map/pallas_call | solution.py:215
  44.4 1.1 %collective-permute-done.6 = bf16[200,512]{1,0:T(8,128)(2,1)S(1)} collective-permute-done((bf16[200,512]{1,0:T(8,128)(2,1)S(1)}, bf16[200,512]{1,0:T(8,128)(2,1)S(1)}, u32[]{:S(2)}, u32[]{:S(2)}) %collective-permute-start.6) | collective-permute-done | bytes 204832 | tf_op jit(solution)/shard_map/ppermute | solution.py:38
  46.7 2.4 %collective-permute-start.10 = (bf16[208,256]{1,0:T(8,128)(2,1)S(1)}, bf16[208,256]{1,0:T(8,128)(2,1)S(1)}, u32[]{:S(2)}, u32[]{:S(2)}) collective-permute-start(bf16[208,256]{1,0:T(8,128)(2,1)S(1)} %get-tuple-element.53), channel_id=1, source_target_pairs={{64,0},{65,1},{66,2},{67,3},{68,4},{69,5},{70,6},{71,7},{72,8},{73... | collective-permute-start | bytes 319496 | tf_op jit(solution)/shard_map/ppermute | solution.py:38
  49.1 2.5 %collective-permute-start.9 = (bf16[208,256]{1,0:T(8,128)(2,1)S(1)}, bf16[208,256]{1,0:T(8,128)(2,1)S(1)}, u32[]{:S(2)}, u32[]{:S(2)}) collective-permute-start(bf16[208,256]{1,0:T(8,128)(2,1)S(1)} %get-tuple-element.53), channel_id=1, source_target_pairs={{32,0},{33,1},{34,2},{35,3},{36,4},{37,5},{38,6},{39,7},{40,8},{41... | collective-permute-start | bytes 319496 | tf_op jit(solution)/shard_map/ppermute | solution.py:38
  51.6 3.8 %shard_map.116 = (f32[2,200,512]{2,1,0:T(8,128)S(1)}, f32[200,2048]{1,0:T(8,128)S(1)}) custom-call(s32[1]{0:T(128)} %bitcast.me, bf16[200,2048]{1,0:T(8,128)(2,1)S(1)} %constant_dynamic-update-slice_fusion.4.slab, bf16[208,512]{1,0:T(8,128)(2,1)S(1)} %get-tuple-element.48.refs_0_, bf16[208,256]{1,0:T(8,128)(2,1)S(1)} %collective-permute-done.3.refs_1_, ...), custom_call_target="tpu_custom_call" | custom-call | tf_op jit(solution)/shard_map/pallas_call | solution.py:358
  55.5 1.6 %collective-permute-done.10.refs_4_.refs_1_ = bf16[208,256]{1,0:T(8,128)(2,1)S(1)} collective-permute-done((bf16[208,256]{1,0:T(8,128)(2,1)S(1)}, bf16[208,256]{1,0:T(8,128)(2,1)S(1)}, u32[]{:S(2)}, u32[]{:S(2)}) %collective-permute-start.10) | collective-permute-done | bytes 106528 | tf_op jit(solution)/shard_map/ppermute | solution.py:38
  57.1 6.9 %shard_map.117 = (f32[4,200,512]{2,1,0:T(8,128)S(1)}, bf16[200,2048]{1,0:T(8,128)(2,1)S(1)}) custom-call(s32[1]{0:T(128)} %bitcast.me, bf16[200,2048]{1,0:T(8,128)(2,1)S(1)} %collective-permute-done.11.slab, bf16[208,512]{1,0:T(8,128)(2,1)S(1)} %get-tuple-element.48.refs_0_, bf16[208,256]{1,0:T(8,128)(2,1)S(1)} %collective-permute-done.3.refs_1_, ...), custom_call_target="tpu_custom_call" | custom-call | tf_op jit(solution)/shard_map/pallas_call | solution.py:358
  64.4 2.8 %shard_map.118 = (f32[4,200,512]{2,1,0:T(8,128)S(1)}, f32[200,1536]{1,0:T(8,128)S(1)}) custom-call(s32[1]{0:T(128)} %bitcast.me, bf16[200,2048]{1,0:T(8,128)(2,1)S(1)} %constant_dynamic-update-slice_fusion.4.slab, bf16[208,256]{1,0:T(8,128)(2,1)S(1)} %collective-permute-done.9.refs_3_.refs_0_, ...), custom_call_target="tpu_custom_call", output_to_operand_aliasing={{0}: (5, {})} | custom-call | tf_op jit(solution)/shard_map/pallas_call | solution.py:358
  68.3 1.4 %collective-permute-start.14 = (bf16[200,512]{1,0:T(8,128)(2,1)S(1)}, bf16[200,512]{1,0:T(8,128)(2,1)S(1)}, u32[]{:S(2)}, u32[]{:S(2)}) collective-permute-start(bf16[200,512]{1,0:T(8,128)(2,1)S(1)} %get-tuple-element.72), channel_id=1, source_target_pairs={{12,0},{13,1},{14,2},{15,3},{0,4},{1,5},{2,6},{3,7},{4,8},{5,9},{6... | collective-permute-start | bytes 614408 | tf_op jit(solution)/shard_map/ppermute | solution.py:38
  69.7 1.1 %collective-permute-start.15 = (bf16[200,512]{1,0:T(8,128)(2,1)S(1)}, bf16[200,512]{1,0:T(8,128)(2,1)S(1)}, u32[]{:S(2)}, u32[]{:S(2)}) collective-permute-start(bf16[200,512]{1,0:T(8,128)(2,1)S(1)} %get-tuple-element.71), channel_id=1, source_target_pairs={{8,0},{9,1},{10,2},{11,3},{12,4},{13,5},{14,6},{15,7},{0,8},{1,9},... | collective-permute-start | bytes 614408 | tf_op jit(solution)/shard_map/ppermute | solution.py:38
  70.8 1.2 %shard_map.119 = (f32[200,512]{1,0:T(8,128)S(1)}, bf16[200,512]{1,0:T(8,128)(2,1)S(1)}, bf16[200,512]{1,0:T(8,128)(2,1)S(1)}, bf16[200,512]{1,0:T(8,128)(2,1)S(1)}, f32[200,512]{1,0:T(8,128)S(1)}) custom-call(s32[1]{0:T(128)} %bitcast.me, bf16[200,2048]{1,0:T(8,128)(2,1)S(1)} %constant_dynamic-update-slice_fusion.4.slab, ...), custom_call_target="tpu_custom_call" | custom-call | tf_op jit(solution)/shard_map/pallas_call | solution.py:358
  72.1 2.2 %collective-permute-start.20 = (bf16[200,512]{1,0:T(8,128)(2,1)S(1)}, bf16[200,512]{1,0:T(8,128)(2,1)S(1)}, u32[]{:S(2)}, u32[]{:S(2)}) collective-permute-start(bf16[200,512]{1,0:T(8,128)(2,1)S(1)} %get-tuple-element.66), channel_id=1, source_target_pairs={{64,0},{65,1},{66,2},{67,3},{68,4},{69,5},{70,6},{71,7},{72,8},{73... | collective-permute-start | bytes 614408 | tf_op jit(solution)/shard_map/ppermute | solution.py:38
  74.3 1.2 %collective-permute-done.13 = bf16[200,512]{1,0:T(8,128)(2,1)S(1)} collective-permute-done((bf16[200,512]{1,0:T(8,128)(2,1)S(1)}, bf16[200,512]{1,0:T(8,128)(2,1)S(1)}, u32[]{:S(2)}, u32[]{:S(2)}) %collective-permute-start.13) | collective-permute-done | bytes 204832 | tf_op jit(solution)/shard_map/ppermute | solution.py:38
  76.5 4.6 %collective-permute-done.14 = bf16[200,512]{1,0:T(8,128)(2,1)S(1)} collective-permute-done((bf16[200,512]{1,0:T(8,128)(2,1)S(1)}, bf16[200,512]{1,0:T(8,128)(2,1)S(1)}, u32[]{:S(2)}, u32[]{:S(2)}) %collective-permute-start.14) | collective-permute-done | bytes 204832 | tf_op jit(solution)/shard_map/ppermute | solution.py:38
  81.3 1.3 %collective-permute-start.16 = (bf16[200,128]{1,0:T(8,128)(2,1)S(1)}, bf16[200,128]{1,0:T(8,128)(2,1)S(1)}, u32[]{:S(2)}, u32[]{:S(2)}) collective-permute-start(bf16[200,128]{1,0:T(8,128)(2,1)S(1)} %get-tuple-element.73), channel_id=1, source_target_pairs={{2,0},{3,1},{0,2},{1,3},{6,4},{7,5},{4,6},{5,7},{10,8},{11,9},{8,1... | collective-permute-start | bytes 153608 | tf_op jit(solution)/shard_map/ppermute | solution.py:38
  83.4 1.1 %collective-permute-done.19 = bf16[200,512]{1,0:T(8,128)(2,1)S(1)} collective-permute-done((bf16[200,512]{1,0:T(8,128)(2,1)S(1)}, bf16[200,512]{1,0:T(8,128)(2,1)S(1)}, u32[]{:S(2)}, u32[]{:S(2)}) %collective-permute-start.19) | collective-permute-done | bytes 204832 | tf_op jit(solution)/shard_map/ppermute | solution.py:38
  84.6 1.4 %collective-permute-start.18 = (bf16[200,128]{1,0:T(8,128)(2,1)S(1)}, bf16[200,128]{1,0:T(8,128)(2,1)S(1)}, u32[]{:S(2)}, u32[]{:S(2)}) collective-permute-start(bf16[200,128]{1,0:T(8,128)(2,1)S(1)} %get-tuple-element.74), channel_id=1, source_target_pairs={{16,0},{17,1},{18,2},{19,3},{20,4},{21,5},{22,6},{23,7},{24,8},{25... | collective-permute-start | bytes 153608 | tf_op jit(solution)/shard_map/ppermute | solution.py:38
  (52 shorter events, 10.3 us)
Async XLA Ops:
  2.8 16.8 %copy-start.2 = (s32[512,4]{0,1:T(4,128)S(1)}, s32[512,4]{0,1:T(4,128)}, u32[]{:S(2)}) copy-start(s32[512,4]{0,1:T(4,128)} %param.15) | copy-start | bytes 24580
  2.8 16.8 %copy-start.3 = (s32[512]{0:T(512)S(1)}, s32[512]{0:T(512)}, u32[]{:S(2)}) copy-start(s32[512]{0:T(512)} %param.14) | copy-start | bytes 6148
  14.4 16.9 %collective-permute-start = (bf16[200,128]{1,0:T(8,128)(2,1)S(1)}, bf16[200,128]{1,0:T(8,128)(2,1)S(1)}, u32[]{:S(2)}, u32[]{:S(2)}) collective-permute-start(bf16[200,128]{1,0:T(8,128)(2,1)S(1)} %get-tuple-element.35.echo), channel_id=1, source_target_pairs={{16,0},{17,1},{18,2},{19,3},{20,4},{21,5},{22,6},{23,7},{24,8},{25... | collective-permute-start | bytes 153608 | tf_op jit(solution)/shard_map/ppermute | solution.py:38
  17.3 14.0 %collective-permute-start.1 = (bf16[200,128]{1,0:T(8,128)(2,1)S(1)}, bf16[200,128]{1,0:T(8,128)(2,1)S(1)}, u32[]{:S(2)}, u32[]{:S(2)}) collective-permute-start(bf16[200,128]{1,0:T(8,128)(2,1)S(1)} %get-tuple-element.35.echo), channel_id=1, source_target_pairs={{18,0},{19,1},{16,2},{17,3},{22,4},{23,5},{20,6},{21,7},{26,8},{27... | collective-permute-start | bytes 153608 | tf_op jit(solution)/shard_map/ppermute | solution.py:38
  17.3 14.1 %collective-permute-start.2 = (bf16[200,128]{1,0:T(8,128)(2,1)S(1)}, bf16[200,128]{1,0:T(8,128)(2,1)S(1)}, u32[]{:S(2)}, u32[]{:S(2)}) collective-permute-start(bf16[200,128]{1,0:T(8,128)(2,1)S(1)} %get-tuple-element.35.echo), channel_id=1, source_target_pairs={{2,0},{3,1},{0,2},{1,3},{6,4},{7,5},{4,6},{5,7},{10,8},{11,9},{8,1... | collective-permute-start | bytes 153608 | tf_op jit(solution)/shard_map/ppermute | solution.py:38
  27.2 17.1 %collective-permute-start.3 = (bf16[208,256]{1,0:T(8,128)(2,1)S(1)}, bf16[208,256]{1,0:T(8,128)(2,1)S(1)}, u32[]{:S(2)}, u32[]{:S(2)}) collective-permute-start(bf16[208,256]{1,0:T(8,128)(2,1)S(1)} %get-tuple-element.43.refs_0_), channel_id=1, source_target_pairs={{32,0},{33,1},{34,2},{35,3},{36,4},{37,5},{38,6},{39,7},{40,8},{41... | collective-permute-start | bytes 319496 | tf_op jit(solution)/shard_map/ppermute | solution.py:38
  31.3 13.0 %collective-permute-start.4 = (bf16[208,256]{1,0:T(8,128)(2,1)S(1)}, bf16[208,256]{1,0:T(8,128)(2,1)S(1)}, u32[]{:S(2)}, u32[]{:S(2)}) collective-permute-start(bf16[208,256]{1,0:T(8,128)(2,1)S(1)} %get-tuple-element.43.refs_0_), channel_id=1, source_target_pairs={{64,0},{65,1},{66,2},{67,3},{68,4},{69,5},{70,6},{71,7},{72,8},{73... | collective-permute-start | bytes 319496 | tf_op jit(solution)/shard_map/ppermute | solution.py:38
  31.4 12.9 %collective-permute-start.5 = (bf16[200,512]{1,0:T(8,128)(2,1)S(1)}, bf16[200,512]{1,0:T(8,128)(2,1)S(1)}, u32[]{:S(2)}, u32[]{:S(2)}) collective-permute-start(bf16[200,512]{1,0:T(8,128)(2,1)S(1)} %constant_dynamic-update-slice_fusion.echo), channel_id=1, source_target_pairs={{4,0},{5,1},{6,2},{7,3},{8,4},{9,5},{10,6},{11,7},{12,8},{13,9},{1... | collective-permute-start | bytes 614408 | tf_op jit(solution)/shard_map/ppermute | solution.py:38
  34.5 11.0 %collective-permute-start.6 = (bf16[200,512]{1,0:T(8,128)(2,1)S(1)}, bf16[200,512]{1,0:T(8,128)(2,1)S(1)}, u32[]{:S(2)}, u32[]{:S(2)}) collective-permute-start(bf16[200,512]{1,0:T(8,128)(2,1)S(1)} %constant_dynamic-update-slice_fusion.echo), channel_id=1, source_target_pairs={{12,0},{13,1},{14,2},{15,3},{0,4},{1,5},{2,6},{3,7},{4,8},{5,9},{6... | collective-permute-start | bytes 614408 | tf_op jit(solution)/shard_map/ppermute | solution.py:38
  34.5 11.0 %collective-permute-start.7 = (bf16[200,512]{1,0:T(8,128)(2,1)S(1)}, bf16[200,512]{1,0:T(8,128)(2,1)S(1)}, u32[]{:S(2)}, u32[]{:S(2)}) collective-permute-start(bf16[200,512]{1,0:T(8,128)(2,1)S(1)} %constant_dynamic-update-slice_fusion.echo), channel_id=1, source_target_pairs={{8,0},{9,1},{10,2},{11,3},{12,4},{13,5},{14,6},{15,7},{0,8},{1,9},... | collective-permute-start | bytes 614408 | tf_op jit(solution)/shard_map/ppermute | solution.py:38
  45.6 11.5 %collective-permute-start.11 = (bf16[200,2048]{1,0:T(8,128)(2,1)S(1)}, bf16[200,2048]{1,0:T(8,128)(2,1)S(1)}, u32[]{:S(2)}, u32[]{:S(2)}) collective-permute-start(bf16[200,2048]{1,0:T(8,128)(2,1)S(1)} %constant_dynamic-update-slice_fusion.4.slab), channel_id=1, source_target_pairs={{1,0},{0,1},{3,2},{2,3},{5,4},{4,5},{7,6},{6,7},{9,8},{8,9},{11,10... | collective-permute-start | bytes 2457608 | tf_op jit(solution)/shard_map/ppermute | solution.py:38
  45.7 11.4 %collective-permute-start.8 = (bf16[208,512]{1,0:T(8,128)(2,1)S(1)}, bf16[208,512]{1,0:T(8,128)(2,1)S(1)}, u32[]{:S(2)}, u32[]{:S(2)}) collective-permute-start(bf16[208,512]{1,0:T(8,128)(2,1)S(1)} %get-tuple-element.48.refs_0_), channel_id=1, source_target_pairs={{96,0},{97,1},{98,2},{99,3},{100,4},{101,5},{102,6},{103,7},{104,8... | collective-permute-start | bytes 638984 | tf_op jit(solution)/shard_map/ppermute | solution.py:38
  46.7 10.4 %collective-permute-start.10 = (bf16[208,256]{1,0:T(8,128)(2,1)S(1)}, bf16[208,256]{1,0:T(8,128)(2,1)S(1)}, u32[]{:S(2)}, u32[]{:S(2)}) collective-permute-start(bf16[208,256]{1,0:T(8,128)(2,1)S(1)} %get-tuple-element.53), channel_id=1, source_target_pairs={{64,0},{65,1},{66,2},{67,3},{68,4},{69,5},{70,6},{71,7},{72,8},{73... | collective-permute-start | bytes 319496 | tf_op jit(solution)/shard_map/ppermute | solution.py:38
  49.1 8.0 %collective-permute-start.9 = (bf16[208,256]{1,0:T(8,128)(2,1)S(1)}, bf16[208,256]{1,0:T(8,128)(2,1)S(1)}, u32[]{:S(2)}, u32[]{:S(2)}) collective-permute-start(bf16[208,256]{1,0:T(8,128)(2,1)S(1)} %get-tuple-element.53), channel_id=1, source_target_pairs={{32,0},{33,1},{34,2},{35,3},{36,4},{37,5},{38,6},{39,7},{40,8},{41... | collective-permute-start | bytes 319496 | tf_op jit(solution)/shard_map/ppermute | solution.py:38
  64.1 3.1 %collective-permute-start.12 = (bf16[200,2048]{1,0:T(8,128)(2,1)S(1)}, bf16[200,2048]{1,0:T(8,128)(2,1)S(1)}, u32[]{:S(2)}, u32[]{:S(2)}) collective-permute-start(bf16[200,2048]{1,0:T(8,128)(2,1)S(1)} %get-tuple-element.62), channel_id=1, source_target_pairs={{1,0},{0,1},{3,2},{2,3},{5,4},{4,5},{7,6},{6,7},{9,8},{8,9},{11,10... | collective-permute-start | bytes 2457608 | tf_op jit(solution)/shard_map/ppermute | solution.py:38
  67.6 7.9 %collective-permute-start.13 = (bf16[200,512]{1,0:T(8,128)(2,1)S(1)}, bf16[200,512]{1,0:T(8,128)(2,1)S(1)}, u32[]{:S(2)}, u32[]{:S(2)}) collective-permute-start(bf16[200,512]{1,0:T(8,128)(2,1)S(1)} %get-tuple-element.70), channel_id=1, source_target_pairs={{4,0},{5,1},{6,2},{7,3},{8,4},{9,5},{10,6},{11,7},{12,8},{13,9},{1... | collective-permute-start | bytes 614408 | tf_op jit(solution)/shard_map/ppermute | solution.py:38
  68.3 12.8 %collective-permute-start.14 = (bf16[200,512]{1,0:T(8,128)(2,1)S(1)}, bf16[200,512]{1,0:T(8,128)(2,1)S(1)}, u32[]{:S(2)}, u32[]{:S(2)}) collective-permute-start(bf16[200,512]{1,0:T(8,128)(2,1)S(1)} %get-tuple-element.72), channel_id=1, source_target_pairs={{12,0},{13,1},{14,2},{15,3},{0,4},{1,5},{2,6},{3,7},{4,8},{5,9},{6... | collective-permute-start | bytes 614408 | tf_op jit(solution)/shard_map/ppermute | solution.py:38
  69.7 11.4 %collective-permute-start.15 = (bf16[200,512]{1,0:T(8,128)(2,1)S(1)}, bf16[200,512]{1,0:T(8,128)(2,1)S(1)}, u32[]{:S(2)}, u32[]{:S(2)}) collective-permute-start(bf16[200,512]{1,0:T(8,128)(2,1)S(1)} %get-tuple-element.71), channel_id=1, source_target_pairs={{8,0},{9,1},{10,2},{11,3},{12,4},{13,5},{14,6},{15,7},{0,8},{1,9},... | collective-permute-start | bytes 614408 | tf_op jit(solution)/shard_map/ppermute | solution.py:38
  72.0 12.6 %collective-permute-start.19 = (bf16[200,512]{1,0:T(8,128)(2,1)S(1)}, bf16[200,512]{1,0:T(8,128)(2,1)S(1)}, u32[]{:S(2)}, u32[]{:S(2)}) collective-permute-start(bf16[200,512]{1,0:T(8,128)(2,1)S(1)} %get-tuple-element.65), channel_id=1, source_target_pairs={{96,0},{97,1},{98,2},{99,3},{100,4},{101,5},{102,6},{103,7},{104,8... | collective-permute-start | bytes 614408 | tf_op jit(solution)/shard_map/ppermute | solution.py:38
  72.1 13.9 %collective-permute-start.20 = (bf16[200,512]{1,0:T(8,128)(2,1)S(1)}, bf16[200,512]{1,0:T(8,128)(2,1)S(1)}, u32[]{:S(2)}, u32[]{:S(2)}) collective-permute-start(bf16[200,512]{1,0:T(8,128)(2,1)S(1)} %get-tuple-element.66), channel_id=1, source_target_pairs={{64,0},{65,1},{66,2},{67,3},{68,4},{69,5},{70,6},{71,7},{72,8},{73... | collective-permute-start | bytes 614408 | tf_op jit(solution)/shard_map/ppermute | solution.py:38
  75.5 10.4 %collective-permute-start.21 = (bf16[200,512]{1,0:T(8,128)(2,1)S(1)}, bf16[200,512]{1,0:T(8,128)(2,1)S(1)}, u32[]{:S(2)}, u32[]{:S(2)}) collective-permute-start(bf16[200,512]{1,0:T(8,128)(2,1)S(1)} %get-tuple-element.67), channel_id=1, source_target_pairs={{32,0},{33,1},{34,2},{35,3},{36,4},{37,5},{38,6},{39,7},{40,8},{41... | collective-permute-start | bytes 614408 | tf_op jit(solution)/shard_map/ppermute | solution.py:38
  81.3 5.9 %collective-permute-start.16 = (bf16[200,128]{1,0:T(8,128)(2,1)S(1)}, bf16[200,128]{1,0:T(8,128)(2,1)S(1)}, u32[]{:S(2)}, u32[]{:S(2)}) collective-permute-start(bf16[200,128]{1,0:T(8,128)(2,1)S(1)} %get-tuple-element.73), channel_id=1, source_target_pairs={{2,0},{3,1},{0,2},{1,3},{6,4},{7,5},{4,6},{5,7},{10,8},{11,9},{8,1... | collective-permute-start | bytes 153608 | tf_op jit(solution)/shard_map/ppermute | solution.py:38
  82.7 5.3 %collective-permute-start.17 = (bf16[200,128]{1,0:T(8,128)(2,1)S(1)}, bf16[200,128]{1,0:T(8,128)(2,1)S(1)}, u32[]{:S(2)}, u32[]{:S(2)}) collective-permute-start(bf16[200,128]{1,0:T(8,128)(2,1)S(1)} %get-tuple-element.75), channel_id=1, source_target_pairs={{18,0},{19,1},{16,2},{17,3},{22,4},{23,5},{20,6},{21,7},{26,8},{27... | collective-permute-start | bytes 153608 | tf_op jit(solution)/shard_map/ppermute | solution.py:38
  84.6 4.1 %collective-permute-start.18 = (bf16[200,128]{1,0:T(8,128)(2,1)S(1)}, bf16[200,128]{1,0:T(8,128)(2,1)S(1)}, u32[]{:S(2)}, u32[]{:S(2)}) collective-permute-start(bf16[200,128]{1,0:T(8,128)(2,1)S(1)} %get-tuple-element.74), channel_id=1, source_target_pairs={{16,0},{17,1},{18,2},{19,3},{20,4},{21,5},{22,6},{23,7},{24,8},{25... | collective-permute-start | bytes 153608 | tf_op jit(solution)/shard_map/ppermute | solution.py:38
  (3 other events, 34.2 us)
